TPU v7x, 32 devices: a whole 2x2x4 slice. The times are simulated.
32 devices in a mesh: aux: 4 (over y, core), pair: 8 (over z, x).
Axes of the slice: x: 2, y: 2, z: 4, core: 2. Of those that a mesh axis runs over, the one named last changes fastest.
Arguments:
- amplitudes: bfloat16 [16384, 512], P('pair', 'aux'), may hold values from -4 to 4
- coulomb: bfloat16 [16384, 512], P('pair'), may hold values from -12 to 12
- df_factors: bfloat16 [16384, 2048], P('pair', 'aux'), may hold values from -0.111328125 to 0.111328125
- thc_left: bfloat16 [512, 1536], P('pair', 'aux'), may hold values from -0.50390625 to 0.50390625
- thc_right: bfloat16 [512, 1536], P('pair', 'aux'), may hold values from -0.50390625 to 0.50390625
- occ_energy: float32 [32], P('pair'), may hold values from -2 to -0.5
- vir_energy: float32 [512], replicated, may hold values from 0.5 to 3
- pivot_energy: float32 [1], replicated, may hold values from -2 to -0.5
Outputs:
- updated: bfloat16 [16384, 512], P('pair', 'aux')
All inputs are finite; a program needn't handle non-finite values.
Results may differ from a plain program's by a relative error of at most 0.0051.
Values may be sent and summed in bfloat16 or wider, within the bound.
No kernel may reach another device: no remote copies, remote signals or barrier semaphores. Data moves between devices by JAX's collectives and lax.ppermute only.
A program may use at most 64 MiB of HBM per device.

v0:
```python
import jax
import jax.numpy as jnp
from jax import lax
from jax.sharding import PartitionSpec as P

ITERS = 2


def per_device(
    amplitudes, coulomb, df_factors, thc_left, thc_right, occ_energy, vir_energy, pivot_energy
):
    column_index = lax.axis_index("aux")
    width = amplitudes.shape[1]
    rows = amplitudes.shape[0]
    nvirt = vir_energy.shape[0]
    nocc_local = rows // nvirt
    denom_full = (
        vir_energy[None, :, None]
        + vir_energy[None, None, :]
        - occ_energy[:, None, None]
        - pivot_energy[0]
    ).reshape(rows, nvirt)
    local = amplitudes
    whole = None
    for step in range(ITERS):
        whole = lax.all_gather(local, "aux", axis=1, tiled=True)
        left, right = (
            lax.all_gather(thc_left, "pair", axis=0, tiled=True),
            lax.all_gather(thc_right, "pair", axis=0, tiled=True),
        )
        gram = lax.dot_general(
            df_factors, whole, (((0,), (0,)), ((), ())), preferred_element_type=jnp.float32
        )
        gram = lax.psum(gram, "pair").astype(jnp.bfloat16)
        proj = jnp.dot(whole, right, preferred_element_type=jnp.float32).reshape(
            nocc_local, nvirt, right.shape[1]
        )
        middle = jnp.sum(proj * left.astype(jnp.float32)[None], axis=1)
        weighted = (
            (left.astype(jnp.float32)[None] * middle[:, None, :])
            .astype(jnp.bfloat16)
            .reshape(rows, right.shape[1])
        )
        ladder = lax.dot_general(
            weighted, right, (((1,), (1,)), ((), ())), preferred_element_type=jnp.float32
        )
        cycle = jnp.dot(df_factors, gram, preferred_element_type=jnp.float32)
        part = cycle + ladder
        share = lax.psum_scatter(part, "aux", scatter_dimension=1, tiled=True)
        coulomb_block = lax.dynamic_slice_in_dim(coulomb, column_index * width, width, 1)
        denom_block = lax.dynamic_slice_in_dim(denom_full, column_index * width, width, 1)
        local = ((coulomb_block.astype(jnp.float32) + share) / denom_block).astype(jnp.bfloat16)
        whole = None
    return local


def solution(mesh):
    in_specs = (
        P("pair", "aux"),
        P("pair", None),
        P("pair", "aux"),
        P("pair", "aux"),
        P("pair", "aux"),
        P("pair"),
        P(),
        P(),
    )
    out_specs = P("pair", "aux")
    return jax.shard_map(
        per_device, mesh=mesh, in_specs=in_specs, out_specs=out_specs, check_vma=False
    )
```

profile of v0, /device:TPU:0, one launch (start us, length us, event | category | flops | bytes accessed | tf_op | source)
XLA Modules:
  0.0 362.0 jit_solution(3160497509930236617)
XLA Ops:
  6.5 0.0 copy-start
  6.5 0.0 all-gather.3.cloned.1.call-start
  6.5 0.7 all-gather.3.cloned.1.call-update
  7.3 0.0 reduce-scatter.3.cloned.1.call-start
  7.3 33.0 %all_gather.15 = bf16[512,384]{1,0:T(8,128)(2,1)S(1)} all-gather(bf16[64,384]{1,0:T(8,128)(2,1)} %param.11), channel_id=1, replica_groups=mesh['aux'=4,'pair'=8] {'pair'}, dimensions={0}, use_global_device_ids=true | all-gather | bytes 442368 | tf_op jit(solution)/shard_map/all_gather | solution.py:28
  40.3 0.1 convert_element_type.38
  40.4 0.0 copy-done.6
  40.4 31.1 %all_gather.16 = bf16[512,384]{1,0:T(8,128)(2,1)S(1)} all-gather(bf16[64,384]{1,0:T(8,128)(2,1)S(1)} %copy-done.6), channel_id=1, replica_groups=mesh['aux'=4,'pair'=8] {'pair'}, dimensions={0}, use_global_device_ids=true | all-gather | bytes 442368 | tf_op jit(solution)/shard_map/all_gather | solution.py:29
  71.5 3.0 multiply_reduce_fusion.1
  74.5 1.5 multiply_convert_fusion.1
  76.0 0.0 copy-done
  76.0 0.0 copy-done.4
  76.0 2.3 fusion.9
  78.2 73.6 %all-reduce.2 = bf16[512,512]{1,0:T(8,128)(2,1)} all-reduce(f32[512,512]{1,0:T(8,128)} %fusion.9), channel_id=1, replica_groups=mesh['aux'=4,'pair'=8] {'pair'}, use_global_device_ids=true, to_apply=%region_0.0 | all-reduce | flops 262144 | bytes 1572864 | tf_op jit(solution)/shard_map/psum | solution.py:34
  151.8 2.5 fusion.11
  154.3 0.0 copy-done.2
  154.3 3.3 bitcast_add_fusion.1
  157.6 0.0 reduce-scatter.3.cloned.1.call-update
  157.6 0.0 copy-start.7
  157.6 0.0 all-gather.5.cloned.1.call-start
  157.7 1.9 constant_dynamic-slice_fusion
  159.6 2.1 copy.15
  161.6 0.0 copy-done.7
  161.6 0.1 broadcast_add_fusion
  161.8 0.7 sub.27
  162.5 0.0 copy-start.8
  162.5 3.9 %copy.17 = f32[64,8,4,512]{3,1,2,0:T(8,128)} copy(f32[64,8,4,512]{3,2,1,0:T(4,128)S(1)} %bitcast.38) | data formatting | bytes 8388608
  166.4 0.0 copy-done.8
  166.4 0.1 broadcast_bitcast_fusion
  167.1 32.7 %reduce-scatter.3.cloned.1.call-done = f32[2048,128]{0,1:T(8,128)} async-done(((f32[2048,512]{0,1:T(8,128)}), f32[2048,128]{0,1:T(8,128)}) %reduce-scatter.3.cloned.1.call-update) | async-done | bytes 1048592 | tf_op jit(solution)/shard_map/reduce_scatter | solution.py:49
  199.9 2.7 fusion.1
  202.6 0.0 all-gather.5.cloned.1.call-update
  202.6 0.0 reduce-scatter.5.cloned.1.call-start
  202.7 22.7 %all-gather.5.cloned.1.call-done = bf16[2048,512]{0,1:T(8,128)(2,1)} async-done(((bf16[2048,128]{0,1:T(8,128)(2,1)}), bf16[2048,512]{0,1:T(8,128)(2,1)}) %all-gather.5.cloned.1.call-update) | async-done | bytes 2097168 | tf_op jit(solution)/shard_map/all_gather | solution.py:26
  225.4 3.0 multiply_reduce_fusion
  228.4 1.5 multiply_convert_fusion
  229.9 0.0 copy-done.5
  229.9 2.2 convolution_bitcast_fusion
  232.2 73.3 %all-reduce.3 = bf16[512,512]{0,1:T(8,128)(2,1)S(1)} all-reduce(f32[512,512]{0,1:T(8,128)} %convolution_bitcast_fusion), channel_id=1, replica_groups=mesh['aux'=4,'pair'=8] {'pair'}, use_global_device_ids=true, to_apply=%region_3.0 | all-reduce | flops 262144 | bytes 1572864 | tf_op jit(solution)/shard_map/psum | solution.py:34
  305.5 0.0 copy-start.1
  305.5 1.3 fusion.10
  306.8 0.1 copy-done.1
  306.9 3.3 bitcast_add_fusion
  310.2 0.0 reduce-scatter.5.cloned.1.call-update
  310.2 42.4 %reduce-scatter.5.cloned.1.call-done = f32[2048,128]{0,1:T(8,128)} async-done(((f32[2048,512]{0,1:T(8,128)}), f32[2048,128]{0,1:T(8,128)}) %reduce-scatter.5.cloned.1.call-update) | async-done | bytes 1048592 | tf_op jit(solution)/shard_map/reduce_scatter | solution.py:49
  352.6 0.0 copy-done.3
  352.7 1.8 fusion.3
  354.4 1.0 copy.12
  (7 shorter events, 0.0 us)
Async XLA Ops:
  6.5 69.4 %copy-start = (bf16[2048,512]{1,0:T(8,128)(2,1)S(1)}, bf16[2048,512]{1,0:T(8,128)(2,1)}, u32[]{:S(2)}) copy-start(bf16[2048,512]{1,0:T(8,128)(2,1)} %param.10) | copy-start | bytes 6291460
  6.5 33.9 %copy-start.6 = (bf16[64,384]{1,0:T(8,128)(2,1)S(1)}, bf16[64,384]{1,0:T(8,128)(2,1)}, u32[]{:S(2)}) copy-start(bf16[64,384]{1,0:T(8,128)(2,1)} %param.12) | copy-start | bytes 147460
  6.5 64.9 %all-gather.3.cloned.1.call-start = ((), (), s32[]{:S(2)}) async-start(), calls=%async_computation.2 | async-start | bytes 2621440 | tf_op jit(solution)/shard_map/all_gather | solution.py:26
  7.3 192.6 %reduce-scatter.3.cloned.1.call-start = ((), (), s32[]{:S(2)}) async-start(), calls=%async_computation.3 | async-start | bytes 5242880 | tf_op jit(solution)/shard_map/reduce_scatter | solution.py:49
  71.5 4.5 %copy-start.4 = (bf16[2048,512]{1,0:T(8,128)(2,1)S(1)}, bf16[2048,512]{1,0:T(8,128)(2,1)}, u32[]{:S(2)}) copy-start(bf16[2048,512]{1,0:T(8,128)(2,1)} %all-gather.3.cloned.1.call-done) | copy-start | bytes 6291460
  151.8 2.5 copy-start.2
  157.6 4.0 %copy-start.7 = (f32[512]{0:T(512)S(1)}, f32[512]{0:T(512)}, u32[]{:S(2)}) copy-start(f32[512]{0:T(512)} %param.14) | copy-start | bytes 6148
  157.6 67.7 %all-gather.5.cloned.1.call-start = ((), (), s32[]{:S(2)}) async-start(), calls=%async_computation.4 | async-start | bytes 2621440 | tf_op jit(solution)/shard_map/all_gather | solution.py:26
  162.5 3.9 %copy-start.8 = (f32[4]{0:T(128)S(1)}, f32[4]{0:T(128)}, u32[]{:S(2)}) copy-start(f32[4]{0:T(128)} %param.13) | copy-start | bytes 52
  202.6 150.0 %reduce-scatter.5.cloned.1.call-start = ((), (), s32[]{:S(2)}) async-start(), calls=%async_computation.5 | async-start | bytes 5242880 | tf_op jit(solution)/shard_map/reduce_scatter | solution.py:49
  225.4 4.5 %copy-start.5 = (bf16[2048,512]{0,1:T(8,128)(2,1)S(1)}, bf16[2048,512]{0,1:T(8,128)(2,1)}, u32[]{:S(2)}) copy-start(bf16[2048,512]{0,1:T(8,128)(2,1)} %all-gather.5.cloned.1.call-done) | copy-start | bytes 6291460
  305.5 1.4 copy-start.1
  310.2 42.5 %copy-start.3 = (bf16[2048,128]{0,1:T(8,128)(2,1)S(1)}, bf16[2048,128]{0,1:T(8,128)(2,1)}, u32[]{:S(2)}) copy-start(bf16[2048,128]{0,1:T(8,128)(2,1)} %copy.15) | copy-start | bytes 1572868
Sparse Core Ops, SparseCore 0:
  8.9 25.5 all-gather.2
  157.7 42.0 reduce-scatter.2
  202.8 22.5 all-gather.4
  310.3 42.2 reduce-scatter.4
where the time goes:
time: 362 us
  blocking collectives  211 us (58%)
  waiting for transfers between devices  98.6 us (27%)
  matrix products  20.9 us (6%)
  between operations  13.9 us (4%)
  local copies, waits for them, and re-layouts  9.77 us (3%)
  other arithmetic  7.65 us (2%)
    psum x2, blocking collectives, per_device(): gram = lax.psum(gram, 'pair').astype(jnp.bfloat16)  147 us
    reduce_scatter x2, waiting for transfers between devices, per_device(): share = lax.psum_scatter(part, 'aux', scatter_dimension=1, tiled=True)  75.2 us
    all_gather x1, blocking collectives, per_device(): lax.all_gather(thc_left, 'pair', axis=0, tiled=True)  33 us
    all_gather x1, blocking collectives, per_device(): lax.all_gather(thc_right, 'pair', axis=0, tiled=True)  31.1 us
    all_gather x2, waiting for transfers between devices, per_device(): whole = lax.all_gather(local, 'aux', axis=1, tiled=True)  22.7 us
  transfers between devices with their start and end apart: 4, of which 3 were waited for; matrix products, arithmetic and copies ran while one was open for 2% of the time, Pallas kernels for 0%

commit v1 on v0

v1 whole, which is shorter than its diff:
```python
import jax
import jax.numpy as jnp
from jax import lax
from jax.sharding import PartitionSpec as P

ITERS = 2
BF = jnp.bfloat16
F32 = jnp.float32


def xor(n, s):
    return [(i, i ^ s) for i in range(n)]


def dot(a, b, ca, cb):
    return lax.dot_general(a, b, (((ca,), (cb,)), ((), ())), preferred_element_type=F32)


def take(a, start, size):
    return lax.dynamic_slice_in_dim(a, start, size, 0)


def put(a, block, start):
    return lax.dynamic_update_slice_in_dim(a, block, start, 0)


def all_reduce(v, n):
    me = lax.axis_index("pair")
    low, high = me % 2, me // 2
    m = n // 2
    half = v.shape[0] // 2
    part = half // m

    def send(a, s):
        return lax.ppermute(a, "pair", xor(n, s))

    acc = take(v, low * half, half) + send(
        take(v, (1 - low) * half, half).astype(BF), 1
    ).astype(F32)
    rounded = acc.astype(BF)
    total = take(acc, high * part, part)
    for s in range(1, m):
        total = total + send(take(rounded, (high ^ s) * part, part), 2 * s).astype(F32)
    mine = total.astype(BF)
    line = put(jnp.zeros((half, v.shape[1]), BF), mine, high * part)
    for s in range(1, m):
        line = put(line, send(mine, 2 * s), (high ^ s) * part)
    other = send(line, 1)
    whole = put(jnp.zeros(v.shape, BF), line, low * half)
    return put(whole, other, (1 - low) * half)


def per_device(
    amplitudes, coulomb, df_factors, thc_left, thc_right, occ_energy, vir_energy, pivot_energy
):
    n_pair = lax.axis_size("pair")
    n_aux = lax.axis_size("aux")
    k = lax.axis_index("aux")
    me = lax.axis_index("pair")
    rows, width = amplitudes.shape
    nvirt = vir_energy.shape[0]
    nocc = rows // nvirt
    naux = df_factors.shape[1]

    def over(a, s):
        return lax.ppermute(a, "aux", xor(n_aux, s))

    amps = [amplitudes, over(amplitudes, 1), over(amplitudes, 2)]
    amps.append(over(amps[2], 1))

    fac = jnp.stack([thc_left, thc_right])
    fac = jnp.concatenate([fac, over(fac, 2)], axis=2)
    step, axis = n_pair // 2, 0
    while step:
        got = lax.ppermute(fac, "pair", xor(n_pair, step))
        first = (me // step) % 2 == 0
        fac = jnp.stack([jnp.where(first, fac, got), jnp.where(first, got, fac)], axis=axis)
        step, axis = step // 2, axis + 1
    cols = fac.shape[-1]
    fac = fac.reshape(n_pair, 2, -1, cols)
    left_half = fac[:, 0].reshape(nvirt, cols)
    right_half = fac[:, 1].reshape(nvirt, cols)
    sent = jnp.concatenate([left_half, take(right_half, (k ^ 1) * width, width)], axis=0)
    got = over(sent, 1)
    left = jnp.concatenate([left_half, got[:nvirt]], axis=1)
    right = jnp.concatenate([take(right_half, k * width, width), got[nvirt:]], axis=1)

    own = [df_factors[i * nvirt : (i + 1) * nvirt] for i in range(nocc)]
    core = over(df_factors, 1)
    core = [core[i * nvirt : (i + 1) * nvirt] for i in range(nocc)]
    far = [over(a, 2) for a in own]
    far_core = [over(a, 1) for a in far]
    factors = [list(blocks) for blocks in zip(own, core, far, far_core)]

    gram = jnp.concatenate([dot(df_factors, t, 0, 0) for t in amps], axis=0)
    gram = all_reduce(gram, n_pair)
    blocks = [gram[r * naux : (r + 1) * naux] for r in range(n_aux)]
    blocks = [blocks[0]] + [over(blocks[r], r) for r in range(1, n_aux)]

    t = [amplitudes[i * nvirt : (i + 1) * nvirt] for i in range(nocc)]
    vir_block = lax.dynamic_slice_in_dim(vir_energy, k * width, width, 0)
    coulomb_block = lax.dynamic_slice_in_dim(coulomb, k * width, width, 1)
    for step in range(ITERS):
        if step:
            gram = jnp.concatenate(
                [
                    sum(dot(factors[i][r], t[i], 0, 0) for i in range(nocc))
                    for r in range(n_aux)
                ],
                axis=0,
            )
            gram = all_reduce(gram, n_pair)
            blocks = [gram[r * naux : (r + 1) * naux] for r in range(n_aux)]
        middle = jnp.stack(
            [jnp.sum(dot(a, left, 0, 0) * right.astype(F32), axis=0) for a in t]
        )
        other = over(middle, 1)
        middle = middle + jnp.concatenate([other[:, cols:], other[:, :cols]], axis=1)
        other = over(middle, 2).reshape(nocc, 2, 2, cols // 2)
        middle = middle + other[:, :, ::-1].reshape(nocc, 2 * cols)
        new = []
        for i in range(nocc):
            scaled = (right.astype(F32) * middle[i][None, :]).astype(BF)
            res = dot(left, scaled, 1, 1)
            for r in range(n_aux):
                res = res + dot(factors[i][r], blocks[r], 1, 0)
            denom = (
                vir_energy[:, None] + vir_block[None, :] - occ_energy[i] - pivot_energy[0]
            )
            base = coulomb_block[i * nvirt : (i + 1) * nvirt].astype(F32)
            new.append(((base + res) / denom).astype(BF))
        t = new
    return jnp.concatenate(t, axis=0)


def solution(mesh):
    in_specs = (
        P("pair", "aux"),
        P("pair", None),
        P("pair", "aux"),
        P("pair", "aux"),
        P("pair", "aux"),
        P("pair"),
        P(),
        P(),
    )
    out_specs = P("pair", "aux")
    return jax.shard_map(
        per_device, mesh=mesh, in_specs=in_specs, out_specs=out_specs, check_vma=False
    )
```

time: 362 us -> 199 us (0.55)
  blocking collectives: 211 us -> 0 us
  matrix products: 20.9 us -> 74.7 us
  waiting for transfers between devices: 98.6 us -> 52.3 us
  starting transfers between devices: 0.12 us -> 44.7 us
  between operations: 13.9 us -> 1.82 us
  local copies, waits for them, and re-layouts: 9.77 us -> 16 us
    psum x2 -> x0, blocking collectives: 147 us -> none  [per_device(): gram = lax.psum(gram, 'pair').astype(jnp.bfloat16)]
    reduce_scatter x2 -> x0, waiting for transfers between devices: 75.2 us -> none  [per_device(): share = lax.psum_scatter(part, 'aux', scatter_dimension=1, tiled=True)]
    all_gather x2 -> x0, blocking collectives: 64.1 us -> none  [the longest x1 33 us: per_device(): lax.all_gather(thc_left, 'pair', axis=0, tiled=True)]
    dot_general x8 -> x68, matrix products: 20.9 us -> 74.7 us  [dot(): lax.dot_general(a, b, (((ca,), (cb,)), ((), ())), preferred_element_type=...]
    ppermute x0 -> x40, waiting for transfers between devices: none -> 52.3 us  [the longest x16 37.7 us: send(): return lax.ppermute(a, 'pair', xor(n, s))]
    ppermute x0 -> x40, starting transfers between devices: none -> 44.7 us  [the longest x16 22 us: send(): return lax.ppermute(a, 'pair', xor(n, s))]
    all_gather x2 -> x0, waiting for transfers between devices: 22.7 us -> none  [per_device(): whole = lax.all_gather(local, 'aux', axis=1, tiled=True)]
    convert_element_type x5 -> x3, other arithmetic: 7.52 us -> 1.31 us  [the longest x2 1.27 us: all_reduce(): rounded = acc.astype(BF)]
  transfers between devices with their start and end apart: 4 -> 40, of which waited for: 3 -> 18; matrix products, arithmetic and copies ran while one was open for 2% -> 28% of each run, Pallas kernels for 0% -> 0%
where the time goes in v1:
time: 199 us; the launch traced here: 197 us
  matrix products  74.7 us (38%)
  waiting for transfers between devices  52.3 us (26%)
  starting transfers between devices  44.7 us (22%)
  local copies, waits for them, and re-layouts  16 us (8%)
  other arithmetic  7.25 us (4%)
    dot_general x68, matrix products, dot(): lax.dot_general(a, b, (((ca,), (cb,)), ((), ())), preferred_element_type=...  74.7 us
    ppermute x16, waiting for transfers between devices, send(): return lax.ppermute(a, 'pair', xor(n, s))  37.7 us
    ppermute x16, starting transfers between devices, send(): return lax.ppermute(a, 'pair', xor(n, s))  22 us
    ppermute x21, starting transfers between devices, over(): return lax.ppermute(a, 'aux', xor(n_aux, s))  17.6 us
    ppermute x21, waiting for transfers between devices, over(): return lax.ppermute(a, 'aux', xor(n_aux, s))  9.49 us
    ppermute x3, waiting for transfers between devices, per_device(): got = lax.ppermute(fac, 'pair', xor(n_pair, step))  5.13 us
    ppermute x3, starting transfers between devices, per_device(): got = lax.ppermute(fac, 'pair', xor(n_pair, step))  5.13 us
  transfers between devices with their start and end apart: 40, of which 18 were waited for; matrix products, arithmetic and copies ran while one was open for 28% of the time, Pallas kernels for 0%

profile of v1, /device:TPU:0, one launch (start us, length us, event | category | flops | bytes accessed | tf_op | source)
XLA Modules:
  0.0 196.8 jit_solution(9112321543437908742)
XLA Ops:
  0.9 3.0 %collective-permute-start = (bf16[2,64,384]{2,1,0:T(8,128)(2,1)S(1)}, bf16[2,64,384]{2,1,0:T(8,128)(2,1)S(1)}, u32[]{:S(2)}, u32[]{:S(2)}) collective-permute-start(bf16[2,64,384]{2,1,0:T(8,128)(2,1)S(1)} %pad_maximum_fusion.10), channel_id=1, source_target_pairs={{0,16},{8,24},{16,0},{24,8},{1,17},{9,25},{17,1},{25,9},{2,18},{10... | collective-permute-start | bytes 294920 | tf_op jit(solution)/shard_map/ppermute | solution.py:66
  4.5 2.7 %collective-permute-done = bf16[2,64,384]{2,1,0:T(8,128)(2,1)S(1)} collective-permute-done((bf16[2,64,384]{2,1,0:T(8,128)(2,1)S(1)}, bf16[2,64,384]{2,1,0:T(8,128)(2,1)S(1)}, u32[]{:S(2)}, u32[]{:S(2)}) %collective-permute-start) | collective-permute-done | bytes 98336 | tf_op jit(solution)/shard_map/ppermute | solution.py:66
  8.0 3.2 %collective-permute-start.1 = (bf16[2,64,768]{2,1,0:T(8,128)(2,1)S(1)}, bf16[2,64,768]{2,1,0:T(8,128)(2,1)S(1)}, u32[]{:S(2)}, u32[]{:S(2)}) collective-permute-start(bf16[2,64,768]{2,1,0:T(8,128)(2,1)S(1)} %pad_maximum_fusion.9), channel_id=1, source_target_pairs={{0,4},{1,5},{2,6},{3,7},{4,0},{5,1},{6,2},{7,3},{8,12},{9,13},{10,... | collective-permute-start | bytes 589832 | tf_op jit(solution)/shard_map/ppermute | solution.py:75
  11.3 2.4 %fusion.154 = f32[512,128]{1,0:T(8,128)S(1)} fusion(bf16[2048,512]{1,0:T(8,128)(2,1)} %param.10, bf16[2048,128]{1,0:T(8,128)(2,1)} %param.8), kind=kOutput, calls=%fused_computation.271 | convolution fusion | flops 268435456 | bytes 2883584 | tf_op jit(solution)/shard_map/dot_general | solution.py:16
  13.7 5.1 %collective-permute-done.1 = bf16[2,64,768]{2,1,0:T(8,128)(2,1)S(1)} collective-permute-done((bf16[2,64,768]{2,1,0:T(8,128)(2,1)S(1)}, bf16[2,64,768]{2,1,0:T(8,128)(2,1)S(1)}, u32[]{:S(2)}, u32[]{:S(2)}) %collective-permute-start.1) | collective-permute-done | bytes 196640 | tf_op jit(solution)/shard_map/ppermute | solution.py:75
  19.4 1.8 fusion.156
  21.2 1.8 fusion.155
  27.5 1.5 collective-permute-start.21
  30.9 2.8 %collective-permute-done.10 = bf16[1024,128]{1,0:T(8,128)(2,1)} collective-permute-done((bf16[1024,128]{1,0:T(8,128)(2,1)}, bf16[1024,128]{1,0:T(8,128)(2,1)}, u32[]{:S(2)}, u32[]{:S(2)}) %collective-permute-start.10) | collective-permute-done | bytes 262176 | tf_op jit(solution)/shard_map/ppermute | solution.py:35
  34.9 1.7 collective-permute-start.11
  36.6 1.8 collective-permute-start.12
  39.9 1.6 collective-permute-start.24
  41.5 3.4 %collective-permute-done.12 = bf16[256,128]{1,0:T(8,128)(2,1)S(1)} collective-permute-done((bf16[256,128]{1,0:T(8,128)(2,1)S(1)}, bf16[256,128]{1,0:T(8,128)(2,1)S(1)}, u32[]{:S(2)}, u32[]{:S(2)}) %collective-permute-start.12) | collective-permute-done | bytes 65568 | tf_op jit(solution)/shard_map/ppermute | solution.py:35
  47.2 3.6 %collective-permute-done.14 = bf16[256,128]{1,0:T(8,128)(2,1)S(1)} collective-permute-done((bf16[256,128]{1,0:T(8,128)(2,1)S(1)}, bf16[256,128]{1,0:T(8,128)(2,1)S(1)}, u32[]{:S(2)}, u32[]{:S(2)}) %collective-permute-start.14) | collective-permute-done | bytes 65568 | tf_op jit(solution)/shard_map/ppermute | solution.py:35
  51.8 4.8 %collective-permute-done.15 = bf16[256,128]{1,0:T(8,128)(2,1)S(1)} collective-permute-done((bf16[256,128]{1,0:T(8,128)(2,1)S(1)}, bf16[256,128]{1,0:T(8,128)(2,1)S(1)}, u32[]{:S(2)}, u32[]{:S(2)}) %collective-permute-start.15) | collective-permute-done | bytes 65568 | tf_op jit(solution)/shard_map/ppermute | solution.py:35
  56.6 2.2 %collective-permute-start.16 = (bf16[256,128]{1,0:T(8,128)(2,1)S(1)}, bf16[256,128]{1,0:T(8,128)(2,1)S(1)}, u32[]{:S(2)}, u32[]{:S(2)}) collective-permute-start(bf16[256,128]{1,0:T(8,128)(2,1)S(1)} %get-tuple-element.16), channel_id=1, source_target_pairs={{0,6},{1,7},{2,4},{3,5},{4,2},{5,3},{6,0},{7,1},{8,14},{9,15},{10,... | collective-permute-start | bytes 196616 | tf_op jit(solution)/shard_map/ppermute | solution.py:35
  58.8 3.8 %collective-permute-done.16 = bf16[256,128]{1,0:T(8,128)(2,1)S(1)} collective-permute-done((bf16[256,128]{1,0:T(8,128)(2,1)S(1)}, bf16[256,128]{1,0:T(8,128)(2,1)S(1)}, u32[]{:S(2)}, u32[]{:S(2)}) %collective-permute-start.16) | collective-permute-done | bytes 65568 | tf_op jit(solution)/shard_map/ppermute | solution.py:35
  62.7 1.7 collective-permute-start.26
  65.9 5.1 %collective-permute-done.17 = bf16[1024,128]{1,0:T(8,128)(2,1)S(1)} collective-permute-done((bf16[1024,128]{1,0:T(8,128)(2,1)S(1)}, bf16[1024,128]{1,0:T(8,128)(2,1)S(1)}, u32[]{:S(2)}, u32[]{:S(2)}) %collective-permute-start.17) | collective-permute-done | bytes 262176 | tf_op jit(solution)/shard_map/ppermute | solution.py:35
  75.5 1.7 collective-permute-start.28
  77.2 2.4 %collective-permute-done.20 = bf16[512,128]{1,0:T(8,128)(2,1)S(1)} collective-permute-done((bf16[512,128]{1,0:T(8,128)(2,1)S(1)}, bf16[512,128]{1,0:T(8,128)(2,1)S(1)}, u32[]{:S(2)}, u32[]{:S(2)}) %collective-permute-start.20) | collective-permute-done | bytes 131104 | tf_op jit(solution)/shard_map/ppermute | solution.py:66
  83.5 2.5 %collective-permute-done.28 = bf16[512,512]{1,0:T(8,128)(2,1)} collective-permute-done((bf16[512,512]{1,0:T(8,128)(2,1)S(1)}, bf16[512,512]{1,0:T(8,128)(2,1)}, u32[]{:S(2)}, u32[]{:S(2)}) %collective-permute-start.28) | collective-permute-done | bytes 524320 | tf_op jit(solution)/shard_map/ppermute | solution.py:66
  86.0 2.0 %convolution_bitcast_fusion.21 = f32[512,128]{1,0:T(8,128)} fusion(bf16[512,512]{1,0:T(8,128)(2,1)} %collective-permute-done.28, bf16[512,128]{1,0:T(8,128)(2,1)S(1)} %collective-permute-done.20), kind=kOutput, calls=%fused_computation.52 | convolution fusion | flops 67108864 | bytes 917504 | tf_op jit(solution)/shard_map/dot_general | solution.py:16
  88.6 2.0 %convolution_bitcast_fusion.34 = f32[512,128]{1,0:T(8,128)} fusion(bf16[512,128]{1,0:T(8,128)(2,1)S(1)} %collective-permute-done.18, bf16[2048,512]{1,0:T(8,128)(2,1)} %collective-permute-done.19), kind=kOutput, calls=%fused_computation.68 | convolution fusion | flops 67108864 | bytes 917504 | tf_op jit(solution)/shard_map/dot_general | solution.py:16
  90.7 2.1 %convolution_bitcast_fusion.30 = f32[512,128]{1,0:T(8,128)} fusion(bf16[512,128]{1,0:T(8,128)(2,1)S(1)} %collective-permute-done.18, bf16[2048,512]{1,0:T(8,128)(2,1)} %collective-permute-done.19), kind=kOutput, calls=%fused_computation.63 | convolution fusion | flops 67108864 | bytes 917504 | tf_op jit(solution)/shard_map/dot_general | solution.py:16
  95.2 2.0 %convolution_bitcast_fusion.26 = f32[512,128]{1,0:T(8,128)} fusion(bf16[512,128]{1,0:T(8,128)(2,1)S(1)} %collective-permute-done.18, bf16[2048,512]{1,0:T(8,128)(2,1)} %collective-permute-done.19), kind=kOutput, calls=%fused_computation.58 | convolution fusion | flops 67108864 | bytes 917504 | tf_op jit(solution)/shard_map/dot_general | solution.py:16
  97.3 1.8 collective-permute-start.6
  99.1 2.0 %convolution_bitcast_fusion.22 = f32[512,128]{1,0:T(8,128)} fusion(bf16[512,128]{1,0:T(8,128)(2,1)S(1)} %collective-permute-done.18, bf16[2048,512]{1,0:T(8,128)(2,1)} %collective-permute-done.19), kind=kOutput, calls=%fused_computation.53 | convolution fusion | flops 67108864 | bytes 917504 | tf_op jit(solution)/shard_map/dot_general | solution.py:16
  103.5 2.0 %rev.6 = f32[4,2,2,384]{3,2,1,0:T(2,128)} reverse(f32[4,2,2,384]{3,2,1,0:T(2,128)} %reshape.18), dimensions={2} | reverse | bytes 49152 | tf_op jit(solution)/shard_map/rev | solution.py:120
  107.7 2.4 %fusion.43 = f32[512,128]{1,0:T(8,128)S(1)} fusion(f32[512,128]{1,0:T(8,128)} %convolution_bitcast_fusion.33, f32[512,128]{1,0:T(8,128)} %convolution_bitcast_fusion.34, f32[512,128]{1,0:T(8,128)} %convolution_bitcast_fusion.35, f32[1536]{0:T(1024)S(1)} %get-tuple-element.9, bf16[128,768]{1,0:T(8,128)(2,1)} %copy-done.19, bf16[128,768]{1,0:T(8,128)(2,1)} %copy-done.22, ...), kind=kOutput, calls=%fused_computation.111 | convolution fusion | flops 205848576 | bytes 3020800 | tf_op jit(solution)/shard_map/dot_general | solution.py:16
  110.2 2.1 %fusion.58 = bf16[512,128]{1,0:T(8,128)(2,1)S(1)} fusion(f32[512,128]{1,0:T(8,128)S(1)} %fusion.43, bf16[512,512]{1,0:T(8,128)(2,1)} %collective-permute-done.23, bf16[512,128]{1,0:T(8,128)(2,1)} %collective-permute-done.22, f32[]{:T(128)} %bitcast.250, f32[]{:T(128)} %bitcast.21, f32[128]{0:T(128)S(1)} %dynamic_slice.57, f32[512]{0:T(512)S(1)} %copy-done.30, ...), kind=kOutput, calls=%fused_computation.126 | convolution fusion | flops 67633152 | bytes 1182220 | tf_op jit(solution)/shard_map/dot_general | solution.py:16
  114.1 2.1 %fusion.59 = bf16[512,128]{1,0:T(8,128)(2,1)S(1)} fusion(f32[512,128]{1,0:T(8,128)S(1)} %fusion.41, bf16[512,512]{1,0:T(8,128)(2,1)} %collective-permute-done.25, bf16[512,128]{1,0:T(8,128)(2,1)} %collective-permute-done.22, f32[]{:T(128)} %bitcast.27, f32[]{:T(128)} %bitcast.257, f32[128]{0:T(128)S(1)} %dynamic_slice.57, f32[512]{0:T(512)S(1)} %copy-done.30, ...), kind=kOutput, calls=%fused_computation.127 | convolution fusion | flops 67633152 | bytes 1182224 | tf_op jit(solution)/shard_map/dot_general | solution.py:16
  118.9 2.0 %fusion.60 = bf16[512,128]{1,0:T(8,128)(2,1)S(1)} fusion(f32[512,128]{1,0:T(8,128)S(1)} %fusion.39, bf16[512,512]{1,0:T(8,128)(2,1)} %collective-permute-done.27, bf16[512,128]{1,0:T(8,128)(2,1)} %collective-permute-done.22, f32[]{:T(128)} %bitcast.32, f32[]{:T(128)} %bitcast.256, f32[128]{0:T(128)S(1)} %dynamic_slice.57, f32[512]{0:T(512)S(1)} %copy-done.30, ...), kind=kOutput, calls=%fused_computation.128 | convolution fusion | flops 67633152 | bytes 1182224 | tf_op jit(solution)/shard_map/dot_general | solution.py:16
  121.8 2.1 %fusion.61 = bf16[512,128]{1,0:T(8,128)(2,1)S(1)} fusion(f32[512,128]{1,0:T(8,128)S(1)} %fusion.37, bf16[512,512]{1,0:T(8,128)(2,1)} %collective-permute-done.29, bf16[512,128]{1,0:T(8,128)(2,1)} %collective-permute-done.22, f32[]{:T(128)} %bitcast.37, f32[]{:T(128)} %bitcast.255, f32[128]{0:T(128)S(1)} %dynamic_slice.57, f32[512]{0:T(512)S(1)} %copy-done.30, ...), kind=kOutput, calls=%fused_computation.129 | convolution fusion | flops 67633152 | bytes 1182224 | tf_op jit(solution)/shard_map/dot_general | solution.py:16
  140.5 6.1 %collective-permute-done.32 = bf16[1024,128]{0,1:T(8,128)(2,1)S(1)} collective-permute-done((bf16[1024,128]{0,1:T(8,128)(2,1)S(1)}, bf16[1024,128]{0,1:T(8,128)(2,1)S(1)}, u32[]{:S(2)}, u32[]{:S(2)}) %collective-permute-start.32) | collective-permute-done | bytes 262176 | tf_op jit(solution)/shard_map/ppermute | solution.py:35
  146.7 1.5 collective-permute-start.33
  148.2 3.9 %collective-permute-start.34 = (bf16[256,128]{0,1:T(8,128)(2,1)S(1)}, bf16[256,128]{0,1:T(8,128)(2,1)S(1)}, u32[]{:S(2)}, u32[]{:S(2)}) collective-permute-start(bf16[256,128]{0,1:T(8,128)(2,1)S(1)} %get-tuple-element.38), channel_id=1, source_target_pairs={{0,4},{1,5},{2,6},{3,7},{4,0},{5,1},{6,2},{7,3},{8,12},{9,13},{10,... | collective-permute-start | bytes 196616 | tf_op jit(solution)/shard_map/ppermute | solution.py:35
  152.7 3.4 %collective-permute-done.34 = bf16[256,128]{0,1:T(8,128)(2,1)S(1)} collective-permute-done((bf16[256,128]{0,1:T(8,128)(2,1)S(1)}, bf16[256,128]{0,1:T(8,128)(2,1)S(1)}, u32[]{:S(2)}, u32[]{:S(2)}) %collective-permute-start.34) | collective-permute-done | bytes 65568 | tf_op jit(solution)/shard_map/ppermute | solution.py:35
  156.1 2.1 %collective-permute-done.35 = bf16[256,128]{0,1:T(8,128)(2,1)S(1)} collective-permute-done((bf16[256,128]{0,1:T(8,128)(2,1)S(1)}, bf16[256,128]{0,1:T(8,128)(2,1)S(1)}, u32[]{:S(2)}, u32[]{:S(2)}) %collective-permute-start.35) | collective-permute-done | bytes 65568 | tf_op jit(solution)/shard_map/ppermute | solution.py:35
  159.2 1.7 collective-permute-start.37
  160.9 1.9 collective-permute-start.38
  163.9 1.8 collective-permute-done.37
  169.8 2.1 %collective-permute-start.31 = (f32[4,1536]{1,0:T(4,128)S(1)}, f32[4,1536]{1,0:T(4,128)S(1)}, u32[]{:S(2)}, u32[]{:S(2)}) collective-permute-start(f32[4,1536]{1,0:T(4,128)S(1)} %maximum_add_fusion.1), channel_id=1, source_target_pairs={{0,16},{8,24},{16,0},{24,8},{1,17},{9,25},{17,1},{25,9},{2,18},{10... | collective-permute-start | bytes 73736 | tf_op jit(solution)/shard_map/ppermute | solution.py:66
  171.9 1.8 collective-permute-done.31
  188.0 2.1 %fusion.62 = bf16[512,128]{1,0:T(8,128)(2,1)S(1)} fusion(f32[512,128]{1,0:T(8,128)S(1)} %fusion.35, bf16[512,512]{1,0:T(8,128)(2,1)} %collective-permute-done.23, f32[]{:T(128)} %bitcast.254, f32[]{:T(128)} %bitcast.21, f32[128]{0:T(128)S(1)} %copy-done.33, f32[512]{0:T(512)S(1)} %copy-done.31, bf16[2048,512]{1,0:T(8,128)(2,1)} %param.9, ...), kind=kOutput, calls=%fused_computation.130 | convolution fusion | flops 67633152 | bytes 1182220 | tf_op jit(solution)/shard_map/dot_general | solution.py:16
  190.1 2.0 %fusion.63 = bf16[512,128]{1,0:T(8,128)(2,1)S(1)} fusion(f32[512,128]{1,0:T(8,128)S(1)} %fusion.33, bf16[512,512]{1,0:T(8,128)(2,1)} %collective-permute-done.25, f32[]{:T(128)} %bitcast.27, f32[]{:T(128)} %bitcast.253, f32[128]{0:T(128)S(1)} %copy-done.33, f32[512]{0:T(512)S(1)} %copy-done.31, bf16[2048,512]{1,0:T(8,128)(2,1)} %param.9, s32[]{:T(128)S(6)} %add.423, ...), kind=kOutput, calls=%fused_computation.131 | convolution fusion | flops 67633152 | bytes 1182224 | tf_op jit(solution)/shard_map/dot_general | solution.py:16
  192.1 1.9 fusion.64
  194.0 2.0 %fusion.65 = bf16[512,128]{1,0:T(8,128)(2,1)S(1)} fusion(f32[512,128]{1,0:T(8,128)S(1)} %fusion.29, bf16[512,512]{1,0:T(8,128)(2,1)} %collective-permute-done.29, f32[]{:T(128)} %bitcast.37, f32[]{:T(128)} %bitcast.251, f32[128]{0:T(128)S(1)} %copy-done.33, f32[512]{0:T(512)S(1)} %copy-done.31, bf16[2048,512]{1,0:T(8,128)(2,1)} %param.9, s32[]{:T(128)S(6)} %add.425, ...), kind=kOutput, calls=%fused_computation.133 | convolution fusion | flops 67633152 | bytes 1182224 | tf_op jit(solution)/shard_map/dot_general | solution.py:16
  (245 shorter events, 75.1 us)
Async XLA Ops:
  0.0 18.8 %copy-start.13 = (bf16[64,384]{1,0:T(8,128)(2,1)S(1)}, bf16[64,384]{1,0:T(8,128)(2,1)}, u32[]{:S(2)}) copy-start(bf16[64,384]{1,0:T(8,128)(2,1)} %param.11) | copy-start | bytes 147460
  0.0 18.8 %copy-start.12 = (bf16[64,384]{1,0:T(8,128)(2,1)S(1)}, bf16[64,384]{1,0:T(8,128)(2,1)}, u32[]{:S(2)}) copy-start(bf16[64,384]{1,0:T(8,128)(2,1)} %param.12) | copy-start | bytes 147460
  0.9 6.3 %collective-permute-start = (bf16[2,64,384]{2,1,0:T(8,128)(2,1)S(1)}, bf16[2,64,384]{2,1,0:T(8,128)(2,1)S(1)}, u32[]{:S(2)}, u32[]{:S(2)}) collective-permute-start(bf16[2,64,384]{2,1,0:T(8,128)(2,1)S(1)} %pad_maximum_fusion.10), channel_id=1, source_target_pairs={{0,16},{8,24},{16,0},{24,8},{1,17},{9,25},{17,1},{25,9},{2,18},{10... | collective-permute-start | bytes 294920 | tf_op jit(solution)/shard_map/ppermute | solution.py:66
  3.9 15.5 %collective-permute-start.8 = (bf16[2048,128]{1,0:T(8,128)(2,1)}, bf16[2048,128]{1,0:T(8,128)(2,1)}, u32[]{:S(2)}, u32[]{:S(2)}) collective-permute-start(bf16[2048,128]{1,0:T(8,128)(2,1)} %param.8), channel_id=1, source_target_pairs={{0,16},{8,24},{16,0},{24,8},{1,17},{9,25},{17,1},{25,9},{2,18},{10... | collective-permute-start | bytes 1572872 | tf_op jit(solution)/shard_map/ppermute | solution.py:66
  4.0 17.2 %collective-permute-start.7 = (bf16[2048,128]{1,0:T(8,128)(2,1)}, bf16[2048,128]{1,0:T(8,128)(2,1)}, u32[]{:S(2)}, u32[]{:S(2)}) collective-permute-start(bf16[2048,128]{1,0:T(8,128)(2,1)} %param.8), channel_id=1, source_target_pairs={{0,8},{8,0},{16,24},{24,16},{1,9},{9,1},{17,25},{25,17},{2,10},{10... | collective-permute-start | bytes 1572872 | tf_op jit(solution)/shard_map/ppermute | solution.py:66
  4.0 84.6 %collective-permute-start.19 = (bf16[2048,512]{1,0:T(8,128)(2,1)}, bf16[2048,512]{1,0:T(8,128)(2,1)}, u32[]{:S(2)}, u32[]{:S(2)}) collective-permute-start(bf16[2048,512]{1,0:T(8,128)(2,1)} %param.10), channel_id=1, source_target_pairs={{0,8},{8,0},{16,24},{24,16},{1,9},{9,1},{17,25},{25,17},{2,10},{10... | collective-permute-start | bytes 6291464 | tf_op jit(solution)/shard_map/ppermute | solution.py:66
  8.0 10.8 %collective-permute-start.1 = (bf16[2,64,768]{2,1,0:T(8,128)(2,1)S(1)}, bf16[2,64,768]{2,1,0:T(8,128)(2,1)S(1)}, u32[]{:S(2)}, u32[]{:S(2)}) collective-permute-start(bf16[2,64,768]{2,1,0:T(8,128)(2,1)S(1)} %pad_maximum_fusion.9), channel_id=1, source_target_pairs={{0,4},{1,5},{2,6},{3,7},{4,0},{5,1},{6,2},{7,3},{8,12},{9,13},{10,... | collective-permute-start | bytes 589832 | tf_op jit(solution)/shard_map/ppermute | solution.py:75
  19.0 10.8 %collective-permute-start.2 = (bf16[2,2,64,768]{3,2,1,0:T(8,128)(2,1)S(1)}, bf16[2,2,64,768]{3,2,1,0:T(8,128)(2,1)}, u32[]{:S(2)}, u32[]{:S(2)}) collective-permute-start(bf16[2,2,64,768]{3,2,1,0:T(8,128)(2,1)S(1)} %pad_maximum_fusion.7), channel_id=1, source_target_pairs={{0,2},{1,3},{2,0},{3,1},{4,6},{5,7},{6,4},{7,5},{8,10},{9,11},{10,... | collective-permute-start | bytes 1179656 | tf_op jit(solution)/shard_map/ppermute | solution.py:75
  19.4 3.6 %collective-permute-start.9 = (bf16[2048,128]{1,0:T(8,128)(2,1)}, bf16[2048,128]{1,0:T(8,128)(2,1)S(1)}, u32[]{:S(2)}, u32[]{:S(2)}) collective-permute-start(bf16[2048,128]{1,0:T(8,128)(2,1)} %collective-permute-done.8), channel_id=1, source_target_pairs={{0,8},{8,0},{16,24},{24,16},{1,9},{9,1},{17,25},{25,17},{2,10},{10... | collective-permute-start | bytes 1572872 | tf_op jit(solution)/shard_map/ppermute | solution.py:66
  24.7 9.0 %collective-permute-start.10 = (bf16[1024,128]{1,0:T(8,128)(2,1)}, bf16[1024,128]{1,0:T(8,128)(2,1)}, u32[]{:S(2)}, u32[]{:S(2)}) collective-permute-start(bf16[1024,128]{1,0:T(8,128)(2,1)} %dynamic-slice_convert_fusion.1), channel_id=1, source_target_pairs={{0,1},{1,0},{2,3},{3,2},{4,5},{5,4},{6,7},{7,6},{8,9},{9,8},{10,11... | collective-permute-start | bytes 786440 | tf_op jit(solution)/shard_map/ppermute | solution.py:35
  27.5 48.0 %collective-permute-start.21 = (bf16[512,512]{1,0:T(8,128)(2,1)}, bf16[512,512]{1,0:T(8,128)(2,1)S(1)}, u32[]{:S(2)}, u32[]{:S(2)}) collective-permute-start(bf16[512,512]{1,0:T(8,128)(2,1)} %get-tuple-element.19), channel_id=1, source_target_pairs={{0,16},{8,24},{16,0},{24,8},{1,17},{9,25},{17,1},{25,9},{2,18},{10... | collective-permute-start | bytes 1572872 | tf_op jit(solution)/shard_map/ppermute | solution.py:66
  29.8 92.0 %copy-start.32 = (f32[128]{0:T(128)}, f32[128]{0:T(128)S(1)}, u32[]{:S(2)}) copy-start(f32[128]{0:T(128)S(1)} %dynamic_slice.57) | copy-start | bytes 1540
  30.9 31.8 %copy-start.10 = (bf16[512,512]{1,0:T(8,128)(2,1)S(1)}, bf16[512,512]{1,0:T(8,128)(2,1)}, u32[]{:S(2)}) copy-start(bf16[512,512]{1,0:T(8,128)(2,1)} %get-tuple-element.22) | copy-start | bytes 1572868
  34.9 5.0 %collective-permute-start.11 = (bf16[256,128]{1,0:T(8,128)(2,1)S(1)}, bf16[256,128]{1,0:T(8,128)(2,1)S(1)}, u32[]{:S(2)}, u32[]{:S(2)}) collective-permute-start(bf16[256,128]{1,0:T(8,128)(2,1)S(1)} %get-tuple-element.39), channel_id=1, source_target_pairs={{0,2},{1,3},{2,0},{3,1},{4,6},{5,7},{6,4},{7,5},{8,10},{9,11},{10,... | collective-permute-start | bytes 196616 | tf_op jit(solution)/shard_map/ppermute | solution.py:35
  36.6 8.3 %collective-permute-start.12 = (bf16[256,128]{1,0:T(8,128)(2,1)S(1)}, bf16[256,128]{1,0:T(8,128)(2,1)S(1)}, u32[]{:S(2)}, u32[]{:S(2)}) collective-permute-start(bf16[256,128]{1,0:T(8,128)(2,1)S(1)} %get-tuple-element.41), channel_id=1, source_target_pairs={{0,4},{1,5},{2,6},{3,7},{4,0},{5,1},{6,2},{7,3},{8,12},{9,13},{10,... | collective-permute-start | bytes 196616 | tf_op jit(solution)/shard_map/ppermute | solution.py:35
  38.5 7.9 %collective-permute-start.13 = (bf16[256,128]{1,0:T(8,128)(2,1)S(1)}, bf16[256,128]{1,0:T(8,128)(2,1)S(1)}, u32[]{:S(2)}, u32[]{:S(2)}) collective-permute-start(bf16[256,128]{1,0:T(8,128)(2,1)S(1)} %get-tuple-element.40), channel_id=1, source_target_pairs={{0,6},{1,7},{2,4},{3,5},{4,2},{5,3},{6,0},{7,1},{8,14},{9,15},{10,... | collective-permute-start | bytes 196616 | tf_op jit(solution)/shard_map/ppermute | solution.py:35
  39.9 37.3 %collective-permute-start.24 = (bf16[512,512]{1,0:T(8,128)(2,1)S(1)}, bf16[512,512]{1,0:T(8,128)(2,1)S(1)}, u32[]{:S(2)}, u32[]{:S(2)}) collective-permute-start(bf16[512,512]{1,0:T(8,128)(2,1)S(1)} %copy-done.11), channel_id=1, source_target_pairs={{0,16},{8,24},{16,0},{24,8},{1,17},{9,25},{17,1},{25,9},{2,18},{10... | collective-permute-start | bytes 1572872 | tf_op jit(solution)/shard_map/ppermute | solution.py:66
  45.0 19.6 %collective-permute-start.3 = (bf16[2,2,2,64,768]{4,3,2,1,0:T(8,128)(2,1)S(1)}, bf16[2,2,2,64,768]{4,3,2,1,0:T(8,128)(2,1)S(1)}, u32[]{:S(2)}, u32[]{:S(2)}) collective-permute-start(bf16[2,2,2,64,768]{4,3,2,1,0:T(8,128)(2,1)S(1)} %pad_maximum_fusion.5), channel_id=1, source_target_pairs={{0,1},{1,0},{2,3},{3,2},{4,5},{5,4},{6,7},{7,6},{8,9},{9,8},{10,11... | collective-permute-start | bytes 2359304 | tf_op jit(solution)/shard_map/ppermute | solution.py:75
  46.5 4.3 %collective-permute-start.14 = (bf16[256,128]{1,0:T(8,128)(2,1)S(1)}, bf16[256,128]{1,0:T(8,128)(2,1)S(1)}, u32[]{:S(2)}, u32[]{:S(2)}) collective-permute-start(bf16[256,128]{1,0:T(8,128)(2,1)S(1)} %get-tuple-element.16), channel_id=1, source_target_pairs={{0,2},{1,3},{2,0},{3,1},{4,6},{5,7},{6,4},{7,5},{8,10},{9,11},{10,... | collective-permute-start | bytes 196616 | tf_op jit(solution)/shard_map/ppermute | solution.py:35
  50.8 5.8 %collective-permute-start.15 = (bf16[256,128]{1,0:T(8,128)(2,1)S(1)}, bf16[256,128]{1,0:T(8,128)(2,1)S(1)}, u32[]{:S(2)}, u32[]{:S(2)}) collective-permute-start(bf16[256,128]{1,0:T(8,128)(2,1)S(1)} %get-tuple-element.16), channel_id=1, source_target_pairs={{0,4},{1,5},{2,6},{3,7},{4,0},{5,1},{6,2},{7,3},{8,12},{9,13},{10,... | collective-permute-start | bytes 196616 | tf_op jit(solution)/shard_map/ppermute | solution.py:35
  56.6 6.1 %collective-permute-start.16 = (bf16[256,128]{1,0:T(8,128)(2,1)S(1)}, bf16[256,128]{1,0:T(8,128)(2,1)S(1)}, u32[]{:S(2)}, u32[]{:S(2)}) collective-permute-start(bf16[256,128]{1,0:T(8,128)(2,1)S(1)} %get-tuple-element.16), channel_id=1, source_target_pairs={{0,6},{1,7},{2,4},{3,5},{4,2},{5,3},{6,0},{7,1},{8,14},{9,15},{10,... | collective-permute-start | bytes 196616 | tf_op jit(solution)/shard_map/ppermute | solution.py:35
  62.7 19.0 %collective-permute-start.26 = (bf16[512,512]{1,0:T(8,128)(2,1)S(1)}, bf16[512,512]{1,0:T(8,128)(2,1)}, u32[]{:S(2)}, u32[]{:S(2)}) collective-permute-start(bf16[512,512]{1,0:T(8,128)(2,1)S(1)} %copy-done.10), channel_id=1, source_target_pairs={{0,16},{8,24},{16,0},{24,8},{1,17},{9,25},{17,1},{25,9},{2,18},{10... | collective-permute-start | bytes 1572872 | tf_op jit(solution)/shard_map/ppermute | solution.py:66
  64.6 6.4 %collective-permute-start.17 = (bf16[1024,128]{1,0:T(8,128)(2,1)S(1)}, bf16[1024,128]{1,0:T(8,128)(2,1)S(1)}, u32[]{:S(2)}, u32[]{:S(2)}) collective-permute-start(bf16[1024,128]{1,0:T(8,128)(2,1)S(1)} %constant_dynamic-update-slice_fusion.8), channel_id=1, source_target_pairs={{0,1},{1,0},{2,3},{3,2},{4,5},{5,4},{6,7},{7,6},{8,9},{9,8},{10,11... | collective-permute-start | bytes 786440 | tf_op jit(solution)/shard_map/ppermute | solution.py:35
  65.7 28.5 %copy-start.2 = (bf16[8,1,64,768]{3,2,1,0:T(8,128)(2,1)}, bf16[8,1,64,768]{3,2,1,0:T(8,128)(2,1)S(1)}, u32[]{:S(2)}) copy-start(bf16[8,1,64,768]{3,2,1,0:T(8,128)(2,1)S(1)} %get-tuple-element.23) | copy-start | bytes 2359300
  65.8 28.4 %copy-start.22 = (bf16[128,768]{1,0:T(8,128)(2,1)}, bf16[128,768]{1,0:T(8,128)(2,1)S(1)}, u32[]{:S(2)}) copy-start(bf16[128,768]{1,0:T(8,128)(2,1)S(1)} %get-tuple-element.27) | copy-start | bytes 589828
  73.1 6.5 %collective-permute-start.20 = (bf16[512,128]{1,0:T(8,128)(2,1)S(1)}, bf16[512,128]{1,0:T(8,128)(2,1)S(1)}, u32[]{:S(2)}, u32[]{:S(2)}) collective-permute-start(bf16[512,128]{1,0:T(8,128)(2,1)S(1)} %get-tuple-element.32), channel_id=1, source_target_pairs={{0,16},{8,24},{16,0},{24,8},{1,17},{9,25},{17,1},{25,9},{2,18},{10... | collective-permute-start | bytes 393224 | tf_op jit(solution)/shard_map/ppermute | solution.py:66
  75.5 10.5 %collective-permute-start.28 = (bf16[512,512]{1,0:T(8,128)(2,1)S(1)}, bf16[512,512]{1,0:T(8,128)(2,1)}, u32[]{:S(2)}, u32[]{:S(2)}) collective-permute-start(bf16[512,512]{1,0:T(8,128)(2,1)S(1)} %copy-done.9), channel_id=1, source_target_pairs={{0,16},{8,24},{16,0},{24,8},{1,17},{9,25},{17,1},{25,9},{2,18},{10... | collective-permute-start | bytes 1572872 | tf_op jit(solution)/shard_map/ppermute | solution.py:66
  77.2 33.0 %collective-permute-start.23 = (bf16[512,512]{1,0:T(8,128)(2,1)S(1)}, bf16[512,512]{1,0:T(8,128)(2,1)}, u32[]{:S(2)}, u32[]{:S(2)}) collective-permute-start(bf16[512,512]{1,0:T(8,128)(2,1)S(1)} %collective-permute-done.21), channel_id=1, source_target_pairs={{0,8},{8,0},{16,24},{24,16},{1,9},{9,1},{17,25},{25,17},{2,10},{10... | collective-permute-start | bytes 1572872 | tf_op jit(solution)/shard_map/ppermute | solution.py:66
  79.6 34.5 %collective-permute-start.25 = (bf16[512,512]{1,0:T(8,128)(2,1)S(1)}, bf16[512,512]{1,0:T(8,128)(2,1)}, u32[]{:S(2)}, u32[]{:S(2)}) collective-permute-start(bf16[512,512]{1,0:T(8,128)(2,1)S(1)} %collective-permute-done.24), channel_id=1, source_target_pairs={{0,8},{8,0},{16,24},{24,16},{1,9},{9,1},{17,25},{25,17},{2,10},{10... | collective-permute-start | bytes 1572872 | tf_op jit(solution)/shard_map/ppermute | solution.py:66
  81.6 11.1 %collective-permute-start.4 = (bf16[640,768]{1,0:T(8,128)(2,1)S(1)}, bf16[640,768]{1,0:T(8,128)(2,1)S(1)}, u32[]{:S(2)}, u32[]{:S(2)}) collective-permute-start(bf16[640,768]{1,0:T(8,128)(2,1)S(1)} %pad_maximum_fusion.4), channel_id=1, source_target_pairs={{0,8},{8,0},{16,24},{24,16},{1,9},{9,1},{17,25},{25,17},{2,10},{10... | collective-permute-start | bytes 2949128 | tf_op jit(solution)/shard_map/ppermute | solution.py:66
  86.0 2.0 %collective-permute-start.18 = (bf16[512,128]{1,0:T(8,128)(2,1)S(1)}, bf16[512,128]{1,0:T(8,128)(2,1)S(1)}, u32[]{:S(2)}, u32[]{:S(2)}) collective-permute-start(bf16[512,128]{1,0:T(8,128)(2,1)S(1)} %get-tuple-element.33), channel_id=1, source_target_pairs={{0,8},{8,0},{16,24},{24,16},{1,9},{9,1},{17,25},{25,17},{2,10},{10... | collective-permute-start | bytes 393224 | tf_op jit(solution)/shard_map/ppermute | solution.py:66
  88.1 30.8 %collective-permute-start.27 = (bf16[512,512]{1,0:T(8,128)(2,1)}, bf16[512,512]{1,0:T(8,128)(2,1)}, u32[]{:S(2)}, u32[]{:S(2)}) collective-permute-start(bf16[512,512]{1,0:T(8,128)(2,1)} %collective-permute-done.26), channel_id=1, source_target_pairs={{0,8},{8,0},{16,24},{24,16},{1,9},{9,1},{17,25},{25,17},{2,10},{10... | collective-permute-start | bytes 1572872 | tf_op jit(solution)/shard_map/ppermute | solution.py:66
  88.6 33.3 %collective-permute-start.29 = (bf16[512,512]{1,0:T(8,128)(2,1)}, bf16[512,512]{1,0:T(8,128)(2,1)}, u32[]{:S(2)}, u32[]{:S(2)}) collective-permute-start(bf16[512,512]{1,0:T(8,128)(2,1)} %collective-permute-done.28), channel_id=1, source_target_pairs={{0,8},{8,0},{16,24},{24,16},{1,9},{9,1},{17,25},{25,17},{2,10},{10... | collective-permute-start | bytes 1572872 | tf_op jit(solution)/shard_map/ppermute | solution.py:66
  94.7 2.5 %collective-permute-start.5 = (f32[4,1536]{1,0:T(4,128)S(1)}, f32[4,1536]{1,0:T(4,128)S(1)}, u32[]{:S(2)}, u32[]{:S(2)}) collective-permute-start(f32[4,1536]{1,0:T(4,128)S(1)} %pad_maximum_fusion.11), channel_id=1, source_target_pairs={{0,8},{8,0},{16,24},{24,16},{1,9},{9,1},{17,25},{25,17},{2,10},{10... | collective-permute-start | bytes 73736 | tf_op jit(solution)/shard_map/ppermute | solution.py:66
  97.3 3.9 %collective-permute-start.6 = (f32[4,1536]{1,0:T(4,128)S(1)}, f32[4,1536]{1,0:T(4,128)S(1)}, u32[]{:S(2)}, u32[]{:S(2)}) collective-permute-start(f32[4,1536]{1,0:T(4,128)S(1)} %maximum_add_fusion), channel_id=1, source_target_pairs={{0,16},{8,24},{16,0},{24,8},{1,17},{9,25},{17,1},{25,9},{2,18},{10... | collective-permute-start | bytes 73736 | tf_op jit(solution)/shard_map/ppermute | solution.py:66
  101.8 8.4 %collective-permute-start.22 = (bf16[512,128]{1,0:T(8,128)(2,1)S(1)}, bf16[512,128]{1,0:T(8,128)(2,1)}, u32[]{:S(2)}, u32[]{:S(2)}) collective-permute-start(bf16[512,128]{1,0:T(8,128)(2,1)S(1)} %get-tuple-element.31), channel_id=1, source_target_pairs={{0,24},{8,16},{16,8},{24,0},{1,25},{9,17},{17,9},{25,1},{2,26},{10... | collective-permute-start | bytes 393224 | tf_op jit(solution)/shard_map/ppermute | solution.py:66
  137.9 8.7 %collective-permute-start.32 = (bf16[1024,128]{0,1:T(8,128)(2,1)S(1)}, bf16[1024,128]{0,1:T(8,128)(2,1)S(1)}, u32[]{:S(2)}, u32[]{:S(2)}) collective-permute-start(bf16[1024,128]{0,1:T(8,128)(2,1)S(1)} %dynamic-slice_convert_fusion), channel_id=1, source_target_pairs={{0,1},{1,0},{2,3},{3,2},{4,5},{5,4},{6,7},{7,6},{8,9},{9,8},{10,11... | collective-permute-start | bytes 786440 | tf_op jit(solution)/shard_map/ppermute | solution.py:35
  139.1 19.1 %copy-start.26 = (f32[1,1536]{1,0:T(1,128)}, f32[1,1536]{1,0:T(1,128)S(1)}, u32[]{:S(2)}) copy-start(f32[1,1536]{1,0:T(1,128)S(1)} %stack.85) | copy-start | bytes 18436
  139.2 19.1 %copy-start.27 = (f32[1,1536]{1,0:T(1,128)}, f32[1,1536]{1,0:T(1,128)S(1)}, u32[]{:S(2)}) copy-start(f32[1,1536]{1,0:T(1,128)S(1)} %stack.86) | copy-start | bytes 18436
  139.2 12.9 %collective-permute-start.30 = (f32[4,1536]{1,0:T(4,128)S(1)}, f32[4,1536]{1,0:T(4,128)S(1)}, u32[]{:S(2)}, u32[]{:S(2)}) collective-permute-start(f32[4,1536]{1,0:T(4,128)S(1)} %pad_maximum_fusion.12), channel_id=1, source_target_pairs={{0,8},{8,0},{16,24},{24,16},{1,9},{9,1},{17,25},{25,17},{2,10},{10... | collective-permute-start | bytes 73736 | tf_op jit(solution)/shard_map/ppermute | solution.py:66
  146.7 6.0 %collective-permute-start.33 = (bf16[256,128]{0,1:T(8,128)(2,1)S(1)}, bf16[256,128]{0,1:T(8,128)(2,1)S(1)}, u32[]{:S(2)}, u32[]{:S(2)}) collective-permute-start(bf16[256,128]{0,1:T(8,128)(2,1)S(1)} %get-tuple-element.36), channel_id=1, source_target_pairs={{0,2},{1,3},{2,0},{3,1},{4,6},{5,7},{6,4},{7,5},{8,10},{9,11},{10,... | collective-permute-start | bytes 196616 | tf_op jit(solution)/shard_map/ppermute | solution.py:35
  148.2 7.9 %collective-permute-start.34 = (bf16[256,128]{0,1:T(8,128)(2,1)S(1)}, bf16[256,128]{0,1:T(8,128)(2,1)S(1)}, u32[]{:S(2)}, u32[]{:S(2)}) collective-permute-start(bf16[256,128]{0,1:T(8,128)(2,1)S(1)} %get-tuple-element.38), channel_id=1, source_target_pairs={{0,4},{1,5},{2,6},{3,7},{4,0},{5,1},{6,2},{7,3},{8,12},{9,13},{10,... | collective-permute-start | bytes 196616 | tf_op jit(solution)/shard_map/ppermute | solution.py:35
  152.1 6.2 %collective-permute-start.35 = (bf16[256,128]{0,1:T(8,128)(2,1)S(1)}, bf16[256,128]{0,1:T(8,128)(2,1)S(1)}, u32[]{:S(2)}, u32[]{:S(2)}) collective-permute-start(bf16[256,128]{0,1:T(8,128)(2,1)S(1)} %get-tuple-element.37), channel_id=1, source_target_pairs={{0,6},{1,7},{2,4},{3,5},{4,2},{5,3},{6,0},{7,1},{8,14},{9,15},{10,... | collective-permute-start | bytes 196616 | tf_op jit(solution)/shard_map/ppermute | solution.py:35
  158.4 4.5 %collective-permute-start.36 = (bf16[256,128]{0,1:T(8,128)(2,1)S(1)}, bf16[256,128]{0,1:T(8,128)(2,1)}, u32[]{:S(2)}, u32[]{:S(2)}) collective-permute-start(bf16[256,128]{0,1:T(8,128)(2,1)S(1)} %add_convert_fusion), channel_id=1, source_target_pairs={{0,2},{1,3},{2,0},{3,1},{4,6},{5,7},{6,4},{7,5},{8,10},{9,11},{10,... | collective-permute-start | bytes 196616 | tf_op jit(solution)/shard_map/ppermute | solution.py:35
  159.2 6.5 %collective-permute-start.37 = (bf16[256,128]{0,1:T(8,128)(2,1)S(1)}, bf16[256,128]{0,1:T(8,128)(2,1)}, u32[]{:S(2)}, u32[]{:S(2)}) collective-permute-start(bf16[256,128]{0,1:T(8,128)(2,1)S(1)} %add_convert_fusion), channel_id=1, source_target_pairs={{0,4},{1,5},{2,6},{3,7},{4,0},{5,1},{6,2},{7,3},{8,12},{9,13},{10,... | collective-permute-start | bytes 196616 | tf_op jit(solution)/shard_map/ppermute | solution.py:35
  160.9 6.2 %collective-permute-start.38 = (bf16[256,128]{0,1:T(8,128)(2,1)S(1)}, bf16[256,128]{0,1:T(8,128)(2,1)}, u32[]{:S(2)}, u32[]{:S(2)}) collective-permute-start(bf16[256,128]{0,1:T(8,128)(2,1)S(1)} %add_convert_fusion), channel_id=1, source_target_pairs={{0,6},{1,7},{2,4},{3,5},{4,2},{5,3},{6,0},{7,1},{8,14},{9,15},{10,... | collective-permute-start | bytes 196616 | tf_op jit(solution)/shard_map/ppermute | solution.py:35
  168.1 6.5 %collective-permute-start.39 = (bf16[1024,128]{1,0:T(8,128)(2,1)S(1)}, bf16[1024,128]{1,0:T(8,128)(2,1)}, u32[]{:S(2)}, u32[]{:S(2)}) collective-permute-start(bf16[1024,128]{1,0:T(8,128)(2,1)S(1)} %constant_dynamic-update-slice_fusion.2), channel_id=1, source_target_pairs={{0,1},{1,0},{2,3},{3,2},{4,5},{5,4},{6,7},{7,6},{8,9},{9,8},{10,11... | collective-permute-start | bytes 786440 | tf_op jit(solution)/shard_map/ppermute | solution.py:35
  169.8 3.9 %collective-permute-start.31 = (f32[4,1536]{1,0:T(4,128)S(1)}, f32[4,1536]{1,0:T(4,128)S(1)}, u32[]{:S(2)}, u32[]{:S(2)}) collective-permute-start(f32[4,1536]{1,0:T(4,128)S(1)} %maximum_add_fusion.1), channel_id=1, source_target_pairs={{0,16},{8,24},{16,0},{24,8},{1,17},{9,25},{17,1},{25,9},{2,18},{10... | collective-permute-start | bytes 73736 | tf_op jit(solution)/shard_map/ppermute | solution.py:66
  (29 other events, 99.7 us)

commit v2 on v0

v2 whole, which is shorter than its diff:
```python
import functools

import jax
import jax.numpy as jnp
from jax import lax
from jax.experimental import pallas as pl
from jax.experimental.pallas import tpu as pltpu
from jax.sharding import PartitionSpec as P

ITERS = 2
BF = jnp.bfloat16
F32 = jnp.float32
VMEM = pl.BlockSpec(memory_space=pltpu.VMEM)
SMEM = pl.BlockSpec(memory_space=pltpu.SMEM)
PARAMS = pltpu.CompilerParams(vmem_limit_bytes=24 * 2**20)


def xor(n, s):
    return [(i, i ^ s) for i in range(n)]


def dot(a, b, ca, cb):
    return lax.dot_general(a, b, (((ca,), (cb,)), ((), ())), preferred_element_type=F32)


def take(a, start, size, axis=0):
    return lax.dynamic_slice_in_dim(a, start, size, axis)


def tie(a, *others):
    return lax.optimization_barrier((a, *others))


def all_reduce(v, n, cross=None, beside=lambda stage, a: a):
    me = lax.axis_index("pair")
    low, high = me % 2, me // 2
    m = n // 2
    half = v.shape[1] // 2
    part = half // m

    def send(a, s):
        return lax.ppermute(a, "pair", xor(n, s))

    got = beside(0, send(take(v, (1 - low) * half, half, 1).astype(BF), 1))
    acc = take(v, low * half, half, 1) + got.astype(F32)
    rounded = acc.astype(BF)
    total = take(acc, high * part, part, 1)
    for s in range(1, m):
        total = total + send(take(rounded, (high ^ s) * part, part, 1), 2 * s).astype(F32)
    mine = beside(1, total.astype(BF))
    if cross is not None:
        mine = beside(2, cross(mine))
    parts = [mine] + [send(mine, 2 * s) for s in range(1, m)]
    line = []
    for q in range(m):
        block = parts[0]
        for s in range(1, m):
            block = jnp.where((high ^ s) == q, parts[s], block)
        line.append(block)
    line = beside(3, jnp.concatenate(line, axis=1))
    return line, beside(4, send(line, 1))


def pieces(far):
    start = 0
    for block in far:
        yield start, block
        start += block.shape[0]


def residual_kernel(nfar, side, middle, left, right, line, other, own, *refs):
    far, (mine, theirs, gram) = refs[:nfar], refs[nfar:]
    nvirt, half, width = left.shape[0], line.shape[1], mine.shape[1]
    gram[:, pl.ds(pl.multiple_of(side[0] * half, half), half)] = line[...]
    gram[:, pl.ds(pl.multiple_of((1 - side[0]) * half, half), half)] = other[...]
    last = None
    for start, block in pieces(far):
        size = block.shape[0]
        i, at = start // nvirt, start % nvirt
        if i != last:
            scaled = (right[...].astype(F32) * middle[i : i + 1, :]).astype(BF)
            last = i
        res = dot(left[at : at + size], scaled, 1, 1)
        res += dot(own[start : start + size], gram[0], 1, 1)
        res += dot(block[...], gram[1], 1, 1)
        mine[start : start + size] = res[:, :width]
        theirs[start : start + size] = res[:, width:].astype(BF)


def update_kernel(last, occ, pivot, mine, got, coulomb, vir_col, vir_row, out):
    nvirt = vir_col.shape[0]
    for i in range(mine.shape[0] // nvirt):
        rows = slice(i * nvirt, (i + 1) * nvirt)
        denom = vir_col[...] + vir_row[...] - occ[i] - pivot[0]
        res = mine[rows] + got[rows].astype(F32)
        new = (coulomb[rows].astype(F32) + res) / denom
        if last:
            out[rows] = new.astype(BF)
        else:
            out[:, rows] = new.T.astype(BF)


def gram_kernel(nfar, mine, other, left, right, own, *refs):
    far, (gram, middle, amps) = refs[:nfar], refs[nfar:]
    width, nvirt = mine.shape[0], left.shape[0]
    amps[:width] = mine[...]
    amps[width:] = other[...]
    gram[0] = dot(amps[...], own[...], 1, 0)
    for start, block in pieces(far):
        term = dot(amps[:, start : start + block.shape[0]], block[...], 1, 0)
        if start:
            gram[1] += term
        else:
            gram[1] = term
    for i in range(middle.shape[0]):
        proj = dot(amps[:, i * nvirt : (i + 1) * nvirt], left[...], 1, 0)
        middle[i : i + 1] = jnp.sum(proj * right[...].astype(F32), axis=0, keepdims=True)


def per_device(
    amplitudes, coulomb, df_factors, thc_left, thc_right, occ_energy, vir_energy, pivot_energy
):
    n_pair = lax.axis_size("pair")
    n_aux = lax.axis_size("aux")
    k = lax.axis_index("aux")
    me = lax.axis_index("pair")
    rows, width = amplitudes.shape
    nvirt = vir_energy.shape[0]
    nocc = rows // nvirt
    naux = df_factors.shape[1]
    low = (me % 2).reshape(1)

    def over(a, s):
        return lax.ppermute(a, "aux", xor(n_aux, s))

    fac = jnp.stack([thc_left, thc_right])
    fac = jnp.concatenate([fac, over(fac, 2)], axis=2)
    cols = fac.shape[-1]

    def rows_over_pair(fac, axis):
        step = n_pair >> (axis + 1)
        got = lax.ppermute(fac, "pair", xor(n_pair, step))
        first = (me // step) % 2 == 0
        return jnp.stack([jnp.where(first, fac, got), jnp.where(first, got, fac)], axis=axis)

    n_steps = n_pair.bit_length() - 1

    flipped, fac = tie(amplitudes.T, fac)
    far_amps = over(flipped, 2)
    near = jnp.concatenate([flipped, over(flipped, 1)], axis=0)
    for axis in range(n_steps - 2):
        fac = rows_over_pair(fac, axis)
    far_amps, fac = tie(far_amps, fac)
    amps = jnp.concatenate([near, far_amps, over(far_amps, 1)], axis=0)

    n_far = 2 * nocc
    size = rows // n_far
    far = [over(df_factors[j * size : (j + 1) * size], 2) for j in range(n_far)]
    due = {0: (1,), 1: (2, 3), 2: (), 3: (4, 5), 4: (6, 7)}

    def beside(stage, a):
        nonlocal fac
        wanted = [j for j in due[stage] if j < n_far]
        a, *got = tie(a, *(far[j] for j in wanted))
        for j, b in zip(wanted, got):
            far[j] = b
        if stage == 0:
            a, fac = tie(a, rows_over_pair(fac, n_steps - 2))
        elif stage == 3:
            a, fac = tie(a, rows_over_pair(fac, n_steps - 1))
        return a

    gram = dot(amps, df_factors, 1, 0)
    gram, far[0] = tie(gram, far[0])
    gram = all_reduce(
        gram.reshape(2, -1, naux),
        n_pair,
        lambda a: jnp.stack([a[0], over(a[1], 2)]),
        beside,
    )

    fac = fac.reshape(n_pair, 2, -1, cols)
    left = fac[:, 0].reshape(nvirt, cols)
    right = fac[:, 1].reshape(nvirt, cols)
    right = jnp.concatenate(
        [take(right, k * width, width), take(right, (k ^ 1) * width, width)], axis=0
    )
    middle = jnp.stack(
        [
            jnp.sum(dot(near[:, i * nvirt : (i + 1) * nvirt], left, 1, 0) * right.astype(F32), axis=0)
            for i in range(nocc)
        ]
    )
    vir_col = vir_energy[:, None]
    vir_row = take(vir_energy, k * width, width)[None, :]
    coulomb_block = take(coulomb, k * width, width, 1)
    for step in range(ITERS):
        last = step == ITERS - 1
        other = over(middle, 2)
        middle = middle + jnp.concatenate([other[:, cols // 2 :], other[:, : cols // 2]], axis=1)
        mine, theirs = pl.pallas_call(
            functools.partial(residual_kernel, n_far),
            out_shape=(
                jax.ShapeDtypeStruct((rows, width), F32),
                jax.ShapeDtypeStruct((rows, width), BF),
            ),
            in_specs=[SMEM] + [VMEM] * (6 + n_far),
            out_specs=(VMEM, VMEM),
            scratch_shapes=[pltpu.VMEM((2, 2 * width, naux), BF)],
            compiler_params=PARAMS,
        )(low, middle, left, right, *gram, df_factors, *far)
        got = over(theirs, 1)
        new = pl.pallas_call(
            functools.partial(update_kernel, last),
            out_shape=jax.ShapeDtypeStruct((rows, width) if last else (width, rows), BF),
            in_specs=[SMEM] * 2 + [VMEM] * 5,
            out_specs=VMEM,
            compiler_params=PARAMS,
        )(occ_energy, pivot_energy, mine, got, coulomb_block, vir_col, vir_row)
        if not last:
            gram, middle = pl.pallas_call(
                functools.partial(gram_kernel, n_far),
                out_shape=(
                    jax.ShapeDtypeStruct((2, 2 * width, naux), F32),
                    jax.ShapeDtypeStruct((nocc, cols), F32),
                ),
                in_specs=[VMEM] * (5 + n_far),
                out_specs=(VMEM, VMEM),
                scratch_shapes=[pltpu.VMEM((2 * width, rows), BF)],
                compiler_params=PARAMS,
            )(new, over(new, 1), left, right, df_factors, *far)
            gram = all_reduce(gram, n_pair)
    return new


def solution(mesh):
    in_specs = (
        P("pair", "aux"),
        P("pair", None),
        P("pair", "aux"),
        P("pair", "aux"),
        P("pair", "aux"),
        P("pair"),
        P(),
        P(),
    )
    out_specs = P("pair", "aux")
    return jax.shard_map(
        per_device, mesh=mesh, in_specs=in_specs, out_specs=out_specs, check_vma=False
    )
```

time: 362 us -> 147 us (0.41)
  blocking collectives: 211 us -> 0 us
  starting transfers between devices: 0.12 us -> 47.7 us
  waiting for transfers between devices: 98.6 us -> 67.2 us
  matrix products: 20.9 us -> 4.95 us
  between operations: 13.9 us -> 1.24 us
  Pallas kernels: 0 us -> 10.5 us
    psum x2 -> x0, blocking collectives: 147 us -> none  [per_device(): gram = lax.psum(gram, 'pair').astype(jnp.bfloat16)]
    reduce_scatter x2 -> x0, waiting for transfers between devices: 75.2 us -> none  [per_device(): share = lax.psum_scatter(part, 'aux', scatter_dimension=1, tiled=True)]
    ppermute x0 -> x37, waiting for transfers between devices: none -> 67.2 us  [the longest x18 30 us: over(): return lax.ppermute(a, 'aux', xor(n_aux, s))]
    all_gather x2 -> x0, blocking collectives: 64.1 us -> none  [the longest x1 33 us: per_device(): lax.all_gather(thc_left, 'pair', axis=0, tiled=True)]
    ppermute x0 -> x37, starting transfers between devices: none -> 47.7 us  [the longest x16 24 us: send(): return lax.ppermute(a, 'pair', xor(n, s))]
    all_gather x2 -> x0, waiting for transfers between devices: 22.7 us -> none  [per_device(): whole = lax.all_gather(local, 'aux', axis=1, tiled=True)]
    dot_general x8 -> x5, matrix products: 20.9 us -> 4.95 us  [dot(): lax.dot_general(a, b, (((ca,), (cb,)), ((), ())), preferred_element_type=...]
    pallas_call x0 -> x5, Pallas kernels: none -> 10.5 us  [the longest x2 5.07 us: per_device(): pl.pallas_call(functools.partial(residual_kernel, n_far), out_shape=(jax....]
  transfers between devices with their start and end apart: 4 -> 37, of which waited for: 3 -> 24; matrix products, arithmetic and copies ran while one was open for 2% -> 9% of each run, Pallas kernels for 0% -> 0%
where the time goes in v2:
time: 147 us
  waiting for transfers between devices  67.2 us (46%)
  starting transfers between devices  47.7 us (32%)
  Pallas kernels  10.5 us (7%)
  local copies, waits for them, and re-layouts  9.67 us (7%)
  other arithmetic  5.41 us (4%)
  matrix products  4.95 us (3%)
    ppermute x18, waiting for transfers between devices, over(): return lax.ppermute(a, 'aux', xor(n_aux, s))  30 us
    ppermute x16, waiting for transfers between devices, send(): return lax.ppermute(a, 'pair', xor(n, s))  28.3 us
    ppermute x16, starting transfers between devices, send(): return lax.ppermute(a, 'pair', xor(n, s))  24 us
    ppermute x18, starting transfers between devices, over(): return lax.ppermute(a, 'aux', xor(n_aux, s))  17.7 us
    ppermute x3, waiting for transfers between devices, rows_over_pair(): got = lax.ppermute(fac, 'pair', xor(n_pair, step))  8.87 us
    ppermute x3, starting transfers between devices, rows_over_pair(): got = lax.ppermute(fac, 'pair', xor(n_pair, step))  6.02 us
    pallas_call x2, Pallas kernels, per_device(): pl.pallas_call(functools.partial(residual_kernel, n_far), out_shape=(jax....  5.07 us
    dot_general x5, matrix products, dot(): lax.dot_general(a, b, (((ca,), (cb,)), ((), ())), preferred_element_type=...  4.95 us
  transfers between devices with their start and end apart: 37, of which 24 were waited for; matrix products, arithmetic and copies ran while one was open for 9% of the time, Pallas kernels for 0%

profile of v2, /device:TPU:0, one launch (start us, length us, event | category | flops | bytes accessed | tf_op | source)
XLA Modules:
  0.0 146.6 jit_solution(13025402861745085326)
XLA Ops:
  1.0 3.0 %collective-permute-start = (bf16[2,64,384]{2,1,0:T(8,128)(2,1)S(1)}, bf16[2,64,384]{2,1,0:T(8,128)(2,1)S(1)}, u32[]{:S(2)}, u32[]{:S(2)}) collective-permute-start(bf16[2,64,384]{2,1,0:T(8,128)(2,1)S(1)} %pad_maximum_fusion.7), channel_id=1, source_target_pairs={{0,16},{8,24},{16,0},{24,8},{1,17},{9,25},{17,1},{25,9},{2,18},{10... | collective-permute-start | bytes 294920 | tf_op jit(solution)/shard_map/ppermute | solution.py:134
  4.0 2.8 %collective-permute-done = bf16[2,64,384]{2,1,0:T(8,128)(2,1)S(1)} collective-permute-done((bf16[2,64,384]{2,1,0:T(8,128)(2,1)S(1)}, bf16[2,64,384]{2,1,0:T(8,128)(2,1)S(1)}, u32[]{:S(2)}, u32[]{:S(2)}) %collective-permute-start) | collective-permute-done | bytes 98336 | tf_op jit(solution)/shard_map/ppermute | solution.py:134
  7.7 3.0 %collective-permute-start.3 = (bf16[2,64,768]{2,1,0:T(8,128)(2,1)S(1)}, bf16[2,64,768]{2,1,0:T(8,128)(2,1)S(1)}, u32[]{:S(2)}, u32[]{:S(2)}) collective-permute-start(bf16[2,64,768]{2,1,0:T(8,128)(2,1)S(1)} %pad_maximum_fusion.6), channel_id=1, source_target_pairs={{0,4},{1,5},{2,6},{3,7},{4,0},{5,1},{6,2},{7,3},{8,12},{9,13},{10,... | collective-permute-start | bytes 589832 | tf_op jit(solution)/shard_map/ppermute | solution.py:142
  10.6 1.5 %collective-permute-start.2 = (bf16[128,2048]{0,1:T(8,128)(2,1)}, bf16[128,2048]{0,1:T(8,128)(2,1)}, u32[]{:S(2)}, u32[]{:S(2)}) collective-permute-start(bf16[128,2048]{0,1:T(8,128)(2,1)} %bitcast.46), channel_id=1, source_target_pairs={{0,16},{8,24},{16,0},{24,8},{1,17},{9,25},{17,1},{25,9},{2,18},{10... | collective-permute-start | bytes 1572872 | tf_op jit(solution)/shard_map/ppermute | solution.py:134
  12.1 6.8 %collective-permute-done.3 = bf16[2,64,768]{2,1,0:T(8,128)(2,1)S(1)} collective-permute-done((bf16[2,64,768]{2,1,0:T(8,128)(2,1)S(1)}, bf16[2,64,768]{2,1,0:T(8,128)(2,1)S(1)}, u32[]{:S(2)}, u32[]{:S(2)}) %collective-permute-start.3) | collective-permute-done | bytes 196640 | tf_op jit(solution)/shard_map/ppermute | solution.py:142
  19.0 4.1 %collective-permute-done.2 = bf16[128,2048]{0,1:T(8,128)(2,1)} collective-permute-done((bf16[128,2048]{0,1:T(8,128)(2,1)}, bf16[128,2048]{0,1:T(8,128)(2,1)}, u32[]{:S(2)}, u32[]{:S(2)}) %collective-permute-start.2) | collective-permute-done | bytes 524320 | tf_op jit(solution)/shard_map/ppermute | solution.py:134
  23.2 2.8 %fusion.19 = (bf16[256,512]{1,0:T(8,128)(2,1)}, bf16[256,512]{1,0:T(8,128)(2,1)}, bf16[256,512]{1,0:T(8,128)(2,1)}, bf16[256,512]{1,0:T(8,128)(2,1)}, bf16[256,5...) fusion(bf16[2048,512]{1,0:T(8,128)(2,1)} %own.5), kind=kLoop, calls=%fused_computation.68 | loop fusion | bytes 4194304 | tf_op jit(solution)/shard_map/slice | solution.py:158
  26.0 1.5 %collective-permute-start.5 = (bf16[256,512]{1,0:T(8,128)(2,1)}, bf16[256,512]{1,0:T(8,128)(2,1)S(1)}, u32[]{:S(2)}, u32[]{:S(2)}) collective-permute-start(bf16[256,512]{1,0:T(8,128)(2,1)} %get-tuple-element.70), channel_id=1, source_target_pairs={{0,16},{8,24},{16,0},{24,8},{1,17},{9,25},{17,1},{25,9},{2,18},{10... | collective-permute-start | bytes 786440 | tf_op jit(solution)/shard_map/ppermute | solution.py:134
  28.0 1.6 %collective-permute-start.8 = (bf16[2,2,64,768]{3,2,1,0:T(8,128)(2,1)S(1)}, bf16[2,2,64,768]{3,2,1,0:T(8,128)(2,1)S(1)}, u32[]{:S(2)}, u32[]{:S(2)}) collective-permute-start(bf16[2,2,64,768]{3,2,1,0:T(8,128)(2,1)S(1)} %pad_maximum_fusion.2), channel_id=1, source_target_pairs={{0,2},{1,3},{2,0},{3,1},{4,6},{5,7},{6,4},{7,5},{8,10},{9,11},{10,... | collective-permute-start | bytes 1179656 | tf_op jit(solution)/shard_map/ppermute | solution.py:142
  29.6 3.4 %fusion = f32[512,512]{1,0:T(8,128)S(1)} fusion(bf16[2048,512]{1,0:T(8,128)(2,1)} %own.5, bf16[128,2048]{0,1:T(8,128)(2,1)} %collective-permute-done.4, bf16[128,2048]{0,1:T(8,128)(2,1)} %collective-permute-done.2, bf16[128,2048]{0,1:T(8,128)(2,1)} %collective-permute-done.1, bf16[128,2048]{0,1:T(8,128)(2,1)S(1)} %bitcast.49), kind=kOutput, calls=%fused_computation | convolution fusion | flops 1082130432 | bytes 5242880 | tf_op jit(solution)/shard_map/dot_general | solution.py:23
  33.0 2.3 %collective-permute-done.5.refs_0_ = bf16[256,512]{1,0:T(8,128)(2,1)S(1)} collective-permute-done((bf16[256,512]{1,0:T(8,128)(2,1)}, bf16[256,512]{1,0:T(8,128)(2,1)S(1)}, u32[]{:S(2)}, u32[]{:S(2)}) %collective-permute-start.5) | collective-permute-done | bytes 262176 | tf_op jit(solution)/shard_map/ppermute | solution.py:134
  35.3 1.6 %collective-permute-start.6 = (bf16[2,128,512]{2,1,0:T(8,128)(2,1)S(1)}, bf16[2,128,512]{2,1,0:T(8,128)(2,1)S(1)}, u32[]{:S(2)}, u32[]{:S(2)}) collective-permute-start(bf16[2,128,512]{2,1,0:T(8,128)(2,1)S(1)} %dynamic-slice_convert_fusion.1), channel_id=1, source_target_pairs={{0,1},{1,0},{2,3},{3,2},{4,5},{5,4},{6,7},{7,6},{8,9},{9,8},{10,11... | collective-permute-start | bytes 786440 | tf_op jit(solution)/shard_map/ppermute | solution.py:42
  36.9 2.1 %collective-permute-done.8 = bf16[2,2,64,768]{3,2,1,0:T(8,128)(2,1)S(1)} collective-permute-done((bf16[2,2,64,768]{3,2,1,0:T(8,128)(2,1)S(1)}, bf16[2,2,64,768]{3,2,1,0:T(8,128)(2,1)S(1)}, u32[]{:S(2)}, u32[]{:S(2)}) %collective-permute-start.8) | collective-permute-done | bytes 393248 | tf_op jit(solution)/shard_map/ppermute | solution.py:142
  40.5 2.4 %collective-permute-done.6 = bf16[2,128,512]{2,1,0:T(8,128)(2,1)S(1)} collective-permute-done((bf16[2,128,512]{2,1,0:T(8,128)(2,1)S(1)}, bf16[2,128,512]{2,1,0:T(8,128)(2,1)S(1)}, u32[]{:S(2)}, u32[]{:S(2)}) %collective-permute-start.6) | collective-permute-done | bytes 262176 | tf_op jit(solution)/shard_map/ppermute | solution.py:42
  44.5 1.4 collective-permute-start.11
  45.9 1.7 %collective-permute-start.10 = (bf16[2,32,512]{2,1,0:T(8,128)(2,1)}, bf16[2,32,512]{2,1,0:T(8,128)(2,1)}, u32[]{:S(2)}, u32[]{:S(2)}) collective-permute-start(bf16[2,32,512]{2,1,0:T(8,128)(2,1)} %get-tuple-element.94), channel_id=1, source_target_pairs={{0,4},{1,5},{2,6},{3,7},{4,0},{5,1},{6,2},{7,3},{8,12},{9,13},{10,... | collective-permute-start | bytes 196616 | tf_op jit(solution)/shard_map/ppermute | solution.py:42
  48.9 1.5 %collective-permute-start.12 = (bf16[256,512]{1,0:T(8,128)(2,1)}, bf16[256,512]{1,0:T(8,128)(2,1)S(1)}, u32[]{:S(2)}, u32[]{:S(2)}) collective-permute-start(bf16[256,512]{1,0:T(8,128)(2,1)} %get-tuple-element.68), channel_id=1, source_target_pairs={{0,16},{8,24},{16,0},{24,8},{1,17},{9,25},{17,1},{25,9},{2,18},{10... | collective-permute-start | bytes 786440 | tf_op jit(solution)/shard_map/ppermute | solution.py:134
  50.9 1.5 %collective-permute-start.18 = (bf16[256,512]{1,0:T(8,128)(2,1)}, bf16[256,512]{1,0:T(8,128)(2,1)S(1)}, u32[]{:S(2)}, u32[]{:S(2)}) collective-permute-start(bf16[256,512]{1,0:T(8,128)(2,1)} %get-tuple-element.66), channel_id=1, source_target_pairs={{0,16},{8,24},{16,0},{24,8},{1,17},{9,25},{17,1},{25,9},{2,18},{10... | collective-permute-start | bytes 786440 | tf_op jit(solution)/shard_map/ppermute | solution.py:134
  52.6 1.5 %collective-permute-start.20 = (bf16[2,2,2,64,768]{4,3,2,1,0:T(8,128)(2,1)}, bf16[2,2,2,64,768]{4,3,2,1,0:T(8,128)(2,1)S(1)}, u32[]{:S(2)}, u32[]{:S(2)}) collective-permute-start(bf16[2,2,2,64,768]{4,3,2,1,0:T(8,128)(2,1)} %pad_maximum_fusion.1), channel_id=1, source_target_pairs={{0,1},{1,0},{2,3},{3,2},{4,5},{5,4},{6,7},{7,6},{8,9},{9,8},{10,11... | collective-permute-start | bytes 2359304 | tf_op jit(solution)/shard_map/ppermute | solution.py:142
  55.1 3.2 %collective-permute-done.12.refs_2_ = bf16[256,512]{1,0:T(8,128)(2,1)S(1)} collective-permute-done((bf16[256,512]{1,0:T(8,128)(2,1)}, bf16[256,512]{1,0:T(8,128)(2,1)S(1)}, u32[]{:S(2)}, u32[]{:S(2)}) %collective-permute-start.12) | collective-permute-done | bytes 262176 | tf_op jit(solution)/shard_map/ppermute | solution.py:134
  58.4 5.3 %collective-permute-done.13.refs_3_ = bf16[256,512]{1,0:T(8,128)(2,1)S(1)} collective-permute-done((bf16[256,512]{1,0:T(8,128)(2,1)}, bf16[256,512]{1,0:T(8,128)(2,1)S(1)}, u32[]{:S(2)}, u32[]{:S(2)}) %collective-permute-start.13) | collective-permute-done | bytes 262176 | tf_op jit(solution)/shard_map/ppermute | solution.py:134
  63.7 1.6 %collective-permute-start.14 = (bf16[32,512]{1,0:T(8,128)(2,1)S(1)}, bf16[32,512]{1,0:T(8,128)(2,1)S(1)}, u32[]{:S(2)}, u32[]{:S(2)}) collective-permute-start(bf16[32,512]{1,0:T(8,128)(2,1)S(1)} %get-tuple-element.96), channel_id=1, source_target_pairs={{0,16},{8,24},{16,0},{24,8},{1,17},{9,25},{17,1},{25,9},{2,18},{10... | collective-permute-start | bytes 98312 | tf_op jit(solution)/shard_map/ppermute | solution.py:134
  67.7 1.4 collective-permute-start.15
  69.9 2.2 %collective-permute-start.17 = (bf16[2,32,512]{2,1,0:T(8,128)(2,1)S(1)}, bf16[2,32,512]{2,1,0:T(8,128)(2,1)S(1)}, u32[]{:S(2)}, u32[]{:S(2)}) collective-permute-start(bf16[2,32,512]{2,1,0:T(8,128)(2,1)S(1)} %pad_maximum_fusion.8), channel_id=1, source_target_pairs={{0,2},{1,3},{2,0},{3,1},{4,6},{5,7},{6,4},{7,5},{8,10},{9,11},{10,... | collective-permute-start | bytes 196616 | tf_op jit(solution)/shard_map/ppermute | solution.py:42
  73.9 1.5 %collective-permute-start.19 = (bf16[256,512]{1,0:T(8,128)(2,1)S(1)}, bf16[256,512]{1,0:T(8,128)(2,1)S(1)}, u32[]{:S(2)}, u32[]{:S(2)}) collective-permute-start(bf16[256,512]{1,0:T(8,128)(2,1)S(1)} %copy-done.27), channel_id=1, source_target_pairs={{0,16},{8,24},{16,0},{24,8},{1,17},{9,25},{17,1},{25,9},{2,18},{10... | collective-permute-start | bytes 786440 | tf_op jit(solution)/shard_map/ppermute | solution.py:134
  75.4 1.4 collective-permute-start.23
  77.5 5.1 %collective-permute-done.19.refs_5_ = bf16[256,512]{1,0:T(8,128)(2,1)S(1)} collective-permute-done((bf16[256,512]{1,0:T(8,128)(2,1)S(1)}, bf16[256,512]{1,0:T(8,128)(2,1)S(1)}, u32[]{:S(2)}, u32[]{:S(2)}) %collective-permute-start.19) | collective-permute-done | bytes 262176 | tf_op jit(solution)/shard_map/ppermute | solution.py:134
  84.8 1.6 %collective-permute-start.21 = (f32[4,768]{1,0:T(4,128)S(1)}, f32[4,768]{1,0:T(4,128)S(1)}, u32[]{:S(2)}, u32[]{:S(2)}) collective-permute-start(f32[4,768]{1,0:T(4,128)S(1)} %pad_maximum_fusion.9), channel_id=1, source_target_pairs={{0,16},{8,24},{16,0},{24,8},{1,17},{9,25},{17,1},{25,9},{2,18},{10... | collective-permute-start | bytes 36872 | tf_op jit(solution)/shard_map/ppermute | solution.py:134
  86.4 1.6 %collective-permute-start.22 = (bf16[2,128,512]{2,1,0:T(8,128)(2,1)S(1)}, bf16[2,128,512]{2,1,0:T(8,128)(2,1)S(1)}, u32[]{:S(2)}, u32[]{:S(2)}) collective-permute-start(bf16[2,128,512]{2,1,0:T(8,128)(2,1)S(1)} %pad_maximum_fusion.4.line), channel_id=1, source_target_pairs={{0,1},{1,0},{2,3},{3,2},{4,5},{5,4},{6,7},{7,6},{8,9},{9,8},{10,11... | collective-permute-start | bytes 786440 | tf_op jit(solution)/shard_map/ppermute | solution.py:42
  88.6 4.2 %collective-permute-done.22.other = bf16[2,128,512]{2,1,0:T(8,128)(2,1)S(1)} collective-permute-done((bf16[2,128,512]{2,1,0:T(8,128)(2,1)S(1)}, bf16[2,128,512]{2,1,0:T(8,128)(2,1)S(1)}, u32[]{:S(2)}, u32[]{:S(2)}) %collective-permute-start.22) | collective-permute-done | bytes 262176 | tf_op jit(solution)/shard_map/ppermute | solution.py:42
  92.9 2.9 %shard_map.82 = (f32[2048,128]{1,0:T(8,128)S(1)}, bf16[2048,128]{1,0:T(8,128)(2,1)}) custom-call(s32[1]{0:T(128)} %bitcast.side, f32[4,768]{1,0:T(4,128)S(1)} %maximum_add_fusion.middle, bf16[512,768]{1,0:T(8,128)(2,1)S(1)} %bitcast.39, bf16[256,768]{1,0:T(8,128)(2,1)S(1)} %pad_maximum_fusion.3.right, bf16[2,128,512]{2,1,0:T(8,128)(2,1)S(1)} %pad_maximum_fusion.4.line, ...), custom_call_target="tpu_custom_call" | custom-call | tf_op jit(solution)/shard_map/pallas_call | solution.py:201
  100.4 1.6 %shard_map.83.mine = bf16[128,2048]{1,0:T(8,128)(2,1)S(1)} custom-call(f32[4]{0:T(128)S(1)} %copy-done.24, f32[1]{0:T(128)S(6)} %copy.14.pivot, f32[2048,128]{1,0:T(8,128)S(1)} %copy-done.23, bf16[2048,128]{1,0:T(8,128)(2,1)} %collective-permute-done.25.got, bf16[2048,128]{1,0:T(8,128)(2,1)S(1)} %constant_dynamic-slice_fusion.3.coulomb, ...), custom_call_target="tpu_custom_call" | custom-call | tf_op jit(solution)/shard_map/pallas_call | solution.py:213
  102.3 1.7 %collective-permute-done.26.other = bf16[128,2048]{1,0:T(8,128)(2,1)S(1)} collective-permute-done((bf16[128,2048]{1,0:T(8,128)(2,1)S(1)}, bf16[128,2048]{1,0:T(8,128)(2,1)S(1)}, u32[]{:S(2)}, u32[]{:S(2)}) %collective-permute-start.26) | collective-permute-done | bytes 524320 | tf_op jit(solution)/shard_map/ppermute | solution.py:134
  104.9 2.1 %shard_map.84 = (f32[2,256,512]{2,1,0:T(8,128)S(1)}, f32[4,768]{1,0:T(4,128)S(1)}) custom-call(bf16[128,2048]{1,0:T(8,128)(2,1)S(1)} %shard_map.83.mine, bf16[128,2048]{1,0:T(8,128)(2,1)S(1)} %collective-permute-done.26.other, bf16[512,768]{1,0:T(8,128)(2,1)S(1)} %bitcast.40, bf16[256,768]{1,0:T(8,128)(2,1)S(1)} %pad_maximum_fusion.3.right, ...), custom_call_target="tpu_custom_call" | custom-call | tf_op jit(solution)/shard_map/pallas_call | solution.py:221
  107.1 1.6 %collective-permute-start.28 = (bf16[2,128,512]{2,1,0:T(8,128)(2,1)S(1)}, bf16[2,128,512]{2,1,0:T(8,128)(2,1)S(1)}, u32[]{:S(2)}, u32[]{:S(2)}) collective-permute-start(bf16[2,128,512]{2,1,0:T(8,128)(2,1)S(1)} %dynamic-slice_convert_fusion), channel_id=1, source_target_pairs={{0,1},{1,0},{2,3},{3,2},{4,5},{5,4},{6,7},{7,6},{8,9},{9,8},{10,11... | collective-permute-start | bytes 786440 | tf_op jit(solution)/shard_map/ppermute | solution.py:42
  108.7 7.0 %collective-permute-done.28 = bf16[2,128,512]{2,1,0:T(8,128)(2,1)S(1)} collective-permute-done((bf16[2,128,512]{2,1,0:T(8,128)(2,1)S(1)}, bf16[2,128,512]{2,1,0:T(8,128)(2,1)S(1)}, u32[]{:S(2)}, u32[]{:S(2)}) %collective-permute-start.28) | collective-permute-done | bytes 262176 | tf_op jit(solution)/shard_map/ppermute | solution.py:42
  115.8 1.4 collective-permute-start.31
  117.4 2.9 %collective-permute-start.29 = (bf16[2,32,512]{2,1,0:T(8,128)(2,1)S(1)}, bf16[2,32,512]{2,1,0:T(8,128)(2,1)S(1)}, u32[]{:S(2)}, u32[]{:S(2)}) collective-permute-start(bf16[2,32,512]{2,1,0:T(8,128)(2,1)S(1)} %get-tuple-element.85), channel_id=1, source_target_pairs={{0,2},{1,3},{2,0},{3,1},{4,6},{5,7},{6,4},{7,5},{8,10},{9,11},{10,... | collective-permute-start | bytes 196616 | tf_op jit(solution)/shard_map/ppermute | solution.py:42
  120.2 2.3 %collective-permute-done.31 = bf16[2,32,512]{2,1,0:T(8,128)(2,1)S(1)} collective-permute-done((bf16[2,32,512]{2,1,0:T(8,128)(2,1)S(1)}, bf16[2,32,512]{2,1,0:T(8,128)(2,1)S(1)}, u32[]{:S(2)}, u32[]{:S(2)}) %collective-permute-start.31) | collective-permute-done | bytes 65568 | tf_op jit(solution)/shard_map/ppermute | solution.py:42
  123.9 1.5 %collective-permute-start.32 = (bf16[2,32,512]{2,1,0:T(8,128)(2,1)S(1)}, bf16[2,32,512]{2,1,0:T(8,128)(2,1)S(1)}, u32[]{:S(2)}, u32[]{:S(2)}) collective-permute-start(bf16[2,32,512]{2,1,0:T(8,128)(2,1)S(1)} %add_convert_fusion), channel_id=1, source_target_pairs={{0,6},{1,7},{2,4},{3,5},{4,2},{5,3},{6,0},{7,1},{8,14},{9,15},{10,... | collective-permute-start | bytes 196616 | tf_op jit(solution)/shard_map/ppermute | solution.py:42
  126.0 2.3 %collective-permute-start.34 = (bf16[2,32,512]{2,1,0:T(8,128)(2,1)S(1)}, bf16[2,32,512]{2,1,0:T(8,128)(2,1)S(1)}, u32[]{:S(2)}, u32[]{:S(2)}) collective-permute-start(bf16[2,32,512]{2,1,0:T(8,128)(2,1)S(1)} %add_convert_fusion), channel_id=1, source_target_pairs={{0,2},{1,3},{2,0},{3,1},{4,6},{5,7},{6,4},{7,5},{8,10},{9,11},{10,... | collective-permute-start | bytes 196616 | tf_op jit(solution)/shard_map/ppermute | solution.py:42
  128.9 2.0 %collective-permute-done.32 = bf16[2,32,512]{2,1,0:T(8,128)(2,1)S(1)} collective-permute-done((bf16[2,32,512]{2,1,0:T(8,128)(2,1)S(1)}, bf16[2,32,512]{2,1,0:T(8,128)(2,1)S(1)}, u32[]{:S(2)}, u32[]{:S(2)}) %collective-permute-start.32) | collective-permute-done | bytes 65568 | tf_op jit(solution)/shard_map/ppermute | solution.py:42
  130.8 1.7 %collective-permute-done.33 = bf16[2,32,512]{2,1,0:T(8,128)(2,1)S(1)} collective-permute-done((bf16[2,32,512]{2,1,0:T(8,128)(2,1)S(1)}, bf16[2,32,512]{2,1,0:T(8,128)(2,1)S(1)}, u32[]{:S(2)}, u32[]{:S(2)}) %collective-permute-start.33) | collective-permute-done | bytes 65568 | tf_op jit(solution)/shard_map/ppermute | solution.py:42
  132.6 1.6 %collective-permute-start.35 = (bf16[2,128,512]{2,1,0:T(8,128)(2,1)S(1)}, bf16[2,128,512]{2,1,0:T(8,128)(2,1)S(1)}, u32[]{:S(2)}, u32[]{:S(2)}) collective-permute-start(bf16[2,128,512]{2,1,0:T(8,128)(2,1)S(1)} %pad_maximum_fusion.5.line), channel_id=1, source_target_pairs={{0,1},{1,0},{2,3},{3,2},{4,5},{5,4},{6,7},{7,6},{8,9},{9,8},{10,11... | collective-permute-start | bytes 786440 | tf_op jit(solution)/shard_map/ppermute | solution.py:42
  134.1 6.7 %collective-permute-done.35.other = bf16[2,128,512]{2,1,0:T(8,128)(2,1)S(1)} collective-permute-done((bf16[2,128,512]{2,1,0:T(8,128)(2,1)S(1)}, bf16[2,128,512]{2,1,0:T(8,128)(2,1)S(1)}, u32[]{:S(2)}, u32[]{:S(2)}) %collective-permute-start.35) | collective-permute-done | bytes 262176 | tf_op jit(solution)/shard_map/ppermute | solution.py:42
  140.8 2.1 %shard_map.85 = (f32[2048,128]{1,0:T(8,128)S(1)}, bf16[2048,128]{1,0:T(8,128)(2,1)S(1)}) custom-call(s32[1]{0:T(128)} %bitcast.side, f32[4,768]{1,0:T(4,128)S(1)} %maximum_add_fusion.1.middle, bf16[512,768]{1,0:T(8,128)(2,1)S(1)} %bitcast.41, bf16[256,768]{1,0:T(8,128)(2,1)S(1)} %pad_maximum_fusion.3.right, bf16[2,128,512]{2,1,0:T(8,128)(2,1)S(1)} %pad_maximum_fusion.5.line, ...), custom_call_target="tpu_custom_call" | custom-call | tf_op jit(solution)/shard_map/pallas_call | solution.py:201
  143.0 1.9 %collective-permute-done.36.got = bf16[2048,128]{1,0:T(8,128)(2,1)S(1)} collective-permute-done((bf16[2048,128]{1,0:T(8,128)(2,1)S(1)}, bf16[2048,128]{1,0:T(8,128)(2,1)S(1)}, u32[]{:S(2)}, u32[]{:S(2)}) %collective-permute-start.36) | collective-permute-done | bytes 524320 | tf_op jit(solution)/shard_map/ppermute | solution.py:134
  144.9 1.7 %shard_map.86 = bf16[2048,128]{1,0:T(8,128)(2,1)} custom-call(f32[4]{0:T(128)S(1)} %copy-done.24, f32[1]{0:T(128)S(6)} %copy.14.pivot, f32[2048,128]{1,0:T(8,128)S(1)} %get-tuple-element.57.mine, bf16[2048,128]{1,0:T(8,128)(2,1)S(1)} %collective-permute-done.36.got, bf16[2048,128]{1,0:T(8,128)(2,1)S(1)} %constant_dynamic-slice_fusion.3.coulomb, ...), custom_call_target="tpu_custom_call" | custom-call | tf_op jit(solution)/shard_map/pallas_call | solution.py:213
  (134 shorter events, 25.0 us)
Async XLA Ops:
  0.0 97.9 %copy-start = (bf16[2048,512]{1,0:T(8,128)(2,1)S(1)}, bf16[2048,512]{1,0:T(8,128)(2,1)}, u32[]{:S(2)}) copy-start(bf16[2048,512]{1,0:T(8,128)(2,1)} %param.9) | copy-start | bytes 6291460
  1.0 5.8 %collective-permute-start = (bf16[2,64,384]{2,1,0:T(8,128)(2,1)S(1)}, bf16[2,64,384]{2,1,0:T(8,128)(2,1)S(1)}, u32[]{:S(2)}, u32[]{:S(2)}) collective-permute-start(bf16[2,64,384]{2,1,0:T(8,128)(2,1)S(1)} %pad_maximum_fusion.7), channel_id=1, source_target_pairs={{0,16},{8,24},{16,0},{24,8},{1,17},{9,25},{17,1},{25,9},{2,18},{10... | collective-permute-start | bytes 294920 | tf_op jit(solution)/shard_map/ppermute | solution.py:134
  7.7 11.3 %collective-permute-start.3 = (bf16[2,64,768]{2,1,0:T(8,128)(2,1)S(1)}, bf16[2,64,768]{2,1,0:T(8,128)(2,1)S(1)}, u32[]{:S(2)}, u32[]{:S(2)}) collective-permute-start(bf16[2,64,768]{2,1,0:T(8,128)(2,1)S(1)} %pad_maximum_fusion.6), channel_id=1, source_target_pairs={{0,4},{1,5},{2,6},{3,7},{4,0},{5,1},{6,2},{7,3},{8,12},{9,13},{10,... | collective-permute-start | bytes 589832 | tf_op jit(solution)/shard_map/ppermute | solution.py:142
  10.6 12.6 %collective-permute-start.2 = (bf16[128,2048]{0,1:T(8,128)(2,1)}, bf16[128,2048]{0,1:T(8,128)(2,1)}, u32[]{:S(2)}, u32[]{:S(2)}) collective-permute-start(bf16[128,2048]{0,1:T(8,128)(2,1)} %bitcast.46), channel_id=1, source_target_pairs={{0,16},{8,24},{16,0},{24,8},{1,17},{9,25},{17,1},{25,9},{2,18},{10... | collective-permute-start | bytes 1572872 | tf_op jit(solution)/shard_map/ppermute | solution.py:134
  12.1 17.5 %collective-permute-start.1 = (bf16[128,2048]{0,1:T(8,128)(2,1)}, bf16[128,2048]{0,1:T(8,128)(2,1)}, u32[]{:S(2)}, u32[]{:S(2)}) collective-permute-start(bf16[128,2048]{0,1:T(8,128)(2,1)} %bitcast.47), channel_id=1, source_target_pairs={{0,8},{8,0},{16,24},{24,16},{1,9},{9,1},{17,25},{25,17},{2,10},{10... | collective-permute-start | bytes 1572872 | tf_op jit(solution)/shard_map/ppermute | solution.py:134
  19.0 10.6 %copy-start.26 = (bf16[2048,128]{1,0:T(8,128)(2,1)S(1)}, bf16[2048,128]{1,0:T(8,128)(2,1)}, u32[]{:S(2)}) copy-start(bf16[2048,128]{1,0:T(8,128)(2,1)} %param.8) | copy-start | bytes 1572868
  23.2 6.4 %collective-permute-start.4 = (bf16[128,2048]{0,1:T(8,128)(2,1)}, bf16[128,2048]{0,1:T(8,128)(2,1)}, u32[]{:S(2)}, u32[]{:S(2)}) collective-permute-start(bf16[128,2048]{0,1:T(8,128)(2,1)} %collective-permute-done.2), channel_id=1, source_target_pairs={{0,8},{8,0},{16,24},{24,16},{1,9},{9,1},{17,25},{25,17},{2,10},{10... | collective-permute-start | bytes 1572872 | tf_op jit(solution)/shard_map/ppermute | solution.py:134
  26.0 9.3 %collective-permute-start.5 = (bf16[256,512]{1,0:T(8,128)(2,1)}, bf16[256,512]{1,0:T(8,128)(2,1)S(1)}, u32[]{:S(2)}, u32[]{:S(2)}) collective-permute-start(bf16[256,512]{1,0:T(8,128)(2,1)} %get-tuple-element.70), channel_id=1, source_target_pairs={{0,16},{8,24},{16,0},{24,8},{1,17},{9,25},{17,1},{25,9},{2,18},{10... | collective-permute-start | bytes 786440 | tf_op jit(solution)/shard_map/ppermute | solution.py:134
  27.5 13.0 %collective-permute-start.7 = (bf16[256,512]{1,0:T(8,128)(2,1)}, bf16[256,512]{1,0:T(8,128)(2,1)S(1)}, u32[]{:S(2)}, u32[]{:S(2)}) collective-permute-start(bf16[256,512]{1,0:T(8,128)(2,1)} %get-tuple-element.69), channel_id=1, source_target_pairs={{0,16},{8,24},{16,0},{24,8},{1,17},{9,25},{17,1},{25,9},{2,18},{10... | collective-permute-start | bytes 786440 | tf_op jit(solution)/shard_map/ppermute | solution.py:134
  28.0 11.0 %collective-permute-start.8 = (bf16[2,2,64,768]{3,2,1,0:T(8,128)(2,1)S(1)}, bf16[2,2,64,768]{3,2,1,0:T(8,128)(2,1)S(1)}, u32[]{:S(2)}, u32[]{:S(2)}) collective-permute-start(bf16[2,2,64,768]{3,2,1,0:T(8,128)(2,1)S(1)} %pad_maximum_fusion.2), channel_id=1, source_target_pairs={{0,2},{1,3},{2,0},{3,1},{4,6},{5,7},{6,4},{7,5},{8,10},{9,11},{10,... | collective-permute-start | bytes 1179656 | tf_op jit(solution)/shard_map/ppermute | solution.py:142
  35.3 57.5 %copy-start.3 = (bf16[256,512]{1,0:T(8,128)(2,1)}, bf16[256,512]{1,0:T(8,128)(2,1)S(1)}, u32[]{:S(2)}) copy-start(bf16[256,512]{1,0:T(8,128)(2,1)S(1)} %collective-permute-done.5.refs_0_) | copy-start | bytes 786436
  35.3 7.6 %collective-permute-start.6 = (bf16[2,128,512]{2,1,0:T(8,128)(2,1)S(1)}, bf16[2,128,512]{2,1,0:T(8,128)(2,1)S(1)}, u32[]{:S(2)}, u32[]{:S(2)}) collective-permute-start(bf16[2,128,512]{2,1,0:T(8,128)(2,1)S(1)} %dynamic-slice_convert_fusion.1), channel_id=1, source_target_pairs={{0,1},{1,0},{2,3},{3,2},{4,5},{5,4},{6,7},{7,6},{8,9},{9,8},{10,11... | collective-permute-start | bytes 786440 | tf_op jit(solution)/shard_map/ppermute | solution.py:42
  40.0 33.8 %copy-start.27 = (bf16[256,512]{1,0:T(8,128)(2,1)S(1)}, bf16[256,512]{1,0:T(8,128)(2,1)}, u32[]{:S(2)}) copy-start(bf16[256,512]{1,0:T(8,128)(2,1)} %get-tuple-element.65) | copy-start | bytes 786436
  40.5 32.8 %copy-start.5 = (bf16[256,512]{1,0:T(8,128)(2,1)}, bf16[256,512]{1,0:T(8,128)(2,1)S(1)}, u32[]{:S(2)}) copy-start(bf16[256,512]{1,0:T(8,128)(2,1)S(1)} %collective-permute-done.7.refs_1_) | copy-start | bytes 786436
  44.5 6.4 %collective-permute-start.11 = (bf16[2,32,512]{2,1,0:T(8,128)(2,1)}, bf16[2,32,512]{2,1,0:T(8,128)(2,1)S(1)}, u32[]{:S(2)}, u32[]{:S(2)}) collective-permute-start(bf16[2,32,512]{2,1,0:T(8,128)(2,1)} %get-tuple-element.93), channel_id=1, source_target_pairs={{0,6},{1,7},{2,4},{3,5},{4,2},{5,3},{6,0},{7,1},{8,14},{9,15},{10,... | collective-permute-start | bytes 196616 | tf_op jit(solution)/shard_map/ppermute | solution.py:42
  45.9 6.7 %collective-permute-start.10 = (bf16[2,32,512]{2,1,0:T(8,128)(2,1)}, bf16[2,32,512]{2,1,0:T(8,128)(2,1)}, u32[]{:S(2)}, u32[]{:S(2)}) collective-permute-start(bf16[2,32,512]{2,1,0:T(8,128)(2,1)} %get-tuple-element.94), channel_id=1, source_target_pairs={{0,4},{1,5},{2,6},{3,7},{4,0},{5,1},{6,2},{7,3},{8,12},{9,13},{10,... | collective-permute-start | bytes 196616 | tf_op jit(solution)/shard_map/ppermute | solution.py:42
  47.6 6.6 %collective-permute-start.9 = (bf16[2,32,512]{2,1,0:T(8,128)(2,1)S(1)}, bf16[2,32,512]{2,1,0:T(8,128)(2,1)}, u32[]{:S(2)}, u32[]{:S(2)}) collective-permute-start(bf16[2,32,512]{2,1,0:T(8,128)(2,1)S(1)} %get-tuple-element.92), channel_id=1, source_target_pairs={{0,2},{1,3},{2,0},{3,1},{4,6},{5,7},{6,4},{7,5},{8,10},{9,11},{10,... | collective-permute-start | bytes 196616 | tf_op jit(solution)/shard_map/ppermute | solution.py:42
  48.9 9.5 %collective-permute-start.12 = (bf16[256,512]{1,0:T(8,128)(2,1)}, bf16[256,512]{1,0:T(8,128)(2,1)S(1)}, u32[]{:S(2)}, u32[]{:S(2)}) collective-permute-start(bf16[256,512]{1,0:T(8,128)(2,1)} %get-tuple-element.68), channel_id=1, source_target_pairs={{0,16},{8,24},{16,0},{24,8},{1,17},{9,25},{17,1},{25,9},{2,18},{10... | collective-permute-start | bytes 786440 | tf_op jit(solution)/shard_map/ppermute | solution.py:134
  50.4 13.3 %collective-permute-start.13 = (bf16[256,512]{1,0:T(8,128)(2,1)}, bf16[256,512]{1,0:T(8,128)(2,1)S(1)}, u32[]{:S(2)}, u32[]{:S(2)}) collective-permute-start(bf16[256,512]{1,0:T(8,128)(2,1)} %get-tuple-element.67), channel_id=1, source_target_pairs={{0,16},{8,24},{16,0},{24,8},{1,17},{9,25},{17,1},{25,9},{2,18},{10... | collective-permute-start | bytes 786440 | tf_op jit(solution)/shard_map/ppermute | solution.py:134
  50.9 31.6 %copy-start.25 = (bf16[2,2,2,64,768]{4,3,2,1,0:T(8,128)(2,1)S(1)}, bf16[2,2,2,64,768]{4,3,2,1,0:T(8,128)(2,1)}, u32[]{:S(2)}) copy-start(bf16[2,2,2,64,768]{4,3,2,1,0:T(8,128)(2,1)} %pad_maximum_fusion.1) | copy-start | bytes 2359300
  50.9 26.5 %collective-permute-start.18 = (bf16[256,512]{1,0:T(8,128)(2,1)}, bf16[256,512]{1,0:T(8,128)(2,1)S(1)}, u32[]{:S(2)}, u32[]{:S(2)}) collective-permute-start(bf16[256,512]{1,0:T(8,128)(2,1)} %get-tuple-element.66), channel_id=1, source_target_pairs={{0,16},{8,24},{16,0},{24,8},{1,17},{9,25},{17,1},{25,9},{2,18},{10... | collective-permute-start | bytes 786440 | tf_op jit(solution)/shard_map/ppermute | solution.py:134
  52.6 29.9 %collective-permute-start.20 = (bf16[2,2,2,64,768]{4,3,2,1,0:T(8,128)(2,1)}, bf16[2,2,2,64,768]{4,3,2,1,0:T(8,128)(2,1)S(1)}, u32[]{:S(2)}, u32[]{:S(2)}) collective-permute-start(bf16[2,2,2,64,768]{4,3,2,1,0:T(8,128)(2,1)} %pad_maximum_fusion.1), channel_id=1, source_target_pairs={{0,1},{1,0},{2,3},{3,2},{4,5},{5,4},{6,7},{7,6},{8,9},{9,8},{10,11... | collective-permute-start | bytes 2359304 | tf_op jit(solution)/shard_map/ppermute | solution.py:142
  58.4 24.3 %copy-start.8 = (bf16[256,512]{1,0:T(8,128)(2,1)}, bf16[256,512]{1,0:T(8,128)(2,1)S(1)}, u32[]{:S(2)}) copy-start(bf16[256,512]{1,0:T(8,128)(2,1)S(1)} %collective-permute-done.12.refs_2_) | copy-start | bytes 786436
  63.7 19.0 %copy-start.11 = (bf16[256,512]{1,0:T(8,128)(2,1)}, bf16[256,512]{1,0:T(8,128)(2,1)S(1)}, u32[]{:S(2)}) copy-start(bf16[256,512]{1,0:T(8,128)(2,1)S(1)} %collective-permute-done.13.refs_3_) | copy-start | bytes 786436
  63.7 4.0 %collective-permute-start.14 = (bf16[32,512]{1,0:T(8,128)(2,1)S(1)}, bf16[32,512]{1,0:T(8,128)(2,1)S(1)}, u32[]{:S(2)}, u32[]{:S(2)}) collective-permute-start(bf16[32,512]{1,0:T(8,128)(2,1)S(1)} %get-tuple-element.96), channel_id=1, source_target_pairs={{0,16},{8,24},{16,0},{24,8},{1,17},{9,25},{17,1},{25,9},{2,18},{10... | collective-permute-start | bytes 98312 | tf_op jit(solution)/shard_map/ppermute | solution.py:134
  67.7 6.2 %collective-permute-start.15 = (bf16[2,32,512]{2,1,0:T(8,128)(2,1)S(1)}, bf16[2,32,512]{2,1,0:T(8,128)(2,1)S(1)}, u32[]{:S(2)}, u32[]{:S(2)}) collective-permute-start(bf16[2,32,512]{2,1,0:T(8,128)(2,1)S(1)} %pad_maximum_fusion.8), channel_id=1, source_target_pairs={{0,6},{1,7},{2,4},{3,5},{4,2},{5,3},{6,0},{7,1},{8,14},{9,15},{10,... | collective-permute-start | bytes 196616 | tf_op jit(solution)/shard_map/ppermute | solution.py:42
  69.1 6.3 %collective-permute-start.16 = (bf16[2,32,512]{2,1,0:T(8,128)(2,1)S(1)}, bf16[2,32,512]{2,1,0:T(8,128)(2,1)S(1)}, u32[]{:S(2)}, u32[]{:S(2)}) collective-permute-start(bf16[2,32,512]{2,1,0:T(8,128)(2,1)S(1)} %pad_maximum_fusion.8), channel_id=1, source_target_pairs={{0,4},{1,5},{2,6},{3,7},{4,0},{5,1},{6,2},{7,3},{8,12},{9,13},{10,... | collective-permute-start | bytes 196616 | tf_op jit(solution)/shard_map/ppermute | solution.py:42
  69.9 6.9 %collective-permute-start.17 = (bf16[2,32,512]{2,1,0:T(8,128)(2,1)S(1)}, bf16[2,32,512]{2,1,0:T(8,128)(2,1)S(1)}, u32[]{:S(2)}, u32[]{:S(2)}) collective-permute-start(bf16[2,32,512]{2,1,0:T(8,128)(2,1)S(1)} %pad_maximum_fusion.8), channel_id=1, source_target_pairs={{0,2},{1,3},{2,0},{3,1},{4,6},{5,7},{6,4},{7,5},{8,10},{9,11},{10,... | collective-permute-start | bytes 196616 | tf_op jit(solution)/shard_map/ppermute | solution.py:42
  73.9 8.7 %collective-permute-start.19 = (bf16[256,512]{1,0:T(8,128)(2,1)S(1)}, bf16[256,512]{1,0:T(8,128)(2,1)S(1)}, u32[]{:S(2)}, u32[]{:S(2)}) collective-permute-start(bf16[256,512]{1,0:T(8,128)(2,1)S(1)} %copy-done.27), channel_id=1, source_target_pairs={{0,16},{8,24},{16,0},{24,8},{1,17},{9,25},{17,1},{25,9},{2,18},{10... | collective-permute-start | bytes 786440 | tf_op jit(solution)/shard_map/ppermute | solution.py:134
  75.4 13.2 %collective-permute-start.23 = (bf16[256,512]{1,0:T(8,128)(2,1)}, bf16[256,512]{1,0:T(8,128)(2,1)S(1)}, u32[]{:S(2)}, u32[]{:S(2)}) collective-permute-start(bf16[256,512]{1,0:T(8,128)(2,1)} %get-tuple-element.64), channel_id=1, source_target_pairs={{0,16},{8,24},{16,0},{24,8},{1,17},{9,25},{17,1},{25,9},{2,18},{10... | collective-permute-start | bytes 786440 | tf_op jit(solution)/shard_map/ppermute | solution.py:134
  76.8 11.8 %collective-permute-start.24 = (bf16[256,512]{1,0:T(8,128)(2,1)}, bf16[256,512]{1,0:T(8,128)(2,1)S(1)}, u32[]{:S(2)}, u32[]{:S(2)}) collective-permute-start(bf16[256,512]{1,0:T(8,128)(2,1)} %get-tuple-element.63), channel_id=1, source_target_pairs={{0,16},{8,24},{16,0},{24,8},{1,17},{9,25},{17,1},{25,9},{2,18},{10... | collective-permute-start | bytes 786440 | tf_op jit(solution)/shard_map/ppermute | solution.py:134
  77.5 15.3 %copy-start.14 = (bf16[256,512]{1,0:T(8,128)(2,1)}, bf16[256,512]{1,0:T(8,128)(2,1)S(1)}, u32[]{:S(2)}) copy-start(bf16[256,512]{1,0:T(8,128)(2,1)S(1)} %collective-permute-done.18.refs_4_) | copy-start | bytes 786436
  82.6 10.3 %copy-start.16 = (bf16[256,512]{1,0:T(8,128)(2,1)}, bf16[256,512]{1,0:T(8,128)(2,1)S(1)}, u32[]{:S(2)}) copy-start(bf16[256,512]{1,0:T(8,128)(2,1)S(1)} %collective-permute-done.19.refs_5_) | copy-start | bytes 786436
  84.3 8.6 %copy-start.1 = (bf16[2048,512]{1,0:T(8,128)(2,1)S(1)}, bf16[2048,512]{1,0:T(8,128)(2,1)}, u32[]{:S(2)}) copy-start(bf16[2048,512]{1,0:T(8,128)(2,1)} %own.5) | copy-start | bytes 6291460
  84.8 3.8 %collective-permute-start.21 = (f32[4,768]{1,0:T(4,128)S(1)}, f32[4,768]{1,0:T(4,128)S(1)}, u32[]{:S(2)}, u32[]{:S(2)}) collective-permute-start(f32[4,768]{1,0:T(4,128)S(1)} %pad_maximum_fusion.9), channel_id=1, source_target_pairs={{0,16},{8,24},{16,0},{24,8},{1,17},{9,25},{17,1},{25,9},{2,18},{10... | collective-permute-start | bytes 36872 | tf_op jit(solution)/shard_map/ppermute | solution.py:134
  86.4 6.4 %collective-permute-start.22 = (bf16[2,128,512]{2,1,0:T(8,128)(2,1)S(1)}, bf16[2,128,512]{2,1,0:T(8,128)(2,1)S(1)}, u32[]{:S(2)}, u32[]{:S(2)}) collective-permute-start(bf16[2,128,512]{2,1,0:T(8,128)(2,1)S(1)} %pad_maximum_fusion.4.line), channel_id=1, source_target_pairs={{0,1},{1,0},{2,3},{3,2},{4,5},{5,4},{6,7},{7,6},{8,9},{9,8},{10,11... | collective-permute-start | bytes 786440 | tf_op jit(solution)/shard_map/ppermute | solution.py:42
  96.9 2.3 %collective-permute-start.25 = (bf16[2048,128]{1,0:T(8,128)(2,1)}, bf16[2048,128]{1,0:T(8,128)(2,1)}, u32[]{:S(2)}, u32[]{:S(2)}) collective-permute-start(bf16[2048,128]{1,0:T(8,128)(2,1)} %get-tuple-element.54), channel_id=1, source_target_pairs={{0,8},{8,0},{16,24},{24,16},{1,9},{9,1},{17,25},{25,17},{2,10},{10... | collective-permute-start | bytes 1572872 | tf_op jit(solution)/shard_map/ppermute | solution.py:134
  102.0 2.0 %collective-permute-start.26 = (bf16[128,2048]{1,0:T(8,128)(2,1)S(1)}, bf16[128,2048]{1,0:T(8,128)(2,1)S(1)}, u32[]{:S(2)}, u32[]{:S(2)}) collective-permute-start(bf16[128,2048]{1,0:T(8,128)(2,1)S(1)} %shard_map.83.mine), channel_id=1, source_target_pairs={{0,8},{8,0},{16,24},{24,16},{1,9},{9,1},{17,25},{25,17},{2,10},{10... | collective-permute-start | bytes 1572872 | tf_op jit(solution)/shard_map/ppermute | solution.py:134
  107.1 8.5 %collective-permute-start.28 = (bf16[2,128,512]{2,1,0:T(8,128)(2,1)S(1)}, bf16[2,128,512]{2,1,0:T(8,128)(2,1)S(1)}, u32[]{:S(2)}, u32[]{:S(2)}) collective-permute-start(bf16[2,128,512]{2,1,0:T(8,128)(2,1)S(1)} %dynamic-slice_convert_fusion), channel_id=1, source_target_pairs={{0,1},{1,0},{2,3},{3,2},{4,5},{5,4},{6,7},{7,6},{8,9},{9,8},{10,11... | collective-permute-start | bytes 786440 | tf_op jit(solution)/shard_map/ppermute | solution.py:42
  115.8 6.8 %collective-permute-start.31 = (bf16[2,32,512]{2,1,0:T(8,128)(2,1)S(1)}, bf16[2,32,512]{2,1,0:T(8,128)(2,1)S(1)}, u32[]{:S(2)}, u32[]{:S(2)}) collective-permute-start(bf16[2,32,512]{2,1,0:T(8,128)(2,1)S(1)} %get-tuple-element.86), channel_id=1, source_target_pairs={{0,6},{1,7},{2,4},{3,5},{4,2},{5,3},{6,0},{7,1},{8,14},{9,15},{10,... | collective-permute-start | bytes 196616 | tf_op jit(solution)/shard_map/ppermute | solution.py:42
  117.1 6.8 %collective-permute-start.30 = (bf16[2,32,512]{2,1,0:T(8,128)(2,1)S(1)}, bf16[2,32,512]{2,1,0:T(8,128)(2,1)S(1)}, u32[]{:S(2)}, u32[]{:S(2)}) collective-permute-start(bf16[2,32,512]{2,1,0:T(8,128)(2,1)S(1)} %get-tuple-element.87), channel_id=1, source_target_pairs={{0,4},{1,5},{2,6},{3,7},{4,0},{5,1},{6,2},{7,3},{8,12},{9,13},{10,... | collective-permute-start | bytes 196616 | tf_op jit(solution)/shard_map/ppermute | solution.py:42
  117.4 6.5 %collective-permute-start.29 = (bf16[2,32,512]{2,1,0:T(8,128)(2,1)S(1)}, bf16[2,32,512]{2,1,0:T(8,128)(2,1)S(1)}, u32[]{:S(2)}, u32[]{:S(2)}) collective-permute-start(bf16[2,32,512]{2,1,0:T(8,128)(2,1)S(1)} %get-tuple-element.85), channel_id=1, source_target_pairs={{0,2},{1,3},{2,0},{3,1},{4,6},{5,7},{6,4},{7,5},{8,10},{9,11},{10,... | collective-permute-start | bytes 196616 | tf_op jit(solution)/shard_map/ppermute | solution.py:42
  123.9 6.9 %collective-permute-start.32 = (bf16[2,32,512]{2,1,0:T(8,128)(2,1)S(1)}, bf16[2,32,512]{2,1,0:T(8,128)(2,1)S(1)}, u32[]{:S(2)}, u32[]{:S(2)}) collective-permute-start(bf16[2,32,512]{2,1,0:T(8,128)(2,1)S(1)} %add_convert_fusion), channel_id=1, source_target_pairs={{0,6},{1,7},{2,4},{3,5},{4,2},{5,3},{6,0},{7,1},{8,14},{9,15},{10,... | collective-permute-start | bytes 196616 | tf_op jit(solution)/shard_map/ppermute | solution.py:42
  125.4 7.1 %collective-permute-start.33 = (bf16[2,32,512]{2,1,0:T(8,128)(2,1)S(1)}, bf16[2,32,512]{2,1,0:T(8,128)(2,1)S(1)}, u32[]{:S(2)}, u32[]{:S(2)}) collective-permute-start(bf16[2,32,512]{2,1,0:T(8,128)(2,1)S(1)} %add_convert_fusion), channel_id=1, source_target_pairs={{0,4},{1,5},{2,6},{3,7},{4,0},{5,1},{6,2},{7,3},{8,12},{9,13},{10,... | collective-permute-start | bytes 196616 | tf_op jit(solution)/shard_map/ppermute | solution.py:42
  126.0 6.5 %collective-permute-start.34 = (bf16[2,32,512]{2,1,0:T(8,128)(2,1)S(1)}, bf16[2,32,512]{2,1,0:T(8,128)(2,1)S(1)}, u32[]{:S(2)}, u32[]{:S(2)}) collective-permute-start(bf16[2,32,512]{2,1,0:T(8,128)(2,1)S(1)} %add_convert_fusion), channel_id=1, source_target_pairs={{0,2},{1,3},{2,0},{3,1},{4,6},{5,7},{6,4},{7,5},{8,10},{9,11},{10,... | collective-permute-start | bytes 196616 | tf_op jit(solution)/shard_map/ppermute | solution.py:42
  128.4 5.8 %collective-permute-start.27 = (f32[4,768]{1,0:T(4,128)S(1)}, f32[4,768]{1,0:T(4,128)S(1)}, u32[]{:S(2)}, u32[]{:S(2)}) collective-permute-start(f32[4,768]{1,0:T(4,128)S(1)} %get-tuple-element.55), channel_id=1, source_target_pairs={{0,16},{8,24},{16,0},{24,8},{1,17},{9,25},{17,1},{25,9},{2,18},{10... | collective-permute-start | bytes 36872 | tf_op jit(solution)/shard_map/ppermute | solution.py:134
  132.6 8.2 %collective-permute-start.35 = (bf16[2,128,512]{2,1,0:T(8,128)(2,1)S(1)}, bf16[2,128,512]{2,1,0:T(8,128)(2,1)S(1)}, u32[]{:S(2)}, u32[]{:S(2)}) collective-permute-start(bf16[2,128,512]{2,1,0:T(8,128)(2,1)S(1)} %pad_maximum_fusion.5.line), channel_id=1, source_target_pairs={{0,1},{1,0},{2,3},{3,2},{4,5},{5,4},{6,7},{7,6},{8,9},{9,8},{10,11... | collective-permute-start | bytes 786440 | tf_op jit(solution)/shard_map/ppermute | solution.py:42
  142.9 2.0 %collective-permute-start.36 = (bf16[2048,128]{1,0:T(8,128)(2,1)S(1)}, bf16[2048,128]{1,0:T(8,128)(2,1)S(1)}, u32[]{:S(2)}, u32[]{:S(2)}) collective-permute-start(bf16[2048,128]{1,0:T(8,128)(2,1)S(1)} %get-tuple-element.58), channel_id=1, source_target_pairs={{0,8},{8,0},{16,24},{24,16},{1,9},{9,1},{17,25},{25,17},{2,10},{10... | collective-permute-start | bytes 1572872 | tf_op jit(solution)/shard_map/ppermute | solution.py:134
  (18 other events, 104.1 us)

commit v3 on v2

v3 whole, which is shorter than its diff:
```python
import functools

import jax
import jax.numpy as jnp
from jax import lax
from jax.experimental import pallas as pl
from jax.experimental.pallas import tpu as pltpu
from jax.sharding import PartitionSpec as P

ITERS = 2
BF = jnp.bfloat16
F32 = jnp.float32
VMEM = pl.BlockSpec(memory_space=pltpu.VMEM)
SMEM = pl.BlockSpec(memory_space=pltpu.SMEM)
FAR = lambda rows: [rows // 2, rows // 4, rows // 4]
DUE = {1: (0,), 3: (1,), 4: (2,)}
PARAMS = pltpu.CompilerParams(vmem_limit_bytes=12 * 2**20)


def xor(n, s):
    return [(i, i ^ s) for i in range(n)]


def dot(a, b, ca, cb):
    return lax.dot_general(a, b, (((ca,), (cb,)), ((), ())), preferred_element_type=F32)


def take(a, start, size, axis=0):
    return lax.dynamic_slice_in_dim(a, start, size, axis)


def tie(a, *others):
    return lax.optimization_barrier((a, *others))


def halves(v, low):
    half = v.shape[1] // 2
    return take(v, low * half, half, 1), take(v, (1 - low) * half, half, 1)


def fold(v, n):
    mine, theirs = halves(v, lax.axis_index("pair") % 2)
    return mine, lax.ppermute(theirs.astype(BF), "pair", xor(n, 1))


def all_reduce(mine, got, n, cross=None, beside=lambda stage, a: a):
    high = lax.axis_index("pair") // 2
    m = n // 2
    part = mine.shape[1] // m

    def send(a, s):
        return lax.ppermute(a, "pair", xor(n, s))

    acc = mine + beside(0, got).astype(F32)
    rounded = acc.astype(BF)
    total = take(acc, high * part, part, 1)
    for s in range(1, m):
        total = total + send(take(rounded, (high ^ s) * part, part, 1), 2 * s).astype(F32)
    mine = beside(1, total.astype(BF))
    if cross is not None:
        mine = beside(2, cross(mine))
    parts = [mine] + [send(mine, 2 * s) for s in range(1, m)]
    line = []
    for q in range(m):
        block = parts[0]
        for s in range(1, m):
            block = jnp.where((high ^ s) == q, parts[s], block)
        line.append(block)
    line = beside(3, jnp.concatenate(line, axis=1))
    return line, beside(4, send(line, 1))


def pieces(far, most):
    start = 0
    for block in far:
        at = 0
        while at < block.shape[0]:
            size = min(most - (start + at) % most, block.shape[0] - at)
            yield start + at, block[at : at + size]
            at += size
        start += at


def residual_kernel(nfar, side, middle, left, right, line, other, *refs):
    own, far, (mine, theirs, gram) = refs[0], refs[1 : 1 + nfar], refs[1 + nfar :]
    nvirt, half, width = left.shape[0], line.shape[1], mine.shape[1]
    gram[:, pl.ds(pl.multiple_of(side[0] * half, half), half)] = line[...]
    gram[:, pl.ds(pl.multiple_of((1 - side[0]) * half, half), half)] = other[...]
    last = None
    for start, block in pieces(far, nvirt):
        size = block.shape[0]
        i, at = start // nvirt, start % nvirt
        if i != last:
            scaled = (right[...].astype(F32) * middle[i : i + 1, :]).astype(BF)
            last = i
        res = dot(left[at : at + size], scaled, 1, 1)
        res += dot(own[start : start + size], gram[0], 1, 1)
        res += dot(block, gram[1], 1, 1)
        mine[start : start + size] = res[:, :width]
        theirs[start : start + size] = res[:, width:].astype(BF)


def update_kernel(last, occ, pivot, mine, got, coulomb, vir, vir_row, out):
    nvirt, width = vir.shape[1], mine.shape[1]
    virs = jnp.broadcast_to(vir[...], (width, nvirt)).T + vir_row[...]
    for i in range(mine.shape[0] // nvirt):
        rows = slice(i * nvirt, (i + 1) * nvirt)
        res = mine[rows] + got[rows].astype(F32)
        new = (coulomb[rows].astype(F32) + res) / (virs - occ[i] - pivot[0])
        if last:
            out[rows] = new.astype(BF)
        else:
            out[:, rows] = new.T.astype(BF)


def middle_kernel(mine, other, left, right, middle):
    width, nvirt = mine.shape[1], left.shape[0]
    for i in range(middle.shape[0]):
        total = None
        for at, amps in ((0, mine), (width, other)):
            proj = dot(amps[i * nvirt : (i + 1) * nvirt], left[...], 0, 0)
            term = jnp.sum(proj * right[at : at + width].astype(F32), axis=0, keepdims=True)
            total = term if total is None else total + term
        middle[i : i + 1] = total


def gram_kernel(nfar, mine, other, left, right, *refs):
    own, far, (gram, middle, amps) = refs[:1], refs[1 : 1 + nfar], refs[1 + nfar :]
    width, nvirt = mine.shape[0], left.shape[0]
    amps[:width] = mine[...]
    amps[width:] = other[...]
    for side, blocks in enumerate((own, far)):
        start = 0
        for block in blocks:
            term = dot(amps[:, start : start + block.shape[0]], block[...], 1, 0)
            gram[side] = gram[side] + term if start else term
            start += block.shape[0]
    for i in range(middle.shape[0]):
        proj = dot(amps[:, i * nvirt : (i + 1) * nvirt], left[...], 1, 0)
        middle[i : i + 1] = jnp.sum(proj * right[...].astype(F32), axis=0, keepdims=True)


def near_gram_kernel(mine, other, own, gram, *blocks):
    width = mine.shape[1]
    gram[:width] = dot(mine[...], own[...], 0, 0)
    gram[width:] = dot(other[...], own[...], 0, 0)
    start = 0
    for block in blocks:
        block[...] = own[start : start + block.shape[0]]
        start += block.shape[0]


def far_gram_kernel(mine, other, *refs):
    blocks, gram = refs[:-1], refs[-1]
    width = mine.shape[1]
    for at, amps in ((0, mine), (width, other)):
        start, total = 0, None
        for block in blocks:
            term = dot(amps[start : start + block.shape[0]], block[...], 0, 0)
            total = term if total is None else total + term
            start += block.shape[0]
        gram[at : at + width] = total


def per_device(
    amplitudes, coulomb, df_factors, thc_left, thc_right, occ_energy, vir_energy, pivot_energy
):
    n_pair = lax.axis_size("pair")
    n_aux = lax.axis_size("aux")
    k = lax.axis_index("aux")
    me = lax.axis_index("pair")
    rows, width = amplitudes.shape
    nvirt = vir_energy.shape[0]
    nocc = rows // nvirt
    naux = df_factors.shape[1]
    low = (me % 2).reshape(1)

    def over(a, s):
        return lax.ppermute(a, "aux", xor(n_aux, s))

    fac = jnp.stack([thc_left, thc_right])
    fac = jnp.concatenate([fac, over(fac, 2)], axis=2)
    cols = fac.shape[-1]

    def other_rows(fac, axis):
        bit = n_pair >> (axis + 1)
        got = lax.ppermute(fac, "pair", xor(n_pair, bit))
        first = (me // bit) % 2 == 0
        return jnp.where(first, fac, got), jnp.where(first, got, fac)

    n_bits = n_pair.bit_length() - 1

    far_amps = over(amplitudes, 2)
    near = [amplitudes, over(amplitudes, 1)]

    sizes = FAR(rows)
    n_far = len(sizes)
    gram_shape = jax.ShapeDtypeStruct((2 * width, naux), F32)

    gram, *own = pl.pallas_call(
        near_gram_kernel,
        out_shape=(gram_shape, *(jax.ShapeDtypeStruct((size, naux), BF) for size in sizes)),
        in_specs=[VMEM] * 3,
        out_specs=(VMEM,) * (1 + n_far),
        compiler_params=PARAMS,
    )(*near, df_factors)
    near_mine, near_got = fold(gram[None], n_pair)
    far_amps, near_got, fac = tie(far_amps, near_got, fac)
    far_other = over(far_amps, 1)
    far_other, fac = tie(far_other, fac)
    gram = pl.pallas_call(
        far_gram_kernel,
        out_shape=gram_shape,
        in_specs=[VMEM] * (2 + n_far),
        out_specs=VMEM,
        compiler_params=PARAMS,
    )(far_amps, far_other, *own)
    far_mine, far_got = fold(gram[None], n_pair)

    far = [over(block, 2) for block in own]

    vir = vir_energy[None, :]
    vir_row = take(vir_energy, k * width, width)[None, :]
    coulomb_block = take(coulomb, k * width, width, 1)

    def beside(stage, a):
        nonlocal fac, vir, vir_row, coulomb_block
        a, *got = tie(a, *(far[j] for j in DUE.get(stage, ())))
        for j, b in zip(DUE.get(stage, ()), got):
            far[j] = b
        if stage == 1:
            one, two = other_rows(fac, 0)
            kept = jnp.where(k // 2 == 0, one[1], two[1])
            fac = jnp.stack([one[0], two[0], kept])[:, None]
            a, vir, vir_row, coulomb_block = tie(a, vir, vir_row, coulomb_block)
        elif stage == 2:
            for axis in range(n_bits - 2, 0, -1):
                fac = jnp.stack(other_rows(fac, axis), axis=1)
                fac = fac.reshape(3, -1, *fac.shape[3:])
            a, fac = tie(a, fac)
        elif stage == 3:
            fac = jnp.stack(other_rows(fac, n_bits - 1), axis=2).reshape(3, -1, *fac.shape[2:])
            a, fac = tie(a, fac)
        return a

    gram = all_reduce(
        jnp.concatenate([near_mine, far_mine], axis=0),
        jnp.concatenate([near_got, beside(5, far_got)], axis=0),
        n_pair,
        lambda a: jnp.stack([a[0], over(a[1], 2)]),
        beside,
    )

    left = fac[:2].reshape(nvirt, cols)
    right = fac[2].reshape(2, width, cols)
    right = jnp.where(k % 2 == 0, right, right[::-1]).reshape(2 * width, cols)
    middle = pl.pallas_call(
        middle_kernel,
        out_shape=jax.ShapeDtypeStruct((nocc, cols), F32),
        in_specs=[VMEM] * 4,
        out_specs=VMEM,
        compiler_params=PARAMS,
    )(*near, left, right)
    for step in range(ITERS):
        last = step == ITERS - 1
        other = over(middle, 2)
        middle = middle + jnp.concatenate([other[:, cols // 2 :], other[:, : cols // 2]], axis=1)
        mine, theirs = pl.pallas_call(
            functools.partial(residual_kernel, n_far),
            out_shape=(
                jax.ShapeDtypeStruct((rows, width), F32),
                jax.ShapeDtypeStruct((rows, width), BF),
            ),
            in_specs=[SMEM] + [VMEM] * (6 + n_far),
            out_specs=(VMEM, VMEM),
            scratch_shapes=[pltpu.VMEM((2, 2 * width, naux), BF)],
            compiler_params=PARAMS,
        )(low, middle, left, right, *gram, df_factors, *far)
        got = over(theirs, 1)
        new = pl.pallas_call(
            functools.partial(update_kernel, last),
            out_shape=jax.ShapeDtypeStruct((rows, width) if last else (width, rows), BF),
            in_specs=[SMEM] * 2 + [VMEM] * 5,
            out_specs=VMEM,
            compiler_params=PARAMS,
        )(occ_energy, pivot_energy, mine, got, coulomb_block, vir, vir_row)
        if not last:
            gram, middle = pl.pallas_call(
                functools.partial(gram_kernel, n_far),
                out_shape=(
                    jax.ShapeDtypeStruct((2, 2 * width, naux), F32),
                    jax.ShapeDtypeStruct((nocc, cols), F32),
                ),
                in_specs=[VMEM] * (5 + n_far),
                out_specs=(VMEM, VMEM),
                scratch_shapes=[pltpu.VMEM((2 * width, rows), BF)],
                compiler_params=PARAMS,
            )(new, over(new, 1), left, right, df_factors, *far)
            gram = all_reduce(*fold(gram, n_pair), n_pair)
    return new


def solution(mesh):
    in_specs = (
        P("pair", "aux"),
        P("pair", None),
        P("pair", "aux"),
        P("pair", "aux"),
        P("pair", "aux"),
        P("pair"),
        P(),
        P(),
    )
    out_specs = P("pair", "aux")
    return jax.shard_map(
        per_device, mesh=mesh, in_specs=in_specs, out_specs=out_specs, check_vma=False
    )
```

time: 147 us -> 132 us (0.90)
  starting transfers between devices: 47.7 us -> 38.7 us
  waiting for transfers between devices: 67.2 us -> 59.5 us
  Pallas kernels: 10.5 us -> 17 us
  matrix products: 4.95 us -> 0 us
  other arithmetic: 5.41 us -> 7.16 us
    ppermute x18 -> x13, waiting for transfers between devices: 30 us -> 22.5 us  [over(): return lax.ppermute(a, 'aux', xor(n_aux, s))]
    ppermute x16 -> x14, waiting for transfers between devices: 28.3 us -> 20.8 us  [send(): return lax.ppermute(a, 'pair', xor(n, s))]
    ppermute x3 -> x6, waiting for transfers between devices: 8.87 us -> 16.3 us  [the longest x3 9.11 us: fold(): return (mine, lax.ppermute(theirs.astype(BF), 'pair', xor(n, 1)))]
    ppermute x18 -> x13, starting transfers between devices: 17.7 us -> 11.3 us  [over(): return lax.ppermute(a, 'aux', xor(n_aux, s))]
    ppermute x16 -> x14, starting transfers between devices: 24 us -> 18.9 us  [send(): return lax.ppermute(a, 'pair', xor(n, s))]
    dot_general x5 -> x0, matrix products: 4.95 us -> none  [dot(): lax.dot_general(a, b, (((ca,), (cb,)), ((), ())), preferred_element_type=...]
    pallas_call x0 -> x3, Pallas kernels: none -> 4.72 us  [the longest x1 2.17 us: per_device(): pl.pallas_call(far_gram_kernel, out_shape=gram_shape, in_specs=[VMEM] * (...]
    slice x2, local copies, waits for them, and re-layouts: 2.93 us -> 0.08 us  [the longest x1 0.05 us: per_device(): left = fac[:2].reshape(nvirt, cols)]
  transfers between devices with their start and end apart: 37 -> 33, of which waited for: 24 -> 20; matrix products, arithmetic and copies ran while one was open for 9% -> 5% of each run, Pallas kernels for 0% -> 4%
where the time goes in v3:
time: 132 us
  waiting for transfers between devices  59.5 us (45%)
  starting transfers between devices  38.7 us (29%)
  Pallas kernels  17 us (13%)
  local copies, waits for them, and re-layouts  8.36 us (6%)
  other arithmetic  7.16 us (5%)
    ppermute x13, waiting for transfers between devices, over(): return lax.ppermute(a, 'aux', xor(n_aux, s))  22.5 us
    ppermute x14, waiting for transfers between devices, send(): return lax.ppermute(a, 'pair', xor(n, s))  20.8 us
    ppermute x14, starting transfers between devices, send(): return lax.ppermute(a, 'pair', xor(n, s))  18.9 us
    ppermute x13, starting transfers between devices, over(): return lax.ppermute(a, 'aux', xor(n_aux, s))  11.3 us
    ppermute x3, waiting for transfers between devices, fold(): return (mine, lax.ppermute(theirs.astype(BF), 'pair', xor(n, 1)))  9.11 us
    ppermute x3, waiting for transfers between devices, other_rows(): got = lax.ppermute(fac, 'pair', xor(n_pair, bit))  7.16 us
    unnamed x38, local copies, waits for them, and re-layouts  7.16 us
    pallas_call x2, Pallas kernels, per_device(): pl.pallas_call(functools.partial(residual_kernel, n_far), out_shape=(jax....  6.4 us
  transfers between devices with their start and end apart: 33, of which 20 were waited for; matrix products, arithmetic and copies ran while one was open for 5% of the time, Pallas kernels for 4%

profile of v3, /device:TPU:0, one launch (start us, length us, event | category | flops | bytes accessed | tf_op | source)
XLA Modules:
  0.0 131.8 jit_solution(3366574555427063588)
XLA Ops:
  0.5 2.6 %collective-permute-start.1 = (bf16[2048,128]{1,0:T(8,128)(2,1)}, bf16[2048,128]{1,0:T(8,128)(2,1)}, u32[]{:S(2)}, u32[]{:S(2)}) collective-permute-start(bf16[2048,128]{1,0:T(8,128)(2,1)} %mine.3), channel_id=1, source_target_pairs={{0,16},{8,24},{16,0},{24,8},{1,17},{9,25},{17,1},{25,9},{2,18},{10... | collective-permute-start | bytes 1572872 | tf_op jit(solution)/shard_map/ppermute | solution.py:179
  4.1 1.6 %copy-done.1 = bf16[2048,512]{1,0:T(8,128)(2,1)S(1)} copy-done((bf16[2048,512]{1,0:T(8,128)(2,1)S(1)}, bf16[2048,512]{1,0:T(8,128)(2,1)}, u32[]{:S(2)}) %copy-start.1) | copy-done | bytes 2097176
  5.7 1.0 copy-done.4
  6.7 1.5 %shard_map.82 = (f32[256,512]{1,0:T(8,128)S(1)}, bf16[1024,512]{1,0:T(8,128)(2,1)S(1)}, bf16[512,512]{1,0:T(8,128)(2,1)}, bf16[512,512]{1,0:T(8,128)(2,1)S(1)}) custom-call(bf16[2048,128]{1,0:T(8,128)(2,1)S(1)} %copy-done.4, bf16[2048,128]{1,0:T(8,128)(2,1)S(1)} %collective-permute-done.other, bf16[2048,512]{1,0:T(8,128)(2,1)S(1)} %copy-done.1), custom_call_target="tpu_custom_call" | custom-call | tf_op jit(solution)/shard_map/pallas_call | solution.py:200
  8.3 1.0 copy-done.8
  10.1 2.0 %collective-permute-start.2 = (bf16[1,128,512]{2,1,0:T(8,128)(2,1)S(1)}, bf16[1,128,512]{2,1,0:T(8,128)(2,1)S(1)}, u32[]{:S(2)}, u32[]{:S(2)}) collective-permute-start(bf16[1,128,512]{2,1,0:T(8,128)(2,1)S(1)} %fusion), channel_id=1, source_target_pairs={{0,1},{1,0},{2,3},{3,2},{4,5},{5,4},{6,7},{7,6},{8,9},{9,8},{10,11... | collective-permute-start | bytes 393224 | tf_op jit(solution)/shard_map/ppermute | solution.py:43
  12.1 5.9 %collective-permute-done.3 = bf16[2,64,384]{2,1,0:T(8,128)(2,1)} collective-permute-done((bf16[2,64,384]{2,1,0:T(8,128)(2,1)S(1)}, bf16[2,64,384]{2,1,0:T(8,128)(2,1)}, u32[]{:S(2)}, u32[]{:S(2)}) %collective-permute-start.3) | collective-permute-done | bytes 98336 | tf_op jit(solution)/shard_map/ppermute | solution.py:179
  18.0 0.9 pad_maximum_fusion.4
  20.1 1.8 %collective-permute-start.9 = (bf16[1024,512]{1,0:T(8,128)(2,1)}, bf16[1024,512]{1,0:T(8,128)(2,1)S(1)}, u32[]{:S(2)}, u32[]{:S(2)}) collective-permute-start(bf16[1024,512]{1,0:T(8,128)(2,1)} %copy-done.8), channel_id=1, source_target_pairs={{0,16},{8,24},{16,0},{24,8},{1,17},{9,25},{17,1},{25,9},{2,18},{10... | collective-permute-start | bytes 3145736 | tf_op jit(solution)/shard_map/ppermute | solution.py:179
  21.8 1.0 copy-done.11
  22.9 2.2 %shard_map.83 = f32[256,512]{1,0:T(8,128)S(1)} custom-call(bf16[2048,128]{1,0:T(8,128)(2,1)} %collective-permute-done.1.mine, bf16[2048,128]{1,0:T(8,128)(2,1)} %collective-permute-done.4.other, bf16[1024,512]{1,0:T(8,128)(2,1)S(1)} %copy-done.9, bf16[512,512]{1,0:T(8,128)(2,1)} %get-tuple-element.39.refs_1_, bf16[512,512]{1,0:T(8,128)(2,1)S(1)} %copy-done.11), custom_call_target="tpu_custom_call" | custom-call | tf_op jit(solution)/shard_map/pallas_call | solution.py:211
  25.1 1.6 %collective-permute-start.5 = (bf16[1,128,512]{2,1,0:T(8,128)(2,1)S(1)}, bf16[1,128,512]{2,1,0:T(8,128)(2,1)S(1)}, u32[]{:S(2)}, u32[]{:S(2)}) collective-permute-start(bf16[1,128,512]{2,1,0:T(8,128)(2,1)S(1)} %fusion.1), channel_id=1, source_target_pairs={{0,1},{1,0},{2,3},{3,2},{4,5},{5,4},{6,7},{7,6},{8,9},{9,8},{10,11... | collective-permute-start | bytes 393224 | tf_op jit(solution)/shard_map/ppermute | solution.py:43
  26.7 2.6 %collective-permute-start.11 = (bf16[2,64,768]{2,1,0:T(8,128)(2,1)S(1)}, bf16[2,64,768]{2,1,0:T(8,128)(2,1)S(1)}, u32[]{:S(2)}, u32[]{:S(2)}) collective-permute-start(bf16[2,64,768]{2,1,0:T(8,128)(2,1)S(1)} %pad_maximum_fusion.4), channel_id=1, source_target_pairs={{0,4},{1,5},{2,6},{3,7},{4,0},{5,1},{6,2},{7,3},{8,12},{9,13},{10,... | collective-permute-start | bytes 589832 | tf_op jit(solution)/shard_map/ppermute | solution.py:187
  29.3 1.3 collective-permute-done.5
  30.8 3.7 %collective-permute-start.8 = (bf16[2,32,512]{2,1,0:T(8,128)(2,1)S(1)}, bf16[2,32,512]{2,1,0:T(8,128)(2,1)S(1)}, u32[]{:S(2)}, u32[]{:S(2)}) collective-permute-start(bf16[2,32,512]{2,1,0:T(8,128)(2,1)S(1)} %get-tuple-element.85), channel_id=1, source_target_pairs={{0,6},{1,7},{2,4},{3,5},{4,2},{5,3},{6,0},{7,1},{8,14},{9,15},{10,... | collective-permute-start | bytes 196616 | tf_op jit(solution)/shard_map/ppermute | solution.py:52
  35.3 7.2 %collective-permute-done.11 = bf16[2,64,768]{2,1,0:T(8,128)(2,1)S(1)} collective-permute-done((bf16[2,64,768]{2,1,0:T(8,128)(2,1)S(1)}, bf16[2,64,768]{2,1,0:T(8,128)(2,1)S(1)}, u32[]{:S(2)}, u32[]{:S(2)}) %collective-permute-start.11) | collective-permute-done | bytes 196640 | tf_op jit(solution)/shard_map/ppermute | solution.py:187
  44.2 1.6 %collective-permute-done.9.refs_1_ = bf16[1024,512]{1,0:T(8,128)(2,1)S(1)} collective-permute-done((bf16[1024,512]{1,0:T(8,128)(2,1)}, bf16[1024,512]{1,0:T(8,128)(2,1)S(1)}, u32[]{:S(2)}, u32[]{:S(2)}) %collective-permute-start.9) | collective-permute-done | bytes 1048608 | tf_op jit(solution)/shard_map/ppermute | solution.py:179
  45.7 1.7 %collective-permute-start.10 = (bf16[32,512]{1,0:T(8,128)(2,1)S(1)}, bf16[32,512]{1,0:T(8,128)(2,1)S(1)}, u32[]{:S(2)}, u32[]{:S(2)}) collective-permute-start(bf16[32,512]{1,0:T(8,128)(2,1)S(1)} %get-tuple-element.91), channel_id=1, source_target_pairs={{0,16},{8,24},{16,0},{24,8},{1,17},{9,25},{17,1},{25,9},{2,18},{10... | collective-permute-start | bytes 98312 | tf_op jit(solution)/shard_map/ppermute | solution.py:179
  47.5 2.2 %collective-permute-done.10 = bf16[32,512]{1,0:T(8,128)(2,1)S(1)} collective-permute-done((bf16[32,512]{1,0:T(8,128)(2,1)S(1)}, bf16[32,512]{1,0:T(8,128)(2,1)S(1)}, u32[]{:S(2)}, u32[]{:S(2)}) %collective-permute-start.10) | collective-permute-done | bytes 32800 | tf_op jit(solution)/shard_map/ppermute | solution.py:179
  51.0 1.1 select_bitcast_fusion.3
  52.9 1.7 %collective-permute-start.17 = (bf16[3,2,64,768]{3,2,1,0:T(8,128)(2,1)}, bf16[3,2,64,768]{3,2,1,0:T(8,128)(2,1)}, u32[]{:S(2)}, u32[]{:S(2)}) collective-permute-start(bf16[3,2,64,768]{3,2,1,0:T(8,128)(2,1)} %maximum_bitcast_fusion), channel_id=1, source_target_pairs={{0,1},{1,0},{2,3},{3,2},{4,5},{5,4},{6,7},{7,6},{8,9},{9,8},{10,11... | collective-permute-start | bytes 1769480 | tf_op jit(solution)/shard_map/ppermute | solution.py:187
  54.7 1.5 %collective-permute-start.16 = (bf16[512,512]{1,0:T(8,128)(2,1)}, bf16[512,512]{1,0:T(8,128)(2,1)}, u32[]{:S(2)}, u32[]{:S(2)}) collective-permute-start(bf16[512,512]{1,0:T(8,128)(2,1)} %get-tuple-element.39.refs_1_), channel_id=1, source_target_pairs={{0,16},{8,24},{16,0},{24,8},{1,17},{9,25},{17,1},{25,9},{2,18},{10... | collective-permute-start | bytes 1572872 | tf_op jit(solution)/shard_map/ppermute | solution.py:179
  56.2 3.6 %collective-permute-start.13 = (bf16[2,32,512]{2,1,0:T(8,128)(2,1)S(1)}, bf16[2,32,512]{2,1,0:T(8,128)(2,1)S(1)}, u32[]{:S(2)}, u32[]{:S(2)}) collective-permute-start(bf16[2,32,512]{2,1,0:T(8,128)(2,1)S(1)} %pad_maximum_fusion.6), channel_id=1, source_target_pairs={{0,6},{1,7},{2,4},{3,5},{4,2},{5,3},{6,0},{7,1},{8,14},{9,15},{10,... | collective-permute-start | bytes 196616 | tf_op jit(solution)/shard_map/ppermute | solution.py:52
  60.6 1.8 %collective-permute-done.13 = bf16[2,32,512]{2,1,0:T(8,128)(2,1)S(1)} collective-permute-done((bf16[2,32,512]{2,1,0:T(8,128)(2,1)S(1)}, bf16[2,32,512]{2,1,0:T(8,128)(2,1)S(1)}, u32[]{:S(2)}, u32[]{:S(2)}) %collective-permute-start.13) | collective-permute-done | bytes 65568 | tf_op jit(solution)/shard_map/ppermute | solution.py:52
  62.8 2.1 %collective-permute-done.14 = bf16[2,32,512]{2,1,0:T(8,128)(2,1)S(1)} collective-permute-done((bf16[2,32,512]{2,1,0:T(8,128)(2,1)S(1)}, bf16[2,32,512]{2,1,0:T(8,128)(2,1)S(1)}, u32[]{:S(2)}, u32[]{:S(2)}) %collective-permute-start.14) | collective-permute-done | bytes 65568 | tf_op jit(solution)/shard_map/ppermute | solution.py:52
  65.0 4.8 %collective-permute-done.16.refs_2_ = bf16[512,512]{1,0:T(8,128)(2,1)} collective-permute-done((bf16[512,512]{1,0:T(8,128)(2,1)}, bf16[512,512]{1,0:T(8,128)(2,1)}, u32[]{:S(2)}, u32[]{:S(2)}) %collective-permute-start.16) | collective-permute-done | bytes 524320 | tf_op jit(solution)/shard_map/ppermute | solution.py:179
  69.8 1.3 %select_bitcast_fusion.1 = (bf16[3,2,1,64,768]{4,3,2,1,0:T(8,128)(2,1)S(1)}, bf16[3,2,1,64,768]{4,3,2,1,0:T(8,128)(2,1)S(1)}) fusion(bf16[3,2,64,768]{3,2,1,0:T(8,128)(2,1)} %maximum_bitcast_fusion, bf16[3,2,64,768]{3,2,1,0:T(8,128)(2,1)} %collective-permute-done.17, pred[]{:T(512)S(6)} %eq.87), kind=kLoop, calls=%fused_computation.4 | loop fusion | flops 589824 | bytes 2359297 | tf_op jit(solution)/shard_map/stack | solution.py:242
  72.5 1.0 shard_map.84
  73.6 1.6 %collective-permute-start.18 = (f32[4,768]{1,0:T(4,128)S(1)}, f32[4,768]{1,0:T(4,128)S(1)}, u32[]{:S(2)}, u32[]{:S(2)}) collective-permute-start(f32[4,768]{1,0:T(4,128)S(1)} %shard_map.84), channel_id=1, source_target_pairs={{0,16},{8,24},{16,0},{24,8},{1,17},{9,25},{17,1},{25,9},{2,18},{10... | collective-permute-start | bytes 36872 | tf_op jit(solution)/shard_map/ppermute | solution.py:179
  75.7 3.0 %collective-permute-done.18 = f32[4,768]{1,0:T(4,128)S(1)} collective-permute-done((f32[4,768]{1,0:T(4,128)S(1)}, f32[4,768]{1,0:T(4,128)S(1)}, u32[]{:S(2)}, u32[]{:S(2)}) %collective-permute-start.18) | collective-permute-done | bytes 12320 | tf_op jit(solution)/shard_map/ppermute | solution.py:179
  78.7 2.8 %collective-permute-done.19.other = bf16[2,128,512]{2,1,0:T(8,128)(2,1)S(1)} collective-permute-done((bf16[2,128,512]{2,1,0:T(8,128)(2,1)S(1)}, bf16[2,128,512]{2,1,0:T(8,128)(2,1)S(1)}, u32[]{:S(2)}, u32[]{:S(2)}) %collective-permute-start.19) | collective-permute-done | bytes 262176 | tf_op jit(solution)/shard_map/ppermute | solution.py:52
  81.5 3.2 %shard_map.85 = (f32[2048,128]{1,0:T(8,128)S(1)}, bf16[2048,128]{1,0:T(8,128)(2,1)S(1)}) custom-call(s32[1]{0:T(128)} %bitcast.side, f32[4,768]{1,0:T(4,128)S(1)} %maximum_add_fusion.1.middle, bf16[512,768]{1,0:T(8,128)(2,1)S(1)} %bitcast.42, bf16[256,768]{1,0:T(8,128)(2,1)S(1)} %bitcast.46, bf16[2,128,512]{2,1,0:T(8,128)(2,1)S(1)} %pad_maximum_fusion.2.line, ...), custom_call_target="tpu_custom_call" | custom-call | tf_op jit(solution)/shard_map/pallas_call | solution.py:268
  85.5 1.2 collective-permute-done.21.got
  86.7 1.0 shard_map.86.mine
  88.0 1.8 %collective-permute-done.22.other = bf16[128,2048]{1,0:T(8,128)(2,1)S(1)} collective-permute-done((bf16[128,2048]{1,0:T(8,128)(2,1)S(1)}, bf16[128,2048]{1,0:T(8,128)(2,1)S(1)}, u32[]{:S(2)}, u32[]{:S(2)}) %collective-permute-start.22) | collective-permute-done | bytes 524320 | tf_op jit(solution)/shard_map/ppermute | solution.py:179
  89.7 3.2 %shard_map.87 = (f32[2,256,512]{2,1,0:T(8,128)S(1)}, f32[4,768]{1,0:T(4,128)S(1)}) custom-call(bf16[128,2048]{1,0:T(8,128)(2,1)S(1)} %shard_map.86.mine, bf16[128,2048]{1,0:T(8,128)(2,1)S(1)} %collective-permute-done.22.other, bf16[512,768]{1,0:T(8,128)(2,1)S(1)} %bitcast.43, bf16[256,768]{1,0:T(8,128)(2,1)S(1)} %bitcast.47, ...), custom_call_target="tpu_custom_call" | custom-call | tf_op jit(solution)/shard_map/pallas_call | solution.py:288
  93.6 7.8 %collective-permute-done.24 = bf16[2,128,512]{2,1,0:T(8,128)(2,1)S(1)} collective-permute-done((bf16[2,128,512]{2,1,0:T(8,128)(2,1)S(1)}, bf16[2,128,512]{2,1,0:T(8,128)(2,1)S(1)}, u32[]{:S(2)}, u32[]{:S(2)}) %collective-permute-start.24) | collective-permute-done | bytes 262176 | tf_op jit(solution)/shard_map/ppermute | solution.py:43
  101.5 3.7 %collective-permute-start.27 = (bf16[2,32,512]{2,1,0:T(8,128)(2,1)S(1)}, bf16[2,32,512]{2,1,0:T(8,128)(2,1)S(1)}, u32[]{:S(2)}, u32[]{:S(2)}) collective-permute-start(bf16[2,32,512]{2,1,0:T(8,128)(2,1)S(1)} %get-tuple-element.78), channel_id=1, source_target_pairs={{0,6},{1,7},{2,4},{3,5},{4,2},{5,3},{6,0},{7,1},{8,14},{9,15},{10,... | collective-permute-start | bytes 196616 | tf_op jit(solution)/shard_map/ppermute | solution.py:52
  106.0 2.2 %collective-permute-done.27 = bf16[2,32,512]{2,1,0:T(8,128)(2,1)S(1)} collective-permute-done((bf16[2,32,512]{2,1,0:T(8,128)(2,1)S(1)}, bf16[2,32,512]{2,1,0:T(8,128)(2,1)S(1)}, u32[]{:S(2)}, u32[]{:S(2)}) %collective-permute-start.27) | collective-permute-done | bytes 65568 | tf_op jit(solution)/shard_map/ppermute | solution.py:52
  108.2 2.3 %collective-permute-done.26 = bf16[2,32,512]{2,1,0:T(8,128)(2,1)S(1)} collective-permute-done((bf16[2,32,512]{2,1,0:T(8,128)(2,1)S(1)}, bf16[2,32,512]{2,1,0:T(8,128)(2,1)S(1)}, u32[]{:S(2)}, u32[]{:S(2)}) %collective-permute-start.26) | collective-permute-done | bytes 65568 | tf_op jit(solution)/shard_map/ppermute | solution.py:52
  110.5 2.6 %collective-permute-start.28 = (bf16[2,32,512]{2,1,0:T(8,128)(2,1)S(1)}, bf16[2,32,512]{2,1,0:T(8,128)(2,1)S(1)}, u32[]{:S(2)}, u32[]{:S(2)}) collective-permute-start(bf16[2,32,512]{2,1,0:T(8,128)(2,1)S(1)} %add_convert_fusion), channel_id=1, source_target_pairs={{0,6},{1,7},{2,4},{3,5},{4,2},{5,3},{6,0},{7,1},{8,14},{9,15},{10,... | collective-permute-start | bytes 196616 | tf_op jit(solution)/shard_map/ppermute | solution.py:52
  113.1 1.9 %collective-permute-start.30 = (bf16[2,32,512]{2,1,0:T(8,128)(2,1)S(1)}, bf16[2,32,512]{2,1,0:T(8,128)(2,1)S(1)}, u32[]{:S(2)}, u32[]{:S(2)}) collective-permute-start(bf16[2,32,512]{2,1,0:T(8,128)(2,1)S(1)} %add_convert_fusion), channel_id=1, source_target_pairs={{0,2},{1,3},{2,0},{3,1},{4,6},{5,7},{6,4},{7,5},{8,10},{9,11},{10,... | collective-permute-start | bytes 196616 | tf_op jit(solution)/shard_map/ppermute | solution.py:52
  115.5 1.3 %collective-permute-done.28 = bf16[2,32,512]{2,1,0:T(8,128)(2,1)S(1)} collective-permute-done((bf16[2,32,512]{2,1,0:T(8,128)(2,1)S(1)}, bf16[2,32,512]{2,1,0:T(8,128)(2,1)S(1)}, u32[]{:S(2)}, u32[]{:S(2)}) %collective-permute-start.28) | collective-permute-done | bytes 65568 | tf_op jit(solution)/shard_map/ppermute | solution.py:52
  116.8 1.6 %collective-permute-done.29 = bf16[2,32,512]{2,1,0:T(8,128)(2,1)S(1)} collective-permute-done((bf16[2,32,512]{2,1,0:T(8,128)(2,1)S(1)}, bf16[2,32,512]{2,1,0:T(8,128)(2,1)S(1)}, u32[]{:S(2)}, u32[]{:S(2)}) %collective-permute-start.29) | collective-permute-done | bytes 65568 | tf_op jit(solution)/shard_map/ppermute | solution.py:52
  119.1 5.8 %collective-permute-done.31.other = bf16[2,128,512]{2,1,0:T(8,128)(2,1)S(1)} collective-permute-done((bf16[2,128,512]{2,1,0:T(8,128)(2,1)S(1)}, bf16[2,128,512]{2,1,0:T(8,128)(2,1)S(1)}, u32[]{:S(2)}, u32[]{:S(2)}) %collective-permute-start.31) | collective-permute-done | bytes 262176 | tf_op jit(solution)/shard_map/ppermute | solution.py:52
  124.9 3.2 %shard_map.88 = (f32[2048,128]{1,0:T(8,128)S(1)}, bf16[2048,128]{1,0:T(8,128)(2,1)S(1)}) custom-call(s32[1]{0:T(128)} %bitcast.side, f32[4,768]{1,0:T(4,128)S(1)} %maximum_add_fusion.2.middle, bf16[512,768]{1,0:T(8,128)(2,1)S(1)} %bitcast.44, bf16[256,768]{1,0:T(8,128)(2,1)S(1)} %bitcast.48, bf16[2,128,512]{2,1,0:T(8,128)(2,1)S(1)} %pad_maximum_fusion.3.line, ...), custom_call_target="tpu_custom_call" | custom-call | tf_op jit(solution)/shard_map/pallas_call | solution.py:268
  128.2 1.9 %collective-permute-done.32.got = bf16[2048,128]{1,0:T(8,128)(2,1)S(1)} collective-permute-done((bf16[2048,128]{1,0:T(8,128)(2,1)S(1)}, bf16[2048,128]{1,0:T(8,128)(2,1)S(1)}, u32[]{:S(2)}, u32[]{:S(2)}) %collective-permute-start.32) | collective-permute-done | bytes 524320 | tf_op jit(solution)/shard_map/ppermute | solution.py:179
  130.1 1.7 %shard_map.89 = bf16[2048,128]{1,0:T(8,128)(2,1)} custom-call(f32[4]{0:T(128)S(1)} %copy-done.15, f32[1]{0:T(128)S(6)} %copy.11.pivot, f32[2048,128]{1,0:T(8,128)S(1)} %get-tuple-element.61.mine, bf16[2048,128]{1,0:T(8,128)(2,1)S(1)} %collective-permute-done.32.got, bf16[2048,128]{1,0:T(8,128)(2,1)S(1)} %copy-done.3, f32[1,512]{1,0:T(1,128)S(1)} %bitcast.50, ...), custom_call_target="tpu_custom_call" | custom-call | tf_op jit(solution)/shard_map/pallas_call | solution.py:280
  (100 shorter events, 14.7 us)
Async XLA Ops:
  0.0 19.2 %copy-start = (bf16[2048,512]{1,0:T(8,128)(2,1)S(1)}, bf16[2048,512]{1,0:T(8,128)(2,1)}, u32[]{:S(2)}) copy-start(bf16[2048,512]{1,0:T(8,128)(2,1)} %param.9) | copy-start | bytes 6291460
  0.0 4.1 %collective-permute-start = (bf16[2048,128]{1,0:T(8,128)(2,1)}, bf16[2048,128]{1,0:T(8,128)(2,1)S(1)}, u32[]{:S(2)}, u32[]{:S(2)}) collective-permute-start(bf16[2048,128]{1,0:T(8,128)(2,1)} %mine.3), channel_id=1, source_target_pairs={{0,8},{8,0},{16,24},{24,16},{1,9},{9,1},{17,25},{25,17},{2,10},{10... | collective-permute-start | bytes 1572872 | tf_op jit(solution)/shard_map/ppermute | solution.py:179
  0.5 18.5 %collective-permute-start.1 = (bf16[2048,128]{1,0:T(8,128)(2,1)}, bf16[2048,128]{1,0:T(8,128)(2,1)}, u32[]{:S(2)}, u32[]{:S(2)}) collective-permute-start(bf16[2048,128]{1,0:T(8,128)(2,1)} %mine.3), channel_id=1, source_target_pairs={{0,16},{8,24},{16,0},{24,8},{1,17},{9,25},{17,1},{25,9},{2,18},{10... | collective-permute-start | bytes 1572872 | tf_op jit(solution)/shard_map/ppermute | solution.py:179
  3.9 14.1 %collective-permute-start.3 = (bf16[2,64,384]{2,1,0:T(8,128)(2,1)S(1)}, bf16[2,64,384]{2,1,0:T(8,128)(2,1)}, u32[]{:S(2)}, u32[]{:S(2)}) collective-permute-start(bf16[2,64,384]{2,1,0:T(8,128)(2,1)S(1)} %pad_maximum_fusion.5), channel_id=1, source_target_pairs={{0,16},{8,24},{16,0},{24,8},{1,17},{9,25},{17,1},{25,9},{2,18},{10... | collective-permute-start | bytes 294920 | tf_op jit(solution)/shard_map/ppermute | solution.py:179
  4.1 1.6 %copy-start.1 = (bf16[2048,512]{1,0:T(8,128)(2,1)S(1)}, bf16[2048,512]{1,0:T(8,128)(2,1)}, u32[]{:S(2)}) copy-start(bf16[2048,512]{1,0:T(8,128)(2,1)} %refs_0_.5) | copy-start | bytes 6291460
  6.7 1.5 %copy-start.6 = (bf16[2048,128]{1,0:T(8,128)(2,1)}, bf16[2048,128]{1,0:T(8,128)(2,1)S(1)}, u32[]{:S(2)}) copy-start(bf16[2048,128]{1,0:T(8,128)(2,1)S(1)} %collective-permute-done.other) | copy-start | bytes 1572868
  6.7 11.3 %copy-start.16 = (bf16[64,384]{1,0:T(8,128)(2,1)S(1)}, bf16[64,384]{1,0:T(8,128)(2,1)}, u32[]{:S(2)}) copy-start(bf16[64,384]{1,0:T(8,128)(2,1)} %param.12) | copy-start | bytes 147460
  6.7 11.3 %copy-start.17 = (bf16[64,384]{1,0:T(8,128)(2,1)S(1)}, bf16[64,384]{1,0:T(8,128)(2,1)}, u32[]{:S(2)}) copy-start(bf16[64,384]{1,0:T(8,128)(2,1)} %param.11) | copy-start | bytes 147460
  6.7 12.4 %copy-start.14 = (f32[512]{0:T(512)S(1)}, f32[512]{0:T(512)}, u32[]{:S(2)}) copy-start(f32[512]{0:T(512)} %param.14) | copy-start | bytes 6148
  10.1 10.0 %copy-start.12 = (f32[256,512]{1,0:T(8,128)}, f32[256,512]{1,0:T(8,128)S(1)}, u32[]{:S(2)}) copy-start(f32[256,512]{1,0:T(8,128)S(1)} %get-tuple-element.34) | copy-start | bytes 1572868
  10.1 8.8 %collective-permute-start.2 = (bf16[1,128,512]{2,1,0:T(8,128)(2,1)S(1)}, bf16[1,128,512]{2,1,0:T(8,128)(2,1)S(1)}, u32[]{:S(2)}, u32[]{:S(2)}) collective-permute-start(bf16[1,128,512]{2,1,0:T(8,128)(2,1)S(1)} %fusion), channel_id=1, source_target_pairs={{0,1},{1,0},{2,3},{3,2},{4,5},{5,4},{6,7},{7,6},{8,9},{9,8},{10,11... | collective-permute-start | bytes 393224 | tf_op jit(solution)/shard_map/ppermute | solution.py:43
  18.9 2.9 %collective-permute-start.4 = (bf16[2048,128]{1,0:T(8,128)(2,1)}, bf16[2048,128]{1,0:T(8,128)(2,1)}, u32[]{:S(2)}, u32[]{:S(2)}) collective-permute-start(bf16[2048,128]{1,0:T(8,128)(2,1)} %collective-permute-done.1.mine), channel_id=1, source_target_pairs={{0,8},{8,0},{16,24},{24,16},{1,9},{9,1},{17,25},{25,17},{2,10},{10... | collective-permute-start | bytes 1572872 | tf_op jit(solution)/shard_map/ppermute | solution.py:179
  19.1 2.7 %copy-start.9 = (bf16[1024,512]{1,0:T(8,128)(2,1)S(1)}, bf16[1024,512]{1,0:T(8,128)(2,1)}, u32[]{:S(2)}) copy-start(bf16[1024,512]{1,0:T(8,128)(2,1)} %copy-done.8) | copy-start | bytes 3145732
  20.1 25.7 %collective-permute-start.9 = (bf16[1024,512]{1,0:T(8,128)(2,1)}, bf16[1024,512]{1,0:T(8,128)(2,1)S(1)}, u32[]{:S(2)}, u32[]{:S(2)}) collective-permute-start(bf16[1024,512]{1,0:T(8,128)(2,1)} %copy-done.8), channel_id=1, source_target_pairs={{0,16},{8,24},{16,0},{24,8},{1,17},{9,25},{17,1},{25,9},{2,18},{10... | collective-permute-start | bytes 3145736 | tf_op jit(solution)/shard_map/ppermute | solution.py:179
  21.8 1.0 copy-start.11
  22.9 3.8 %copy-start.13 = (f32[256,512]{1,0:T(8,128)S(1)}, f32[256,512]{1,0:T(8,128)}, u32[]{:S(2)}) copy-start(f32[256,512]{1,0:T(8,128)} %copy-done.12) | copy-start | bytes 1572868
  25.1 5.5 %collective-permute-start.5 = (bf16[1,128,512]{2,1,0:T(8,128)(2,1)S(1)}, bf16[1,128,512]{2,1,0:T(8,128)(2,1)S(1)}, u32[]{:S(2)}, u32[]{:S(2)}) collective-permute-start(bf16[1,128,512]{2,1,0:T(8,128)(2,1)S(1)} %fusion.1), channel_id=1, source_target_pairs={{0,1},{1,0},{2,3},{3,2},{4,5},{5,4},{6,7},{7,6},{8,9},{9,8},{10,11... | collective-permute-start | bytes 393224 | tf_op jit(solution)/shard_map/ppermute | solution.py:43
  26.7 15.7 %collective-permute-start.11 = (bf16[2,64,768]{2,1,0:T(8,128)(2,1)S(1)}, bf16[2,64,768]{2,1,0:T(8,128)(2,1)S(1)}, u32[]{:S(2)}, u32[]{:S(2)}) collective-permute-start(bf16[2,64,768]{2,1,0:T(8,128)(2,1)S(1)} %pad_maximum_fusion.4), channel_id=1, source_target_pairs={{0,4},{1,5},{2,6},{3,7},{4,0},{5,1},{6,2},{7,3},{8,12},{9,13},{10,... | collective-permute-start | bytes 589832 | tf_op jit(solution)/shard_map/ppermute | solution.py:187
  30.8 12.4 %collective-permute-start.8 = (bf16[2,32,512]{2,1,0:T(8,128)(2,1)S(1)}, bf16[2,32,512]{2,1,0:T(8,128)(2,1)S(1)}, u32[]{:S(2)}, u32[]{:S(2)}) collective-permute-start(bf16[2,32,512]{2,1,0:T(8,128)(2,1)S(1)} %get-tuple-element.85), channel_id=1, source_target_pairs={{0,6},{1,7},{2,4},{3,5},{4,2},{5,3},{6,0},{7,1},{8,14},{9,15},{10,... | collective-permute-start | bytes 196616 | tf_op jit(solution)/shard_map/ppermute | solution.py:52
  34.5 9.6 %collective-permute-start.7 = (bf16[2,32,512]{2,1,0:T(8,128)(2,1)S(1)}, bf16[2,32,512]{2,1,0:T(8,128)(2,1)S(1)}, u32[]{:S(2)}, u32[]{:S(2)}) collective-permute-start(bf16[2,32,512]{2,1,0:T(8,128)(2,1)S(1)} %get-tuple-element.86), channel_id=1, source_target_pairs={{0,4},{1,5},{2,6},{3,7},{4,0},{5,1},{6,2},{7,3},{8,12},{9,13},{10,... | collective-permute-start | bytes 196616 | tf_op jit(solution)/shard_map/ppermute | solution.py:52
  34.5 9.6 %collective-permute-start.6 = (bf16[2,32,512]{2,1,0:T(8,128)(2,1)S(1)}, bf16[2,32,512]{2,1,0:T(8,128)(2,1)S(1)}, u32[]{:S(2)}, u32[]{:S(2)}) collective-permute-start(bf16[2,32,512]{2,1,0:T(8,128)(2,1)S(1)} %get-tuple-element.84), channel_id=1, source_target_pairs={{0,2},{1,3},{2,0},{3,1},{4,6},{5,7},{6,4},{7,5},{8,10},{9,11},{10,... | collective-permute-start | bytes 196616 | tf_op jit(solution)/shard_map/ppermute | solution.py:52
  43.2 7.8 %collective-permute-start.12 = (bf16[3,1,64,768]{3,2,0,1:T(8,128)(2,1)}, bf16[3,1,64,768]{3,2,0,1:T(8,128)(2,1)}, u32[]{:S(2)}, u32[]{:S(2)}) collective-permute-start(bf16[3,1,64,768]{3,2,0,1:T(8,128)(2,1)} %maximum_bitcast_fusion.1), channel_id=1, source_target_pairs={{0,2},{1,3},{2,0},{3,1},{4,6},{5,7},{6,4},{7,5},{8,10},{9,11},{10,... | collective-permute-start | bytes 884744 | tf_op jit(solution)/shard_map/ppermute | solution.py:187
  45.7 3.9 %collective-permute-start.10 = (bf16[32,512]{1,0:T(8,128)(2,1)S(1)}, bf16[32,512]{1,0:T(8,128)(2,1)S(1)}, u32[]{:S(2)}, u32[]{:S(2)}) collective-permute-start(bf16[32,512]{1,0:T(8,128)(2,1)S(1)} %get-tuple-element.91), channel_id=1, source_target_pairs={{0,16},{8,24},{16,0},{24,8},{1,17},{9,25},{17,1},{25,9},{2,18},{10... | collective-permute-start | bytes 98312 | tf_op jit(solution)/shard_map/ppermute | solution.py:179
  52.9 16.9 %collective-permute-start.17 = (bf16[3,2,64,768]{3,2,1,0:T(8,128)(2,1)}, bf16[3,2,64,768]{3,2,1,0:T(8,128)(2,1)}, u32[]{:S(2)}, u32[]{:S(2)}) collective-permute-start(bf16[3,2,64,768]{3,2,1,0:T(8,128)(2,1)} %maximum_bitcast_fusion), channel_id=1, source_target_pairs={{0,1},{1,0},{2,3},{3,2},{4,5},{5,4},{6,7},{7,6},{8,9},{9,8},{10,11... | collective-permute-start | bytes 1769480 | tf_op jit(solution)/shard_map/ppermute | solution.py:187
  54.7 15.2 %collective-permute-start.16 = (bf16[512,512]{1,0:T(8,128)(2,1)}, bf16[512,512]{1,0:T(8,128)(2,1)}, u32[]{:S(2)}, u32[]{:S(2)}) collective-permute-start(bf16[512,512]{1,0:T(8,128)(2,1)} %get-tuple-element.39.refs_1_), channel_id=1, source_target_pairs={{0,16},{8,24},{16,0},{24,8},{1,17},{9,25},{17,1},{25,9},{2,18},{10... | collective-permute-start | bytes 1572872 | tf_op jit(solution)/shard_map/ppermute | solution.py:179
  56.2 6.2 %collective-permute-start.13 = (bf16[2,32,512]{2,1,0:T(8,128)(2,1)S(1)}, bf16[2,32,512]{2,1,0:T(8,128)(2,1)S(1)}, u32[]{:S(2)}, u32[]{:S(2)}) collective-permute-start(bf16[2,32,512]{2,1,0:T(8,128)(2,1)S(1)} %pad_maximum_fusion.6), channel_id=1, source_target_pairs={{0,6},{1,7},{2,4},{3,5},{4,2},{5,3},{6,0},{7,1},{8,14},{9,15},{10,... | collective-permute-start | bytes 196616 | tf_op jit(solution)/shard_map/ppermute | solution.py:52
  59.8 5.2 %collective-permute-start.14 = (bf16[2,32,512]{2,1,0:T(8,128)(2,1)S(1)}, bf16[2,32,512]{2,1,0:T(8,128)(2,1)S(1)}, u32[]{:S(2)}, u32[]{:S(2)}) collective-permute-start(bf16[2,32,512]{2,1,0:T(8,128)(2,1)S(1)} %pad_maximum_fusion.6), channel_id=1, source_target_pairs={{0,4},{1,5},{2,6},{3,7},{4,0},{5,1},{6,2},{7,3},{8,12},{9,13},{10,... | collective-permute-start | bytes 196616 | tf_op jit(solution)/shard_map/ppermute | solution.py:52
  59.8 5.2 %collective-permute-start.15 = (bf16[2,32,512]{2,1,0:T(8,128)(2,1)S(1)}, bf16[2,32,512]{2,1,0:T(8,128)(2,1)S(1)}, u32[]{:S(2)}, u32[]{:S(2)}) collective-permute-start(bf16[2,32,512]{2,1,0:T(8,128)(2,1)S(1)} %pad_maximum_fusion.6), channel_id=1, source_target_pairs={{0,2},{1,3},{2,0},{3,1},{4,6},{5,7},{6,4},{7,5},{8,10},{9,11},{10,... | collective-permute-start | bytes 196616 | tf_op jit(solution)/shard_map/ppermute | solution.py:52
  62.3 16.4 %collective-permute-start.20 = (bf16[512,512]{1,0:T(8,128)(2,1)}, bf16[512,512]{1,0:T(8,128)(2,1)S(1)}, u32[]{:S(2)}, u32[]{:S(2)}) collective-permute-start(bf16[512,512]{1,0:T(8,128)(2,1)} %copy-done.10), channel_id=1, source_target_pairs={{0,16},{8,24},{16,0},{24,8},{1,17},{9,25},{17,1},{25,9},{2,18},{10... | collective-permute-start | bytes 1572872 | tf_op jit(solution)/shard_map/ppermute | solution.py:179
  71.3 1.0 copy-start.5
  71.3 1.2 copy-start.7
  71.5 10.0 %copy-start.2 = (bf16[2048,512]{1,0:T(8,128)(2,1)S(1)}, bf16[2048,512]{1,0:T(8,128)(2,1)}, u32[]{:S(2)}) copy-start(bf16[2048,512]{1,0:T(8,128)(2,1)} %refs_0_.5) | copy-start | bytes 6291460
  73.6 5.2 %collective-permute-start.18 = (f32[4,768]{1,0:T(4,128)S(1)}, f32[4,768]{1,0:T(4,128)S(1)}, u32[]{:S(2)}, u32[]{:S(2)}) collective-permute-start(f32[4,768]{1,0:T(4,128)S(1)} %shard_map.84), channel_id=1, source_target_pairs={{0,16},{8,24},{16,0},{24,8},{1,17},{9,25},{17,1},{25,9},{2,18},{10... | collective-permute-start | bytes 36872 | tf_op jit(solution)/shard_map/ppermute | solution.py:179
  75.1 6.4 %collective-permute-start.19 = (bf16[2,128,512]{2,1,0:T(8,128)(2,1)S(1)}, bf16[2,128,512]{2,1,0:T(8,128)(2,1)S(1)}, u32[]{:S(2)}, u32[]{:S(2)}) collective-permute-start(bf16[2,128,512]{2,1,0:T(8,128)(2,1)S(1)} %pad_maximum_fusion.2.line), channel_id=1, source_target_pairs={{0,1},{1,0},{2,3},{3,2},{4,5},{5,4},{6,7},{7,6},{8,9},{9,8},{10,11... | collective-permute-start | bytes 786440 | tf_op jit(solution)/shard_map/ppermute | solution.py:52
  81.5 5.2 %copy-start.3 = (bf16[2048,128]{1,0:T(8,128)(2,1)S(1)}, bf16[2048,128]{1,0:T(8,128)(2,1)}, u32[]{:S(2)}) copy-start(bf16[2048,128]{1,0:T(8,128)(2,1)} %constant_dynamic-slice_fusion.3.coulomb) | copy-start | bytes 1572868
  81.5 5.2 %copy-start.15 = (f32[4]{0:T(128)S(1)}, f32[4]{0:T(128)}, u32[]{:S(2)}) copy-start(f32[4]{0:T(128)} %occ.3) | copy-start | bytes 52
  84.8 2.0 %collective-permute-start.21 = (bf16[2048,128]{1,0:T(8,128)(2,1)S(1)}, bf16[2048,128]{1,0:T(8,128)(2,1)S(1)}, u32[]{:S(2)}, u32[]{:S(2)}) collective-permute-start(bf16[2048,128]{1,0:T(8,128)(2,1)S(1)} %get-tuple-element.55), channel_id=1, source_target_pairs={{0,8},{8,0},{16,24},{24,16},{1,9},{9,1},{17,25},{25,17},{2,10},{10... | collective-permute-start | bytes 1572872 | tf_op jit(solution)/shard_map/ppermute | solution.py:179
  87.8 2.0 %collective-permute-start.22 = (bf16[128,2048]{1,0:T(8,128)(2,1)S(1)}, bf16[128,2048]{1,0:T(8,128)(2,1)S(1)}, u32[]{:S(2)}, u32[]{:S(2)}) collective-permute-start(bf16[128,2048]{1,0:T(8,128)(2,1)S(1)} %shard_map.86.mine), channel_id=1, source_target_pairs={{0,8},{8,0},{16,24},{24,16},{1,9},{9,1},{17,25},{25,17},{2,10},{10... | collective-permute-start | bytes 1572872 | tf_op jit(solution)/shard_map/ppermute | solution.py:179
  93.0 8.4 %collective-permute-start.24 = (bf16[2,128,512]{2,1,0:T(8,128)(2,1)S(1)}, bf16[2,128,512]{2,1,0:T(8,128)(2,1)S(1)}, u32[]{:S(2)}, u32[]{:S(2)}) collective-permute-start(bf16[2,128,512]{2,1,0:T(8,128)(2,1)S(1)} %dynamic-slice_convert_fusion), channel_id=1, source_target_pairs={{0,1},{1,0},{2,3},{3,2},{4,5},{5,4},{6,7},{7,6},{8,9},{9,8},{10,11... | collective-permute-start | bytes 786440 | tf_op jit(solution)/shard_map/ppermute | solution.py:43
  101.5 6.7 %collective-permute-start.27 = (bf16[2,32,512]{2,1,0:T(8,128)(2,1)S(1)}, bf16[2,32,512]{2,1,0:T(8,128)(2,1)S(1)}, u32[]{:S(2)}, u32[]{:S(2)}) collective-permute-start(bf16[2,32,512]{2,1,0:T(8,128)(2,1)S(1)} %get-tuple-element.78), channel_id=1, source_target_pairs={{0,6},{1,7},{2,4},{3,5},{4,2},{5,3},{6,0},{7,1},{8,14},{9,15},{10,... | collective-permute-start | bytes 196616 | tf_op jit(solution)/shard_map/ppermute | solution.py:52
  105.2 5.3 %collective-permute-start.26 = (bf16[2,32,512]{2,1,0:T(8,128)(2,1)S(1)}, bf16[2,32,512]{2,1,0:T(8,128)(2,1)S(1)}, u32[]{:S(2)}, u32[]{:S(2)}) collective-permute-start(bf16[2,32,512]{2,1,0:T(8,128)(2,1)S(1)} %get-tuple-element.79), channel_id=1, source_target_pairs={{0,4},{1,5},{2,6},{3,7},{4,0},{5,1},{6,2},{7,3},{8,12},{9,13},{10,... | collective-permute-start | bytes 196616 | tf_op jit(solution)/shard_map/ppermute | solution.py:52
  105.2 5.3 %collective-permute-start.25 = (bf16[2,32,512]{2,1,0:T(8,128)(2,1)S(1)}, bf16[2,32,512]{2,1,0:T(8,128)(2,1)S(1)}, u32[]{:S(2)}, u32[]{:S(2)}) collective-permute-start(bf16[2,32,512]{2,1,0:T(8,128)(2,1)S(1)} %get-tuple-element.77), channel_id=1, source_target_pairs={{0,2},{1,3},{2,0},{3,1},{4,6},{5,7},{6,4},{7,5},{8,10},{9,11},{10,... | collective-permute-start | bytes 196616 | tf_op jit(solution)/shard_map/ppermute | solution.py:52
  110.5 6.3 %collective-permute-start.28 = (bf16[2,32,512]{2,1,0:T(8,128)(2,1)S(1)}, bf16[2,32,512]{2,1,0:T(8,128)(2,1)S(1)}, u32[]{:S(2)}, u32[]{:S(2)}) collective-permute-start(bf16[2,32,512]{2,1,0:T(8,128)(2,1)S(1)} %add_convert_fusion), channel_id=1, source_target_pairs={{0,6},{1,7},{2,4},{3,5},{4,2},{5,3},{6,0},{7,1},{8,14},{9,15},{10,... | collective-permute-start | bytes 196616 | tf_op jit(solution)/shard_map/ppermute | solution.py:52
  113.1 5.4 %collective-permute-start.29 = (bf16[2,32,512]{2,1,0:T(8,128)(2,1)S(1)}, bf16[2,32,512]{2,1,0:T(8,128)(2,1)S(1)}, u32[]{:S(2)}, u32[]{:S(2)}) collective-permute-start(bf16[2,32,512]{2,1,0:T(8,128)(2,1)S(1)} %add_convert_fusion), channel_id=1, source_target_pairs={{0,4},{1,5},{2,6},{3,7},{4,0},{5,1},{6,2},{7,3},{8,12},{9,13},{10,... | collective-permute-start | bytes 196616 | tf_op jit(solution)/shard_map/ppermute | solution.py:52
  113.1 5.4 %collective-permute-start.30 = (bf16[2,32,512]{2,1,0:T(8,128)(2,1)S(1)}, bf16[2,32,512]{2,1,0:T(8,128)(2,1)S(1)}, u32[]{:S(2)}, u32[]{:S(2)}) collective-permute-start(bf16[2,32,512]{2,1,0:T(8,128)(2,1)S(1)} %add_convert_fusion), channel_id=1, source_target_pairs={{0,2},{1,3},{2,0},{3,1},{4,6},{5,7},{6,4},{7,5},{8,10},{9,11},{10,... | collective-permute-start | bytes 196616 | tf_op jit(solution)/shard_map/ppermute | solution.py:52
  115.0 4.1 %collective-permute-start.23 = (f32[4,768]{1,0:T(4,128)S(1)}, f32[4,768]{1,0:T(4,128)S(1)}, u32[]{:S(2)}, u32[]{:S(2)}) collective-permute-start(f32[4,768]{1,0:T(4,128)S(1)} %get-tuple-element.59), channel_id=1, source_target_pairs={{0,16},{8,24},{16,0},{24,8},{1,17},{9,25},{17,1},{25,9},{2,18},{10... | collective-permute-start | bytes 36872 | tf_op jit(solution)/shard_map/ppermute | solution.py:179
  118.5 6.4 %collective-permute-start.31 = (bf16[2,128,512]{2,1,0:T(8,128)(2,1)S(1)}, bf16[2,128,512]{2,1,0:T(8,128)(2,1)S(1)}, u32[]{:S(2)}, u32[]{:S(2)}) collective-permute-start(bf16[2,128,512]{2,1,0:T(8,128)(2,1)S(1)} %pad_maximum_fusion.3.line), channel_id=1, source_target_pairs={{0,1},{1,0},{2,3},{3,2},{4,5},{5,4},{6,7},{7,6},{8,9},{9,8},{10,11... | collective-permute-start | bytes 786440 | tf_op jit(solution)/shard_map/ppermute | solution.py:52
  128.1 2.0 %collective-permute-start.32 = (bf16[2048,128]{1,0:T(8,128)(2,1)S(1)}, bf16[2048,128]{1,0:T(8,128)(2,1)S(1)}, u32[]{:S(2)}, u32[]{:S(2)}) collective-permute-start(bf16[2048,128]{1,0:T(8,128)(2,1)S(1)} %get-tuple-element.62), channel_id=1, source_target_pairs={{0,8},{8,0},{16,24},{24,16},{1,9},{9,1},{17,25},{25,17},{2,10},{10... | collective-permute-start | bytes 1572872 | tf_op jit(solution)/shard_map/ppermute | solution.py:179
  (4 other events, 3.4 us)

commit v4 on v3

v4 whole, which is shorter than its diff:
```python
import functools

import jax
import jax.numpy as jnp
from jax import lax
from jax.experimental import pallas as pl
from jax.experimental.pallas import tpu as pltpu
from jax.sharding import PartitionSpec as P

ITERS = 2
BF = jnp.bfloat16
F32 = jnp.float32
VMEM = pl.BlockSpec(memory_space=pltpu.VMEM)
SMEM = pl.BlockSpec(memory_space=pltpu.SMEM)
ANY = pl.BlockSpec(memory_space=pl.ANY)
FAR = lambda rows: [rows // 2, rows // 4, rows // 4]
DUE = {1: (0,), 3: (1,), 4: (2,)}
PARAMS = pltpu.CompilerParams(vmem_limit_bytes=12 * 2**20)


def xor(n, s):
    return [(i, i ^ s) for i in range(n)]


def dot(a, b, ca, cb):
    return lax.dot_general(a, b, (((ca,), (cb,)), ((), ())), preferred_element_type=F32)


def take(a, start, size, axis=0):
    return lax.dynamic_slice_in_dim(a, start, size, axis)


def tie(a, *others):
    return lax.optimization_barrier((a, *others))


def halves(v, low):
    half = v.shape[1] // 2
    return take(v, low * half, half, 1), take(v, (1 - low) * half, half, 1)


def fold(v, n):
    mine, theirs = halves(v, lax.axis_index("pair") % 2)
    return mine, lax.ppermute(theirs.astype(BF), "pair", xor(n, 1))


def all_reduce(mine, got, n, beside=lambda stage, a: a):
    high = lax.axis_index("pair") // 2
    m = n // 2
    part = mine.shape[1] // m

    def send(a, s):
        return lax.ppermute(a, "pair", xor(n, s))

    acc = mine + beside(0, got).astype(F32)
    rounded = acc.astype(BF)
    total = take(acc, high * part, part, 1)
    for s in range(1, m):
        total = total + send(take(rounded, (high ^ s) * part, part, 1), 2 * s).astype(F32)
    mine = beside(1, total.astype(BF))
    parts = [mine] + [send(mine, 2 * s) for s in range(1, m)]
    line = []
    for q in range(m):
        block = parts[0]
        for s in range(1, m):
            block = jnp.where((high ^ s) == q, parts[s], block)
        line.append(block)
    line = beside(2, jnp.concatenate(line, axis=1))
    return line, beside(3, send(line, 1))


def hold_kernel(own, far, out, sems):
    copies = [pltpu.make_async_copy(a, out.at[r], sems.at[r]) for r, a in enumerate((own, far))]
    for copy in copies:
        copy.start()
    for copy in copies:
        copy.wait()


def residual_kernel(swapped, side, middle, left, right, factors, line, other, *refs):
    mine, theirs, gram = refs[-3:]
    nvirt, half, width = left.shape[0], line.shape[1], mine.shape[1]
    near = (line, other)
    for j in range(2):
        rows = pl.ds(pl.multiple_of((side[0] if j == 0 else 1 - side[0]) * half, half), half)
        gram[0, rows] = near[j][0]
        gram[1, rows] = refs[0][j] if swapped else near[j][1]
    size = min(nvirt, 256)
    for start in range(0, mine.shape[0], size):
        i, at = start // nvirt, start % nvirt
        if at == 0:
            scaled = (right[...].astype(F32) * middle[i : i + 1, :]).astype(BF)
        rows = slice(start, start + size)
        res = dot(left[at : at + size], scaled, 1, 1)
        for r in range(2):
            res += dot(factors[r, rows], gram[r], 1, 1)
        mine[rows] = res[:, :width]
        theirs[rows] = res[:, width:].astype(BF)


def update_kernel(last, occ, pivot, mine, got, coulomb, vir, vir_row, out):
    nvirt, width = vir.shape[1], mine.shape[1]
    virs = jnp.broadcast_to(vir[...], (width, nvirt)).T + vir_row[...]
    for i in range(mine.shape[0] // nvirt):
        rows = slice(i * nvirt, (i + 1) * nvirt)
        res = mine[rows] + got[rows].astype(F32)
        new = (coulomb[rows].astype(F32) + res) / (virs - occ[i] - pivot[0])
        if last:
            out[rows] = new.astype(BF)
        else:
            out[:, rows] = new.T.astype(BF)


def middle_kernel(mine, other, left, right, middle):
    width, nvirt = mine.shape[1], left.shape[0]
    for i in range(middle.shape[0]):
        total = None
        for at, amps in ((0, mine), (width, other)):
            proj = dot(amps[i * nvirt : (i + 1) * nvirt], left[...], 0, 0)
            term = jnp.sum(proj * right[at : at + width].astype(F32), axis=0, keepdims=True)
            total = term if total is None else total + term
        middle[i : i + 1] = total


def gram_kernel(mine, other, left, right, factors, gram, middle, amps):
    width, nvirt = mine.shape[0], left.shape[0]
    amps[:width] = mine[...]
    amps[width:] = other[...]
    for r in range(2):
        gram[r] = dot(amps[...], factors[r], 1, 0)
    for i in range(middle.shape[0]):
        proj = dot(amps[:, i * nvirt : (i + 1) * nvirt], left[...], 1, 0)
        middle[i : i + 1] = jnp.sum(proj * right[...].astype(F32), axis=0, keepdims=True)


def first_gram_kernel(mine, other, own, gram):
    width = mine.shape[1]
    gram[:width] = dot(mine[...], own[...], 0, 0)
    gram[width:] = dot(other[...], own[...], 0, 0)


def per_device(
    amplitudes, coulomb, df_factors, thc_left, thc_right, occ_energy, vir_energy, pivot_energy
):
    n_pair = lax.axis_size("pair")
    n_aux = lax.axis_size("aux")
    k = lax.axis_index("aux")
    me = lax.axis_index("pair")
    rows, width = amplitudes.shape
    nvirt = vir_energy.shape[0]
    nocc = rows // nvirt
    naux = df_factors.shape[1]
    low = (me % 2).reshape(1)

    def over(a, s):
        return lax.ppermute(a, "aux", xor(n_aux, s))

    fac = jnp.stack([thc_left, thc_right])
    fac = jnp.concatenate([fac, over(fac, 2)], axis=2)
    cols = fac.shape[-1]

    def other_rows(fac, axis):
        bit = n_pair >> (axis + 1)
        got = lax.ppermute(fac, "pair", xor(n_pair, bit))
        first = (me // bit) % 2 == 0
        return jnp.where(first, fac, got), jnp.where(first, got, fac)

    n_bits = n_pair.bit_length() - 1

    far_amps = over(amplitudes, 2)
    near = [amplitudes, over(amplitudes, 1)]

    def first_gram(pair_of):
        return pl.pallas_call(
            first_gram_kernel,
            out_shape=jax.ShapeDtypeStruct((2 * width, naux), F32),
            in_specs=[VMEM] * 3,
            out_specs=VMEM,
            compiler_params=PARAMS,
        )(*pair_of, df_factors)[None]

    near_mine, near_got = fold(first_gram(near), n_pair)
    far_amps, near_got, fac = tie(far_amps, near_got, fac)
    far_other, fac = tie(over(far_amps, 1), fac)
    far_gram = first_gram([far_amps, far_other])

    one, two = other_rows(fac, 0)
    kept = jnp.where(k // 2 == 0, one[1], two[1])
    fac = jnp.stack([one[0], two[0], kept])[:, None]
    far_gram, fac = tie(far_gram, fac)
    far_mine, far_got = fold(far_gram, n_pair)

    far = over(df_factors, 2)
    vir = vir_energy[None, :]
    vir_row = take(vir_energy, k * width, width)[None, :]
    coulomb_block = take(coulomb, k * width, width, 1)

    left = right = middle = factors = None

    def beside(stage, a):
        nonlocal fac, far, vir, vir_row, coulomb_block, left, right, middle, factors
        if stage == 1:
            fac = jnp.stack(other_rows(fac, n_bits - 1), axis=2).reshape(3, 1, -1, *fac.shape[2:])
            a, fac = tie(a, fac)
        if stage == 1:
            a, vir, vir_row, coulomb_block = tie(a, vir, vir_row, coulomb_block)
        if stage == 4:
            for axis in range(n_bits - 2, 0, -1):
                fac = jnp.stack(other_rows(fac, axis), axis=1)
                fac = fac.reshape(3, -1, *fac.shape[3:])
            left = fac[:2].reshape(nvirt, cols)
            right = fac[2].reshape(2, width, cols)
            right = jnp.where(k % 2 == 0, right, right[::-1]).reshape(2 * width, cols)
            middle = pl.pallas_call(
                middle_kernel,
                out_shape=jax.ShapeDtypeStruct((nocc, cols), F32),
                in_specs=[VMEM] * 4,
                out_specs=VMEM,
                compiler_params=PARAMS,
            )(*near, left, right)
        if stage == 4:
            a, far = tie(a, far)
            factors = pl.pallas_call(
                hold_kernel,
                out_shape=jax.ShapeDtypeStruct((2, rows, naux), BF),
                in_specs=[ANY] * 2,
                out_specs=VMEM,
                scratch_shapes=[pltpu.SemaphoreType.DMA((2,))],
                compiler_params=PARAMS,
            )(df_factors, far)
        return a

    line, other = all_reduce(
        jnp.concatenate([near_mine, far_mine], axis=0),
        jnp.concatenate([near_got, far_got], axis=0),
        n_pair,
        beside,
    )
    swapped = beside(4, over(jnp.stack([line[1], other[1]]), 2))
    gram = (line, other, swapped)
    for step in range(ITERS):
        last = step == ITERS - 1
        other = over(middle, 2)
        middle = middle + jnp.concatenate([other[:, cols // 2 :], other[:, : cols // 2]], axis=1)
        mine, theirs = pl.pallas_call(
            functools.partial(residual_kernel, step == 0),
            out_shape=(
                jax.ShapeDtypeStruct((rows, width), F32),
                jax.ShapeDtypeStruct((rows, width), BF),
            ),
            in_specs=[SMEM] + [VMEM] * (4 + len(gram)),
            out_specs=(VMEM, VMEM),
            scratch_shapes=[pltpu.VMEM((2, 2 * width, naux), BF)],
            compiler_params=PARAMS,
        )(low, middle, left, right, factors, *gram)
        got = over(theirs, 1)
        new = pl.pallas_call(
            functools.partial(update_kernel, last),
            out_shape=jax.ShapeDtypeStruct((rows, width) if last else (width, rows), BF),
            in_specs=[SMEM] * 2 + [VMEM] * 5,
            out_specs=VMEM,
            compiler_params=PARAMS,
        )(occ_energy, pivot_energy, mine, got, coulomb_block, vir, vir_row)
        if not last:
            gram, middle = pl.pallas_call(
                gram_kernel,
                out_shape=(
                    jax.ShapeDtypeStruct((2, 2 * width, naux), F32),
                    jax.ShapeDtypeStruct((nocc, cols), F32),
                ),
                in_specs=[VMEM] * 5,
                out_specs=(VMEM, VMEM),
                scratch_shapes=[pltpu.VMEM((2 * width, rows), BF)],
                compiler_params=PARAMS,
            )(new, over(new, 1), left, right, factors)
            gram = all_reduce(*fold(gram, n_pair), n_pair)
    return new


def solution(mesh):
    in_specs = (
        P("pair", "aux"),
        P("pair", None),
        P("pair", "aux"),
        P("pair", "aux"),
        P("pair", "aux"),
        P("pair"),
        P(),
        P(),
    )
    out_specs = P("pair", "aux")
    return jax.shard_map(
        per_device, mesh=mesh, in_specs=in_specs, out_specs=out_specs, check_vma=False
    )
```

time: 132 us -> 125 us (0.947)
  other arithmetic: 7.16 us -> 3.79 us
  waiting for transfers between devices: 59.5 us -> 56.5 us
  local copies, waits for them, and re-layouts: 8.36 us -> 6.41 us
    ppermute x13 -> x11, waiting for transfers between devices: 22.5 us -> 12.8 us  [over(): return lax.ppermute(a, 'aux', xor(n_aux, s))]
    ppermute x14, waiting for transfers between devices: 20.8 us -> 25.8 us  [send(): return lax.ppermute(a, 'pair', xor(n, s))]
    unnamed x38 -> x26, local copies, waits for them, and re-layouts: 7.16 us -> 5.11 us
    ppermute x3, waiting for transfers between devices: 9.11 us -> 11.1 us  [fold(): return (mine, lax.ppermute(theirs.astype(BF), 'pair', xor(n, 1)))]
    ppermute x14, starting transfers between devices: 18.9 us -> 20.9 us  [send(): return lax.ppermute(a, 'pair', xor(n, s))]
    ppermute x13 -> x11, starting transfers between devices: 11.3 us -> 9.33 us  [over(): return lax.ppermute(a, 'aux', xor(n_aux, s))]
    pallas_call x6 -> x7, Pallas kernels: 14.3 us -> 15.5 us  [the longest x2 5.21 us: per_device(): pl.pallas_call(functools.partial(residual_kernel, step == 0), out_shape=(...]
  transfers between devices with their start and end apart: 33 -> 31, of which waited for: 20 -> 20; matrix products, arithmetic and copies ran while one was open for 5% -> 4% of each run, Pallas kernels for 4% -> 7%
where the time goes in v4:
time: 125 us; the launch traced here: 124 us
  waiting for transfers between devices  56.5 us (45%)
  starting transfers between devices  38.5 us (31%)
  Pallas kernels  18.2 us (15%)
  local copies, waits for them, and re-layouts  6.41 us (5%)
  other arithmetic  3.79 us (3%)
    ppermute x14, waiting for transfers between devices, send(): return lax.ppermute(a, 'pair', xor(n, s))  25.8 us
    ppermute x14, starting transfers between devices, send(): return lax.ppermute(a, 'pair', xor(n, s))  20.9 us
    ppermute x11, waiting for transfers between devices, over(): return lax.ppermute(a, 'aux', xor(n_aux, s))  12.8 us
    ppermute x3, waiting for transfers between devices, fold(): return (mine, lax.ppermute(theirs.astype(BF), 'pair', xor(n, 1)))  11.1 us
    ppermute x11, starting transfers between devices, over(): return lax.ppermute(a, 'aux', xor(n_aux, s))  9.33 us
    ppermute x3, waiting for transfers between devices, other_rows(): got = lax.ppermute(fac, 'pair', xor(n_pair, bit))  6.7 us
    pallas_call x2, Pallas kernels, per_device(): pl.pallas_call(functools.partial(residual_kernel, step == 0), out_shape=(...  5.21 us
    unnamed x26, local copies, waits for them, and re-layouts  5.11 us
  transfers between devices with their start and end apart: 31, of which 20 were waited for; matrix products, arithmetic and copies ran while one was open for 4% of the time, Pallas kernels for 7%

profile of v4, /device:TPU:0, one launch (start us, length us, event | category | flops | bytes accessed | tf_op | source)
XLA Modules:
  0.0 124.5 jit_solution(5202999367135264766)
XLA Ops:
  0.5 2.6 %collective-permute-start.1 = (bf16[2048,128]{1,0:T(8,128)(2,1)}, bf16[2048,128]{1,0:T(8,128)(2,1)S(1)}, u32[]{:S(2)}, u32[]{:S(2)}) collective-permute-start(bf16[2048,128]{1,0:T(8,128)(2,1)} %mine.3), channel_id=1, source_target_pairs={{0,16},{8,24},{16,0},{24,8},{1,17},{9,25},{17,1},{25,9},{2,18},{10... | collective-permute-start | bytes 1572872 | tf_op jit(solution)/shard_map/ppermute | solution.py:156
  4.2 1.0 copy-done.1
  5.2 2.3 %shard_map.82 = f32[256,512]{1,0:T(8,128)S(1)} custom-call(bf16[2048,128]{1,0:T(8,128)(2,1)S(1)} %copy-done.1, bf16[2048,128]{1,0:T(8,128)(2,1)S(1)} %collective-permute-done.other, bf16[2048,512]{1,0:T(8,128)(2,1)} %own.5), custom_call_target="tpu_custom_call" | custom-call | tf_op jit(solution)/shard_map/pallas_call | solution.py:174
  8.4 1.9 %collective-permute-start.2 = (bf16[1,128,512]{2,1,0:T(8,128)(2,1)S(1)}, bf16[1,128,512]{2,1,0:T(8,128)(2,1)S(1)}, u32[]{:S(2)}, u32[]{:S(2)}) collective-permute-start(bf16[1,128,512]{2,1,0:T(8,128)(2,1)S(1)} %fusion.1), channel_id=1, source_target_pairs={{0,1},{1,0},{2,3},{3,2},{4,5},{5,4},{6,7},{7,6},{8,9},{9,8},{10,11... | collective-permute-start | bytes 393224 | tf_op jit(solution)/shard_map/ppermute | solution.py:44
  10.3 7.6 %collective-permute-done.3 = bf16[2,64,384]{2,1,0:T(8,128)(2,1)S(1)} collective-permute-done((bf16[2,64,384]{2,1,0:T(8,128)(2,1)S(1)}, bf16[2,64,384]{2,1,0:T(8,128)(2,1)S(1)}, u32[]{:S(2)}, u32[]{:S(2)}) %collective-permute-start.3) | collective-permute-done | bytes 98336 | tf_op jit(solution)/shard_map/ppermute | solution.py:156
  19.5 1.8 %collective-permute-start.18 = (bf16[2048,512]{1,0:T(8,128)(2,1)}, bf16[2048,512]{1,0:T(8,128)(2,1)}, u32[]{:S(2)}, u32[]{:S(2)}) collective-permute-start(bf16[2048,512]{1,0:T(8,128)(2,1)} %own.5), channel_id=1, source_target_pairs={{0,16},{8,24},{16,0},{24,8},{1,17},{9,25},{17,1},{25,9},{2,18},{10... | collective-permute-start | bytes 6291464 | tf_op jit(solution)/shard_map/ppermute | solution.py:156
  21.2 2.6 %collective-permute-start.5 = (bf16[2,64,768]{2,1,0:T(8,128)(2,1)S(1)}, bf16[2,64,768]{2,1,0:T(8,128)(2,1)S(1)}, u32[]{:S(2)}, u32[]{:S(2)}) collective-permute-start(bf16[2,64,768]{2,1,0:T(8,128)(2,1)S(1)} %pad_maximum_fusion.5), channel_id=1, source_target_pairs={{0,4},{1,5},{2,6},{3,7},{4,0},{5,1},{6,2},{7,3},{8,12},{9,13},{10,... | collective-permute-start | bytes 589832 | tf_op jit(solution)/shard_map/ppermute | solution.py:164
  23.9 1.0 copy-done.6
  24.9 2.5 %shard_map.83 = f32[256,512]{1,0:T(8,128)S(1)} custom-call(bf16[2048,128]{1,0:T(8,128)(2,1)S(1)} %copy-done.6, bf16[2048,128]{1,0:T(8,128)(2,1)} %collective-permute-done.4.other, bf16[2048,512]{1,0:T(8,128)(2,1)} %own.5), custom_call_target="tpu_custom_call" | custom-call | tf_op jit(solution)/shard_map/pallas_call | solution.py:174
  27.5 5.3 %collective-permute-done.5 = bf16[2,64,768]{2,1,0:T(8,128)(2,1)S(1)} collective-permute-done((bf16[2,64,768]{2,1,0:T(8,128)(2,1)S(1)}, bf16[2,64,768]{2,1,0:T(8,128)(2,1)S(1)}, u32[]{:S(2)}, u32[]{:S(2)}) %collective-permute-start.5) | collective-permute-done | bytes 196640 | tf_op jit(solution)/shard_map/ppermute | solution.py:164
  33.0 1.6 %collective-permute-start.6 = (bf16[1,128,512]{2,1,0:T(8,128)(2,1)S(1)}, bf16[1,128,512]{2,1,0:T(8,128)(2,1)S(1)}, u32[]{:S(2)}, u32[]{:S(2)}) collective-permute-start(bf16[1,128,512]{2,1,0:T(8,128)(2,1)S(1)} %dynamic-slice_convert_fusion.1), channel_id=1, source_target_pairs={{0,1},{1,0},{2,3},{3,2},{4,5},{5,4},{6,7},{7,6},{8,9},{9,8},{10,11... | collective-permute-start | bytes 393224 | tf_op jit(solution)/shard_map/ppermute | solution.py:44
  35.2 4.3 %collective-permute-done.6 = bf16[1,128,512]{2,1,0:T(8,128)(2,1)S(1)} collective-permute-done((bf16[1,128,512]{2,1,0:T(8,128)(2,1)S(1)}, bf16[1,128,512]{2,1,0:T(8,128)(2,1)S(1)}, u32[]{:S(2)}, u32[]{:S(2)}) %collective-permute-start.6) | collective-permute-done | bytes 131104 | tf_op jit(solution)/shard_map/ppermute | solution.py:44
  40.3 3.4 %collective-permute-start.8 = (bf16[2,32,512]{2,1,0:T(8,128)(2,1)S(1)}, bf16[2,32,512]{2,1,0:T(8,128)(2,1)S(1)}, u32[]{:S(2)}, u32[]{:S(2)}) collective-permute-start(bf16[2,32,512]{2,1,0:T(8,128)(2,1)S(1)} %get-tuple-element.70), channel_id=1, source_target_pairs={{0,4},{1,5},{2,6},{3,7},{4,0},{5,1},{6,2},{7,3},{8,12},{9,13},{10,... | collective-permute-start | bytes 196616 | tf_op jit(solution)/shard_map/ppermute | solution.py:53
  44.1 3.2 %collective-permute-done.8 = bf16[2,32,512]{2,1,0:T(8,128)(2,1)S(1)} collective-permute-done((bf16[2,32,512]{2,1,0:T(8,128)(2,1)S(1)}, bf16[2,32,512]{2,1,0:T(8,128)(2,1)S(1)}, u32[]{:S(2)}, u32[]{:S(2)}) %collective-permute-start.8) | collective-permute-done | bytes 65568 | tf_op jit(solution)/shard_map/ppermute | solution.py:53
  47.3 2.5 %collective-permute-done.9 = bf16[2,32,512]{2,1,0:T(8,128)(2,1)S(1)} collective-permute-done((bf16[2,32,512]{2,1,0:T(8,128)(2,1)S(1)}, bf16[2,32,512]{2,1,0:T(8,128)(2,1)S(1)}, u32[]{:S(2)}, u32[]{:S(2)}) %collective-permute-start.9) | collective-permute-done | bytes 65568 | tf_op jit(solution)/shard_map/ppermute | solution.py:53
  49.9 0.9 pad_maximum_fusion
  51.5 3.7 %collective-permute-start.15 = (bf16[2,32,512]{2,1,0:T(8,128)(2,1)S(1)}, bf16[2,32,512]{2,1,0:T(8,128)(2,1)S(1)}, u32[]{:S(2)}, u32[]{:S(2)}) collective-permute-start(bf16[2,32,512]{2,1,0:T(8,128)(2,1)S(1)} %add_convert_fusion.1), channel_id=1, source_target_pairs={{0,2},{1,3},{2,0},{3,1},{4,6},{5,7},{6,4},{7,5},{8,10},{9,11},{10,... | collective-permute-start | bytes 196616 | tf_op jit(solution)/shard_map/ppermute | solution.py:53
  55.2 2.4 %collective-permute-done.13 = bf16[2,32,512]{2,1,0:T(8,128)(2,1)S(1)} collective-permute-done((bf16[2,32,512]{2,1,0:T(8,128)(2,1)S(1)}, bf16[2,32,512]{2,1,0:T(8,128)(2,1)S(1)}, u32[]{:S(2)}, u32[]{:S(2)}) %collective-permute-start.13) | collective-permute-done | bytes 65568 | tf_op jit(solution)/shard_map/ppermute | solution.py:53
  57.6 1.3 %collective-permute-done.15 = bf16[2,32,512]{2,1,0:T(8,128)(2,1)S(1)} collective-permute-done((bf16[2,32,512]{2,1,0:T(8,128)(2,1)S(1)}, bf16[2,32,512]{2,1,0:T(8,128)(2,1)S(1)}, u32[]{:S(2)}, u32[]{:S(2)}) %collective-permute-start.15) | collective-permute-done | bytes 65568 | tf_op jit(solution)/shard_map/ppermute | solution.py:53
  59.0 1.6 %collective-permute-start.16 = (bf16[2,128,512]{2,1,0:T(8,128)(2,1)S(1)}, bf16[2,128,512]{2,1,0:T(8,128)(2,1)}, u32[]{:S(2)}, u32[]{:S(2)}) collective-permute-start(bf16[2,128,512]{2,1,0:T(8,128)(2,1)S(1)} %pad_maximum_fusion.2.line), channel_id=1, source_target_pairs={{0,1},{1,0},{2,3},{3,2},{4,5},{5,4},{6,7},{7,6},{8,9},{9,8},{10,11... | collective-permute-start | bytes 786440 | tf_op jit(solution)/shard_map/ppermute | solution.py:53
  60.6 5.0 %collective-permute-done.16.other = bf16[2,128,512]{2,1,0:T(8,128)(2,1)} collective-permute-done((bf16[2,128,512]{2,1,0:T(8,128)(2,1)S(1)}, bf16[2,128,512]{2,1,0:T(8,128)(2,1)}, u32[]{:S(2)}, u32[]{:S(2)}) %collective-permute-start.16) | collective-permute-done | bytes 262176 | tf_op jit(solution)/shard_map/ppermute | solution.py:53
  65.5 0.9 slice.59
  66.5 1.2 collective-permute-start.17
  67.7 1.4 %collective-permute-done.11 = bf16[3,1,2,64,768]{4,3,0,2,1:T(8,128)(2,1)} collective-permute-done((bf16[3,1,2,64,768]{4,3,0,2,1:T(8,128)(2,1)}, bf16[3,1,2,64,768]{4,3,0,2,1:T(8,128)(2,1)}, u32[]{:S(2)}, u32[]{:S(2)}) %collective-permute-start.11) | collective-permute-done | bytes 589856 | tf_op jit(solution)/shard_map/ppermute | solution.py:164
  69.1 1.3 %select_bitcast_fusion = (bf16[3,1,1,2,64,768]{5,4,0,3,2,1:T(8,128)(2,1)S(1)}, bf16[3,1,1,2,64,768]{5,4,0,3,2,1:T(8,128)(2,1)S(1)}) fusion(bf16[3,1,2,64,768]{4,3,0,2,1:T(8,128)(2,1)} %collective-permute-done.11, bf16[3,1,2,64,768]{4,3,0,2,1:T(8,128)(2,1)} %pad_maximum_fusion, pred[]{:T(512)S(6)} %eq.72), kind=kLoop, calls=%fused_computation.5 | loop fusion | flops 589824 | bytes 2359297 | tf_op jit(solution)/shard_map/stack | solution.py:209
  71.5 1.1 shard_map.84
  72.6 1.2 collective-permute-start.12
  73.9 2.2 %shard_map.85.factors = bf16[2,2048,512]{2,1,0:T(8,128)(2,1)S(1)} custom-call(bf16[2048,512]{1,0:T(8,128)(2,1)} %own.5, bf16[2048,512]{1,0:T(8,128)(2,1)} %collective-permute-done.18.far), custom_call_target="tpu_custom_call" | custom-call | tf_op jit(solution)/shard_map/pallas_call | solution.py:223
  76.4 3.1 %shard_map.86 = (f32[2048,128]{1,0:T(8,128)S(1)}, bf16[2048,128]{1,0:T(8,128)(2,1)S(1)}) custom-call(s32[1]{0:T(128)} %bitcast.side, f32[4,768]{1,0:T(4,128)S(1)} %maximum_add_fusion.1.middle, bf16[512,768]{1,0:T(8,128)(2,1)S(1)} %bitcast.25, bf16[256,768]{1,0:T(8,128)(2,1)S(1)} %bitcast.29, bf16[2,2048,512]{2,1,0:T(8,128)(2,1)S(1)} %shard_map.85.factors, ...), custom_call_target="tpu_custom_call" | custom-call | tf_op jit(solution)/shard_map/pallas_call | solution.py:245
  80.2 1.2 %collective-permute-done.19.got = bf16[2048,128]{1,0:T(8,128)(2,1)S(1)} collective-permute-done((bf16[2048,128]{1,0:T(8,128)(2,1)S(1)}, bf16[2048,128]{1,0:T(8,128)(2,1)S(1)}, u32[]{:S(2)}, u32[]{:S(2)}) %collective-permute-start.19) | collective-permute-done | bytes 524320 | tf_op jit(solution)/shard_map/ppermute | solution.py:156
  81.5 1.0 shard_map.87.mine
  82.7 1.8 %collective-permute-done.20.other = bf16[128,2048]{1,0:T(8,128)(2,1)S(1)} collective-permute-done((bf16[128,2048]{1,0:T(8,128)(2,1)S(1)}, bf16[128,2048]{1,0:T(8,128)(2,1)S(1)}, u32[]{:S(2)}, u32[]{:S(2)}) %collective-permute-start.20) | collective-permute-done | bytes 524320 | tf_op jit(solution)/shard_map/ppermute | solution.py:156
  84.5 2.1 %shard_map.88 = (f32[2,256,512]{2,1,0:T(8,128)S(1)}, f32[4,768]{1,0:T(4,128)S(1)}) custom-call(bf16[128,2048]{1,0:T(8,128)(2,1)S(1)} %shard_map.87.mine, bf16[128,2048]{1,0:T(8,128)(2,1)S(1)} %collective-permute-done.20.other, bf16[512,768]{1,0:T(8,128)(2,1)S(1)} %bitcast.26, bf16[256,768]{1,0:T(8,128)(2,1)S(1)} %bitcast.30, ...), custom_call_target="tpu_custom_call" | custom-call | tf_op jit(solution)/shard_map/pallas_call | solution.py:265
  86.7 1.6 %collective-permute-start.22 = (bf16[2,128,512]{2,1,0:T(8,128)(2,1)S(1)}, bf16[2,128,512]{2,1,0:T(8,128)(2,1)S(1)}, u32[]{:S(2)}, u32[]{:S(2)}) collective-permute-start(bf16[2,128,512]{2,1,0:T(8,128)(2,1)S(1)} %dynamic-slice_convert_fusion), channel_id=1, source_target_pairs={{0,1},{1,0},{2,3},{3,2},{4,5},{5,4},{6,7},{7,6},{8,9},{9,8},{10,11... | collective-permute-start | bytes 786440 | tf_op jit(solution)/shard_map/ppermute | solution.py:44
  88.2 6.9 %collective-permute-done.22 = bf16[2,128,512]{2,1,0:T(8,128)(2,1)S(1)} collective-permute-done((bf16[2,128,512]{2,1,0:T(8,128)(2,1)S(1)}, bf16[2,128,512]{2,1,0:T(8,128)(2,1)S(1)}, u32[]{:S(2)}, u32[]{:S(2)}) %collective-permute-start.22) | collective-permute-done | bytes 262176 | tf_op jit(solution)/shard_map/ppermute | solution.py:44
  96.1 2.4 %collective-permute-start.24 = (bf16[2,32,512]{2,1,0:T(8,128)(2,1)S(1)}, bf16[2,32,512]{2,1,0:T(8,128)(2,1)S(1)}, u32[]{:S(2)}, u32[]{:S(2)}) collective-permute-start(bf16[2,32,512]{2,1,0:T(8,128)(2,1)S(1)} %get-tuple-element.63), channel_id=1, source_target_pairs={{0,4},{1,5},{2,6},{3,7},{4,0},{5,1},{6,2},{7,3},{8,12},{9,13},{10,... | collective-permute-start | bytes 196616 | tf_op jit(solution)/shard_map/ppermute | solution.py:53
  98.4 1.2 collective-permute-start.25
  100.0 2.8 %collective-permute-done.24 = bf16[2,32,512]{2,1,0:T(8,128)(2,1)S(1)} collective-permute-done((bf16[2,32,512]{2,1,0:T(8,128)(2,1)S(1)}, bf16[2,32,512]{2,1,0:T(8,128)(2,1)S(1)}, u32[]{:S(2)}, u32[]{:S(2)}) %collective-permute-start.24) | collective-permute-done | bytes 65568 | tf_op jit(solution)/shard_map/ppermute | solution.py:53
  102.8 1.8 %collective-permute-done.25 = bf16[2,32,512]{2,1,0:T(8,128)(2,1)S(1)} collective-permute-done((bf16[2,32,512]{2,1,0:T(8,128)(2,1)S(1)}, bf16[2,32,512]{2,1,0:T(8,128)(2,1)S(1)}, u32[]{:S(2)}, u32[]{:S(2)}) %collective-permute-start.25) | collective-permute-done | bytes 65568 | tf_op jit(solution)/shard_map/ppermute | solution.py:53
  104.7 1.3 %collective-permute-start.26 = (bf16[2,32,512]{2,1,0:T(8,128)(2,1)S(1)}, bf16[2,32,512]{2,1,0:T(8,128)(2,1)S(1)}, u32[]{:S(2)}, u32[]{:S(2)}) collective-permute-start(bf16[2,32,512]{2,1,0:T(8,128)(2,1)S(1)} %add_convert_fusion), channel_id=1, source_target_pairs={{0,6},{1,7},{2,4},{3,5},{4,2},{5,3},{6,0},{7,1},{8,14},{9,15},{10,... | collective-permute-start | bytes 196616 | tf_op jit(solution)/shard_map/ppermute | solution.py:53
  105.9 3.2 %collective-permute-start.28 = (bf16[2,32,512]{2,1,0:T(8,128)(2,1)S(1)}, bf16[2,32,512]{2,1,0:T(8,128)(2,1)S(1)}, u32[]{:S(2)}, u32[]{:S(2)}) collective-permute-start(bf16[2,32,512]{2,1,0:T(8,128)(2,1)S(1)} %add_convert_fusion), channel_id=1, source_target_pairs={{0,2},{1,3},{2,0},{3,1},{4,6},{5,7},{6,4},{7,5},{8,10},{9,11},{10,... | collective-permute-start | bytes 196616 | tf_op jit(solution)/shard_map/ppermute | solution.py:53
  109.1 1.4 %collective-permute-start.21 = (f32[4,768]{1,0:T(4,128)S(1)}, f32[4,768]{1,0:T(4,128)S(1)}, u32[]{:S(2)}, u32[]{:S(2)}) collective-permute-start(f32[4,768]{1,0:T(4,128)S(1)} %get-tuple-element.43), channel_id=1, source_target_pairs={{0,16},{8,24},{16,0},{24,8},{1,17},{9,25},{17,1},{25,9},{2,18},{10... | collective-permute-start | bytes 36872 | tf_op jit(solution)/shard_map/ppermute | solution.py:156
  110.8 1.3 %collective-permute-done.27 = bf16[2,32,512]{2,1,0:T(8,128)(2,1)S(1)} collective-permute-done((bf16[2,32,512]{2,1,0:T(8,128)(2,1)S(1)}, bf16[2,32,512]{2,1,0:T(8,128)(2,1)S(1)}, u32[]{:S(2)}, u32[]{:S(2)}) %collective-permute-start.27) | collective-permute-done | bytes 65568 | tf_op jit(solution)/shard_map/ppermute | solution.py:53
  112.3 1.5 %collective-permute-start.29 = (bf16[2,128,512]{2,1,0:T(8,128)(2,1)S(1)}, bf16[2,128,512]{2,1,0:T(8,128)(2,1)S(1)}, u32[]{:S(2)}, u32[]{:S(2)}) collective-permute-start(bf16[2,128,512]{2,1,0:T(8,128)(2,1)S(1)} %pad_maximum_fusion.4.line), channel_id=1, source_target_pairs={{0,1},{1,0},{2,3},{3,2},{4,5},{5,4},{6,7},{7,6},{8,9},{9,8},{10,11... | collective-permute-start | bytes 786440 | tf_op jit(solution)/shard_map/ppermute | solution.py:53
  113.8 4.9 %collective-permute-done.29.other = bf16[2,128,512]{2,1,0:T(8,128)(2,1)S(1)} collective-permute-done((bf16[2,128,512]{2,1,0:T(8,128)(2,1)S(1)}, bf16[2,128,512]{2,1,0:T(8,128)(2,1)S(1)}, u32[]{:S(2)}, u32[]{:S(2)}) %collective-permute-start.29) | collective-permute-done | bytes 262176 | tf_op jit(solution)/shard_map/ppermute | solution.py:53
  118.7 2.1 %shard_map.89 = (f32[2048,128]{1,0:T(8,128)S(1)}, bf16[2048,128]{1,0:T(8,128)(2,1)S(1)}) custom-call(s32[1]{0:T(128)} %bitcast.side, f32[4,768]{1,0:T(4,128)S(1)} %maximum_add_fusion.2.middle, bf16[512,768]{1,0:T(8,128)(2,1)S(1)} %bitcast.27, bf16[256,768]{1,0:T(8,128)(2,1)S(1)} %bitcast.31, bf16[2,2048,512]{2,1,0:T(8,128)(2,1)S(1)} %shard_map.85.factors, ...), custom_call_target="tpu_custom_call" | custom-call | tf_op jit(solution)/shard_map/pallas_call | solution.py:245
  120.9 1.9 %collective-permute-done.30.got = bf16[2048,128]{1,0:T(8,128)(2,1)S(1)} collective-permute-done((bf16[2048,128]{1,0:T(8,128)(2,1)S(1)}, bf16[2048,128]{1,0:T(8,128)(2,1)S(1)}, u32[]{:S(2)}, u32[]{:S(2)}) %collective-permute-start.30) | collective-permute-done | bytes 524320 | tf_op jit(solution)/shard_map/ppermute | solution.py:156
  122.8 1.7 %shard_map.90 = bf16[2048,128]{1,0:T(8,128)(2,1)} custom-call(f32[4]{0:T(128)S(1)} %copy-done.8, f32[1]{0:T(128)S(6)} %copy.10.pivot, f32[2048,128]{1,0:T(8,128)S(1)} %get-tuple-element.45.mine, bf16[2048,128]{1,0:T(8,128)(2,1)S(1)} %collective-permute-done.30.got, bf16[2048,128]{1,0:T(8,128)(2,1)S(1)} %constant_dynamic-slice_fusion.3.coulomb, ...), custom_call_target="tpu_custom_call" | custom-call | tf_op jit(solution)/shard_map/pallas_call | solution.py:257
  (85 shorter events, 10.4 us)
Async XLA Ops:
  0.0 23.8 %copy-start = (bf16[2048,512]{1,0:T(8,128)(2,1)S(1)}, bf16[2048,512]{1,0:T(8,128)(2,1)}, u32[]{:S(2)}) copy-start(bf16[2048,512]{1,0:T(8,128)(2,1)} %param.9) | copy-start | bytes 6291460
  0.0 18.0 %copy-start.10 = (bf16[64,384]{1,0:T(8,128)(2,1)S(1)}, bf16[64,384]{1,0:T(8,128)(2,1)}, u32[]{:S(2)}) copy-start(bf16[64,384]{1,0:T(8,128)(2,1)} %param.11) | copy-start | bytes 147460
  0.0 18.0 %copy-start.9 = (bf16[64,384]{1,0:T(8,128)(2,1)S(1)}, bf16[64,384]{1,0:T(8,128)(2,1)}, u32[]{:S(2)}) copy-start(bf16[64,384]{1,0:T(8,128)(2,1)} %param.12) | copy-start | bytes 147460
  0.0 4.2 %collective-permute-start = (bf16[2048,128]{1,0:T(8,128)(2,1)}, bf16[2048,128]{1,0:T(8,128)(2,1)S(1)}, u32[]{:S(2)}, u32[]{:S(2)}) collective-permute-start(bf16[2048,128]{1,0:T(8,128)(2,1)} %mine.3), channel_id=1, source_target_pairs={{0,8},{8,0},{16,24},{24,16},{1,9},{9,1},{17,25},{25,17},{2,10},{10... | collective-permute-start | bytes 1572872 | tf_op jit(solution)/shard_map/ppermute | solution.py:156
  0.5 17.5 %collective-permute-start.1 = (bf16[2048,128]{1,0:T(8,128)(2,1)}, bf16[2048,128]{1,0:T(8,128)(2,1)S(1)}, u32[]{:S(2)}, u32[]{:S(2)}) collective-permute-start(bf16[2048,128]{1,0:T(8,128)(2,1)} %mine.3), channel_id=1, source_target_pairs={{0,16},{8,24},{16,0},{24,8},{1,17},{9,25},{17,1},{25,9},{2,18},{10... | collective-permute-start | bytes 1572872 | tf_op jit(solution)/shard_map/ppermute | solution.py:156
  4.0 14.0 %collective-permute-start.3 = (bf16[2,64,384]{2,1,0:T(8,128)(2,1)S(1)}, bf16[2,64,384]{2,1,0:T(8,128)(2,1)S(1)}, u32[]{:S(2)}, u32[]{:S(2)}) collective-permute-start(bf16[2,64,384]{2,1,0:T(8,128)(2,1)S(1)} %pad_maximum_fusion.6), channel_id=1, source_target_pairs={{0,16},{8,24},{16,0},{24,8},{1,17},{9,25},{17,1},{25,9},{2,18},{10... | collective-permute-start | bytes 294920 | tf_op jit(solution)/shard_map/ppermute | solution.py:156
  4.2 1.0 copy-start.1
  7.6 0.8 copy-start.3
  8.4 9.6 %collective-permute-start.2 = (bf16[1,128,512]{2,1,0:T(8,128)(2,1)S(1)}, bf16[1,128,512]{2,1,0:T(8,128)(2,1)S(1)}, u32[]{:S(2)}, u32[]{:S(2)}) collective-permute-start(bf16[1,128,512]{2,1,0:T(8,128)(2,1)S(1)} %fusion.1), channel_id=1, source_target_pairs={{0,1},{1,0},{2,3},{3,2},{4,5},{5,4},{6,7},{7,6},{8,9},{9,8},{10,11... | collective-permute-start | bytes 393224 | tf_op jit(solution)/shard_map/ppermute | solution.py:44
  18.0 0.7 copy-start.11
  18.0 3.2 %collective-permute-start.4 = (bf16[2048,128]{1,0:T(8,128)(2,1)S(1)}, bf16[2048,128]{1,0:T(8,128)(2,1)}, u32[]{:S(2)}, u32[]{:S(2)}) collective-permute-start(bf16[2048,128]{1,0:T(8,128)(2,1)S(1)} %collective-permute-done.1.mine), channel_id=1, source_target_pairs={{0,8},{8,0},{16,24},{24,16},{1,9},{9,1},{17,25},{25,17},{2,10},{10... | collective-permute-start | bytes 1572872 | tf_op jit(solution)/shard_map/ppermute | solution.py:156
  18.7 0.8 copy-start.5
  19.5 54.4 %collective-permute-start.18 = (bf16[2048,512]{1,0:T(8,128)(2,1)}, bf16[2048,512]{1,0:T(8,128)(2,1)}, u32[]{:S(2)}, u32[]{:S(2)}) collective-permute-start(bf16[2048,512]{1,0:T(8,128)(2,1)} %own.5), channel_id=1, source_target_pairs={{0,16},{8,24},{16,0},{24,8},{1,17},{9,25},{17,1},{25,9},{2,18},{10... | collective-permute-start | bytes 6291464 | tf_op jit(solution)/shard_map/ppermute | solution.py:156
  21.2 11.6 %collective-permute-start.5 = (bf16[2,64,768]{2,1,0:T(8,128)(2,1)S(1)}, bf16[2,64,768]{2,1,0:T(8,128)(2,1)S(1)}, u32[]{:S(2)}, u32[]{:S(2)}) collective-permute-start(bf16[2,64,768]{2,1,0:T(8,128)(2,1)S(1)} %pad_maximum_fusion.5), channel_id=1, source_target_pairs={{0,4},{1,5},{2,6},{3,7},{4,0},{5,1},{6,2},{7,3},{8,12},{9,13},{10,... | collective-permute-start | bytes 589832 | tf_op jit(solution)/shard_map/ppermute | solution.py:164
  23.9 1.0 copy-start.6
  24.9 9.6 %copy-start.4 = (f32[256,512]{1,0:T(8,128)S(1)}, f32[256,512]{1,0:T(8,128)}, u32[]{:S(2)}) copy-start(f32[256,512]{1,0:T(8,128)} %copy-done.3) | copy-start | bytes 1572868
  27.5 12.0 %copy-start.12 = (bf16[1,128,512]{2,1,0:T(8,128)(2,1)S(1)}, bf16[1,128,512]{2,1,0:T(8,128)(2,1)}, u32[]{:S(2)}) copy-start(bf16[1,128,512]{2,1,0:T(8,128)(2,1)} %copy-done.11) | copy-start | bytes 393220
  32.9 11.2 %copy-start.7 = (f32[512]{0:T(512)S(1)}, f32[512]{0:T(512)}, u32[]{:S(2)}) copy-start(f32[512]{0:T(512)} %param.14) | copy-start | bytes 6148
  33.0 6.5 %collective-permute-start.6 = (bf16[1,128,512]{2,1,0:T(8,128)(2,1)S(1)}, bf16[1,128,512]{2,1,0:T(8,128)(2,1)S(1)}, u32[]{:S(2)}, u32[]{:S(2)}) collective-permute-start(bf16[1,128,512]{2,1,0:T(8,128)(2,1)S(1)} %dynamic-slice_convert_fusion.1), channel_id=1, source_target_pairs={{0,1},{1,0},{2,3},{3,2},{4,5},{5,4},{6,7},{7,6},{8,9},{9,8},{10,11... | collective-permute-start | bytes 393224 | tf_op jit(solution)/shard_map/ppermute | solution.py:44
  34.5 15.3 %collective-permute-start.10 = (bf16[3,1,64,768]{3,2,0,1:T(8,128)(2,1)S(1)}, bf16[3,1,64,768]{3,2,0,1:T(8,128)(2,1)S(1)}, u32[]{:S(2)}, u32[]{:S(2)}) collective-permute-start(bf16[3,1,64,768]{3,2,0,1:T(8,128)(2,1)S(1)} %maximum_bitcast_fusion), channel_id=1, source_target_pairs={{0,1},{1,0},{2,3},{3,2},{4,5},{5,4},{6,7},{7,6},{8,9},{9,8},{10,11... | collective-permute-start | bytes 884744 | tf_op jit(solution)/shard_map/ppermute | solution.py:164
  39.6 4.5 %collective-permute-start.7 = (bf16[2,32,512]{2,1,0:T(8,128)(2,1)S(1)}, bf16[2,32,512]{2,1,0:T(8,128)(2,1)S(1)}, u32[]{:S(2)}, u32[]{:S(2)}) collective-permute-start(bf16[2,32,512]{2,1,0:T(8,128)(2,1)S(1)} %get-tuple-element.68), channel_id=1, source_target_pairs={{0,2},{1,3},{2,0},{3,1},{4,6},{5,7},{6,4},{7,5},{8,10},{9,11},{10,... | collective-permute-start | bytes 196616 | tf_op jit(solution)/shard_map/ppermute | solution.py:53
  40.3 7.0 %collective-permute-start.8 = (bf16[2,32,512]{2,1,0:T(8,128)(2,1)S(1)}, bf16[2,32,512]{2,1,0:T(8,128)(2,1)S(1)}, u32[]{:S(2)}, u32[]{:S(2)}) collective-permute-start(bf16[2,32,512]{2,1,0:T(8,128)(2,1)S(1)} %get-tuple-element.70), channel_id=1, source_target_pairs={{0,4},{1,5},{2,6},{3,7},{4,0},{5,1},{6,2},{7,3},{8,12},{9,13},{10,... | collective-permute-start | bytes 196616 | tf_op jit(solution)/shard_map/ppermute | solution.py:53
  43.6 6.2 %collective-permute-start.9 = (bf16[2,32,512]{2,1,0:T(8,128)(2,1)S(1)}, bf16[2,32,512]{2,1,0:T(8,128)(2,1)S(1)}, u32[]{:S(2)}, u32[]{:S(2)}) collective-permute-start(bf16[2,32,512]{2,1,0:T(8,128)(2,1)S(1)} %get-tuple-element.69), channel_id=1, source_target_pairs={{0,6},{1,7},{2,4},{3,5},{4,2},{5,3},{6,0},{7,1},{8,14},{9,15},{10,... | collective-permute-start | bytes 196616 | tf_op jit(solution)/shard_map/ppermute | solution.py:53
  50.8 6.8 %collective-permute-start.13 = (bf16[2,32,512]{2,1,0:T(8,128)(2,1)S(1)}, bf16[2,32,512]{2,1,0:T(8,128)(2,1)S(1)}, u32[]{:S(2)}, u32[]{:S(2)}) collective-permute-start(bf16[2,32,512]{2,1,0:T(8,128)(2,1)S(1)} %add_convert_fusion.1), channel_id=1, source_target_pairs={{0,6},{1,7},{2,4},{3,5},{4,2},{5,3},{6,0},{7,1},{8,14},{9,15},{10,... | collective-permute-start | bytes 196616 | tf_op jit(solution)/shard_map/ppermute | solution.py:53
  51.5 6.1 %collective-permute-start.14 = (bf16[2,32,512]{2,1,0:T(8,128)(2,1)S(1)}, bf16[2,32,512]{2,1,0:T(8,128)(2,1)S(1)}, u32[]{:S(2)}, u32[]{:S(2)}) collective-permute-start(bf16[2,32,512]{2,1,0:T(8,128)(2,1)S(1)} %add_convert_fusion.1), channel_id=1, source_target_pairs={{0,4},{1,5},{2,6},{3,7},{4,0},{5,1},{6,2},{7,3},{8,12},{9,13},{10,... | collective-permute-start | bytes 196616 | tf_op jit(solution)/shard_map/ppermute | solution.py:53
  51.5 7.4 %collective-permute-start.15 = (bf16[2,32,512]{2,1,0:T(8,128)(2,1)S(1)}, bf16[2,32,512]{2,1,0:T(8,128)(2,1)S(1)}, u32[]{:S(2)}, u32[]{:S(2)}) collective-permute-start(bf16[2,32,512]{2,1,0:T(8,128)(2,1)S(1)} %add_convert_fusion.1), channel_id=1, source_target_pairs={{0,2},{1,3},{2,0},{3,1},{4,6},{5,7},{6,4},{7,5},{8,10},{9,11},{10,... | collective-permute-start | bytes 196616 | tf_op jit(solution)/shard_map/ppermute | solution.py:53
  55.2 13.9 %collective-permute-start.11 = (bf16[3,1,2,64,768]{4,3,0,2,1:T(8,128)(2,1)}, bf16[3,1,2,64,768]{4,3,0,2,1:T(8,128)(2,1)}, u32[]{:S(2)}, u32[]{:S(2)}) collective-permute-start(bf16[3,1,2,64,768]{4,3,0,2,1:T(8,128)(2,1)} %pad_maximum_fusion), channel_id=1, source_target_pairs={{0,2},{1,3},{2,0},{3,1},{4,6},{5,7},{6,4},{7,5},{8,10},{9,11},{10,... | collective-permute-start | bytes 1769480 | tf_op jit(solution)/shard_map/ppermute | solution.py:164
  59.0 6.5 %collective-permute-start.16 = (bf16[2,128,512]{2,1,0:T(8,128)(2,1)S(1)}, bf16[2,128,512]{2,1,0:T(8,128)(2,1)}, u32[]{:S(2)}, u32[]{:S(2)}) collective-permute-start(bf16[2,128,512]{2,1,0:T(8,128)(2,1)S(1)} %pad_maximum_fusion.2.line), channel_id=1, source_target_pairs={{0,1},{1,0},{2,3},{3,2},{4,5},{5,4},{6,7},{7,6},{8,9},{9,8},{10,11... | collective-permute-start | bytes 786440 | tf_op jit(solution)/shard_map/ppermute | solution.py:53
  66.5 7.4 %collective-permute-start.17 = (bf16[2,128,512]{2,1,0:T(8,128)(2,1)S(1)}, bf16[2,128,512]{2,1,0:T(8,128)(2,1)S(1)}, u32[]{:S(2)}, u32[]{:S(2)}) collective-permute-start(bf16[2,128,512]{2,1,0:T(8,128)(2,1)S(1)} %pad_maximum_fusion.3), channel_id=1, source_target_pairs={{0,16},{8,24},{16,0},{24,8},{1,17},{9,25},{17,1},{25,9},{2,18},{10... | collective-permute-start | bytes 786440 | tf_op jit(solution)/shard_map/ppermute | solution.py:156
  70.5 1.0 copy-start.2
  72.6 3.8 %collective-permute-start.12 = (f32[4,768]{1,0:T(4,128)S(1)}, f32[4,768]{1,0:T(4,128)S(1)}, u32[]{:S(2)}, u32[]{:S(2)}) collective-permute-start(f32[4,768]{1,0:T(4,128)S(1)} %shard_map.84), channel_id=1, source_target_pairs={{0,16},{8,24},{16,0},{24,8},{1,17},{9,25},{17,1},{25,9},{2,18},{10... | collective-permute-start | bytes 36872 | tf_op jit(solution)/shard_map/ppermute | solution.py:156
  76.4 5.1 %copy-start.8 = (f32[4]{0:T(128)S(1)}, f32[4]{0:T(128)}, u32[]{:S(2)}) copy-start(f32[4]{0:T(128)} %occ.3) | copy-start | bytes 52
  79.5 2.0 %collective-permute-start.19 = (bf16[2048,128]{1,0:T(8,128)(2,1)S(1)}, bf16[2048,128]{1,0:T(8,128)(2,1)S(1)}, u32[]{:S(2)}, u32[]{:S(2)}) collective-permute-start(bf16[2048,128]{1,0:T(8,128)(2,1)S(1)} %get-tuple-element.39), channel_id=1, source_target_pairs={{0,8},{8,0},{16,24},{24,16},{1,9},{9,1},{17,25},{25,17},{2,10},{10... | collective-permute-start | bytes 1572872 | tf_op jit(solution)/shard_map/ppermute | solution.py:156
  82.5 2.0 %collective-permute-start.20 = (bf16[128,2048]{1,0:T(8,128)(2,1)S(1)}, bf16[128,2048]{1,0:T(8,128)(2,1)S(1)}, u32[]{:S(2)}, u32[]{:S(2)}) collective-permute-start(bf16[128,2048]{1,0:T(8,128)(2,1)S(1)} %shard_map.87.mine), channel_id=1, source_target_pairs={{0,8},{8,0},{16,24},{24,16},{1,9},{9,1},{17,25},{25,17},{2,10},{10... | collective-permute-start | bytes 1572872 | tf_op jit(solution)/shard_map/ppermute | solution.py:156
  86.7 8.4 %collective-permute-start.22 = (bf16[2,128,512]{2,1,0:T(8,128)(2,1)S(1)}, bf16[2,128,512]{2,1,0:T(8,128)(2,1)S(1)}, u32[]{:S(2)}, u32[]{:S(2)}) collective-permute-start(bf16[2,128,512]{2,1,0:T(8,128)(2,1)S(1)} %dynamic-slice_convert_fusion), channel_id=1, source_target_pairs={{0,1},{1,0},{2,3},{3,2},{4,5},{5,4},{6,7},{7,6},{8,9},{9,8},{10,11... | collective-permute-start | bytes 786440 | tf_op jit(solution)/shard_map/ppermute | solution.py:44
  95.2 4.8 %collective-permute-start.23 = (bf16[2,32,512]{2,1,0:T(8,128)(2,1)S(1)}, bf16[2,32,512]{2,1,0:T(8,128)(2,1)S(1)}, u32[]{:S(2)}, u32[]{:S(2)}) collective-permute-start(bf16[2,32,512]{2,1,0:T(8,128)(2,1)S(1)} %get-tuple-element.61), channel_id=1, source_target_pairs={{0,2},{1,3},{2,0},{3,1},{4,6},{5,7},{6,4},{7,5},{8,10},{9,11},{10,... | collective-permute-start | bytes 196616 | tf_op jit(solution)/shard_map/ppermute | solution.py:53
  96.1 6.7 %collective-permute-start.24 = (bf16[2,32,512]{2,1,0:T(8,128)(2,1)S(1)}, bf16[2,32,512]{2,1,0:T(8,128)(2,1)S(1)}, u32[]{:S(2)}, u32[]{:S(2)}) collective-permute-start(bf16[2,32,512]{2,1,0:T(8,128)(2,1)S(1)} %get-tuple-element.63), channel_id=1, source_target_pairs={{0,4},{1,5},{2,6},{3,7},{4,0},{5,1},{6,2},{7,3},{8,12},{9,13},{10,... | collective-permute-start | bytes 196616 | tf_op jit(solution)/shard_map/ppermute | solution.py:53
  98.4 6.2 %collective-permute-start.25 = (bf16[2,32,512]{2,1,0:T(8,128)(2,1)S(1)}, bf16[2,32,512]{2,1,0:T(8,128)(2,1)S(1)}, u32[]{:S(2)}, u32[]{:S(2)}) collective-permute-start(bf16[2,32,512]{2,1,0:T(8,128)(2,1)S(1)} %get-tuple-element.62), channel_id=1, source_target_pairs={{0,6},{1,7},{2,4},{3,5},{4,2},{5,3},{6,0},{7,1},{8,14},{9,15},{10,... | collective-permute-start | bytes 196616 | tf_op jit(solution)/shard_map/ppermute | solution.py:53
  104.7 6.2 %collective-permute-start.26 = (bf16[2,32,512]{2,1,0:T(8,128)(2,1)S(1)}, bf16[2,32,512]{2,1,0:T(8,128)(2,1)S(1)}, u32[]{:S(2)}, u32[]{:S(2)}) collective-permute-start(bf16[2,32,512]{2,1,0:T(8,128)(2,1)S(1)} %add_convert_fusion), channel_id=1, source_target_pairs={{0,6},{1,7},{2,4},{3,5},{4,2},{5,3},{6,0},{7,1},{8,14},{9,15},{10,... | collective-permute-start | bytes 196616 | tf_op jit(solution)/shard_map/ppermute | solution.py:53
  105.9 6.2 %collective-permute-start.27 = (bf16[2,32,512]{2,1,0:T(8,128)(2,1)S(1)}, bf16[2,32,512]{2,1,0:T(8,128)(2,1)S(1)}, u32[]{:S(2)}, u32[]{:S(2)}) collective-permute-start(bf16[2,32,512]{2,1,0:T(8,128)(2,1)S(1)} %add_convert_fusion), channel_id=1, source_target_pairs={{0,4},{1,5},{2,6},{3,7},{4,0},{5,1},{6,2},{7,3},{8,12},{9,13},{10,... | collective-permute-start | bytes 196616 | tf_op jit(solution)/shard_map/ppermute | solution.py:53
  105.9 6.2 %collective-permute-start.28 = (bf16[2,32,512]{2,1,0:T(8,128)(2,1)S(1)}, bf16[2,32,512]{2,1,0:T(8,128)(2,1)S(1)}, u32[]{:S(2)}, u32[]{:S(2)}) collective-permute-start(bf16[2,32,512]{2,1,0:T(8,128)(2,1)S(1)} %add_convert_fusion), channel_id=1, source_target_pairs={{0,2},{1,3},{2,0},{3,1},{4,6},{5,7},{6,4},{7,5},{8,10},{9,11},{10,... | collective-permute-start | bytes 196616 | tf_op jit(solution)/shard_map/ppermute | solution.py:53
  109.1 4.7 %collective-permute-start.21 = (f32[4,768]{1,0:T(4,128)S(1)}, f32[4,768]{1,0:T(4,128)S(1)}, u32[]{:S(2)}, u32[]{:S(2)}) collective-permute-start(f32[4,768]{1,0:T(4,128)S(1)} %get-tuple-element.43), channel_id=1, source_target_pairs={{0,16},{8,24},{16,0},{24,8},{1,17},{9,25},{17,1},{25,9},{2,18},{10... | collective-permute-start | bytes 36872 | tf_op jit(solution)/shard_map/ppermute | solution.py:156
  112.3 6.4 %collective-permute-start.29 = (bf16[2,128,512]{2,1,0:T(8,128)(2,1)S(1)}, bf16[2,128,512]{2,1,0:T(8,128)(2,1)S(1)}, u32[]{:S(2)}, u32[]{:S(2)}) collective-permute-start(bf16[2,128,512]{2,1,0:T(8,128)(2,1)S(1)} %pad_maximum_fusion.4.line), channel_id=1, source_target_pairs={{0,1},{1,0},{2,3},{3,2},{4,5},{5,4},{6,7},{7,6},{8,9},{9,8},{10,11... | collective-permute-start | bytes 786440 | tf_op jit(solution)/shard_map/ppermute | solution.py:53
  120.8 2.0 %collective-permute-start.30 = (bf16[2048,128]{1,0:T(8,128)(2,1)S(1)}, bf16[2048,128]{1,0:T(8,128)(2,1)S(1)}, u32[]{:S(2)}, u32[]{:S(2)}) collective-permute-start(bf16[2048,128]{1,0:T(8,128)(2,1)S(1)} %get-tuple-element.46), channel_id=1, source_target_pairs={{0,8},{8,0},{16,24},{24,16},{1,9},{9,1},{17,25},{25,17},{2,10},{10... | collective-permute-start | bytes 1572872 | tf_op jit(solution)/shard_map/ppermute | solution.py:156

commit v5 on v4

--- a/solution.py
+++ b/solution.py
@@ -77,14 +77,12 @@
         copy.wait()
 
 
-def residual_kernel(swapped, side, middle, left, right, factors, line, other, *refs):
-    mine, theirs, gram = refs[-3:]
-    nvirt, half, width = left.shape[0], line.shape[1], mine.shape[1]
-    near = (line, other)
+def residual_kernel(swapped, side, middle, left, right, factors, one, two, mine, theirs, gram):
+    nvirt, half, width = left.shape[0], one.shape[1], mine.shape[1]
     for j in range(2):
         rows = pl.ds(pl.multiple_of((side[0] if j == 0 else 1 - side[0]) * half, half), half)
-        gram[0, rows] = near[j][0]
-        gram[1, rows] = refs[0][j] if swapped else near[j][1]
+        for r in range(2):
+            gram[r, rows] = (one, two)[r][j] if swapped else (one, two)[j][r]
     size = min(nvirt, 256)
     for start in range(0, mine.shape[0], size):
         i, at = start // nvirt, start % nvirt
@@ -111,8 +109,13 @@
             out[:, rows] = new.T.astype(BF)
 
 
-def middle_kernel(mine, other, left, right, middle):
+def middle_kernel(mine, other, places, one, two, left, right, middle):
     width, nvirt = mine.shape[1], left.shape[0]
+    part = one.shape[1]
+    for a, at, column in ((one, places[0], places[1]), (two, 1 - places[0], 1 - places[1])):
+        for top in range(2):
+            left[pl.ds(pl.multiple_of(top * 2 * part + at * part, part), part)] = a[top]
+        right[pl.ds(pl.multiple_of(column * part, part), part)] = a[2]
     for i in range(middle.shape[0]):
         total = None
         for at, amps in ((0, mine), (width, other)):
@@ -137,6 +140,10 @@
     width = mine.shape[1]
     gram[:width] = dot(mine[...], own[...], 0, 0)
     gram[width:] = dot(other[...], own[...], 0, 0)
+
+
+def scheduled(micros):
+    return pl.CostEstimate(flops=int(micros * 1e9), bytes_accessed=int(micros * 3e6), transcendentals=0)
 
 
 def per_device(
@@ -186,7 +193,7 @@
 
     one, two = other_rows(fac, 0)
     kept = jnp.where(k // 2 == 0, one[1], two[1])
-    fac = jnp.stack([one[0], two[0], kept])[:, None]
+    fac = jnp.stack([one[0], two[0], kept])
     far_gram, fac = tie(far_gram, fac)
     far_mine, far_got = fold(far_gram, n_pair)
 
@@ -200,24 +207,27 @@
     def beside(stage, a):
         nonlocal fac, far, vir, vir_row, coulomb_block, left, right, middle, factors
         if stage == 1:
-            fac = jnp.stack(other_rows(fac, n_bits - 1), axis=2).reshape(3, 1, -1, *fac.shape[2:])
+            fac = jnp.concatenate(other_rows(fac, n_bits - 1), axis=1)
             a, fac = tie(a, fac)
         if stage == 1:
             a, vir, vir_row, coulomb_block = tie(a, vir, vir_row, coulomb_block)
         if stage == 4:
-            for axis in range(n_bits - 2, 0, -1):
-                fac = jnp.stack(other_rows(fac, axis), axis=1)
-                fac = fac.reshape(3, -1, *fac.shape[3:])
-            left = fac[:2].reshape(nvirt, cols)
-            right = fac[2].reshape(2, width, cols)
-            right = jnp.where(k % 2 == 0, right, right[::-1]).reshape(2 * width, cols)
-            middle = pl.pallas_call(
+            for axis in range(n_bits - 2, 1, -1):
+                fac = jnp.concatenate(other_rows(fac, axis), axis=1)
+            got = lax.ppermute(fac, "pair", xor(n_pair, n_pair // 4))
+            bit = (me >> (n_bits - 2)) % 2
+            left, right, middle = pl.pallas_call(
                 middle_kernel,
-                out_shape=jax.ShapeDtypeStruct((nocc, cols), F32),
-                in_specs=[VMEM] * 4,
-                out_specs=VMEM,
+                out_shape=(
+                    jax.ShapeDtypeStruct((nvirt, cols), BF),
+                    jax.ShapeDtypeStruct((2 * width, cols), BF),
+                    jax.ShapeDtypeStruct((nocc, cols), F32),
+                ),
+                in_specs=[VMEM] * 2 + [SMEM] + [VMEM] * 2,
+                out_specs=(VMEM,) * 3,
+                cost_estimate=scheduled(6),
                 compiler_params=PARAMS,
-            )(*near, left, right)
+            )(*near, jnp.stack([bit, bit ^ (k % 2)]), fac, got)
         if stage == 4:
             a, far = tie(a, far)
             factors = pl.pallas_call(
@@ -236,8 +246,7 @@
         n_pair,
         beside,
     )
-    swapped = beside(4, over(jnp.stack([line[1], other[1]]), 2))
-    gram = (line, other, swapped)
+    gram = (jnp.stack([line[0], other[0]]), beside(4, over(jnp.stack([line[1], other[1]]), 2)))
     for step in range(ITERS):
         last = step == ITERS - 1
         other = over(middle, 2)

time: 125 us -> 123 us (0.984)
  local copies, waits for them, and re-layouts: 6.41 us -> 3.28 us
  waiting for transfers between devices: 56.5 us -> 58.3 us
  other arithmetic: 3.79 us -> 2.44 us
    another operation x6 -> x4, other arithmetic: 2.38 us -> 0.16 us  [the longest x1 0.07 us: beside(): jnp.stack([bit, bit ^ k % 2])]
    unnamed x26 -> x22, local copies, waits for them, and re-layouts: 5.11 us -> 2.91 us
    ppermute x0 -> x1, waiting for transfers between devices: none -> 1.82 us  [beside(): got = lax.ppermute(fac, 'pair', xor(n_pair, n_pair // 4))]
    ppermute x3 -> x2, waiting for transfers between devices: 6.7 us -> 5.8 us  [other_rows(): got = lax.ppermute(fac, 'pair', xor(n_pair, bit))]
    ppermute x3 -> x2, starting transfers between devices: 3.22 us -> 3.37 us  [other_rows(): got = lax.ppermute(fac, 'pair', xor(n_pair, bit))]
  transfers between devices with their start and end apart: 31 -> 31, of which waited for: 20 -> 20; matrix products, arithmetic and copies ran while one was open for 4% -> 2% of each run, Pallas kernels for 7% -> 7%
where the time goes in v5:
time: 123 us
  waiting for transfers between devices  58.3 us (47%)
  starting transfers between devices  39.7 us (32%)
  Pallas kernels  17.9 us (15%)
  local copies, waits for them, and re-layouts  3.28 us (3%)
  other arithmetic  2.44 us (2%)
    ppermute x14, waiting for transfers between devices, send(): return lax.ppermute(a, 'pair', xor(n, s))  26 us
    ppermute x14, starting transfers between devices, send(): return lax.ppermute(a, 'pair', xor(n, s))  20.9 us
    ppermute x11, waiting for transfers between devices, over(): return lax.ppermute(a, 'aux', xor(n_aux, s))  13.5 us
    ppermute x3, waiting for transfers between devices, fold(): return (mine, lax.ppermute(theirs.astype(BF), 'pair', xor(n, 1)))  11.1 us
    ppermute x11, starting transfers between devices, over(): return lax.ppermute(a, 'aux', xor(n_aux, s))  10.3 us
    ppermute x2, waiting for transfers between devices, other_rows(): got = lax.ppermute(fac, 'pair', xor(n_pair, bit))  5.8 us
    ppermute x3, starting transfers between devices, fold(): return (mine, lax.ppermute(theirs.astype(BF), 'pair', xor(n, 1)))  5.1 us
    pallas_call x2, Pallas kernels, first_gram(): pl.pallas_call(first_gram_kernel, out_shape=jax.ShapeDtypeStruct((2 * wid...  5.01 us
  transfers between devices with their start and end apart: 31, of which 20 were waited for; matrix products, arithmetic and copies ran while one was open for 2% of the time, Pallas kernels for 7%

profile of v5, /device:TPU:0, one launch (start us, length us, event | category | flops | bytes accessed | tf_op | source)
XLA Modules:
  0.0 122.6 jit_solution(10190257144686583278)
XLA Ops:
  0.5 2.6 %collective-permute-start.1 = (bf16[2048,128]{1,0:T(8,128)(2,1)}, bf16[2048,128]{1,0:T(8,128)(2,1)}, u32[]{:S(2)}, u32[]{:S(2)}) collective-permute-start(bf16[2048,128]{1,0:T(8,128)(2,1)} %mine.3), channel_id=1, source_target_pairs={{0,16},{8,24},{16,0},{24,8},{1,17},{9,25},{17,1},{25,9},{2,18},{10... | collective-permute-start | bytes 1572872 | tf_op jit(solution)/shard_map/ppermute | solution.py:163
  3.1 0.8 pad_maximum_fusion.7
  4.2 1.0 copy-done.1
  5.2 2.5 %shard_map.82 = f32[256,512]{1,0:T(8,128)S(1)} custom-call(bf16[2048,128]{1,0:T(8,128)(2,1)S(1)} %copy-done.1, bf16[2048,128]{1,0:T(8,128)(2,1)S(1)} %collective-permute-done.other, bf16[2048,512]{1,0:T(8,128)(2,1)} %own.5), custom_call_target="tpu_custom_call" | custom-call | tf_op jit(solution)/shard_map/pallas_call | solution.py:181
  7.8 1.9 %collective-permute-start.2 = (bf16[1,128,512]{2,1,0:T(8,128)(2,1)S(1)}, bf16[1,128,512]{2,1,0:T(8,128)(2,1)}, u32[]{:S(2)}, u32[]{:S(2)}) collective-permute-start(bf16[1,128,512]{2,1,0:T(8,128)(2,1)S(1)} %fusion), channel_id=1, source_target_pairs={{0,1},{1,0},{2,3},{3,2},{4,5},{5,4},{6,7},{7,6},{8,9},{9,8},{10,11... | collective-permute-start | bytes 393224 | tf_op jit(solution)/shard_map/ppermute | solution.py:44
  9.7 8.3 %collective-permute-done.3 = bf16[2,64,384]{2,1,0:T(8,128)(2,1)S(1)} collective-permute-done((bf16[2,64,384]{2,1,0:T(8,128)(2,1)S(1)}, bf16[2,64,384]{2,1,0:T(8,128)(2,1)S(1)}, u32[]{:S(2)}, u32[]{:S(2)}) %collective-permute-start.3) | collective-permute-done | bytes 98336 | tf_op jit(solution)/shard_map/ppermute | solution.py:163
  18.1 1.8 %collective-permute-start.18 = (bf16[2048,512]{1,0:T(8,128)(2,1)}, bf16[2048,512]{1,0:T(8,128)(2,1)}, u32[]{:S(2)}, u32[]{:S(2)}) collective-permute-start(bf16[2048,512]{1,0:T(8,128)(2,1)} %own.5), channel_id=1, source_target_pairs={{0,16},{8,24},{16,0},{24,8},{1,17},{9,25},{17,1},{25,9},{2,18},{10... | collective-permute-start | bytes 6291464 | tf_op jit(solution)/shard_map/ppermute | solution.py:163
  21.0 2.8 %collective-permute-start.5 = (bf16[2,64,768]{2,1,0:T(8,128)(2,1)S(1)}, bf16[2,64,768]{2,1,0:T(8,128)(2,1)S(1)}, u32[]{:S(2)}, u32[]{:S(2)}) collective-permute-start(bf16[2,64,768]{2,1,0:T(8,128)(2,1)S(1)} %pad_maximum_fusion.6), channel_id=1, source_target_pairs={{0,4},{1,5},{2,6},{3,7},{4,0},{5,1},{6,2},{7,3},{8,12},{9,13},{10,... | collective-permute-start | bytes 589832 | tf_op jit(solution)/shard_map/ppermute | solution.py:171
  23.9 1.0 copy-done.6
  24.9 2.5 %shard_map.83 = f32[256,512]{1,0:T(8,128)S(1)} custom-call(bf16[2048,128]{1,0:T(8,128)(2,1)} %collective-permute-done.1.mine, bf16[2048,128]{1,0:T(8,128)(2,1)S(1)} %copy-done.6, bf16[2048,512]{1,0:T(8,128)(2,1)} %own.5), custom_call_target="tpu_custom_call" | custom-call | tf_op jit(solution)/shard_map/pallas_call | solution.py:181
  27.4 5.8 %collective-permute-done.5 = bf16[2,64,768]{2,1,0:T(8,128)(2,1)S(1)} collective-permute-done((bf16[2,64,768]{2,1,0:T(8,128)(2,1)S(1)}, bf16[2,64,768]{2,1,0:T(8,128)(2,1)S(1)}, u32[]{:S(2)}, u32[]{:S(2)}) %collective-permute-start.5) | collective-permute-done | bytes 196640 | tf_op jit(solution)/shard_map/ppermute | solution.py:171
  33.4 1.6 %collective-permute-start.6 = (bf16[1,128,512]{2,1,0:T(8,128)(2,1)S(1)}, bf16[1,128,512]{2,1,0:T(8,128)(2,1)S(1)}, u32[]{:S(2)}, u32[]{:S(2)}) collective-permute-start(bf16[1,128,512]{2,1,0:T(8,128)(2,1)S(1)} %dynamic-slice_convert_fusion.1), channel_id=1, source_target_pairs={{0,1},{1,0},{2,3},{3,2},{4,5},{5,4},{6,7},{7,6},{8,9},{9,8},{10,11... | collective-permute-start | bytes 393224 | tf_op jit(solution)/shard_map/ppermute | solution.py:44
  35.6 4.3 %collective-permute-done.6 = bf16[1,128,512]{2,1,0:T(8,128)(2,1)S(1)} collective-permute-done((bf16[1,128,512]{2,1,0:T(8,128)(2,1)S(1)}, bf16[1,128,512]{2,1,0:T(8,128)(2,1)S(1)}, u32[]{:S(2)}, u32[]{:S(2)}) %collective-permute-start.6) | collective-permute-done | bytes 131104 | tf_op jit(solution)/shard_map/ppermute | solution.py:44
  39.9 1.0 fusion.2
  41.7 3.4 %collective-permute-start.8 = (bf16[2,32,512]{2,1,0:T(8,128)(2,1)S(1)}, bf16[2,32,512]{2,1,0:T(8,128)(2,1)S(1)}, u32[]{:S(2)}, u32[]{:S(2)}) collective-permute-start(bf16[2,32,512]{2,1,0:T(8,128)(2,1)S(1)} %get-tuple-element.78), channel_id=1, source_target_pairs={{0,4},{1,5},{2,6},{3,7},{4,0},{5,1},{6,2},{7,3},{8,12},{9,13},{10,... | collective-permute-start | bytes 196616 | tf_op jit(solution)/shard_map/ppermute | solution.py:53
  45.5 3.2 %collective-permute-done.8 = bf16[2,32,512]{2,1,0:T(8,128)(2,1)S(1)} collective-permute-done((bf16[2,32,512]{2,1,0:T(8,128)(2,1)S(1)}, bf16[2,32,512]{2,1,0:T(8,128)(2,1)S(1)}, u32[]{:S(2)}, u32[]{:S(2)}) %collective-permute-start.8) | collective-permute-done | bytes 65568 | tf_op jit(solution)/shard_map/ppermute | solution.py:53
  48.7 2.4 %collective-permute-done.9 = bf16[2,32,512]{2,1,0:T(8,128)(2,1)S(1)} collective-permute-done((bf16[2,32,512]{2,1,0:T(8,128)(2,1)S(1)}, bf16[2,32,512]{2,1,0:T(8,128)(2,1)S(1)}, u32[]{:S(2)}, u32[]{:S(2)}) %collective-permute-start.9) | collective-permute-done | bytes 65568 | tf_op jit(solution)/shard_map/ppermute | solution.py:53
  51.2 0.9 collective-permute-start.13
  52.1 3.6 %collective-permute-start.15 = (bf16[2,32,512]{2,1,0:T(8,128)(2,1)S(1)}, bf16[2,32,512]{2,1,0:T(8,128)(2,1)S(1)}, u32[]{:S(2)}, u32[]{:S(2)}) collective-permute-start(bf16[2,32,512]{2,1,0:T(8,128)(2,1)S(1)} %add_convert_fusion.1), channel_id=1, source_target_pairs={{0,2},{1,3},{2,0},{3,1},{4,6},{5,7},{6,4},{7,5},{8,10},{9,11},{10,... | collective-permute-start | bytes 196616 | tf_op jit(solution)/shard_map/ppermute | solution.py:53
  55.7 2.4 %collective-permute-done.13 = bf16[2,32,512]{2,1,0:T(8,128)(2,1)S(1)} collective-permute-done((bf16[2,32,512]{2,1,0:T(8,128)(2,1)S(1)}, bf16[2,32,512]{2,1,0:T(8,128)(2,1)S(1)}, u32[]{:S(2)}, u32[]{:S(2)}) %collective-permute-start.13) | collective-permute-done | bytes 65568 | tf_op jit(solution)/shard_map/ppermute | solution.py:53
  58.1 1.4 %collective-permute-done.15 = bf16[2,32,512]{2,1,0:T(8,128)(2,1)S(1)} collective-permute-done((bf16[2,32,512]{2,1,0:T(8,128)(2,1)S(1)}, bf16[2,32,512]{2,1,0:T(8,128)(2,1)S(1)}, u32[]{:S(2)}, u32[]{:S(2)}) %collective-permute-start.15) | collective-permute-done | bytes 65568 | tf_op jit(solution)/shard_map/ppermute | solution.py:53
  59.6 1.6 %collective-permute-start.16 = (bf16[2,128,512]{2,1,0:T(8,128)(2,1)S(1)}, bf16[2,128,512]{2,1,0:T(8,128)(2,1)S(1)}, u32[]{:S(2)}, u32[]{:S(2)}) collective-permute-start(bf16[2,128,512]{2,1,0:T(8,128)(2,1)S(1)} %pad_maximum_fusion.2), channel_id=1, source_target_pairs={{0,1},{1,0},{2,3},{3,2},{4,5},{5,4},{6,7},{7,6},{8,9},{9,8},{10,11... | collective-permute-start | bytes 786440 | tf_op jit(solution)/shard_map/ppermute | solution.py:53
  61.3 4.8 %collective-permute-done.16 = bf16[2,128,512]{2,1,0:T(8,128)(2,1)S(1)} collective-permute-done((bf16[2,128,512]{2,1,0:T(8,128)(2,1)S(1)}, bf16[2,128,512]{2,1,0:T(8,128)(2,1)S(1)}, u32[]{:S(2)}, u32[]{:S(2)}) %collective-permute-start.16) | collective-permute-done | bytes 262176 | tf_op jit(solution)/shard_map/ppermute | solution.py:53
  66.1 1.6 %collective-permute-start.17 = (bf16[2,128,512]{2,1,0:T(8,128)(2,1)S(1)}, bf16[2,128,512]{2,1,0:T(8,128)(2,1)S(1)}, u32[]{:S(2)}, u32[]{:S(2)}) collective-permute-start(bf16[2,128,512]{2,1,0:T(8,128)(2,1)S(1)} %pad_maximum_fusion.3), channel_id=1, source_target_pairs={{0,16},{8,24},{16,0},{24,8},{1,17},{9,25},{17,1},{25,9},{2,18},{10... | collective-permute-start | bytes 786440 | tf_op jit(solution)/shard_map/ppermute | solution.py:163
  67.7 1.8 %collective-permute-done.11.two = bf16[3,128,768]{2,1,0:T(8,128)(2,1)S(1)} collective-permute-done((bf16[3,128,768]{2,1,0:T(8,128)(2,1)S(1)}, bf16[3,128,768]{2,1,0:T(8,128)(2,1)S(1)}, u32[]{:S(2)}, u32[]{:S(2)}) %collective-permute-start.11) | collective-permute-done | bytes 589856 | tf_op jit(solution)/shard_map/ppermute | solution.py:217
  69.5 1.6 %shard_map.84 = (bf16[512,768]{1,0:T(8,128)(2,1)S(1)}, bf16[256,768]{1,0:T(8,128)(2,1)S(1)}, f32[4,768]{1,0:T(4,128)S(1)}) custom-call(bf16[2048,128]{1,0:T(8,128)(2,1)S(1)} %copy-done.2, bf16[2048,128]{1,0:T(8,128)(2,1)S(1)} %copy-done.4, s32[2]{0:T(128)S(1)} %pad_add_fusion.places, bf16[3,128,768]{2,1,0:T(8,128)(2,1)S(1)} %pad_maximum_fusion.one, ...), custom_call_target="tpu_custom_call" | custom-call | flops 6000000000 | bytes 18000000 | tf_op jit(solution)/shard_map/pallas_call | solution.py:219
  71.2 1.6 %collective-permute-start.12 = (f32[4,768]{1,0:T(4,128)S(1)}, f32[4,768]{1,0:T(4,128)S(1)}, u32[]{:S(2)}, u32[]{:S(2)}) collective-permute-start(f32[4,768]{1,0:T(4,128)S(1)} %get-tuple-element.37), channel_id=1, source_target_pairs={{0,16},{8,24},{16,0},{24,8},{1,17},{9,25},{17,1},{25,9},{2,18},{10... | collective-permute-start | bytes 36872 | tf_op jit(solution)/shard_map/ppermute | solution.py:163
  72.8 2.2 %shard_map.85.factors = bf16[2,2048,512]{2,1,0:T(8,128)(2,1)S(1)} custom-call(bf16[2048,512]{1,0:T(8,128)(2,1)} %own.5, bf16[2048,512]{1,0:T(8,128)(2,1)} %collective-permute-done.18.far), custom_call_target="tpu_custom_call" | custom-call | tf_op jit(solution)/shard_map/pallas_call | solution.py:233
  75.1 2.1 %shard_map.86 = (f32[2048,128]{1,0:T(8,128)S(1)}, bf16[2048,128]{1,0:T(8,128)(2,1)S(1)}) custom-call(s32[1]{0:T(128)} %bitcast.side, f32[4,768]{1,0:T(4,128)S(1)} %maximum_add_fusion.1.middle, bf16[512,768]{1,0:T(8,128)(2,1)S(1)} %get-tuple-element.38.left, bf16[256,768]{1,0:T(8,128)(2,1)S(1)} %get-tuple-element.39.right, ...), custom_call_target="tpu_custom_call" | custom-call | tf_op jit(solution)/shard_map/pallas_call | solution.py:254
  78.0 1.2 %collective-permute-done.19.got = bf16[2048,128]{1,0:T(8,128)(2,1)S(1)} collective-permute-done((bf16[2048,128]{1,0:T(8,128)(2,1)S(1)}, bf16[2048,128]{1,0:T(8,128)(2,1)S(1)}, u32[]{:S(2)}, u32[]{:S(2)}) %collective-permute-start.19) | collective-permute-done | bytes 524320 | tf_op jit(solution)/shard_map/ppermute | solution.py:163
  79.2 1.0 shard_map.87.mine
  80.4 1.8 %collective-permute-done.20.other = bf16[128,2048]{1,0:T(8,128)(2,1)S(1)} collective-permute-done((bf16[128,2048]{1,0:T(8,128)(2,1)S(1)}, bf16[128,2048]{1,0:T(8,128)(2,1)S(1)}, u32[]{:S(2)}, u32[]{:S(2)}) %collective-permute-start.20) | collective-permute-done | bytes 524320 | tf_op jit(solution)/shard_map/ppermute | solution.py:163
  82.2 2.1 %shard_map.88 = (f32[2,256,512]{2,1,0:T(8,128)S(1)}, f32[4,768]{1,0:T(4,128)S(1)}) custom-call(bf16[128,2048]{1,0:T(8,128)(2,1)S(1)} %shard_map.87.mine, bf16[128,2048]{1,0:T(8,128)(2,1)S(1)} %collective-permute-done.20.other, bf16[512,768]{1,0:T(8,128)(2,1)S(1)} %get-tuple-element.38.left, bf16[256,768]{1,0:T(8,128)(2,1)S(1)} %get-tuple-element.39.right, ...), custom_call_target="tpu_custom_call" | custom-call | tf_op jit(solution)/shard_map/pallas_call | solution.py:274
  84.3 1.6 %collective-permute-start.22 = (bf16[2,128,512]{2,1,0:T(8,128)(2,1)S(1)}, bf16[2,128,512]{2,1,0:T(8,128)(2,1)S(1)}, u32[]{:S(2)}, u32[]{:S(2)}) collective-permute-start(bf16[2,128,512]{2,1,0:T(8,128)(2,1)S(1)} %dynamic-slice_convert_fusion), channel_id=1, source_target_pairs={{0,1},{1,0},{2,3},{3,2},{4,5},{5,4},{6,7},{7,6},{8,9},{9,8},{10,11... | collective-permute-start | bytes 786440 | tf_op jit(solution)/shard_map/ppermute | solution.py:44
  85.9 6.8 %collective-permute-done.22 = bf16[2,128,512]{2,1,0:T(8,128)(2,1)S(1)} collective-permute-done((bf16[2,128,512]{2,1,0:T(8,128)(2,1)S(1)}, bf16[2,128,512]{2,1,0:T(8,128)(2,1)S(1)}, u32[]{:S(2)}, u32[]{:S(2)}) %collective-permute-start.22) | collective-permute-done | bytes 262176 | tf_op jit(solution)/shard_map/ppermute | solution.py:44
  92.9 1.2 collective-permute-start.23
  94.1 2.6 %collective-permute-start.24 = (bf16[2,32,512]{2,1,0:T(8,128)(2,1)S(1)}, bf16[2,32,512]{2,1,0:T(8,128)(2,1)S(1)}, u32[]{:S(2)}, u32[]{:S(2)}) collective-permute-start(bf16[2,32,512]{2,1,0:T(8,128)(2,1)S(1)} %get-tuple-element.67), channel_id=1, source_target_pairs={{0,4},{1,5},{2,6},{3,7},{4,0},{5,1},{6,2},{7,3},{8,12},{9,13},{10,... | collective-permute-start | bytes 196616 | tf_op jit(solution)/shard_map/ppermute | solution.py:53
  97.9 2.9 %collective-permute-done.24 = bf16[2,32,512]{2,1,0:T(8,128)(2,1)S(1)} collective-permute-done((bf16[2,32,512]{2,1,0:T(8,128)(2,1)S(1)}, bf16[2,32,512]{2,1,0:T(8,128)(2,1)S(1)}, u32[]{:S(2)}, u32[]{:S(2)}) %collective-permute-start.24) | collective-permute-done | bytes 65568 | tf_op jit(solution)/shard_map/ppermute | solution.py:53
  100.8 1.9 %collective-permute-done.25 = bf16[2,32,512]{2,1,0:T(8,128)(2,1)S(1)} collective-permute-done((bf16[2,32,512]{2,1,0:T(8,128)(2,1)S(1)}, bf16[2,32,512]{2,1,0:T(8,128)(2,1)S(1)}, u32[]{:S(2)}, u32[]{:S(2)}) %collective-permute-start.25) | collective-permute-done | bytes 65568 | tf_op jit(solution)/shard_map/ppermute | solution.py:53
  102.8 1.3 %collective-permute-start.26 = (bf16[2,32,512]{2,1,0:T(8,128)(2,1)S(1)}, bf16[2,32,512]{2,1,0:T(8,128)(2,1)S(1)}, u32[]{:S(2)}, u32[]{:S(2)}) collective-permute-start(bf16[2,32,512]{2,1,0:T(8,128)(2,1)S(1)} %add_convert_fusion), channel_id=1, source_target_pairs={{0,6},{1,7},{2,4},{3,5},{4,2},{5,3},{6,0},{7,1},{8,14},{9,15},{10,... | collective-permute-start | bytes 196616 | tf_op jit(solution)/shard_map/ppermute | solution.py:53
  104.1 3.1 %collective-permute-start.28 = (bf16[2,32,512]{2,1,0:T(8,128)(2,1)S(1)}, bf16[2,32,512]{2,1,0:T(8,128)(2,1)S(1)}, u32[]{:S(2)}, u32[]{:S(2)}) collective-permute-start(bf16[2,32,512]{2,1,0:T(8,128)(2,1)S(1)} %add_convert_fusion), channel_id=1, source_target_pairs={{0,2},{1,3},{2,0},{3,1},{4,6},{5,7},{6,4},{7,5},{8,10},{9,11},{10,... | collective-permute-start | bytes 196616 | tf_op jit(solution)/shard_map/ppermute | solution.py:53
  107.2 1.5 %collective-permute-start.21 = (f32[4,768]{1,0:T(4,128)S(1)}, f32[4,768]{1,0:T(4,128)S(1)}, u32[]{:S(2)}, u32[]{:S(2)}) collective-permute-start(f32[4,768]{1,0:T(4,128)S(1)} %get-tuple-element.49), channel_id=1, source_target_pairs={{0,16},{8,24},{16,0},{24,8},{1,17},{9,25},{17,1},{25,9},{2,18},{10... | collective-permute-start | bytes 36872 | tf_op jit(solution)/shard_map/ppermute | solution.py:163
  108.9 1.4 %collective-permute-done.27 = bf16[2,32,512]{2,1,0:T(8,128)(2,1)S(1)} collective-permute-done((bf16[2,32,512]{2,1,0:T(8,128)(2,1)S(1)}, bf16[2,32,512]{2,1,0:T(8,128)(2,1)S(1)}, u32[]{:S(2)}, u32[]{:S(2)}) %collective-permute-start.27) | collective-permute-done | bytes 65568 | tf_op jit(solution)/shard_map/ppermute | solution.py:53
  110.4 1.6 %collective-permute-start.29 = (bf16[2,128,512]{2,1,0:T(8,128)(2,1)S(1)}, bf16[2,128,512]{2,1,0:T(8,128)(2,1)S(1)}, u32[]{:S(2)}, u32[]{:S(2)}) collective-permute-start(bf16[2,128,512]{2,1,0:T(8,128)(2,1)S(1)} %pad_maximum_fusion.5.one), channel_id=1, source_target_pairs={{0,1},{1,0},{2,3},{3,2},{4,5},{5,4},{6,7},{7,6},{8,9},{9,8},{10,11... | collective-permute-start | bytes 786440 | tf_op jit(solution)/shard_map/ppermute | solution.py:53
  111.9 4.9 %collective-permute-done.29.two = bf16[2,128,512]{2,1,0:T(8,128)(2,1)S(1)} collective-permute-done((bf16[2,128,512]{2,1,0:T(8,128)(2,1)S(1)}, bf16[2,128,512]{2,1,0:T(8,128)(2,1)S(1)}, u32[]{:S(2)}, u32[]{:S(2)}) %collective-permute-start.29) | collective-permute-done | bytes 262176 | tf_op jit(solution)/shard_map/ppermute | solution.py:53
  116.8 2.1 %shard_map.89 = (f32[2048,128]{1,0:T(8,128)S(1)}, bf16[2048,128]{1,0:T(8,128)(2,1)S(1)}) custom-call(s32[1]{0:T(128)} %bitcast.side, f32[4,768]{1,0:T(4,128)S(1)} %maximum_add_fusion.2.middle, bf16[512,768]{1,0:T(8,128)(2,1)S(1)} %get-tuple-element.38.left, bf16[256,768]{1,0:T(8,128)(2,1)S(1)} %get-tuple-element.39.right, ...), custom_call_target="tpu_custom_call" | custom-call | tf_op jit(solution)/shard_map/pallas_call | solution.py:254
  119.0 1.9 %collective-permute-done.30.got = bf16[2048,128]{1,0:T(8,128)(2,1)S(1)} collective-permute-done((bf16[2048,128]{1,0:T(8,128)(2,1)S(1)}, bf16[2048,128]{1,0:T(8,128)(2,1)S(1)}, u32[]{:S(2)}, u32[]{:S(2)}) %collective-permute-start.30) | collective-permute-done | bytes 524320 | tf_op jit(solution)/shard_map/ppermute | solution.py:163
  120.9 1.7 %shard_map.90 = bf16[2048,128]{1,0:T(8,128)(2,1)} custom-call(f32[4]{0:T(128)S(1)} %copy-done.8, f32[1]{0:T(128)S(6)} %copy.9.pivot, f32[2048,128]{1,0:T(8,128)S(1)} %get-tuple-element.51.mine, bf16[2048,128]{1,0:T(8,128)(2,1)S(1)} %collective-permute-done.30.got, bf16[2048,128]{1,0:T(8,128)(2,1)S(1)} %constant_dynamic-slice_fusion.3.coulomb, ...), custom_call_target="tpu_custom_call" | custom-call | tf_op jit(solution)/shard_map/pallas_call | solution.py:266
  (78 shorter events, 6.3 us)
Async XLA Ops:
  0.0 23.8 %copy-start = (bf16[2048,512]{1,0:T(8,128)(2,1)S(1)}, bf16[2048,512]{1,0:T(8,128)(2,1)}, u32[]{:S(2)}) copy-start(bf16[2048,512]{1,0:T(8,128)(2,1)} %param.9) | copy-start | bytes 6291460
  0.0 18.0 %copy-start.10 = (bf16[64,384]{1,0:T(8,128)(2,1)S(1)}, bf16[64,384]{1,0:T(8,128)(2,1)}, u32[]{:S(2)}) copy-start(bf16[64,384]{1,0:T(8,128)(2,1)} %param.11) | copy-start | bytes 147460
  0.0 18.0 %copy-start.9 = (bf16[64,384]{1,0:T(8,128)(2,1)S(1)}, bf16[64,384]{1,0:T(8,128)(2,1)}, u32[]{:S(2)}) copy-start(bf16[64,384]{1,0:T(8,128)(2,1)} %param.12) | copy-start | bytes 147460
  0.0 4.2 %collective-permute-start = (bf16[2048,128]{1,0:T(8,128)(2,1)}, bf16[2048,128]{1,0:T(8,128)(2,1)S(1)}, u32[]{:S(2)}, u32[]{:S(2)}) collective-permute-start(bf16[2048,128]{1,0:T(8,128)(2,1)} %mine.3), channel_id=1, source_target_pairs={{0,8},{8,0},{16,24},{24,16},{1,9},{9,1},{17,25},{25,17},{2,10},{10... | collective-permute-start | bytes 1572872 | tf_op jit(solution)/shard_map/ppermute | solution.py:163
  0.5 17.5 %collective-permute-start.1 = (bf16[2048,128]{1,0:T(8,128)(2,1)}, bf16[2048,128]{1,0:T(8,128)(2,1)}, u32[]{:S(2)}, u32[]{:S(2)}) collective-permute-start(bf16[2048,128]{1,0:T(8,128)(2,1)} %mine.3), channel_id=1, source_target_pairs={{0,16},{8,24},{16,0},{24,8},{1,17},{9,25},{17,1},{25,9},{2,18},{10... | collective-permute-start | bytes 1572872 | tf_op jit(solution)/shard_map/ppermute | solution.py:163
  4.0 14.0 %collective-permute-start.3 = (bf16[2,64,384]{2,1,0:T(8,128)(2,1)S(1)}, bf16[2,64,384]{2,1,0:T(8,128)(2,1)S(1)}, u32[]{:S(2)}, u32[]{:S(2)}) collective-permute-start(bf16[2,64,384]{2,1,0:T(8,128)(2,1)S(1)} %pad_maximum_fusion.7), channel_id=1, source_target_pairs={{0,16},{8,24},{16,0},{24,8},{1,17},{9,25},{17,1},{25,9},{2,18},{10... | collective-permute-start | bytes 294920 | tf_op jit(solution)/shard_map/ppermute | solution.py:163
  4.2 1.0 copy-start.1
  5.2 12.8 %copy-start.3 = (bf16[2048,128]{1,0:T(8,128)(2,1)}, bf16[2048,128]{1,0:T(8,128)(2,1)S(1)}, u32[]{:S(2)}) copy-start(bf16[2048,128]{1,0:T(8,128)(2,1)S(1)} %collective-permute-done.other) | copy-start | bytes 1572868
  7.8 10.2 %collective-permute-start.2 = (bf16[1,128,512]{2,1,0:T(8,128)(2,1)S(1)}, bf16[1,128,512]{2,1,0:T(8,128)(2,1)}, u32[]{:S(2)}, u32[]{:S(2)}) collective-permute-start(bf16[1,128,512]{2,1,0:T(8,128)(2,1)S(1)} %fusion), channel_id=1, source_target_pairs={{0,1},{1,0},{2,3},{3,2},{4,5},{5,4},{6,7},{7,6},{8,9},{9,8},{10,11... | collective-permute-start | bytes 393224 | tf_op jit(solution)/shard_map/ppermute | solution.py:44
  18.0 2.2 %collective-permute-start.4 = (bf16[2048,128]{1,0:T(8,128)(2,1)}, bf16[2048,128]{1,0:T(8,128)(2,1)S(1)}, u32[]{:S(2)}, u32[]{:S(2)}) collective-permute-start(bf16[2048,128]{1,0:T(8,128)(2,1)} %collective-permute-done.1.mine), channel_id=1, source_target_pairs={{0,8},{8,0},{16,24},{24,16},{1,9},{9,1},{17,25},{25,17},{2,10},{10... | collective-permute-start | bytes 1572872 | tf_op jit(solution)/shard_map/ppermute | solution.py:163
  18.1 54.7 %collective-permute-start.18 = (bf16[2048,512]{1,0:T(8,128)(2,1)}, bf16[2048,512]{1,0:T(8,128)(2,1)}, u32[]{:S(2)}, u32[]{:S(2)}) collective-permute-start(bf16[2048,512]{1,0:T(8,128)(2,1)} %own.5), channel_id=1, source_target_pairs={{0,16},{8,24},{16,0},{24,8},{1,17},{9,25},{17,1},{25,9},{2,18},{10... | collective-permute-start | bytes 6291464 | tf_op jit(solution)/shard_map/ppermute | solution.py:163
  20.2 0.8 copy-start.5
  21.0 12.2 %collective-permute-start.5 = (bf16[2,64,768]{2,1,0:T(8,128)(2,1)S(1)}, bf16[2,64,768]{2,1,0:T(8,128)(2,1)S(1)}, u32[]{:S(2)}, u32[]{:S(2)}) collective-permute-start(bf16[2,64,768]{2,1,0:T(8,128)(2,1)S(1)} %pad_maximum_fusion.6), channel_id=1, source_target_pairs={{0,4},{1,5},{2,6},{3,7},{4,0},{5,1},{6,2},{7,3},{8,12},{9,13},{10,... | collective-permute-start | bytes 589832 | tf_op jit(solution)/shard_map/ppermute | solution.py:171
  23.9 1.0 copy-start.6
  33.3 12.1 %copy-start.7 = (f32[512]{0:T(512)S(1)}, f32[512]{0:T(512)}, u32[]{:S(2)}) copy-start(f32[512]{0:T(512)} %param.14) | copy-start | bytes 6148
  33.4 6.5 %collective-permute-start.6 = (bf16[1,128,512]{2,1,0:T(8,128)(2,1)S(1)}, bf16[1,128,512]{2,1,0:T(8,128)(2,1)S(1)}, u32[]{:S(2)}, u32[]{:S(2)}) collective-permute-start(bf16[1,128,512]{2,1,0:T(8,128)(2,1)S(1)} %dynamic-slice_convert_fusion.1), channel_id=1, source_target_pairs={{0,1},{1,0},{2,3},{3,2},{4,5},{5,4},{6,7},{7,6},{8,9},{9,8},{10,11... | collective-permute-start | bytes 393224 | tf_op jit(solution)/shard_map/ppermute | solution.py:44
  35.0 16.1 %collective-permute-start.10 = (bf16[3,64,768]{2,1,0:T(8,128)(2,1)S(1)}, bf16[3,64,768]{2,1,0:T(8,128)(2,1)S(1)}, u32[]{:S(2)}, u32[]{:S(2)}) collective-permute-start(bf16[3,64,768]{2,1,0:T(8,128)(2,1)S(1)} %pad_maximum_fusion.1), channel_id=1, source_target_pairs={{0,1},{1,0},{2,3},{3,2},{4,5},{5,4},{6,7},{7,6},{8,9},{9,8},{10,11... | collective-permute-start | bytes 884744 | tf_op jit(solution)/shard_map/ppermute | solution.py:171
  40.9 4.5 %collective-permute-start.7 = (bf16[2,32,512]{2,1,0:T(8,128)(2,1)S(1)}, bf16[2,32,512]{2,1,0:T(8,128)(2,1)S(1)}, u32[]{:S(2)}, u32[]{:S(2)}) collective-permute-start(bf16[2,32,512]{2,1,0:T(8,128)(2,1)S(1)} %get-tuple-element.76), channel_id=1, source_target_pairs={{0,2},{1,3},{2,0},{3,1},{4,6},{5,7},{6,4},{7,5},{8,10},{9,11},{10,... | collective-permute-start | bytes 196616 | tf_op jit(solution)/shard_map/ppermute | solution.py:53
  41.7 7.0 %collective-permute-start.8 = (bf16[2,32,512]{2,1,0:T(8,128)(2,1)S(1)}, bf16[2,32,512]{2,1,0:T(8,128)(2,1)S(1)}, u32[]{:S(2)}, u32[]{:S(2)}) collective-permute-start(bf16[2,32,512]{2,1,0:T(8,128)(2,1)S(1)} %get-tuple-element.78), channel_id=1, source_target_pairs={{0,4},{1,5},{2,6},{3,7},{4,0},{5,1},{6,2},{7,3},{8,12},{9,13},{10,... | collective-permute-start | bytes 196616 | tf_op jit(solution)/shard_map/ppermute | solution.py:53
  45.0 6.1 %collective-permute-start.9 = (bf16[2,32,512]{2,1,0:T(8,128)(2,1)S(1)}, bf16[2,32,512]{2,1,0:T(8,128)(2,1)S(1)}, u32[]{:S(2)}, u32[]{:S(2)}) collective-permute-start(bf16[2,32,512]{2,1,0:T(8,128)(2,1)S(1)} %get-tuple-element.77), channel_id=1, source_target_pairs={{0,6},{1,7},{2,4},{3,5},{4,2},{5,3},{6,0},{7,1},{8,14},{9,15},{10,... | collective-permute-start | bytes 196616 | tf_op jit(solution)/shard_map/ppermute | solution.py:53
  51.2 6.9 %collective-permute-start.13 = (bf16[2,32,512]{2,1,0:T(8,128)(2,1)S(1)}, bf16[2,32,512]{2,1,0:T(8,128)(2,1)S(1)}, u32[]{:S(2)}, u32[]{:S(2)}) collective-permute-start(bf16[2,32,512]{2,1,0:T(8,128)(2,1)S(1)} %add_convert_fusion.1), channel_id=1, source_target_pairs={{0,6},{1,7},{2,4},{3,5},{4,2},{5,3},{6,0},{7,1},{8,14},{9,15},{10,... | collective-permute-start | bytes 196616 | tf_op jit(solution)/shard_map/ppermute | solution.py:53
  52.1 6.0 %collective-permute-start.14 = (bf16[2,32,512]{2,1,0:T(8,128)(2,1)S(1)}, bf16[2,32,512]{2,1,0:T(8,128)(2,1)S(1)}, u32[]{:S(2)}, u32[]{:S(2)}) collective-permute-start(bf16[2,32,512]{2,1,0:T(8,128)(2,1)S(1)} %add_convert_fusion.1), channel_id=1, source_target_pairs={{0,4},{1,5},{2,6},{3,7},{4,0},{5,1},{6,2},{7,3},{8,12},{9,13},{10,... | collective-permute-start | bytes 196616 | tf_op jit(solution)/shard_map/ppermute | solution.py:53
  52.1 7.4 %collective-permute-start.15 = (bf16[2,32,512]{2,1,0:T(8,128)(2,1)S(1)}, bf16[2,32,512]{2,1,0:T(8,128)(2,1)S(1)}, u32[]{:S(2)}, u32[]{:S(2)}) collective-permute-start(bf16[2,32,512]{2,1,0:T(8,128)(2,1)S(1)} %add_convert_fusion.1), channel_id=1, source_target_pairs={{0,2},{1,3},{2,0},{3,1},{4,6},{5,7},{6,4},{7,5},{8,10},{9,11},{10,... | collective-permute-start | bytes 196616 | tf_op jit(solution)/shard_map/ppermute | solution.py:53
  55.7 13.8 %copy-start.2 = (bf16[2048,128]{1,0:T(8,128)(2,1)S(1)}, bf16[2048,128]{1,0:T(8,128)(2,1)}, u32[]{:S(2)}) copy-start(bf16[2048,128]{1,0:T(8,128)(2,1)} %mine.3) | copy-start | bytes 1572868
  55.7 13.8 %copy-start.4 = (bf16[2048,128]{1,0:T(8,128)(2,1)S(1)}, bf16[2048,128]{1,0:T(8,128)(2,1)}, u32[]{:S(2)}) copy-start(bf16[2048,128]{1,0:T(8,128)(2,1)} %copy-done.3) | copy-start | bytes 1572868
  55.7 13.8 %collective-permute-start.11 = (bf16[3,128,768]{2,1,0:T(8,128)(2,1)S(1)}, bf16[3,128,768]{2,1,0:T(8,128)(2,1)S(1)}, u32[]{:S(2)}, u32[]{:S(2)}) collective-permute-start(bf16[3,128,768]{2,1,0:T(8,128)(2,1)S(1)} %pad_maximum_fusion.one), channel_id=1, source_target_pairs={{0,2},{1,3},{2,0},{3,1},{4,6},{5,7},{6,4},{7,5},{8,10},{9,11},{10,... | collective-permute-start | bytes 1769480 | tf_op jit(solution)/shard_map/ppermute | solution.py:217
  59.6 6.4 %collective-permute-start.16 = (bf16[2,128,512]{2,1,0:T(8,128)(2,1)S(1)}, bf16[2,128,512]{2,1,0:T(8,128)(2,1)S(1)}, u32[]{:S(2)}, u32[]{:S(2)}) collective-permute-start(bf16[2,128,512]{2,1,0:T(8,128)(2,1)S(1)} %pad_maximum_fusion.2), channel_id=1, source_target_pairs={{0,1},{1,0},{2,3},{3,2},{4,5},{5,4},{6,7},{7,6},{8,9},{9,8},{10,11... | collective-permute-start | bytes 786440 | tf_op jit(solution)/shard_map/ppermute | solution.py:53
  66.1 6.7 %collective-permute-start.17 = (bf16[2,128,512]{2,1,0:T(8,128)(2,1)S(1)}, bf16[2,128,512]{2,1,0:T(8,128)(2,1)S(1)}, u32[]{:S(2)}, u32[]{:S(2)}) collective-permute-start(bf16[2,128,512]{2,1,0:T(8,128)(2,1)S(1)} %pad_maximum_fusion.3), channel_id=1, source_target_pairs={{0,16},{8,24},{16,0},{24,8},{1,17},{9,25},{17,1},{25,9},{2,18},{10... | collective-permute-start | bytes 786440 | tf_op jit(solution)/shard_map/ppermute | solution.py:163
  71.2 3.9 %collective-permute-start.12 = (f32[4,768]{1,0:T(4,128)S(1)}, f32[4,768]{1,0:T(4,128)S(1)}, u32[]{:S(2)}, u32[]{:S(2)}) collective-permute-start(f32[4,768]{1,0:T(4,128)S(1)} %get-tuple-element.37), channel_id=1, source_target_pairs={{0,16},{8,24},{16,0},{24,8},{1,17},{9,25},{17,1},{25,9},{2,18},{10... | collective-permute-start | bytes 36872 | tf_op jit(solution)/shard_map/ppermute | solution.py:163
  75.1 4.1 %copy-start.8 = (f32[4]{0:T(128)S(1)}, f32[4]{0:T(128)}, u32[]{:S(2)}) copy-start(f32[4]{0:T(128)} %occ.3) | copy-start | bytes 52
  77.2 2.0 %collective-permute-start.19 = (bf16[2048,128]{1,0:T(8,128)(2,1)S(1)}, bf16[2048,128]{1,0:T(8,128)(2,1)S(1)}, u32[]{:S(2)}, u32[]{:S(2)}) collective-permute-start(bf16[2048,128]{1,0:T(8,128)(2,1)S(1)} %get-tuple-element.45), channel_id=1, source_target_pairs={{0,8},{8,0},{16,24},{24,16},{1,9},{9,1},{17,25},{25,17},{2,10},{10... | collective-permute-start | bytes 1572872 | tf_op jit(solution)/shard_map/ppermute | solution.py:163
  80.2 2.0 %collective-permute-start.20 = (bf16[128,2048]{1,0:T(8,128)(2,1)S(1)}, bf16[128,2048]{1,0:T(8,128)(2,1)S(1)}, u32[]{:S(2)}, u32[]{:S(2)}) collective-permute-start(bf16[128,2048]{1,0:T(8,128)(2,1)S(1)} %shard_map.87.mine), channel_id=1, source_target_pairs={{0,8},{8,0},{16,24},{24,16},{1,9},{9,1},{17,25},{25,17},{2,10},{10... | collective-permute-start | bytes 1572872 | tf_op jit(solution)/shard_map/ppermute | solution.py:163
  84.3 8.4 %collective-permute-start.22 = (bf16[2,128,512]{2,1,0:T(8,128)(2,1)S(1)}, bf16[2,128,512]{2,1,0:T(8,128)(2,1)S(1)}, u32[]{:S(2)}, u32[]{:S(2)}) collective-permute-start(bf16[2,128,512]{2,1,0:T(8,128)(2,1)S(1)} %dynamic-slice_convert_fusion), channel_id=1, source_target_pairs={{0,1},{1,0},{2,3},{3,2},{4,5},{5,4},{6,7},{7,6},{8,9},{9,8},{10,11... | collective-permute-start | bytes 786440 | tf_op jit(solution)/shard_map/ppermute | solution.py:44
  92.9 5.0 %collective-permute-start.23 = (bf16[2,32,512]{2,1,0:T(8,128)(2,1)S(1)}, bf16[2,32,512]{2,1,0:T(8,128)(2,1)S(1)}, u32[]{:S(2)}, u32[]{:S(2)}) collective-permute-start(bf16[2,32,512]{2,1,0:T(8,128)(2,1)S(1)} %get-tuple-element.65), channel_id=1, source_target_pairs={{0,2},{1,3},{2,0},{3,1},{4,6},{5,7},{6,4},{7,5},{8,10},{9,11},{10,... | collective-permute-start | bytes 196616 | tf_op jit(solution)/shard_map/ppermute | solution.py:53
  94.1 6.7 %collective-permute-start.24 = (bf16[2,32,512]{2,1,0:T(8,128)(2,1)S(1)}, bf16[2,32,512]{2,1,0:T(8,128)(2,1)S(1)}, u32[]{:S(2)}, u32[]{:S(2)}) collective-permute-start(bf16[2,32,512]{2,1,0:T(8,128)(2,1)S(1)} %get-tuple-element.67), channel_id=1, source_target_pairs={{0,4},{1,5},{2,6},{3,7},{4,0},{5,1},{6,2},{7,3},{8,12},{9,13},{10,... | collective-permute-start | bytes 196616 | tf_op jit(solution)/shard_map/ppermute | solution.py:53
  96.7 6.1 %collective-permute-start.25 = (bf16[2,32,512]{2,1,0:T(8,128)(2,1)S(1)}, bf16[2,32,512]{2,1,0:T(8,128)(2,1)S(1)}, u32[]{:S(2)}, u32[]{:S(2)}) collective-permute-start(bf16[2,32,512]{2,1,0:T(8,128)(2,1)S(1)} %get-tuple-element.66), channel_id=1, source_target_pairs={{0,6},{1,7},{2,4},{3,5},{4,2},{5,3},{6,0},{7,1},{8,14},{9,15},{10,... | collective-permute-start | bytes 196616 | tf_op jit(solution)/shard_map/ppermute | solution.py:53
  102.8 6.2 %collective-permute-start.26 = (bf16[2,32,512]{2,1,0:T(8,128)(2,1)S(1)}, bf16[2,32,512]{2,1,0:T(8,128)(2,1)S(1)}, u32[]{:S(2)}, u32[]{:S(2)}) collective-permute-start(bf16[2,32,512]{2,1,0:T(8,128)(2,1)S(1)} %add_convert_fusion), channel_id=1, source_target_pairs={{0,6},{1,7},{2,4},{3,5},{4,2},{5,3},{6,0},{7,1},{8,14},{9,15},{10,... | collective-permute-start | bytes 196616 | tf_op jit(solution)/shard_map/ppermute | solution.py:53
  104.1 6.2 %collective-permute-start.27 = (bf16[2,32,512]{2,1,0:T(8,128)(2,1)S(1)}, bf16[2,32,512]{2,1,0:T(8,128)(2,1)S(1)}, u32[]{:S(2)}, u32[]{:S(2)}) collective-permute-start(bf16[2,32,512]{2,1,0:T(8,128)(2,1)S(1)} %add_convert_fusion), channel_id=1, source_target_pairs={{0,4},{1,5},{2,6},{3,7},{4,0},{5,1},{6,2},{7,3},{8,12},{9,13},{10,... | collective-permute-start | bytes 196616 | tf_op jit(solution)/shard_map/ppermute | solution.py:53
  104.1 6.2 %collective-permute-start.28 = (bf16[2,32,512]{2,1,0:T(8,128)(2,1)S(1)}, bf16[2,32,512]{2,1,0:T(8,128)(2,1)S(1)}, u32[]{:S(2)}, u32[]{:S(2)}) collective-permute-start(bf16[2,32,512]{2,1,0:T(8,128)(2,1)S(1)} %add_convert_fusion), channel_id=1, source_target_pairs={{0,2},{1,3},{2,0},{3,1},{4,6},{5,7},{6,4},{7,5},{8,10},{9,11},{10,... | collective-permute-start | bytes 196616 | tf_op jit(solution)/shard_map/ppermute | solution.py:53
  107.2 4.7 %collective-permute-start.21 = (f32[4,768]{1,0:T(4,128)S(1)}, f32[4,768]{1,0:T(4,128)S(1)}, u32[]{:S(2)}, u32[]{:S(2)}) collective-permute-start(f32[4,768]{1,0:T(4,128)S(1)} %get-tuple-element.49), channel_id=1, source_target_pairs={{0,16},{8,24},{16,0},{24,8},{1,17},{9,25},{17,1},{25,9},{2,18},{10... | collective-permute-start | bytes 36872 | tf_op jit(solution)/shard_map/ppermute | solution.py:163
  110.4 6.4 %collective-permute-start.29 = (bf16[2,128,512]{2,1,0:T(8,128)(2,1)S(1)}, bf16[2,128,512]{2,1,0:T(8,128)(2,1)S(1)}, u32[]{:S(2)}, u32[]{:S(2)}) collective-permute-start(bf16[2,128,512]{2,1,0:T(8,128)(2,1)S(1)} %pad_maximum_fusion.5.one), channel_id=1, source_target_pairs={{0,1},{1,0},{2,3},{3,2},{4,5},{5,4},{6,7},{7,6},{8,9},{9,8},{10,11... | collective-permute-start | bytes 786440 | tf_op jit(solution)/shard_map/ppermute | solution.py:53
  118.9 2.0 %collective-permute-start.30 = (bf16[2048,128]{1,0:T(8,128)(2,1)S(1)}, bf16[2048,128]{1,0:T(8,128)(2,1)S(1)}, u32[]{:S(2)}, u32[]{:S(2)}) collective-permute-start(bf16[2048,128]{1,0:T(8,128)(2,1)S(1)} %get-tuple-element.52), channel_id=1, source_target_pairs={{0,8},{8,0},{16,24},{24,16},{1,9},{9,1},{17,25},{25,17},{2,10},{10... | collective-permute-start | bytes 1572872 | tf_op jit(solution)/shard_map/ppermute | solution.py:163

commit v6 on v5

--- a/solution.py
+++ b/solution.py
@@ -194,7 +194,6 @@
     one, two = other_rows(fac, 0)
     kept = jnp.where(k // 2 == 0, one[1], two[1])
     fac = jnp.stack([one[0], two[0], kept])
-    far_gram, fac = tie(far_gram, fac)
     far_mine, far_got = fold(far_gram, n_pair)
 
     far = over(df_factors, 2)
@@ -207,6 +206,8 @@
     def beside(stage, a):
         nonlocal fac, far, vir, vir_row, coulomb_block, left, right, middle, factors
         if stage == 1:
+            a, fac = tie(a, fac)
+        if stage == 2:
             fac = jnp.concatenate(other_rows(fac, n_bits - 1), axis=1)
             a, fac = tie(a, fac)
         if stage == 1:
@@ -225,11 +226,10 @@
                 ),
                 in_specs=[VMEM] * 2 + [SMEM] + [VMEM] * 2,
                 out_specs=(VMEM,) * 3,
-                cost_estimate=scheduled(6),
+                cost_estimate=scheduled(3),
                 compiler_params=PARAMS,
             )(*near, jnp.stack([bit, bit ^ (k % 2)]), fac, got)
         if stage == 4:
-            a, far = tie(a, far)
             factors = pl.pallas_call(
                 hold_kernel,
                 out_shape=jax.ShapeDtypeStruct((2, rows, naux), BF),
@@ -238,6 +238,7 @@
                 scratch_shapes=[pltpu.SemaphoreType.DMA((2,))],
                 compiler_params=PARAMS,
             )(df_factors, far)
+            a, factors = tie(a, factors)
         return a
 
     line, other = all_reduce(

time: 123 us -> 122 us (level)
  local copies, waits for them, and re-layouts: 3.28 us -> 1.44 us
    ppermute x14, waiting for transfers between devices: 26 us -> 21.5 us  [send(): return lax.ppermute(a, 'pair', xor(n, s))]
    ppermute x1, waiting for transfers between devices: 1.82 us -> 5.92 us  [beside(): got = lax.ppermute(fac, 'pair', xor(n_pair, n_pair // 4))]
    ppermute x2, waiting for transfers between devices: 5.8 us -> 9.47 us  [other_rows(): got = lax.ppermute(fac, 'pair', xor(n_pair, bit))]
    ppermute x3, waiting for transfers between devices: 11.1 us -> 7.96 us  [fold(): return (mine, lax.ppermute(theirs.astype(BF), 'pair', xor(n, 1)))]
    unnamed x22 -> x18, local copies, waits for them, and re-layouts: 2.91 us -> 1.08 us
    ppermute x1, starting transfers between devices: 0.03 us -> 1.54 us  [beside(): got = lax.ppermute(fac, 'pair', xor(n_pair, n_pair // 4))]
  transfers between devices with their start and end apart: 31 -> 31, of which waited for: 20 -> 19; matrix products, arithmetic and copies ran while one was open for 2% -> 2% of each run, Pallas kernels for 7% -> 7%
where the time goes in v6:
time: 122 us; the launch traced here: 121 us
  waiting for transfers between devices  58.3 us (48%)
  starting transfers between devices  40 us (33%)
  Pallas kernels  18.1 us (15%)
  other arithmetic  2.47 us (2%)
  local copies, waits for them, and re-layouts  1.44 us (1%)
    ppermute x14, waiting for transfers between devices, send(): return lax.ppermute(a, 'pair', xor(n, s))  21.5 us
    ppermute x14, starting transfers between devices, send(): return lax.ppermute(a, 'pair', xor(n, s))  20 us
    ppermute x11, waiting for transfers between devices, over(): return lax.ppermute(a, 'aux', xor(n_aux, s))  13.4 us
    ppermute x11, starting transfers between devices, over(): return lax.ppermute(a, 'aux', xor(n_aux, s))  10.1 us
    ppermute x2, waiting for transfers between devices, other_rows(): got = lax.ppermute(fac, 'pair', xor(n_pair, bit))  9.47 us
    ppermute x3, waiting for transfers between devices, fold(): return (mine, lax.ppermute(theirs.astype(BF), 'pair', xor(n, 1)))  7.96 us
    ppermute x1, waiting for transfers between devices, beside(): got = lax.ppermute(fac, 'pair', xor(n_pair, n_pair // 4))  5.92 us
    ppermute x3, starting transfers between devices, fold(): return (mine, lax.ppermute(theirs.astype(BF), 'pair', xor(n, 1)))  5.31 us
  transfers between devices with their start and end apart: 31, of which 19 were waited for; matrix products, arithmetic and copies ran while one was open for 2% of the time, Pallas kernels for 7%

profile of v6, /device:TPU:0, one launch (start us, length us, event | category | flops | bytes accessed | tf_op | source)
XLA Modules:
  0.0 121.3 jit_solution(7545545881879344417)
XLA Ops:
  0.5 2.6 %collective-permute-start.1 = (bf16[2048,128]{1,0:T(8,128)(2,1)}, bf16[2048,128]{1,0:T(8,128)(2,1)}, u32[]{:S(2)}, u32[]{:S(2)}) collective-permute-start(bf16[2048,128]{1,0:T(8,128)(2,1)} %mine.3), channel_id=1, source_target_pairs={{0,16},{8,24},{16,0},{24,8},{1,17},{9,25},{17,1},{25,9},{2,18},{10... | collective-permute-start | bytes 1572872 | tf_op jit(solution)/shard_map/ppermute | solution.py:163
  4.2 1.0 copy-done.1
  5.2 2.5 %shard_map.82 = f32[256,512]{1,0:T(8,128)S(1)} custom-call(bf16[2048,128]{1,0:T(8,128)(2,1)S(1)} %copy-done.1, bf16[2048,128]{1,0:T(8,128)(2,1)S(1)} %collective-permute-done.other, bf16[2048,512]{1,0:T(8,128)(2,1)} %own.5), custom_call_target="tpu_custom_call" | custom-call | tf_op jit(solution)/shard_map/pallas_call | solution.py:181
  7.8 1.9 %collective-permute-start.2 = (bf16[1,128,512]{2,1,0:T(8,128)(2,1)S(1)}, bf16[1,128,512]{2,1,0:T(8,128)(2,1)}, u32[]{:S(2)}, u32[]{:S(2)}) collective-permute-start(bf16[1,128,512]{2,1,0:T(8,128)(2,1)S(1)} %fusion), channel_id=1, source_target_pairs={{0,1},{1,0},{2,3},{3,2},{4,5},{5,4},{6,7},{7,6},{8,9},{9,8},{10,11... | collective-permute-start | bytes 393224 | tf_op jit(solution)/shard_map/ppermute | solution.py:44
  9.7 8.2 %collective-permute-done.3 = bf16[2,64,384]{2,1,0:T(8,128)(2,1)S(1)} collective-permute-done((bf16[2,64,384]{2,1,0:T(8,128)(2,1)S(1)}, bf16[2,64,384]{2,1,0:T(8,128)(2,1)S(1)}, u32[]{:S(2)}, u32[]{:S(2)}) %collective-permute-start.3) | collective-permute-done | bytes 98336 | tf_op jit(solution)/shard_map/ppermute | solution.py:163
  18.1 1.8 %collective-permute-start.18 = (bf16[2048,512]{1,0:T(8,128)(2,1)}, bf16[2048,512]{1,0:T(8,128)(2,1)}, u32[]{:S(2)}, u32[]{:S(2)}) collective-permute-start(bf16[2048,512]{1,0:T(8,128)(2,1)} %own.5), channel_id=1, source_target_pairs={{0,16},{8,24},{16,0},{24,8},{1,17},{9,25},{17,1},{25,9},{2,18},{10... | collective-permute-start | bytes 6291464 | tf_op jit(solution)/shard_map/ppermute | solution.py:163
  20.3 2.7 %shard_map.83 = f32[256,512]{1,0:T(8,128)S(1)} custom-call(bf16[2048,128]{1,0:T(8,128)(2,1)} %collective-permute-done.1.mine, bf16[2048,128]{1,0:T(8,128)(2,1)} %collective-permute-done.4.other, bf16[2048,512]{1,0:T(8,128)(2,1)} %own.5), custom_call_target="tpu_custom_call" | custom-call | tf_op jit(solution)/shard_map/pallas_call | solution.py:181
  23.0 1.8 %collective-permute-start.5 = (bf16[1,128,512]{2,1,0:T(8,128)(2,1)S(1)}, bf16[1,128,512]{2,1,0:T(8,128)(2,1)S(1)}, u32[]{:S(2)}, u32[]{:S(2)}) collective-permute-start(bf16[1,128,512]{2,1,0:T(8,128)(2,1)S(1)} %fusion.1), channel_id=1, source_target_pairs={{0,1},{1,0},{2,3},{3,2},{4,5},{5,4},{6,7},{7,6},{8,9},{9,8},{10,11... | collective-permute-start | bytes 393224 | tf_op jit(solution)/shard_map/ppermute | solution.py:44
  24.9 2.6 %collective-permute-start.9 = (bf16[2,64,768]{2,1,0:T(8,128)(2,1)S(1)}, bf16[2,64,768]{2,1,0:T(8,128)(2,1)S(1)}, u32[]{:S(2)}, u32[]{:S(2)}) collective-permute-start(bf16[2,64,768]{2,1,0:T(8,128)(2,1)S(1)} %pad_maximum_fusion.6), channel_id=1, source_target_pairs={{0,4},{1,5},{2,6},{3,7},{4,0},{5,1},{6,2},{7,3},{8,12},{9,13},{10,... | collective-permute-start | bytes 589832 | tf_op jit(solution)/shard_map/ppermute | solution.py:171
  27.5 1.1 collective-permute-done.5
  28.6 1.0 fusion.3
  29.7 1.9 %collective-permute-start.6 = (bf16[2,32,512]{2,1,0:T(8,128)(2,1)S(1)}, bf16[2,32,512]{2,1,0:T(8,128)(2,1)S(1)}, u32[]{:S(2)}, u32[]{:S(2)}) collective-permute-start(bf16[2,32,512]{2,1,0:T(8,128)(2,1)S(1)} %get-tuple-element.76), channel_id=1, source_target_pairs={{0,2},{1,3},{2,0},{3,1},{4,6},{5,7},{6,4},{7,5},{8,10},{9,11},{10,... | collective-permute-start | bytes 196616 | tf_op jit(solution)/shard_map/ppermute | solution.py:53
  31.5 2.6 %collective-permute-start.7 = (bf16[2,32,512]{2,1,0:T(8,128)(2,1)S(1)}, bf16[2,32,512]{2,1,0:T(8,128)(2,1)S(1)}, u32[]{:S(2)}, u32[]{:S(2)}) collective-permute-start(bf16[2,32,512]{2,1,0:T(8,128)(2,1)S(1)} %get-tuple-element.78), channel_id=1, source_target_pairs={{0,4},{1,5},{2,6},{3,7},{4,0},{5,1},{6,2},{7,3},{8,12},{9,13},{10,... | collective-permute-start | bytes 196616 | tf_op jit(solution)/shard_map/ppermute | solution.py:53
  34.2 6.5 %collective-permute-done.9 = bf16[2,64,768]{2,1,0:T(8,128)(2,1)S(1)} collective-permute-done((bf16[2,64,768]{2,1,0:T(8,128)(2,1)S(1)}, bf16[2,64,768]{2,1,0:T(8,128)(2,1)S(1)}, u32[]{:S(2)}, u32[]{:S(2)}) %collective-permute-start.9) | collective-permute-done | bytes 196640 | tf_op jit(solution)/shard_map/ppermute | solution.py:171
  40.8 0.9 collective-permute-done.7
  41.7 3.0 %collective-permute-start.10 = (bf16[2,32,512]{2,1,0:T(8,128)(2,1)S(1)}, bf16[2,32,512]{2,1,0:T(8,128)(2,1)S(1)}, u32[]{:S(2)}, u32[]{:S(2)}) collective-permute-start(bf16[2,32,512]{2,1,0:T(8,128)(2,1)S(1)} %add_convert_fusion.1), channel_id=1, source_target_pairs={{0,6},{1,7},{2,4},{3,5},{4,2},{5,3},{6,0},{7,1},{8,14},{9,15},{10,... | collective-permute-start | bytes 196616 | tf_op jit(solution)/shard_map/ppermute | solution.py:53
  45.2 1.0 collective-permute-start.12
  46.6 1.4 %collective-permute-done.10 = bf16[2,32,512]{2,1,0:T(8,128)(2,1)S(1)} collective-permute-done((bf16[2,32,512]{2,1,0:T(8,128)(2,1)S(1)}, bf16[2,32,512]{2,1,0:T(8,128)(2,1)S(1)}, u32[]{:S(2)}, u32[]{:S(2)}) %collective-permute-start.10) | collective-permute-done | bytes 65568 | tf_op jit(solution)/shard_map/ppermute | solution.py:53
  48.0 3.1 %collective-permute-done.11 = bf16[2,32,512]{2,1,0:T(8,128)(2,1)S(1)} collective-permute-done((bf16[2,32,512]{2,1,0:T(8,128)(2,1)S(1)}, bf16[2,32,512]{2,1,0:T(8,128)(2,1)S(1)}, u32[]{:S(2)}, u32[]{:S(2)}) %collective-permute-start.11) | collective-permute-done | bytes 65568 | tf_op jit(solution)/shard_map/ppermute | solution.py:53
  51.2 3.0 %collective-permute-done.13 = bf16[3,64,768]{2,1,0:T(8,128)(2,1)S(1)} collective-permute-done((bf16[3,64,768]{2,1,0:T(8,128)(2,1)S(1)}, bf16[3,64,768]{2,1,0:T(8,128)(2,1)S(1)}, u32[]{:S(2)}, u32[]{:S(2)}) %collective-permute-start.13) | collective-permute-done | bytes 294944 | tf_op jit(solution)/shard_map/ppermute | solution.py:171
  54.8 1.5 %collective-permute-start.14 = (bf16[3,128,768]{2,1,0:T(8,128)(2,1)S(1)}, bf16[3,128,768]{2,1,0:T(8,128)(2,1)S(1)}, u32[]{:S(2)}, u32[]{:S(2)}) collective-permute-start(bf16[3,128,768]{2,1,0:T(8,128)(2,1)S(1)} %pad_maximum_fusion.one), channel_id=1, source_target_pairs={{0,2},{1,3},{2,0},{3,1},{4,6},{5,7},{6,4},{7,5},{8,10},{9,11},{10,... | collective-permute-start | bytes 1769480 | tf_op jit(solution)/shard_map/ppermute | solution.py:218
  56.5 4.3 %collective-permute-done.16 = bf16[2,128,512]{2,1,0:T(8,128)(2,1)S(1)} collective-permute-done((bf16[2,128,512]{2,1,0:T(8,128)(2,1)S(1)}, bf16[2,128,512]{2,1,0:T(8,128)(2,1)S(1)}, u32[]{:S(2)}, u32[]{:S(2)}) %collective-permute-start.16) | collective-permute-done | bytes 262176 | tf_op jit(solution)/shard_map/ppermute | solution.py:53
  60.8 1.6 %collective-permute-start.17 = (bf16[2,128,512]{2,1,0:T(8,128)(2,1)S(1)}, bf16[2,128,512]{2,1,0:T(8,128)(2,1)S(1)}, u32[]{:S(2)}, u32[]{:S(2)}) collective-permute-start(bf16[2,128,512]{2,1,0:T(8,128)(2,1)S(1)} %pad_maximum_fusion.3), channel_id=1, source_target_pairs={{0,16},{8,24},{16,0},{24,8},{1,17},{9,25},{17,1},{25,9},{2,18},{10... | collective-permute-start | bytes 786440 | tf_op jit(solution)/shard_map/ppermute | solution.py:163
  62.4 5.9 %collective-permute-done.14.two = bf16[3,128,768]{2,1,0:T(8,128)(2,1)S(1)} collective-permute-done((bf16[3,128,768]{2,1,0:T(8,128)(2,1)S(1)}, bf16[3,128,768]{2,1,0:T(8,128)(2,1)S(1)}, u32[]{:S(2)}, u32[]{:S(2)}) %collective-permute-start.14) | collective-permute-done | bytes 589856 | tf_op jit(solution)/shard_map/ppermute | solution.py:218
  68.4 1.7 %shard_map.84 = (bf16[512,768]{1,0:T(8,128)(2,1)S(1)}, bf16[256,768]{1,0:T(8,128)(2,1)S(1)}, f32[4,768]{1,0:T(4,128)S(1)}) custom-call(bf16[2048,128]{1,0:T(8,128)(2,1)S(1)} %copy-done.2, bf16[2048,128]{1,0:T(8,128)(2,1)S(1)} %copy-done.4, s32[2]{0:T(128)S(1)} %pad_add_fusion.places, bf16[3,128,768]{2,1,0:T(8,128)(2,1)S(1)} %pad_maximum_fusion.one, ...), custom_call_target="tpu_custom_call" | custom-call | flops 3000000000 | bytes 9000000 | tf_op jit(solution)/shard_map/pallas_call | solution.py:220
  70.0 1.6 %collective-permute-start.15 = (f32[4,768]{1,0:T(4,128)S(1)}, f32[4,768]{1,0:T(4,128)S(1)}, u32[]{:S(2)}, u32[]{:S(2)}) collective-permute-start(f32[4,768]{1,0:T(4,128)S(1)} %get-tuple-element.38), channel_id=1, source_target_pairs={{0,16},{8,24},{16,0},{24,8},{1,17},{9,25},{17,1},{25,9},{2,18},{10... | collective-permute-start | bytes 36872 | tf_op jit(solution)/shard_map/ppermute | solution.py:163
  71.6 2.2 %shard_map.85.factors = bf16[2,2048,512]{2,1,0:T(8,128)(2,1)S(1)} custom-call(bf16[2048,512]{1,0:T(8,128)(2,1)} %own.5, bf16[2048,512]{1,0:T(8,128)(2,1)} %collective-permute-done.18.far), custom_call_target="tpu_custom_call" | custom-call | tf_op jit(solution)/shard_map/pallas_call | solution.py:233
  73.9 2.1 %shard_map.86 = (f32[2048,128]{1,0:T(8,128)S(1)}, bf16[2048,128]{1,0:T(8,128)(2,1)S(1)}) custom-call(s32[1]{0:T(128)} %bitcast.side, f32[4,768]{1,0:T(4,128)S(1)} %maximum_add_fusion.1.middle, bf16[512,768]{1,0:T(8,128)(2,1)S(1)} %get-tuple-element.39.left, bf16[256,768]{1,0:T(8,128)(2,1)S(1)} %get-tuple-element.40.right, ...), custom_call_target="tpu_custom_call" | custom-call | tf_op jit(solution)/shard_map/pallas_call | solution.py:255
  76.8 1.2 %collective-permute-done.19.got = bf16[2048,128]{1,0:T(8,128)(2,1)S(1)} collective-permute-done((bf16[2048,128]{1,0:T(8,128)(2,1)S(1)}, bf16[2048,128]{1,0:T(8,128)(2,1)S(1)}, u32[]{:S(2)}, u32[]{:S(2)}) %collective-permute-start.19) | collective-permute-done | bytes 524320 | tf_op jit(solution)/shard_map/ppermute | solution.py:163
  78.1 1.0 shard_map.87.mine
  79.3 1.8 %collective-permute-done.20.other = bf16[128,2048]{1,0:T(8,128)(2,1)S(1)} collective-permute-done((bf16[128,2048]{1,0:T(8,128)(2,1)S(1)}, bf16[128,2048]{1,0:T(8,128)(2,1)S(1)}, u32[]{:S(2)}, u32[]{:S(2)}) %collective-permute-start.20) | collective-permute-done | bytes 524320 | tf_op jit(solution)/shard_map/ppermute | solution.py:163
  81.0 2.1 %shard_map.88 = (f32[2,256,512]{2,1,0:T(8,128)S(1)}, f32[4,768]{1,0:T(4,128)S(1)}) custom-call(bf16[128,2048]{1,0:T(8,128)(2,1)S(1)} %shard_map.87.mine, bf16[128,2048]{1,0:T(8,128)(2,1)S(1)} %collective-permute-done.20.other, bf16[512,768]{1,0:T(8,128)(2,1)S(1)} %get-tuple-element.39.left, bf16[256,768]{1,0:T(8,128)(2,1)S(1)} %get-tuple-element.40.right, ...), custom_call_target="tpu_custom_call" | custom-call | tf_op jit(solution)/shard_map/pallas_call | solution.py:275
  83.2 1.6 %collective-permute-start.22 = (bf16[2,128,512]{2,1,0:T(8,128)(2,1)S(1)}, bf16[2,128,512]{2,1,0:T(8,128)(2,1)S(1)}, u32[]{:S(2)}, u32[]{:S(2)}) collective-permute-start(bf16[2,128,512]{2,1,0:T(8,128)(2,1)S(1)} %dynamic-slice_convert_fusion), channel_id=1, source_target_pairs={{0,1},{1,0},{2,3},{3,2},{4,5},{5,4},{6,7},{7,6},{8,9},{9,8},{10,11... | collective-permute-start | bytes 786440 | tf_op jit(solution)/shard_map/ppermute | solution.py:44
  84.8 6.8 %collective-permute-done.22 = bf16[2,128,512]{2,1,0:T(8,128)(2,1)S(1)} collective-permute-done((bf16[2,128,512]{2,1,0:T(8,128)(2,1)S(1)}, bf16[2,128,512]{2,1,0:T(8,128)(2,1)S(1)}, u32[]{:S(2)}, u32[]{:S(2)}) %collective-permute-start.22) | collective-permute-done | bytes 262176 | tf_op jit(solution)/shard_map/ppermute | solution.py:44
  91.7 1.8 %collective-permute-start.23 = (bf16[2,32,512]{2,1,0:T(8,128)(2,1)S(1)}, bf16[2,32,512]{2,1,0:T(8,128)(2,1)S(1)}, u32[]{:S(2)}, u32[]{:S(2)}) collective-permute-start(bf16[2,32,512]{2,1,0:T(8,128)(2,1)S(1)} %get-tuple-element.65), channel_id=1, source_target_pairs={{0,2},{1,3},{2,0},{3,1},{4,6},{5,7},{6,4},{7,5},{8,10},{9,11},{10,... | collective-permute-start | bytes 196616 | tf_op jit(solution)/shard_map/ppermute | solution.py:53
  93.5 1.5 %collective-permute-start.24 = (bf16[2,32,512]{2,1,0:T(8,128)(2,1)S(1)}, bf16[2,32,512]{2,1,0:T(8,128)(2,1)S(1)}, u32[]{:S(2)}, u32[]{:S(2)}) collective-permute-start(bf16[2,32,512]{2,1,0:T(8,128)(2,1)S(1)} %get-tuple-element.67), channel_id=1, source_target_pairs={{0,4},{1,5},{2,6},{3,7},{4,0},{5,1},{6,2},{7,3},{8,12},{9,13},{10,... | collective-permute-start | bytes 196616 | tf_op jit(solution)/shard_map/ppermute | solution.py:53
  95.0 1.2 collective-permute-start.25
  96.2 4.1 %collective-permute-done.24 = bf16[2,32,512]{2,1,0:T(8,128)(2,1)S(1)} collective-permute-done((bf16[2,32,512]{2,1,0:T(8,128)(2,1)S(1)}, bf16[2,32,512]{2,1,0:T(8,128)(2,1)S(1)}, u32[]{:S(2)}, u32[]{:S(2)}) %collective-permute-start.24) | collective-permute-done | bytes 65568 | tf_op jit(solution)/shard_map/ppermute | solution.py:53
  100.3 0.9 collective-permute-done.25
  101.2 2.1 %collective-permute-start.26 = (bf16[2,32,512]{2,1,0:T(8,128)(2,1)S(1)}, bf16[2,32,512]{2,1,0:T(8,128)(2,1)S(1)}, u32[]{:S(2)}, u32[]{:S(2)}) collective-permute-start(bf16[2,32,512]{2,1,0:T(8,128)(2,1)S(1)} %add_convert_fusion), channel_id=1, source_target_pairs={{0,6},{1,7},{2,4},{3,5},{4,2},{5,3},{6,0},{7,1},{8,14},{9,15},{10,... | collective-permute-start | bytes 196616 | tf_op jit(solution)/shard_map/ppermute | solution.py:53
  103.8 1.9 %collective-permute-start.28 = (bf16[2,32,512]{2,1,0:T(8,128)(2,1)S(1)}, bf16[2,32,512]{2,1,0:T(8,128)(2,1)S(1)}, u32[]{:S(2)}, u32[]{:S(2)}) collective-permute-start(bf16[2,32,512]{2,1,0:T(8,128)(2,1)S(1)} %add_convert_fusion), channel_id=1, source_target_pairs={{0,2},{1,3},{2,0},{3,1},{4,6},{5,7},{6,4},{7,5},{8,10},{9,11},{10,... | collective-permute-start | bytes 196616 | tf_op jit(solution)/shard_map/ppermute | solution.py:53
  105.7 1.4 %collective-permute-start.21 = (f32[4,768]{1,0:T(4,128)S(1)}, f32[4,768]{1,0:T(4,128)S(1)}, u32[]{:S(2)}, u32[]{:S(2)}) collective-permute-start(f32[4,768]{1,0:T(4,128)S(1)} %get-tuple-element.49), channel_id=1, source_target_pairs={{0,16},{8,24},{16,0},{24,8},{1,17},{9,25},{17,1},{25,9},{2,18},{10... | collective-permute-start | bytes 36872 | tf_op jit(solution)/shard_map/ppermute | solution.py:163
  107.4 1.6 %collective-permute-done.27 = bf16[2,32,512]{2,1,0:T(8,128)(2,1)S(1)} collective-permute-done((bf16[2,32,512]{2,1,0:T(8,128)(2,1)S(1)}, bf16[2,32,512]{2,1,0:T(8,128)(2,1)S(1)}, u32[]{:S(2)}, u32[]{:S(2)}) %collective-permute-start.27) | collective-permute-done | bytes 65568 | tf_op jit(solution)/shard_map/ppermute | solution.py:53
  109.1 1.6 %collective-permute-start.29 = (bf16[2,128,512]{2,1,0:T(8,128)(2,1)S(1)}, bf16[2,128,512]{2,1,0:T(8,128)(2,1)S(1)}, u32[]{:S(2)}, u32[]{:S(2)}) collective-permute-start(bf16[2,128,512]{2,1,0:T(8,128)(2,1)S(1)} %pad_maximum_fusion.5.one), channel_id=1, source_target_pairs={{0,1},{1,0},{2,3},{3,2},{4,5},{5,4},{6,7},{7,6},{8,9},{9,8},{10,11... | collective-permute-start | bytes 786440 | tf_op jit(solution)/shard_map/ppermute | solution.py:53
  110.7 4.9 %collective-permute-done.29.two = bf16[2,128,512]{2,1,0:T(8,128)(2,1)S(1)} collective-permute-done((bf16[2,128,512]{2,1,0:T(8,128)(2,1)S(1)}, bf16[2,128,512]{2,1,0:T(8,128)(2,1)S(1)}, u32[]{:S(2)}, u32[]{:S(2)}) %collective-permute-start.29) | collective-permute-done | bytes 262176 | tf_op jit(solution)/shard_map/ppermute | solution.py:53
  115.5 2.1 %shard_map.89 = (f32[2048,128]{1,0:T(8,128)S(1)}, bf16[2048,128]{1,0:T(8,128)(2,1)S(1)}) custom-call(s32[1]{0:T(128)} %bitcast.side, f32[4,768]{1,0:T(4,128)S(1)} %maximum_add_fusion.2.middle, bf16[512,768]{1,0:T(8,128)(2,1)S(1)} %get-tuple-element.39.left, bf16[256,768]{1,0:T(8,128)(2,1)S(1)} %get-tuple-element.40.right, ...), custom_call_target="tpu_custom_call" | custom-call | tf_op jit(solution)/shard_map/pallas_call | solution.py:255
  117.8 1.9 %collective-permute-done.30.got = bf16[2048,128]{1,0:T(8,128)(2,1)S(1)} collective-permute-done((bf16[2048,128]{1,0:T(8,128)(2,1)S(1)}, bf16[2048,128]{1,0:T(8,128)(2,1)S(1)}, u32[]{:S(2)}, u32[]{:S(2)}) %collective-permute-start.30) | collective-permute-done | bytes 524320 | tf_op jit(solution)/shard_map/ppermute | solution.py:163
  119.7 1.7 %shard_map.90 = bf16[2048,128]{1,0:T(8,128)(2,1)} custom-call(f32[4]{0:T(128)S(1)} %copy-done.6, f32[1]{0:T(128)S(6)} %copy.9.pivot, f32[2048,128]{1,0:T(8,128)S(1)} %get-tuple-element.51.mine, bf16[2048,128]{1,0:T(8,128)(2,1)S(1)} %collective-permute-done.30.got, bf16[2048,128]{1,0:T(8,128)(2,1)S(1)} %constant_dynamic-slice_fusion.3.coulomb, ...), custom_call_target="tpu_custom_call" | custom-call | tf_op jit(solution)/shard_map/pallas_call | solution.py:267
  (74 shorter events, 5.7 us)
Async XLA Ops:
  0.0 20.0 %copy-start = (bf16[2048,512]{1,0:T(8,128)(2,1)S(1)}, bf16[2048,512]{1,0:T(8,128)(2,1)}, u32[]{:S(2)}) copy-start(bf16[2048,512]{1,0:T(8,128)(2,1)} %param.9) | copy-start | bytes 6291460
  0.0 18.0 %copy-start.8 = (bf16[64,384]{1,0:T(8,128)(2,1)S(1)}, bf16[64,384]{1,0:T(8,128)(2,1)}, u32[]{:S(2)}) copy-start(bf16[64,384]{1,0:T(8,128)(2,1)} %param.11) | copy-start | bytes 147460
  0.0 18.0 %copy-start.7 = (bf16[64,384]{1,0:T(8,128)(2,1)S(1)}, bf16[64,384]{1,0:T(8,128)(2,1)}, u32[]{:S(2)}) copy-start(bf16[64,384]{1,0:T(8,128)(2,1)} %param.12) | copy-start | bytes 147460
  0.0 4.2 %collective-permute-start = (bf16[2048,128]{1,0:T(8,128)(2,1)}, bf16[2048,128]{1,0:T(8,128)(2,1)S(1)}, u32[]{:S(2)}, u32[]{:S(2)}) collective-permute-start(bf16[2048,128]{1,0:T(8,128)(2,1)} %mine.3), channel_id=1, source_target_pairs={{0,8},{8,0},{16,24},{24,16},{1,9},{9,1},{17,25},{25,17},{2,10},{10... | collective-permute-start | bytes 1572872 | tf_op jit(solution)/shard_map/ppermute | solution.py:163
  0.5 17.5 %collective-permute-start.1 = (bf16[2048,128]{1,0:T(8,128)(2,1)}, bf16[2048,128]{1,0:T(8,128)(2,1)}, u32[]{:S(2)}, u32[]{:S(2)}) collective-permute-start(bf16[2048,128]{1,0:T(8,128)(2,1)} %mine.3), channel_id=1, source_target_pairs={{0,16},{8,24},{16,0},{24,8},{1,17},{9,25},{17,1},{25,9},{2,18},{10... | collective-permute-start | bytes 1572872 | tf_op jit(solution)/shard_map/ppermute | solution.py:163
  4.0 14.0 %collective-permute-start.3 = (bf16[2,64,384]{2,1,0:T(8,128)(2,1)S(1)}, bf16[2,64,384]{2,1,0:T(8,128)(2,1)S(1)}, u32[]{:S(2)}, u32[]{:S(2)}) collective-permute-start(bf16[2,64,384]{2,1,0:T(8,128)(2,1)S(1)} %pad_maximum_fusion.7), channel_id=1, source_target_pairs={{0,16},{8,24},{16,0},{24,8},{1,17},{9,25},{17,1},{25,9},{2,18},{10... | collective-permute-start | bytes 294920 | tf_op jit(solution)/shard_map/ppermute | solution.py:163
  4.2 1.0 copy-start.1
  5.2 12.8 %copy-start.3 = (bf16[2048,128]{1,0:T(8,128)(2,1)}, bf16[2048,128]{1,0:T(8,128)(2,1)S(1)}, u32[]{:S(2)}) copy-start(bf16[2048,128]{1,0:T(8,128)(2,1)S(1)} %collective-permute-done.other) | copy-start | bytes 1572868
  5.2 14.7 %copy-start.5 = (f32[512]{0:T(512)S(1)}, f32[512]{0:T(512)}, u32[]{:S(2)}) copy-start(f32[512]{0:T(512)} %param.14) | copy-start | bytes 6148
  7.8 10.2 %collective-permute-start.2 = (bf16[1,128,512]{2,1,0:T(8,128)(2,1)S(1)}, bf16[1,128,512]{2,1,0:T(8,128)(2,1)}, u32[]{:S(2)}, u32[]{:S(2)}) collective-permute-start(bf16[1,128,512]{2,1,0:T(8,128)(2,1)S(1)} %fusion), channel_id=1, source_target_pairs={{0,1},{1,0},{2,3},{3,2},{4,5},{5,4},{6,7},{7,6},{8,9},{9,8},{10,11... | collective-permute-start | bytes 393224 | tf_op jit(solution)/shard_map/ppermute | solution.py:44
  18.0 2.3 %collective-permute-start.4 = (bf16[2048,128]{1,0:T(8,128)(2,1)}, bf16[2048,128]{1,0:T(8,128)(2,1)}, u32[]{:S(2)}, u32[]{:S(2)}) collective-permute-start(bf16[2048,128]{1,0:T(8,128)(2,1)} %collective-permute-done.1.mine), channel_id=1, source_target_pairs={{0,8},{8,0},{16,24},{24,16},{1,9},{9,1},{17,25},{25,17},{2,10},{10... | collective-permute-start | bytes 1572872 | tf_op jit(solution)/shard_map/ppermute | solution.py:163
  18.1 53.5 %collective-permute-start.18 = (bf16[2048,512]{1,0:T(8,128)(2,1)}, bf16[2048,512]{1,0:T(8,128)(2,1)}, u32[]{:S(2)}, u32[]{:S(2)}) collective-permute-start(bf16[2048,512]{1,0:T(8,128)(2,1)} %own.5), channel_id=1, source_target_pairs={{0,16},{8,24},{16,0},{24,8},{1,17},{9,25},{17,1},{25,9},{2,18},{10... | collective-permute-start | bytes 6291464 | tf_op jit(solution)/shard_map/ppermute | solution.py:163
  23.0 5.6 %collective-permute-start.5 = (bf16[1,128,512]{2,1,0:T(8,128)(2,1)S(1)}, bf16[1,128,512]{2,1,0:T(8,128)(2,1)S(1)}, u32[]{:S(2)}, u32[]{:S(2)}) collective-permute-start(bf16[1,128,512]{2,1,0:T(8,128)(2,1)S(1)} %fusion.1), channel_id=1, source_target_pairs={{0,1},{1,0},{2,3},{3,2},{4,5},{5,4},{6,7},{7,6},{8,9},{9,8},{10,11... | collective-permute-start | bytes 393224 | tf_op jit(solution)/shard_map/ppermute | solution.py:44
  24.9 15.8 %collective-permute-start.9 = (bf16[2,64,768]{2,1,0:T(8,128)(2,1)S(1)}, bf16[2,64,768]{2,1,0:T(8,128)(2,1)S(1)}, u32[]{:S(2)}, u32[]{:S(2)}) collective-permute-start(bf16[2,64,768]{2,1,0:T(8,128)(2,1)S(1)} %pad_maximum_fusion.6), channel_id=1, source_target_pairs={{0,4},{1,5},{2,6},{3,7},{4,0},{5,1},{6,2},{7,3},{8,12},{9,13},{10,... | collective-permute-start | bytes 589832 | tf_op jit(solution)/shard_map/ppermute | solution.py:171
  29.7 11.1 %collective-permute-start.6 = (bf16[2,32,512]{2,1,0:T(8,128)(2,1)S(1)}, bf16[2,32,512]{2,1,0:T(8,128)(2,1)S(1)}, u32[]{:S(2)}, u32[]{:S(2)}) collective-permute-start(bf16[2,32,512]{2,1,0:T(8,128)(2,1)S(1)} %get-tuple-element.76), channel_id=1, source_target_pairs={{0,2},{1,3},{2,0},{3,1},{4,6},{5,7},{6,4},{7,5},{8,10},{9,11},{10,... | collective-permute-start | bytes 196616 | tf_op jit(solution)/shard_map/ppermute | solution.py:53
  31.5 10.1 %collective-permute-start.7 = (bf16[2,32,512]{2,1,0:T(8,128)(2,1)S(1)}, bf16[2,32,512]{2,1,0:T(8,128)(2,1)S(1)}, u32[]{:S(2)}, u32[]{:S(2)}) collective-permute-start(bf16[2,32,512]{2,1,0:T(8,128)(2,1)S(1)} %get-tuple-element.78), channel_id=1, source_target_pairs={{0,4},{1,5},{2,6},{3,7},{4,0},{5,1},{6,2},{7,3},{8,12},{9,13},{10,... | collective-permute-start | bytes 196616 | tf_op jit(solution)/shard_map/ppermute | solution.py:53
  34.1 7.5 %collective-permute-start.8 = (bf16[2,32,512]{2,1,0:T(8,128)(2,1)S(1)}, bf16[2,32,512]{2,1,0:T(8,128)(2,1)S(1)}, u32[]{:S(2)}, u32[]{:S(2)}) collective-permute-start(bf16[2,32,512]{2,1,0:T(8,128)(2,1)S(1)} %get-tuple-element.77), channel_id=1, source_target_pairs={{0,6},{1,7},{2,4},{3,5},{4,2},{5,3},{6,0},{7,1},{8,14},{9,15},{10,... | collective-permute-start | bytes 196616 | tf_op jit(solution)/shard_map/ppermute | solution.py:53
  41.7 6.3 %collective-permute-start.10 = (bf16[2,32,512]{2,1,0:T(8,128)(2,1)S(1)}, bf16[2,32,512]{2,1,0:T(8,128)(2,1)S(1)}, u32[]{:S(2)}, u32[]{:S(2)}) collective-permute-start(bf16[2,32,512]{2,1,0:T(8,128)(2,1)S(1)} %add_convert_fusion.1), channel_id=1, source_target_pairs={{0,6},{1,7},{2,4},{3,5},{4,2},{5,3},{6,0},{7,1},{8,14},{9,15},{10,... | collective-permute-start | bytes 196616 | tf_op jit(solution)/shard_map/ppermute | solution.py:53
  44.7 6.4 %collective-permute-start.11 = (bf16[2,32,512]{2,1,0:T(8,128)(2,1)S(1)}, bf16[2,32,512]{2,1,0:T(8,128)(2,1)S(1)}, u32[]{:S(2)}, u32[]{:S(2)}) collective-permute-start(bf16[2,32,512]{2,1,0:T(8,128)(2,1)S(1)} %add_convert_fusion.1), channel_id=1, source_target_pairs={{0,4},{1,5},{2,6},{3,7},{4,0},{5,1},{6,2},{7,3},{8,12},{9,13},{10,... | collective-permute-start | bytes 196616 | tf_op jit(solution)/shard_map/ppermute | solution.py:53
  45.2 5.9 %collective-permute-start.12 = (bf16[2,32,512]{2,1,0:T(8,128)(2,1)S(1)}, bf16[2,32,512]{2,1,0:T(8,128)(2,1)S(1)}, u32[]{:S(2)}, u32[]{:S(2)}) collective-permute-start(bf16[2,32,512]{2,1,0:T(8,128)(2,1)S(1)} %add_convert_fusion.1), channel_id=1, source_target_pairs={{0,2},{1,3},{2,0},{3,1},{4,6},{5,7},{6,4},{7,5},{8,10},{9,11},{10,... | collective-permute-start | bytes 196616 | tf_op jit(solution)/shard_map/ppermute | solution.py:53
  46.1 8.0 %collective-permute-start.13 = (bf16[3,64,768]{2,1,0:T(8,128)(2,1)S(1)}, bf16[3,64,768]{2,1,0:T(8,128)(2,1)S(1)}, u32[]{:S(2)}, u32[]{:S(2)}) collective-permute-start(bf16[3,64,768]{2,1,0:T(8,128)(2,1)S(1)} %pad_maximum_fusion.1), channel_id=1, source_target_pairs={{0,1},{1,0},{2,3},{3,2},{4,5},{5,4},{6,7},{7,6},{8,9},{9,8},{10,11... | collective-permute-start | bytes 884744 | tf_op jit(solution)/shard_map/ppermute | solution.py:171
  51.1 17.2 %copy-start.2 = (bf16[2048,128]{1,0:T(8,128)(2,1)S(1)}, bf16[2048,128]{1,0:T(8,128)(2,1)}, u32[]{:S(2)}) copy-start(bf16[2048,128]{1,0:T(8,128)(2,1)} %mine.3) | copy-start | bytes 1572868
  51.2 17.2 %copy-start.4 = (bf16[2048,128]{1,0:T(8,128)(2,1)S(1)}, bf16[2048,128]{1,0:T(8,128)(2,1)}, u32[]{:S(2)}) copy-start(bf16[2048,128]{1,0:T(8,128)(2,1)} %copy-done.3) | copy-start | bytes 1572868
  54.2 6.5 %collective-permute-start.16 = (bf16[2,128,512]{2,1,0:T(8,128)(2,1)S(1)}, bf16[2,128,512]{2,1,0:T(8,128)(2,1)S(1)}, u32[]{:S(2)}, u32[]{:S(2)}) collective-permute-start(bf16[2,128,512]{2,1,0:T(8,128)(2,1)S(1)} %pad_maximum_fusion.2), channel_id=1, source_target_pairs={{0,1},{1,0},{2,3},{3,2},{4,5},{5,4},{6,7},{7,6},{8,9},{9,8},{10,11... | collective-permute-start | bytes 786440 | tf_op jit(solution)/shard_map/ppermute | solution.py:53
  54.8 13.5 %collective-permute-start.14 = (bf16[3,128,768]{2,1,0:T(8,128)(2,1)S(1)}, bf16[3,128,768]{2,1,0:T(8,128)(2,1)S(1)}, u32[]{:S(2)}, u32[]{:S(2)}) collective-permute-start(bf16[3,128,768]{2,1,0:T(8,128)(2,1)S(1)} %pad_maximum_fusion.one), channel_id=1, source_target_pairs={{0,2},{1,3},{2,0},{3,1},{4,6},{5,7},{6,4},{7,5},{8,10},{9,11},{10,... | collective-permute-start | bytes 1769480 | tf_op jit(solution)/shard_map/ppermute | solution.py:218
  60.8 13.1 %collective-permute-start.17 = (bf16[2,128,512]{2,1,0:T(8,128)(2,1)S(1)}, bf16[2,128,512]{2,1,0:T(8,128)(2,1)S(1)}, u32[]{:S(2)}, u32[]{:S(2)}) collective-permute-start(bf16[2,128,512]{2,1,0:T(8,128)(2,1)S(1)} %pad_maximum_fusion.3), channel_id=1, source_target_pairs={{0,16},{8,24},{16,0},{24,8},{1,17},{9,25},{17,1},{25,9},{2,18},{10... | collective-permute-start | bytes 786440 | tf_op jit(solution)/shard_map/ppermute | solution.py:163
  70.0 3.9 %collective-permute-start.15 = (f32[4,768]{1,0:T(4,128)S(1)}, f32[4,768]{1,0:T(4,128)S(1)}, u32[]{:S(2)}, u32[]{:S(2)}) collective-permute-start(f32[4,768]{1,0:T(4,128)S(1)} %get-tuple-element.38), channel_id=1, source_target_pairs={{0,16},{8,24},{16,0},{24,8},{1,17},{9,25},{17,1},{25,9},{2,18},{10... | collective-permute-start | bytes 36872 | tf_op jit(solution)/shard_map/ppermute | solution.py:163
  73.9 4.1 %copy-start.6 = (f32[4]{0:T(128)S(1)}, f32[4]{0:T(128)}, u32[]{:S(2)}) copy-start(f32[4]{0:T(128)} %occ.3) | copy-start | bytes 52
  76.1 2.0 %collective-permute-start.19 = (bf16[2048,128]{1,0:T(8,128)(2,1)S(1)}, bf16[2048,128]{1,0:T(8,128)(2,1)S(1)}, u32[]{:S(2)}, u32[]{:S(2)}) collective-permute-start(bf16[2048,128]{1,0:T(8,128)(2,1)S(1)} %get-tuple-element.45), channel_id=1, source_target_pairs={{0,8},{8,0},{16,24},{24,16},{1,9},{9,1},{17,25},{25,17},{2,10},{10... | collective-permute-start | bytes 1572872 | tf_op jit(solution)/shard_map/ppermute | solution.py:163
  79.1 2.0 %collective-permute-start.20 = (bf16[128,2048]{1,0:T(8,128)(2,1)S(1)}, bf16[128,2048]{1,0:T(8,128)(2,1)S(1)}, u32[]{:S(2)}, u32[]{:S(2)}) collective-permute-start(bf16[128,2048]{1,0:T(8,128)(2,1)S(1)} %shard_map.87.mine), channel_id=1, source_target_pairs={{0,8},{8,0},{16,24},{24,16},{1,9},{9,1},{17,25},{25,17},{2,10},{10... | collective-permute-start | bytes 1572872 | tf_op jit(solution)/shard_map/ppermute | solution.py:163
  83.2 8.4 %collective-permute-start.22 = (bf16[2,128,512]{2,1,0:T(8,128)(2,1)S(1)}, bf16[2,128,512]{2,1,0:T(8,128)(2,1)S(1)}, u32[]{:S(2)}, u32[]{:S(2)}) collective-permute-start(bf16[2,128,512]{2,1,0:T(8,128)(2,1)S(1)} %dynamic-slice_convert_fusion), channel_id=1, source_target_pairs={{0,1},{1,0},{2,3},{3,2},{4,5},{5,4},{6,7},{7,6},{8,9},{9,8},{10,11... | collective-permute-start | bytes 786440 | tf_op jit(solution)/shard_map/ppermute | solution.py:44
  91.7 4.5 %collective-permute-start.23 = (bf16[2,32,512]{2,1,0:T(8,128)(2,1)S(1)}, bf16[2,32,512]{2,1,0:T(8,128)(2,1)S(1)}, u32[]{:S(2)}, u32[]{:S(2)}) collective-permute-start(bf16[2,32,512]{2,1,0:T(8,128)(2,1)S(1)} %get-tuple-element.65), channel_id=1, source_target_pairs={{0,2},{1,3},{2,0},{3,1},{4,6},{5,7},{6,4},{7,5},{8,10},{9,11},{10,... | collective-permute-start | bytes 196616 | tf_op jit(solution)/shard_map/ppermute | solution.py:53
  93.5 6.7 %collective-permute-start.24 = (bf16[2,32,512]{2,1,0:T(8,128)(2,1)S(1)}, bf16[2,32,512]{2,1,0:T(8,128)(2,1)S(1)}, u32[]{:S(2)}, u32[]{:S(2)}) collective-permute-start(bf16[2,32,512]{2,1,0:T(8,128)(2,1)S(1)} %get-tuple-element.67), channel_id=1, source_target_pairs={{0,4},{1,5},{2,6},{3,7},{4,0},{5,1},{6,2},{7,3},{8,12},{9,13},{10,... | collective-permute-start | bytes 196616 | tf_op jit(solution)/shard_map/ppermute | solution.py:53
  95.0 6.2 %collective-permute-start.25 = (bf16[2,32,512]{2,1,0:T(8,128)(2,1)S(1)}, bf16[2,32,512]{2,1,0:T(8,128)(2,1)S(1)}, u32[]{:S(2)}, u32[]{:S(2)}) collective-permute-start(bf16[2,32,512]{2,1,0:T(8,128)(2,1)S(1)} %get-tuple-element.66), channel_id=1, source_target_pairs={{0,6},{1,7},{2,4},{3,5},{4,2},{5,3},{6,0},{7,1},{8,14},{9,15},{10,... | collective-permute-start | bytes 196616 | tf_op jit(solution)/shard_map/ppermute | solution.py:53
  101.2 6.2 %collective-permute-start.26 = (bf16[2,32,512]{2,1,0:T(8,128)(2,1)S(1)}, bf16[2,32,512]{2,1,0:T(8,128)(2,1)S(1)}, u32[]{:S(2)}, u32[]{:S(2)}) collective-permute-start(bf16[2,32,512]{2,1,0:T(8,128)(2,1)S(1)} %add_convert_fusion), channel_id=1, source_target_pairs={{0,6},{1,7},{2,4},{3,5},{4,2},{5,3},{6,0},{7,1},{8,14},{9,15},{10,... | collective-permute-start | bytes 196616 | tf_op jit(solution)/shard_map/ppermute | solution.py:53
  103.4 5.7 %collective-permute-start.27 = (bf16[2,32,512]{2,1,0:T(8,128)(2,1)S(1)}, bf16[2,32,512]{2,1,0:T(8,128)(2,1)S(1)}, u32[]{:S(2)}, u32[]{:S(2)}) collective-permute-start(bf16[2,32,512]{2,1,0:T(8,128)(2,1)S(1)} %add_convert_fusion), channel_id=1, source_target_pairs={{0,4},{1,5},{2,6},{3,7},{4,0},{5,1},{6,2},{7,3},{8,12},{9,13},{10,... | collective-permute-start | bytes 196616 | tf_op jit(solution)/shard_map/ppermute | solution.py:53
  103.8 5.2 %collective-permute-start.28 = (bf16[2,32,512]{2,1,0:T(8,128)(2,1)S(1)}, bf16[2,32,512]{2,1,0:T(8,128)(2,1)S(1)}, u32[]{:S(2)}, u32[]{:S(2)}) collective-permute-start(bf16[2,32,512]{2,1,0:T(8,128)(2,1)S(1)} %add_convert_fusion), channel_id=1, source_target_pairs={{0,2},{1,3},{2,0},{3,1},{4,6},{5,7},{6,4},{7,5},{8,10},{9,11},{10,... | collective-permute-start | bytes 196616 | tf_op jit(solution)/shard_map/ppermute | solution.py:53
  105.7 5.0 %collective-permute-start.21 = (f32[4,768]{1,0:T(4,128)S(1)}, f32[4,768]{1,0:T(4,128)S(1)}, u32[]{:S(2)}, u32[]{:S(2)}) collective-permute-start(f32[4,768]{1,0:T(4,128)S(1)} %get-tuple-element.49), channel_id=1, source_target_pairs={{0,16},{8,24},{16,0},{24,8},{1,17},{9,25},{17,1},{25,9},{2,18},{10... | collective-permute-start | bytes 36872 | tf_op jit(solution)/shard_map/ppermute | solution.py:163
  109.1 6.4 %collective-permute-start.29 = (bf16[2,128,512]{2,1,0:T(8,128)(2,1)S(1)}, bf16[2,128,512]{2,1,0:T(8,128)(2,1)S(1)}, u32[]{:S(2)}, u32[]{:S(2)}) collective-permute-start(bf16[2,128,512]{2,1,0:T(8,128)(2,1)S(1)} %pad_maximum_fusion.5.one), channel_id=1, source_target_pairs={{0,1},{1,0},{2,3},{3,2},{4,5},{5,4},{6,7},{7,6},{8,9},{9,8},{10,11... | collective-permute-start | bytes 786440 | tf_op jit(solution)/shard_map/ppermute | solution.py:53
  117.7 2.0 %collective-permute-start.30 = (bf16[2048,128]{1,0:T(8,128)(2,1)S(1)}, bf16[2048,128]{1,0:T(8,128)(2,1)S(1)}, u32[]{:S(2)}, u32[]{:S(2)}) collective-permute-start(bf16[2048,128]{1,0:T(8,128)(2,1)S(1)} %get-tuple-element.52), channel_id=1, source_target_pairs={{0,8},{8,0},{16,24},{24,16},{1,9},{9,1},{17,25},{25,17},{2,10},{10... | collective-permute-start | bytes 1572872 | tf_op jit(solution)/shard_map/ppermute | solution.py:163

commit v7 on v6

--- a/solution.py
+++ b/solution.py
@@ -125,15 +125,18 @@
         middle[i : i + 1] = total
 
 
-def gram_kernel(mine, other, left, right, factors, gram, middle, amps):
+def gram_kernel(side, mine, other, left, right, factors, gram, *middle):
     width, nvirt = mine.shape[0], left.shape[0]
-    amps[:width] = mine[...]
-    amps[width:] = other[...]
-    for r in range(2):
-        gram[r] = dot(amps[...], factors[r], 1, 0)
-    for i in range(middle.shape[0]):
-        proj = dot(amps[:, i * nvirt : (i + 1) * nvirt], left[...], 1, 0)
-        middle[i : i + 1] = jnp.sum(proj * right[...].astype(F32), axis=0, keepdims=True)
+    for r, amps in enumerate((mine, other)):
+        gram[0, r * width : (r + 1) * width] = dot(amps[...], factors[side], 1, 0)
+    for out in middle:
+        for i in range(out.shape[0]):
+            total = None
+            for r, amps in enumerate((mine, other)):
+                proj = dot(amps[:, i * nvirt : (i + 1) * nvirt], left[...], 1, 0)
+                term = proj * right[r * width : (r + 1) * width].astype(F32)
+                total = term if total is None else total + term
+            out[i : i + 1] = jnp.sum(total, axis=0, keepdims=True)
 
 
 def first_gram_kernel(mine, other, own, gram):
@@ -272,18 +275,22 @@
             compiler_params=PARAMS,
         )(occ_energy, pivot_energy, mine, got, coulomb_block, vir, vir_row)
         if not last:
-            gram, middle = pl.pallas_call(
-                gram_kernel,
-                out_shape=(
-                    jax.ShapeDtypeStruct((2, 2 * width, naux), F32),
-                    jax.ShapeDtypeStruct((nocc, cols), F32),
-                ),
-                in_specs=[VMEM] * 5,
-                out_specs=(VMEM, VMEM),
-                scratch_shapes=[pltpu.VMEM((2 * width, rows), BF)],
-                compiler_params=PARAMS,
-            )(new, over(new, 1), left, right, factors)
-            gram = all_reduce(*fold(gram, n_pair), n_pair)
+            amps = (new, over(new, 1))
+            folded = []
+            for side in range(2):
+                shape = (jax.ShapeDtypeStruct((1, 2 * width, naux), F32),)
+                if side:
+                    shape += (jax.ShapeDtypeStruct((nocc, cols), F32),)
+                terms = pl.pallas_call(
+                    functools.partial(gram_kernel, side),
+                    out_shape=shape,
+                    in_specs=[VMEM] * 5,
+                    out_specs=(VMEM,) * len(shape),
+                    compiler_params=PARAMS,
+                )(*amps, left, right, factors)
+                folded.append(fold(terms[0], n_pair))
+            middle = terms[1]
+            gram = all_reduce(*(jnp.concatenate(a, axis=0) for a in zip(*folded)), n_pair)
     return new
 
 

time: 122 us -> 120 us (0.984)
  waiting for transfers between devices: 58.3 us -> 55.7 us
    ppermute x3 -> x4, waiting for transfers between devices: 7.96 us -> 5.82 us  [fold(): return (mine, lax.ppermute(theirs.astype(BF), 'pair', xor(n, 1)))]
    ppermute x3 -> x4, starting transfers between devices: 5.31 us -> 5.9 us  [fold(): return (mine, lax.ppermute(theirs.astype(BF), 'pair', xor(n, 1)))]
  transfers between devices with their start and end apart: 31 -> 32, of which waited for: 19 -> 21; matrix products, arithmetic and copies ran while one was open for 2% -> 2% of each run, Pallas kernels for 7% -> 9%
where the time goes in v7:
time: 120 us
  waiting for transfers between devices  55.7 us (46%)
  starting transfers between devices  40.7 us (34%)
  Pallas kernels  18.4 us (15%)
  other arithmetic  2.48 us (2%)
  local copies, waits for them, and re-layouts  1.49 us (1%)
    ppermute x14, waiting for transfers between devices, send(): return lax.ppermute(a, 'pair', xor(n, s))  21.1 us
    ppermute x14, starting transfers between devices, send(): return lax.ppermute(a, 'pair', xor(n, s))  20.1 us
    ppermute x11, waiting for transfers between devices, over(): return lax.ppermute(a, 'aux', xor(n_aux, s))  13.4 us
    ppermute x11, starting transfers between devices, over(): return lax.ppermute(a, 'aux', xor(n_aux, s))  10.1 us
    ppermute x2, waiting for transfers between devices, other_rows(): got = lax.ppermute(fac, 'pair', xor(n_pair, bit))  9.47 us
    ppermute x1, waiting for transfers between devices, beside(): got = lax.ppermute(fac, 'pair', xor(n_pair, n_pair // 4))  5.92 us
    ppermute x4, starting transfers between devices, fold(): return (mine, lax.ppermute(theirs.astype(BF), 'pair', xor(n, 1)))  5.9 us
    ppermute x4, waiting for transfers between devices, fold(): return (mine, lax.ppermute(theirs.astype(BF), 'pair', xor(n, 1)))  5.82 us
  transfers between devices with their start and end apart: 32, of which 21 were waited for; matrix products, arithmetic and copies ran while one was open for 2% of the time, Pallas kernels for 9%

profile of v7, /device:TPU:0, one launch (start us, length us, event | category | flops | bytes accessed | tf_op | source)
XLA Modules:
  0.0 119.8 jit_solution(447231804454106385)
XLA Ops:
  0.5 2.6 %collective-permute-start.1 = (bf16[2048,128]{1,0:T(8,128)(2,1)}, bf16[2048,128]{1,0:T(8,128)(2,1)}, u32[]{:S(2)}, u32[]{:S(2)}) collective-permute-start(bf16[2048,128]{1,0:T(8,128)(2,1)} %mine.3), channel_id=1, source_target_pairs={{0,16},{8,24},{16,0},{24,8},{1,17},{9,25},{17,1},{25,9},{2,18},{10... | collective-permute-start | bytes 1572872 | tf_op jit(solution)/shard_map/ppermute | solution.py:166
  4.2 1.0 copy-done.1
  5.2 2.5 %shard_map.82 = f32[256,512]{1,0:T(8,128)S(1)} custom-call(bf16[2048,128]{1,0:T(8,128)(2,1)S(1)} %copy-done.1, bf16[2048,128]{1,0:T(8,128)(2,1)S(1)} %collective-permute-done.other, bf16[2048,512]{1,0:T(8,128)(2,1)} %own.5), custom_call_target="tpu_custom_call" | custom-call | tf_op jit(solution)/shard_map/pallas_call | solution.py:184
  7.8 1.9 %collective-permute-start.2 = (bf16[1,128,512]{2,1,0:T(8,128)(2,1)S(1)}, bf16[1,128,512]{2,1,0:T(8,128)(2,1)}, u32[]{:S(2)}, u32[]{:S(2)}) collective-permute-start(bf16[1,128,512]{2,1,0:T(8,128)(2,1)S(1)} %fusion), channel_id=1, source_target_pairs={{0,1},{1,0},{2,3},{3,2},{4,5},{5,4},{6,7},{7,6},{8,9},{9,8},{10,11... | collective-permute-start | bytes 393224 | tf_op jit(solution)/shard_map/ppermute | solution.py:44
  9.7 8.2 %collective-permute-done.3 = bf16[2,64,384]{2,1,0:T(8,128)(2,1)S(1)} collective-permute-done((bf16[2,64,384]{2,1,0:T(8,128)(2,1)S(1)}, bf16[2,64,384]{2,1,0:T(8,128)(2,1)S(1)}, u32[]{:S(2)}, u32[]{:S(2)}) %collective-permute-start.3) | collective-permute-done | bytes 98336 | tf_op jit(solution)/shard_map/ppermute | solution.py:166
  18.1 1.8 %collective-permute-start.18 = (bf16[2048,512]{1,0:T(8,128)(2,1)}, bf16[2048,512]{1,0:T(8,128)(2,1)}, u32[]{:S(2)}, u32[]{:S(2)}) collective-permute-start(bf16[2048,512]{1,0:T(8,128)(2,1)} %own.5), channel_id=1, source_target_pairs={{0,16},{8,24},{16,0},{24,8},{1,17},{9,25},{17,1},{25,9},{2,18},{10... | collective-permute-start | bytes 6291464 | tf_op jit(solution)/shard_map/ppermute | solution.py:166
  20.3 2.7 %shard_map.83 = f32[256,512]{1,0:T(8,128)S(1)} custom-call(bf16[2048,128]{1,0:T(8,128)(2,1)} %collective-permute-done.1.mine, bf16[2048,128]{1,0:T(8,128)(2,1)} %collective-permute-done.4.other, bf16[2048,512]{1,0:T(8,128)(2,1)} %own.5), custom_call_target="tpu_custom_call" | custom-call | tf_op jit(solution)/shard_map/pallas_call | solution.py:184
  23.0 1.8 %collective-permute-start.5 = (bf16[1,128,512]{2,1,0:T(8,128)(2,1)S(1)}, bf16[1,128,512]{2,1,0:T(8,128)(2,1)S(1)}, u32[]{:S(2)}, u32[]{:S(2)}) collective-permute-start(bf16[1,128,512]{2,1,0:T(8,128)(2,1)S(1)} %fusion.1), channel_id=1, source_target_pairs={{0,1},{1,0},{2,3},{3,2},{4,5},{5,4},{6,7},{7,6},{8,9},{9,8},{10,11... | collective-permute-start | bytes 393224 | tf_op jit(solution)/shard_map/ppermute | solution.py:44
  24.9 2.6 %collective-permute-start.9 = (bf16[2,64,768]{2,1,0:T(8,128)(2,1)S(1)}, bf16[2,64,768]{2,1,0:T(8,128)(2,1)S(1)}, u32[]{:S(2)}, u32[]{:S(2)}) collective-permute-start(bf16[2,64,768]{2,1,0:T(8,128)(2,1)S(1)} %pad_maximum_fusion.6), channel_id=1, source_target_pairs={{0,4},{1,5},{2,6},{3,7},{4,0},{5,1},{6,2},{7,3},{8,12},{9,13},{10,... | collective-permute-start | bytes 589832 | tf_op jit(solution)/shard_map/ppermute | solution.py:174
  27.5 1.1 collective-permute-done.5
  28.6 1.0 fusion.3
  29.7 1.9 %collective-permute-start.6 = (bf16[2,32,512]{2,1,0:T(8,128)(2,1)S(1)}, bf16[2,32,512]{2,1,0:T(8,128)(2,1)S(1)}, u32[]{:S(2)}, u32[]{:S(2)}) collective-permute-start(bf16[2,32,512]{2,1,0:T(8,128)(2,1)S(1)} %get-tuple-element.76), channel_id=1, source_target_pairs={{0,2},{1,3},{2,0},{3,1},{4,6},{5,7},{6,4},{7,5},{8,10},{9,11},{10,... | collective-permute-start | bytes 196616 | tf_op jit(solution)/shard_map/ppermute | solution.py:53
  31.5 2.6 %collective-permute-start.7 = (bf16[2,32,512]{2,1,0:T(8,128)(2,1)S(1)}, bf16[2,32,512]{2,1,0:T(8,128)(2,1)S(1)}, u32[]{:S(2)}, u32[]{:S(2)}) collective-permute-start(bf16[2,32,512]{2,1,0:T(8,128)(2,1)S(1)} %get-tuple-element.78), channel_id=1, source_target_pairs={{0,4},{1,5},{2,6},{3,7},{4,0},{5,1},{6,2},{7,3},{8,12},{9,13},{10,... | collective-permute-start | bytes 196616 | tf_op jit(solution)/shard_map/ppermute | solution.py:53
  34.2 6.5 %collective-permute-done.9 = bf16[2,64,768]{2,1,0:T(8,128)(2,1)S(1)} collective-permute-done((bf16[2,64,768]{2,1,0:T(8,128)(2,1)S(1)}, bf16[2,64,768]{2,1,0:T(8,128)(2,1)S(1)}, u32[]{:S(2)}, u32[]{:S(2)}) %collective-permute-start.9) | collective-permute-done | bytes 196640 | tf_op jit(solution)/shard_map/ppermute | solution.py:174
  41.7 3.0 %collective-permute-start.10 = (bf16[2,32,512]{2,1,0:T(8,128)(2,1)S(1)}, bf16[2,32,512]{2,1,0:T(8,128)(2,1)S(1)}, u32[]{:S(2)}, u32[]{:S(2)}) collective-permute-start(bf16[2,32,512]{2,1,0:T(8,128)(2,1)S(1)} %add_convert_fusion.1), channel_id=1, source_target_pairs={{0,6},{1,7},{2,4},{3,5},{4,2},{5,3},{6,0},{7,1},{8,14},{9,15},{10,... | collective-permute-start | bytes 196616 | tf_op jit(solution)/shard_map/ppermute | solution.py:53
  45.2 1.0 collective-permute-start.12
  46.6 1.4 %collective-permute-done.10 = bf16[2,32,512]{2,1,0:T(8,128)(2,1)S(1)} collective-permute-done((bf16[2,32,512]{2,1,0:T(8,128)(2,1)S(1)}, bf16[2,32,512]{2,1,0:T(8,128)(2,1)S(1)}, u32[]{:S(2)}, u32[]{:S(2)}) %collective-permute-start.10) | collective-permute-done | bytes 65568 | tf_op jit(solution)/shard_map/ppermute | solution.py:53
  48.0 3.1 %collective-permute-done.11 = bf16[2,32,512]{2,1,0:T(8,128)(2,1)S(1)} collective-permute-done((bf16[2,32,512]{2,1,0:T(8,128)(2,1)S(1)}, bf16[2,32,512]{2,1,0:T(8,128)(2,1)S(1)}, u32[]{:S(2)}, u32[]{:S(2)}) %collective-permute-start.11) | collective-permute-done | bytes 65568 | tf_op jit(solution)/shard_map/ppermute | solution.py:53
  51.2 3.0 %collective-permute-done.13 = bf16[3,64,768]{2,1,0:T(8,128)(2,1)S(1)} collective-permute-done((bf16[3,64,768]{2,1,0:T(8,128)(2,1)S(1)}, bf16[3,64,768]{2,1,0:T(8,128)(2,1)S(1)}, u32[]{:S(2)}, u32[]{:S(2)}) %collective-permute-start.13) | collective-permute-done | bytes 294944 | tf_op jit(solution)/shard_map/ppermute | solution.py:174
  54.8 1.5 %collective-permute-start.14 = (bf16[3,128,768]{2,1,0:T(8,128)(2,1)S(1)}, bf16[3,128,768]{2,1,0:T(8,128)(2,1)S(1)}, u32[]{:S(2)}, u32[]{:S(2)}) collective-permute-start(bf16[3,128,768]{2,1,0:T(8,128)(2,1)S(1)} %pad_maximum_fusion.one), channel_id=1, source_target_pairs={{0,2},{1,3},{2,0},{3,1},{4,6},{5,7},{6,4},{7,5},{8,10},{9,11},{10,... | collective-permute-start | bytes 1769480 | tf_op jit(solution)/shard_map/ppermute | solution.py:221
  56.5 4.3 %collective-permute-done.16 = bf16[2,128,512]{2,1,0:T(8,128)(2,1)S(1)} collective-permute-done((bf16[2,128,512]{2,1,0:T(8,128)(2,1)S(1)}, bf16[2,128,512]{2,1,0:T(8,128)(2,1)S(1)}, u32[]{:S(2)}, u32[]{:S(2)}) %collective-permute-start.16) | collective-permute-done | bytes 262176 | tf_op jit(solution)/shard_map/ppermute | solution.py:53
  60.8 1.6 %collective-permute-start.17 = (bf16[2,128,512]{2,1,0:T(8,128)(2,1)S(1)}, bf16[2,128,512]{2,1,0:T(8,128)(2,1)S(1)}, u32[]{:S(2)}, u32[]{:S(2)}) collective-permute-start(bf16[2,128,512]{2,1,0:T(8,128)(2,1)S(1)} %pad_maximum_fusion.3), channel_id=1, source_target_pairs={{0,16},{8,24},{16,0},{24,8},{1,17},{9,25},{17,1},{25,9},{2,18},{10... | collective-permute-start | bytes 786440 | tf_op jit(solution)/shard_map/ppermute | solution.py:166
  62.4 5.9 %collective-permute-done.14.two = bf16[3,128,768]{2,1,0:T(8,128)(2,1)S(1)} collective-permute-done((bf16[3,128,768]{2,1,0:T(8,128)(2,1)S(1)}, bf16[3,128,768]{2,1,0:T(8,128)(2,1)S(1)}, u32[]{:S(2)}, u32[]{:S(2)}) %collective-permute-start.14) | collective-permute-done | bytes 589856 | tf_op jit(solution)/shard_map/ppermute | solution.py:221
  68.4 1.7 %shard_map.84 = (bf16[512,768]{1,0:T(8,128)(2,1)S(1)}, bf16[256,768]{1,0:T(8,128)(2,1)S(1)}, f32[4,768]{1,0:T(4,128)S(1)}) custom-call(bf16[2048,128]{1,0:T(8,128)(2,1)S(1)} %copy-done.2, bf16[2048,128]{1,0:T(8,128)(2,1)S(1)} %copy-done.4, s32[2]{0:T(128)S(1)} %pad_add_fusion.places, bf16[3,128,768]{2,1,0:T(8,128)(2,1)S(1)} %pad_maximum_fusion.one, ...), custom_call_target="tpu_custom_call" | custom-call | flops 3000000000 | bytes 9000000 | tf_op jit(solution)/shard_map/pallas_call | solution.py:223
  70.0 1.6 %collective-permute-start.15 = (f32[4,768]{1,0:T(4,128)S(1)}, f32[4,768]{1,0:T(4,128)S(1)}, u32[]{:S(2)}, u32[]{:S(2)}) collective-permute-start(f32[4,768]{1,0:T(4,128)S(1)} %get-tuple-element.38), channel_id=1, source_target_pairs={{0,16},{8,24},{16,0},{24,8},{1,17},{9,25},{17,1},{25,9},{2,18},{10... | collective-permute-start | bytes 36872 | tf_op jit(solution)/shard_map/ppermute | solution.py:166
  71.6 2.2 %shard_map.85.factors = bf16[2,2048,512]{2,1,0:T(8,128)(2,1)S(1)} custom-call(bf16[2048,512]{1,0:T(8,128)(2,1)} %own.5, bf16[2048,512]{1,0:T(8,128)(2,1)} %collective-permute-done.18.far), custom_call_target="tpu_custom_call" | custom-call | tf_op jit(solution)/shard_map/pallas_call | solution.py:236
  73.9 2.1 %shard_map.86 = (f32[2048,128]{1,0:T(8,128)S(1)}, bf16[2048,128]{1,0:T(8,128)(2,1)S(1)}) custom-call(s32[1]{0:T(128)} %bitcast.side, f32[4,768]{1,0:T(4,128)S(1)} %maximum_add_fusion.2.middle, bf16[512,768]{1,0:T(8,128)(2,1)S(1)} %get-tuple-element.39.left, bf16[256,768]{1,0:T(8,128)(2,1)S(1)} %get-tuple-element.40.right, ...), custom_call_target="tpu_custom_call" | custom-call | tf_op jit(solution)/shard_map/pallas_call | solution.py:258
  76.8 1.2 %collective-permute-done.19.got = bf16[2048,128]{1,0:T(8,128)(2,1)S(1)} collective-permute-done((bf16[2048,128]{1,0:T(8,128)(2,1)S(1)}, bf16[2048,128]{1,0:T(8,128)(2,1)S(1)}, u32[]{:S(2)}, u32[]{:S(2)}) %collective-permute-start.19) | collective-permute-done | bytes 524320 | tf_op jit(solution)/shard_map/ppermute | solution.py:166
  78.1 1.0 shard_map.87.mine
  79.3 1.8 %collective-permute-done.20.other = bf16[128,2048]{1,0:T(8,128)(2,1)S(1)} collective-permute-done((bf16[128,2048]{1,0:T(8,128)(2,1)S(1)}, bf16[128,2048]{1,0:T(8,128)(2,1)S(1)}, u32[]{:S(2)}, u32[]{:S(2)}) %collective-permute-start.20) | collective-permute-done | bytes 524320 | tf_op jit(solution)/shard_map/ppermute | solution.py:166
  81.8 1.6 %collective-permute-start.22 = (bf16[1,128,512]{2,1,0:T(8,128)(2,1)S(1)}, bf16[1,128,512]{2,1,0:T(8,128)(2,1)S(1)}, u32[]{:S(2)}, u32[]{:S(2)}) collective-permute-start(bf16[1,128,512]{2,1,0:T(8,128)(2,1)S(1)} %dynamic-slice_convert_fusion.1), channel_id=1, source_target_pairs={{0,1},{1,0},{2,3},{3,2},{4,5},{5,4},{6,7},{7,6},{8,9},{9,8},{10,11... | collective-permute-start | bytes 393224 | tf_op jit(solution)/shard_map/ppermute | solution.py:44
  83.4 1.6 %shard_map.88 = (f32[1,256,512]{2,1,0:T(8,128)S(1)}, f32[4,768]{1,0:T(4,128)S(1)}) custom-call(bf16[128,2048]{1,0:T(8,128)(2,1)S(1)} %shard_map.87.mine, bf16[128,2048]{1,0:T(8,128)(2,1)S(1)} %collective-permute-done.20.other, bf16[512,768]{1,0:T(8,128)(2,1)S(1)} %get-tuple-element.39.left, bf16[256,768]{1,0:T(8,128)(2,1)S(1)} %get-tuple-element.40.right, ...), custom_call_target="tpu_custom_call" | custom-call | tf_op jit(solution)/shard_map/pallas_call | solution.py:284
  85.7 1.7 %collective-permute-done.22 = bf16[1,128,512]{2,1,0:T(8,128)(2,1)S(1)} collective-permute-done((bf16[1,128,512]{2,1,0:T(8,128)(2,1)S(1)}, bf16[1,128,512]{2,1,0:T(8,128)(2,1)S(1)}, u32[]{:S(2)}, u32[]{:S(2)}) %collective-permute-start.22) | collective-permute-done | bytes 131104 | tf_op jit(solution)/shard_map/ppermute | solution.py:44
  87.4 3.0 %collective-permute-done.23 = bf16[1,128,512]{2,1,0:T(8,128)(2,1)S(1)} collective-permute-done((bf16[1,128,512]{2,1,0:T(8,128)(2,1)S(1)}, bf16[1,128,512]{2,1,0:T(8,128)(2,1)S(1)}, u32[]{:S(2)}, u32[]{:S(2)}) %collective-permute-start.23) | collective-permute-done | bytes 131104 | tf_op jit(solution)/shard_map/ppermute | solution.py:44
  90.5 1.8 %collective-permute-start.24 = (bf16[2,32,512]{2,1,0:T(8,128)(2,1)S(1)}, bf16[2,32,512]{2,1,0:T(8,128)(2,1)S(1)}, u32[]{:S(2)}, u32[]{:S(2)}) collective-permute-start(bf16[2,32,512]{2,1,0:T(8,128)(2,1)S(1)} %get-tuple-element.65), channel_id=1, source_target_pairs={{0,2},{1,3},{2,0},{3,1},{4,6},{5,7},{6,4},{7,5},{8,10},{9,11},{10,... | collective-permute-start | bytes 196616 | tf_op jit(solution)/shard_map/ppermute | solution.py:53
  92.4 1.5 %collective-permute-start.25 = (bf16[2,32,512]{2,1,0:T(8,128)(2,1)S(1)}, bf16[2,32,512]{2,1,0:T(8,128)(2,1)S(1)}, u32[]{:S(2)}, u32[]{:S(2)}) collective-permute-start(bf16[2,32,512]{2,1,0:T(8,128)(2,1)S(1)} %get-tuple-element.67), channel_id=1, source_target_pairs={{0,4},{1,5},{2,6},{3,7},{4,0},{5,1},{6,2},{7,3},{8,12},{9,13},{10,... | collective-permute-start | bytes 196616 | tf_op jit(solution)/shard_map/ppermute | solution.py:53
  93.8 1.2 collective-permute-start.26
  95.3 3.5 %collective-permute-done.25 = bf16[2,32,512]{2,1,0:T(8,128)(2,1)S(1)} collective-permute-done((bf16[2,32,512]{2,1,0:T(8,128)(2,1)S(1)}, bf16[2,32,512]{2,1,0:T(8,128)(2,1)S(1)}, u32[]{:S(2)}, u32[]{:S(2)}) %collective-permute-start.25) | collective-permute-done | bytes 65568 | tf_op jit(solution)/shard_map/ppermute | solution.py:53
  98.8 1.2 collective-permute-done.26
  100.0 1.8 %collective-permute-start.27 = (bf16[2,32,512]{2,1,0:T(8,128)(2,1)S(1)}, bf16[2,32,512]{2,1,0:T(8,128)(2,1)S(1)}, u32[]{:S(2)}, u32[]{:S(2)}) collective-permute-start(bf16[2,32,512]{2,1,0:T(8,128)(2,1)S(1)} %add_convert_fusion), channel_id=1, source_target_pairs={{0,6},{1,7},{2,4},{3,5},{4,2},{5,3},{6,0},{7,1},{8,14},{9,15},{10,... | collective-permute-start | bytes 196616 | tf_op jit(solution)/shard_map/ppermute | solution.py:53
  102.3 2.2 %collective-permute-start.29 = (bf16[2,32,512]{2,1,0:T(8,128)(2,1)S(1)}, bf16[2,32,512]{2,1,0:T(8,128)(2,1)S(1)}, u32[]{:S(2)}, u32[]{:S(2)}) collective-permute-start(bf16[2,32,512]{2,1,0:T(8,128)(2,1)S(1)} %add_convert_fusion), channel_id=1, source_target_pairs={{0,2},{1,3},{2,0},{3,1},{4,6},{5,7},{6,4},{7,5},{8,10},{9,11},{10,... | collective-permute-start | bytes 196616 | tf_op jit(solution)/shard_map/ppermute | solution.py:53
  104.5 1.4 %collective-permute-start.21 = (f32[4,768]{1,0:T(4,128)S(1)}, f32[4,768]{1,0:T(4,128)S(1)}, u32[]{:S(2)}, u32[]{:S(2)}) collective-permute-start(f32[4,768]{1,0:T(4,128)S(1)} %get-tuple-element.49), channel_id=1, source_target_pairs={{0,16},{8,24},{16,0},{24,8},{1,17},{9,25},{17,1},{25,9},{2,18},{10... | collective-permute-start | bytes 36872 | tf_op jit(solution)/shard_map/ppermute | solution.py:166
  106.2 1.4 %collective-permute-done.28 = bf16[2,32,512]{2,1,0:T(8,128)(2,1)S(1)} collective-permute-done((bf16[2,32,512]{2,1,0:T(8,128)(2,1)S(1)}, bf16[2,32,512]{2,1,0:T(8,128)(2,1)S(1)}, u32[]{:S(2)}, u32[]{:S(2)}) %collective-permute-start.28) | collective-permute-done | bytes 65568 | tf_op jit(solution)/shard_map/ppermute | solution.py:53
  107.6 1.7 %collective-permute-start.30 = (bf16[2,128,512]{2,1,0:T(8,128)(2,1)S(1)}, bf16[2,128,512]{2,1,0:T(8,128)(2,1)S(1)}, u32[]{:S(2)}, u32[]{:S(2)}) collective-permute-start(bf16[2,128,512]{2,1,0:T(8,128)(2,1)S(1)} %pad_maximum_fusion.5.one), channel_id=1, source_target_pairs={{0,1},{1,0},{2,3},{3,2},{4,5},{5,4},{6,7},{7,6},{8,9},{9,8},{10,11... | collective-permute-start | bytes 786440 | tf_op jit(solution)/shard_map/ppermute | solution.py:53
  109.3 4.7 %collective-permute-done.30.two = bf16[2,128,512]{2,1,0:T(8,128)(2,1)S(1)} collective-permute-done((bf16[2,128,512]{2,1,0:T(8,128)(2,1)S(1)}, bf16[2,128,512]{2,1,0:T(8,128)(2,1)S(1)}, u32[]{:S(2)}, u32[]{:S(2)}) %collective-permute-start.30) | collective-permute-done | bytes 262176 | tf_op jit(solution)/shard_map/ppermute | solution.py:53
  114.1 2.1 %shard_map.90 = (f32[2048,128]{1,0:T(8,128)S(1)}, bf16[2048,128]{1,0:T(8,128)(2,1)S(1)}) custom-call(s32[1]{0:T(128)} %bitcast.side, f32[4,768]{1,0:T(4,128)S(1)} %maximum_add_fusion.3.middle, bf16[512,768]{1,0:T(8,128)(2,1)S(1)} %get-tuple-element.39.left, bf16[256,768]{1,0:T(8,128)(2,1)S(1)} %get-tuple-element.40.right, ...), custom_call_target="tpu_custom_call" | custom-call | tf_op jit(solution)/shard_map/pallas_call | solution.py:258
  116.3 1.9 %collective-permute-done.31.got = bf16[2048,128]{1,0:T(8,128)(2,1)S(1)} collective-permute-done((bf16[2048,128]{1,0:T(8,128)(2,1)S(1)}, bf16[2048,128]{1,0:T(8,128)(2,1)S(1)}, u32[]{:S(2)}, u32[]{:S(2)}) %collective-permute-start.31) | collective-permute-done | bytes 524320 | tf_op jit(solution)/shard_map/ppermute | solution.py:166
  118.2 1.7 %shard_map.91 = bf16[2048,128]{1,0:T(8,128)(2,1)} custom-call(f32[4]{0:T(128)S(1)} %copy-done.6, f32[1]{0:T(128)S(6)} %copy.9.pivot, f32[2048,128]{1,0:T(8,128)S(1)} %get-tuple-element.51.mine, bf16[2048,128]{1,0:T(8,128)(2,1)S(1)} %collective-permute-done.31.got, bf16[2048,128]{1,0:T(8,128)(2,1)S(1)} %constant_dynamic-slice_fusion.5.coulomb, ...), custom_call_target="tpu_custom_call" | custom-call | tf_op jit(solution)/shard_map/pallas_call | solution.py:270
  (79 shorter events, 8.2 us)
Async XLA Ops:
  0.0 20.0 %copy-start = (bf16[2048,512]{1,0:T(8,128)(2,1)S(1)}, bf16[2048,512]{1,0:T(8,128)(2,1)}, u32[]{:S(2)}) copy-start(bf16[2048,512]{1,0:T(8,128)(2,1)} %param.9) | copy-start | bytes 6291460
  0.0 18.0 %copy-start.8 = (bf16[64,384]{1,0:T(8,128)(2,1)S(1)}, bf16[64,384]{1,0:T(8,128)(2,1)}, u32[]{:S(2)}) copy-start(bf16[64,384]{1,0:T(8,128)(2,1)} %param.11) | copy-start | bytes 147460
  0.0 18.0 %copy-start.7 = (bf16[64,384]{1,0:T(8,128)(2,1)S(1)}, bf16[64,384]{1,0:T(8,128)(2,1)}, u32[]{:S(2)}) copy-start(bf16[64,384]{1,0:T(8,128)(2,1)} %param.12) | copy-start | bytes 147460
  0.0 4.2 %collective-permute-start = (bf16[2048,128]{1,0:T(8,128)(2,1)}, bf16[2048,128]{1,0:T(8,128)(2,1)S(1)}, u32[]{:S(2)}, u32[]{:S(2)}) collective-permute-start(bf16[2048,128]{1,0:T(8,128)(2,1)} %mine.3), channel_id=1, source_target_pairs={{0,8},{8,0},{16,24},{24,16},{1,9},{9,1},{17,25},{25,17},{2,10},{10... | collective-permute-start | bytes 1572872 | tf_op jit(solution)/shard_map/ppermute | solution.py:166
  0.5 17.5 %collective-permute-start.1 = (bf16[2048,128]{1,0:T(8,128)(2,1)}, bf16[2048,128]{1,0:T(8,128)(2,1)}, u32[]{:S(2)}, u32[]{:S(2)}) collective-permute-start(bf16[2048,128]{1,0:T(8,128)(2,1)} %mine.3), channel_id=1, source_target_pairs={{0,16},{8,24},{16,0},{24,8},{1,17},{9,25},{17,1},{25,9},{2,18},{10... | collective-permute-start | bytes 1572872 | tf_op jit(solution)/shard_map/ppermute | solution.py:166
  4.0 14.0 %collective-permute-start.3 = (bf16[2,64,384]{2,1,0:T(8,128)(2,1)S(1)}, bf16[2,64,384]{2,1,0:T(8,128)(2,1)S(1)}, u32[]{:S(2)}, u32[]{:S(2)}) collective-permute-start(bf16[2,64,384]{2,1,0:T(8,128)(2,1)S(1)} %pad_maximum_fusion.7), channel_id=1, source_target_pairs={{0,16},{8,24},{16,0},{24,8},{1,17},{9,25},{17,1},{25,9},{2,18},{10... | collective-permute-start | bytes 294920 | tf_op jit(solution)/shard_map/ppermute | solution.py:166
  4.2 1.0 copy-start.1
  5.2 12.8 %copy-start.3 = (bf16[2048,128]{1,0:T(8,128)(2,1)}, bf16[2048,128]{1,0:T(8,128)(2,1)S(1)}, u32[]{:S(2)}) copy-start(bf16[2048,128]{1,0:T(8,128)(2,1)S(1)} %collective-permute-done.other) | copy-start | bytes 1572868
  5.2 14.7 %copy-start.5 = (f32[512]{0:T(512)S(1)}, f32[512]{0:T(512)}, u32[]{:S(2)}) copy-start(f32[512]{0:T(512)} %param.14) | copy-start | bytes 6148
  7.8 10.2 %collective-permute-start.2 = (bf16[1,128,512]{2,1,0:T(8,128)(2,1)S(1)}, bf16[1,128,512]{2,1,0:T(8,128)(2,1)}, u32[]{:S(2)}, u32[]{:S(2)}) collective-permute-start(bf16[1,128,512]{2,1,0:T(8,128)(2,1)S(1)} %fusion), channel_id=1, source_target_pairs={{0,1},{1,0},{2,3},{3,2},{4,5},{5,4},{6,7},{7,6},{8,9},{9,8},{10,11... | collective-permute-start | bytes 393224 | tf_op jit(solution)/shard_map/ppermute | solution.py:44
  18.0 2.3 %collective-permute-start.4 = (bf16[2048,128]{1,0:T(8,128)(2,1)}, bf16[2048,128]{1,0:T(8,128)(2,1)}, u32[]{:S(2)}, u32[]{:S(2)}) collective-permute-start(bf16[2048,128]{1,0:T(8,128)(2,1)} %collective-permute-done.1.mine), channel_id=1, source_target_pairs={{0,8},{8,0},{16,24},{24,16},{1,9},{9,1},{17,25},{25,17},{2,10},{10... | collective-permute-start | bytes 1572872 | tf_op jit(solution)/shard_map/ppermute | solution.py:166
  18.1 53.5 %collective-permute-start.18 = (bf16[2048,512]{1,0:T(8,128)(2,1)}, bf16[2048,512]{1,0:T(8,128)(2,1)}, u32[]{:S(2)}, u32[]{:S(2)}) collective-permute-start(bf16[2048,512]{1,0:T(8,128)(2,1)} %own.5), channel_id=1, source_target_pairs={{0,16},{8,24},{16,0},{24,8},{1,17},{9,25},{17,1},{25,9},{2,18},{10... | collective-permute-start | bytes 6291464 | tf_op jit(solution)/shard_map/ppermute | solution.py:166
  23.0 5.6 %collective-permute-start.5 = (bf16[1,128,512]{2,1,0:T(8,128)(2,1)S(1)}, bf16[1,128,512]{2,1,0:T(8,128)(2,1)S(1)}, u32[]{:S(2)}, u32[]{:S(2)}) collective-permute-start(bf16[1,128,512]{2,1,0:T(8,128)(2,1)S(1)} %fusion.1), channel_id=1, source_target_pairs={{0,1},{1,0},{2,3},{3,2},{4,5},{5,4},{6,7},{7,6},{8,9},{9,8},{10,11... | collective-permute-start | bytes 393224 | tf_op jit(solution)/shard_map/ppermute | solution.py:44
  24.9 15.8 %collective-permute-start.9 = (bf16[2,64,768]{2,1,0:T(8,128)(2,1)S(1)}, bf16[2,64,768]{2,1,0:T(8,128)(2,1)S(1)}, u32[]{:S(2)}, u32[]{:S(2)}) collective-permute-start(bf16[2,64,768]{2,1,0:T(8,128)(2,1)S(1)} %pad_maximum_fusion.6), channel_id=1, source_target_pairs={{0,4},{1,5},{2,6},{3,7},{4,0},{5,1},{6,2},{7,3},{8,12},{9,13},{10,... | collective-permute-start | bytes 589832 | tf_op jit(solution)/shard_map/ppermute | solution.py:174
  29.7 11.1 %collective-permute-start.6 = (bf16[2,32,512]{2,1,0:T(8,128)(2,1)S(1)}, bf16[2,32,512]{2,1,0:T(8,128)(2,1)S(1)}, u32[]{:S(2)}, u32[]{:S(2)}) collective-permute-start(bf16[2,32,512]{2,1,0:T(8,128)(2,1)S(1)} %get-tuple-element.76), channel_id=1, source_target_pairs={{0,2},{1,3},{2,0},{3,1},{4,6},{5,7},{6,4},{7,5},{8,10},{9,11},{10,... | collective-permute-start | bytes 196616 | tf_op jit(solution)/shard_map/ppermute | solution.py:53
  31.5 10.1 %collective-permute-start.7 = (bf16[2,32,512]{2,1,0:T(8,128)(2,1)S(1)}, bf16[2,32,512]{2,1,0:T(8,128)(2,1)S(1)}, u32[]{:S(2)}, u32[]{:S(2)}) collective-permute-start(bf16[2,32,512]{2,1,0:T(8,128)(2,1)S(1)} %get-tuple-element.78), channel_id=1, source_target_pairs={{0,4},{1,5},{2,6},{3,7},{4,0},{5,1},{6,2},{7,3},{8,12},{9,13},{10,... | collective-permute-start | bytes 196616 | tf_op jit(solution)/shard_map/ppermute | solution.py:53
  34.1 7.5 %collective-permute-start.8 = (bf16[2,32,512]{2,1,0:T(8,128)(2,1)S(1)}, bf16[2,32,512]{2,1,0:T(8,128)(2,1)S(1)}, u32[]{:S(2)}, u32[]{:S(2)}) collective-permute-start(bf16[2,32,512]{2,1,0:T(8,128)(2,1)S(1)} %get-tuple-element.77), channel_id=1, source_target_pairs={{0,6},{1,7},{2,4},{3,5},{4,2},{5,3},{6,0},{7,1},{8,14},{9,15},{10,... | collective-permute-start | bytes 196616 | tf_op jit(solution)/shard_map/ppermute | solution.py:53
  41.7 6.3 %collective-permute-start.10 = (bf16[2,32,512]{2,1,0:T(8,128)(2,1)S(1)}, bf16[2,32,512]{2,1,0:T(8,128)(2,1)S(1)}, u32[]{:S(2)}, u32[]{:S(2)}) collective-permute-start(bf16[2,32,512]{2,1,0:T(8,128)(2,1)S(1)} %add_convert_fusion.1), channel_id=1, source_target_pairs={{0,6},{1,7},{2,4},{3,5},{4,2},{5,3},{6,0},{7,1},{8,14},{9,15},{10,... | collective-permute-start | bytes 196616 | tf_op jit(solution)/shard_map/ppermute | solution.py:53
  44.7 6.4 %collective-permute-start.11 = (bf16[2,32,512]{2,1,0:T(8,128)(2,1)S(1)}, bf16[2,32,512]{2,1,0:T(8,128)(2,1)S(1)}, u32[]{:S(2)}, u32[]{:S(2)}) collective-permute-start(bf16[2,32,512]{2,1,0:T(8,128)(2,1)S(1)} %add_convert_fusion.1), channel_id=1, source_target_pairs={{0,4},{1,5},{2,6},{3,7},{4,0},{5,1},{6,2},{7,3},{8,12},{9,13},{10,... | collective-permute-start | bytes 196616 | tf_op jit(solution)/shard_map/ppermute | solution.py:53
  45.2 5.9 %collective-permute-start.12 = (bf16[2,32,512]{2,1,0:T(8,128)(2,1)S(1)}, bf16[2,32,512]{2,1,0:T(8,128)(2,1)S(1)}, u32[]{:S(2)}, u32[]{:S(2)}) collective-permute-start(bf16[2,32,512]{2,1,0:T(8,128)(2,1)S(1)} %add_convert_fusion.1), channel_id=1, source_target_pairs={{0,2},{1,3},{2,0},{3,1},{4,6},{5,7},{6,4},{7,5},{8,10},{9,11},{10,... | collective-permute-start | bytes 196616 | tf_op jit(solution)/shard_map/ppermute | solution.py:53
  46.1 8.0 %collective-permute-start.13 = (bf16[3,64,768]{2,1,0:T(8,128)(2,1)S(1)}, bf16[3,64,768]{2,1,0:T(8,128)(2,1)S(1)}, u32[]{:S(2)}, u32[]{:S(2)}) collective-permute-start(bf16[3,64,768]{2,1,0:T(8,128)(2,1)S(1)} %pad_maximum_fusion.1), channel_id=1, source_target_pairs={{0,1},{1,0},{2,3},{3,2},{4,5},{5,4},{6,7},{7,6},{8,9},{9,8},{10,11... | collective-permute-start | bytes 884744 | tf_op jit(solution)/shard_map/ppermute | solution.py:174
  51.1 17.2 %copy-start.2 = (bf16[2048,128]{1,0:T(8,128)(2,1)S(1)}, bf16[2048,128]{1,0:T(8,128)(2,1)}, u32[]{:S(2)}) copy-start(bf16[2048,128]{1,0:T(8,128)(2,1)} %mine.3) | copy-start | bytes 1572868
  51.2 17.2 %copy-start.4 = (bf16[2048,128]{1,0:T(8,128)(2,1)S(1)}, bf16[2048,128]{1,0:T(8,128)(2,1)}, u32[]{:S(2)}) copy-start(bf16[2048,128]{1,0:T(8,128)(2,1)} %copy-done.3) | copy-start | bytes 1572868
  54.2 6.5 %collective-permute-start.16 = (bf16[2,128,512]{2,1,0:T(8,128)(2,1)S(1)}, bf16[2,128,512]{2,1,0:T(8,128)(2,1)S(1)}, u32[]{:S(2)}, u32[]{:S(2)}) collective-permute-start(bf16[2,128,512]{2,1,0:T(8,128)(2,1)S(1)} %pad_maximum_fusion.2), channel_id=1, source_target_pairs={{0,1},{1,0},{2,3},{3,2},{4,5},{5,4},{6,7},{7,6},{8,9},{9,8},{10,11... | collective-permute-start | bytes 786440 | tf_op jit(solution)/shard_map/ppermute | solution.py:53
  54.8 13.5 %collective-permute-start.14 = (bf16[3,128,768]{2,1,0:T(8,128)(2,1)S(1)}, bf16[3,128,768]{2,1,0:T(8,128)(2,1)S(1)}, u32[]{:S(2)}, u32[]{:S(2)}) collective-permute-start(bf16[3,128,768]{2,1,0:T(8,128)(2,1)S(1)} %pad_maximum_fusion.one), channel_id=1, source_target_pairs={{0,2},{1,3},{2,0},{3,1},{4,6},{5,7},{6,4},{7,5},{8,10},{9,11},{10,... | collective-permute-start | bytes 1769480 | tf_op jit(solution)/shard_map/ppermute | solution.py:221
  60.8 13.1 %collective-permute-start.17 = (bf16[2,128,512]{2,1,0:T(8,128)(2,1)S(1)}, bf16[2,128,512]{2,1,0:T(8,128)(2,1)S(1)}, u32[]{:S(2)}, u32[]{:S(2)}) collective-permute-start(bf16[2,128,512]{2,1,0:T(8,128)(2,1)S(1)} %pad_maximum_fusion.3), channel_id=1, source_target_pairs={{0,16},{8,24},{16,0},{24,8},{1,17},{9,25},{17,1},{25,9},{2,18},{10... | collective-permute-start | bytes 786440 | tf_op jit(solution)/shard_map/ppermute | solution.py:166
  70.0 3.9 %collective-permute-start.15 = (f32[4,768]{1,0:T(4,128)S(1)}, f32[4,768]{1,0:T(4,128)S(1)}, u32[]{:S(2)}, u32[]{:S(2)}) collective-permute-start(f32[4,768]{1,0:T(4,128)S(1)} %get-tuple-element.38), channel_id=1, source_target_pairs={{0,16},{8,24},{16,0},{24,8},{1,17},{9,25},{17,1},{25,9},{2,18},{10... | collective-permute-start | bytes 36872 | tf_op jit(solution)/shard_map/ppermute | solution.py:166
  73.9 4.1 %copy-start.6 = (f32[4]{0:T(128)S(1)}, f32[4]{0:T(128)}, u32[]{:S(2)}) copy-start(f32[4]{0:T(128)} %occ.3) | copy-start | bytes 52
  76.1 2.0 %collective-permute-start.19 = (bf16[2048,128]{1,0:T(8,128)(2,1)S(1)}, bf16[2048,128]{1,0:T(8,128)(2,1)S(1)}, u32[]{:S(2)}, u32[]{:S(2)}) collective-permute-start(bf16[2048,128]{1,0:T(8,128)(2,1)S(1)} %get-tuple-element.45), channel_id=1, source_target_pairs={{0,8},{8,0},{16,24},{24,16},{1,9},{9,1},{17,25},{25,17},{2,10},{10... | collective-permute-start | bytes 1572872 | tf_op jit(solution)/shard_map/ppermute | solution.py:166
  79.1 2.0 %collective-permute-start.20 = (bf16[128,2048]{1,0:T(8,128)(2,1)S(1)}, bf16[128,2048]{1,0:T(8,128)(2,1)S(1)}, u32[]{:S(2)}, u32[]{:S(2)}) collective-permute-start(bf16[128,2048]{1,0:T(8,128)(2,1)S(1)} %shard_map.87.mine), channel_id=1, source_target_pairs={{0,8},{8,0},{16,24},{24,16},{1,9},{9,1},{17,25},{25,17},{2,10},{10... | collective-permute-start | bytes 1572872 | tf_op jit(solution)/shard_map/ppermute | solution.py:166
  81.8 5.6 %collective-permute-start.22 = (bf16[1,128,512]{2,1,0:T(8,128)(2,1)S(1)}, bf16[1,128,512]{2,1,0:T(8,128)(2,1)S(1)}, u32[]{:S(2)}, u32[]{:S(2)}) collective-permute-start(bf16[1,128,512]{2,1,0:T(8,128)(2,1)S(1)} %dynamic-slice_convert_fusion.1), channel_id=1, source_target_pairs={{0,1},{1,0},{2,3},{3,2},{4,5},{5,4},{6,7},{7,6},{8,9},{9,8},{10,11... | collective-permute-start | bytes 393224 | tf_op jit(solution)/shard_map/ppermute | solution.py:44
  85.1 5.3 %collective-permute-start.23 = (bf16[1,128,512]{2,1,0:T(8,128)(2,1)S(1)}, bf16[1,128,512]{2,1,0:T(8,128)(2,1)S(1)}, u32[]{:S(2)}, u32[]{:S(2)}) collective-permute-start(bf16[1,128,512]{2,1,0:T(8,128)(2,1)S(1)} %dynamic-slice_convert_fusion), channel_id=1, source_target_pairs={{0,1},{1,0},{2,3},{3,2},{4,5},{5,4},{6,7},{7,6},{8,9},{9,8},{10,11... | collective-permute-start | bytes 393224 | tf_op jit(solution)/shard_map/ppermute | solution.py:44
  90.5 4.7 %collective-permute-start.24 = (bf16[2,32,512]{2,1,0:T(8,128)(2,1)S(1)}, bf16[2,32,512]{2,1,0:T(8,128)(2,1)S(1)}, u32[]{:S(2)}, u32[]{:S(2)}) collective-permute-start(bf16[2,32,512]{2,1,0:T(8,128)(2,1)S(1)} %get-tuple-element.65), channel_id=1, source_target_pairs={{0,2},{1,3},{2,0},{3,1},{4,6},{5,7},{6,4},{7,5},{8,10},{9,11},{10,... | collective-permute-start | bytes 196616 | tf_op jit(solution)/shard_map/ppermute | solution.py:53
  92.4 6.4 %collective-permute-start.25 = (bf16[2,32,512]{2,1,0:T(8,128)(2,1)S(1)}, bf16[2,32,512]{2,1,0:T(8,128)(2,1)S(1)}, u32[]{:S(2)}, u32[]{:S(2)}) collective-permute-start(bf16[2,32,512]{2,1,0:T(8,128)(2,1)S(1)} %get-tuple-element.67), channel_id=1, source_target_pairs={{0,4},{1,5},{2,6},{3,7},{4,0},{5,1},{6,2},{7,3},{8,12},{9,13},{10,... | collective-permute-start | bytes 196616 | tf_op jit(solution)/shard_map/ppermute | solution.py:53
  93.8 6.2 %collective-permute-start.26 = (bf16[2,32,512]{2,1,0:T(8,128)(2,1)S(1)}, bf16[2,32,512]{2,1,0:T(8,128)(2,1)S(1)}, u32[]{:S(2)}, u32[]{:S(2)}) collective-permute-start(bf16[2,32,512]{2,1,0:T(8,128)(2,1)S(1)} %get-tuple-element.66), channel_id=1, source_target_pairs={{0,6},{1,7},{2,4},{3,5},{4,2},{5,3},{6,0},{7,1},{8,14},{9,15},{10,... | collective-permute-start | bytes 196616 | tf_op jit(solution)/shard_map/ppermute | solution.py:53
  100.0 6.1 %collective-permute-start.27 = (bf16[2,32,512]{2,1,0:T(8,128)(2,1)S(1)}, bf16[2,32,512]{2,1,0:T(8,128)(2,1)S(1)}, u32[]{:S(2)}, u32[]{:S(2)}) collective-permute-start(bf16[2,32,512]{2,1,0:T(8,128)(2,1)S(1)} %add_convert_fusion), channel_id=1, source_target_pairs={{0,6},{1,7},{2,4},{3,5},{4,2},{5,3},{6,0},{7,1},{8,14},{9,15},{10,... | collective-permute-start | bytes 196616 | tf_op jit(solution)/shard_map/ppermute | solution.py:53
  101.8 5.7 %collective-permute-start.28 = (bf16[2,32,512]{2,1,0:T(8,128)(2,1)S(1)}, bf16[2,32,512]{2,1,0:T(8,128)(2,1)S(1)}, u32[]{:S(2)}, u32[]{:S(2)}) collective-permute-start(bf16[2,32,512]{2,1,0:T(8,128)(2,1)S(1)} %add_convert_fusion), channel_id=1, source_target_pairs={{0,4},{1,5},{2,6},{3,7},{4,0},{5,1},{6,2},{7,3},{8,12},{9,13},{10,... | collective-permute-start | bytes 196616 | tf_op jit(solution)/shard_map/ppermute | solution.py:53
  102.3 5.2 %collective-permute-start.29 = (bf16[2,32,512]{2,1,0:T(8,128)(2,1)S(1)}, bf16[2,32,512]{2,1,0:T(8,128)(2,1)S(1)}, u32[]{:S(2)}, u32[]{:S(2)}) collective-permute-start(bf16[2,32,512]{2,1,0:T(8,128)(2,1)S(1)} %add_convert_fusion), channel_id=1, source_target_pairs={{0,2},{1,3},{2,0},{3,1},{4,6},{5,7},{6,4},{7,5},{8,10},{9,11},{10,... | collective-permute-start | bytes 196616 | tf_op jit(solution)/shard_map/ppermute | solution.py:53
  104.5 4.8 %collective-permute-start.21 = (f32[4,768]{1,0:T(4,128)S(1)}, f32[4,768]{1,0:T(4,128)S(1)}, u32[]{:S(2)}, u32[]{:S(2)}) collective-permute-start(f32[4,768]{1,0:T(4,128)S(1)} %get-tuple-element.49), channel_id=1, source_target_pairs={{0,16},{8,24},{16,0},{24,8},{1,17},{9,25},{17,1},{25,9},{2,18},{10... | collective-permute-start | bytes 36872 | tf_op jit(solution)/shard_map/ppermute | solution.py:166
  107.6 6.4 %collective-permute-start.30 = (bf16[2,128,512]{2,1,0:T(8,128)(2,1)S(1)}, bf16[2,128,512]{2,1,0:T(8,128)(2,1)S(1)}, u32[]{:S(2)}, u32[]{:S(2)}) collective-permute-start(bf16[2,128,512]{2,1,0:T(8,128)(2,1)S(1)} %pad_maximum_fusion.5.one), channel_id=1, source_target_pairs={{0,1},{1,0},{2,3},{3,2},{4,5},{5,4},{6,7},{7,6},{8,9},{9,8},{10,11... | collective-permute-start | bytes 786440 | tf_op jit(solution)/shard_map/ppermute | solution.py:53
  116.2 2.0 %collective-permute-start.31 = (bf16[2048,128]{1,0:T(8,128)(2,1)S(1)}, bf16[2048,128]{1,0:T(8,128)(2,1)S(1)}, u32[]{:S(2)}, u32[]{:S(2)}) collective-permute-start(bf16[2048,128]{1,0:T(8,128)(2,1)S(1)} %get-tuple-element.52), channel_id=1, source_target_pairs={{0,8},{8,0},{16,24},{24,16},{1,9},{9,1},{17,25},{25,17},{2,10},{10... | collective-permute-start | bytes 1572872 | tf_op jit(solution)/shard_map/ppermute | solution.py:166

commit v8 on v7

--- a/solution.py
+++ b/solution.py
@@ -253,7 +253,7 @@
     gram = (jnp.stack([line[0], other[0]]), beside(4, over(jnp.stack([line[1], other[1]]), 2)))
     for step in range(ITERS):
         last = step == ITERS - 1
-        other = over(middle, 2)
+        other = over(middle, 2) if step == 0 else crossed[0]
         middle = middle + jnp.concatenate([other[:, cols // 2 :], other[:, : cols // 2]], axis=1)
         mine, theirs = pl.pallas_call(
             functools.partial(residual_kernel, step == 0),
@@ -290,7 +290,14 @@
                 )(*amps, left, right, factors)
                 folded.append(fold(terms[0], n_pair))
             middle = terms[1]
-            gram = all_reduce(*(jnp.concatenate(a, axis=0) for a in zip(*folded)), n_pair)
+            crossed = [over(middle, 2)]
+
+            def with_middle(stage, a):
+                if stage == 0:
+                    a, crossed[0] = tie(a, crossed[0])
+                return a
+
+            gram = all_reduce(*(jnp.concatenate(a, axis=0) for a in zip(*folded)), n_pair, with_middle)
     return new
 
 

time: 120 us -> 120 us (level)
    ppermute x4, waiting for transfers between devices: 5.82 us -> 4.38 us  [fold(): return (mine, lax.ppermute(theirs.astype(BF), 'pair', xor(n, 1)))]
    ppermute x14, waiting for transfers between devices: 21.1 us -> 22.5 us  [send(): return lax.ppermute(a, 'pair', xor(n, s))]
where the time goes in v8:
time: 120 us
  waiting for transfers between devices  55.7 us (46%)
  starting transfers between devices  40.8 us (34%)
  Pallas kernels  18.4 us (15%)
  other arithmetic  2.5 us (2%)
  local copies, waits for them, and re-layouts  1.49 us (1%)
    ppermute x14, waiting for transfers between devices, send(): return lax.ppermute(a, 'pair', xor(n, s))  22.5 us
    ppermute x14, starting transfers between devices, send(): return lax.ppermute(a, 'pair', xor(n, s))  20.1 us
    ppermute x11, waiting for transfers between devices, over(): return lax.ppermute(a, 'aux', xor(n_aux, s))  13.4 us
    ppermute x11, starting transfers between devices, over(): return lax.ppermute(a, 'aux', xor(n_aux, s))  10.2 us
    ppermute x2, waiting for transfers between devices, other_rows(): got = lax.ppermute(fac, 'pair', xor(n_pair, bit))  9.47 us
    ppermute x1, waiting for transfers between devices, beside(): got = lax.ppermute(fac, 'pair', xor(n_pair, n_pair // 4))  5.92 us
    ppermute x4, starting transfers between devices, fold(): return (mine, lax.ppermute(theirs.astype(BF), 'pair', xor(n, 1)))  5.9 us
    pallas_call x2, Pallas kernels, first_gram(): pl.pallas_call(first_gram_kernel, out_shape=jax.ShapeDtypeStruct((2 * wid...  5.17 us
  transfers between devices with their start and end apart: 32, of which 21 were waited for; matrix products, arithmetic and copies ran while one was open for 2% of the time, Pallas kernels for 9%

profile of v8, /device:TPU:0, one launch (start us, length us, event | category | flops | bytes accessed | tf_op | source)
XLA Modules:
  0.0 119.9 jit_solution(12478042300467588037)
XLA Ops:
  0.5 2.6 %collective-permute-start.1 = (bf16[2048,128]{1,0:T(8,128)(2,1)}, bf16[2048,128]{1,0:T(8,128)(2,1)}, u32[]{:S(2)}, u32[]{:S(2)}) collective-permute-start(bf16[2048,128]{1,0:T(8,128)(2,1)} %mine.3), channel_id=1, source_target_pairs={{0,16},{8,24},{16,0},{24,8},{1,17},{9,25},{17,1},{25,9},{2,18},{10... | collective-permute-start | bytes 1572872 | tf_op jit(solution)/shard_map/ppermute | solution.py:166
  4.2 1.0 copy-done.1
  5.2 2.5 %shard_map.82 = f32[256,512]{1,0:T(8,128)S(1)} custom-call(bf16[2048,128]{1,0:T(8,128)(2,1)S(1)} %copy-done.1, bf16[2048,128]{1,0:T(8,128)(2,1)S(1)} %collective-permute-done.other, bf16[2048,512]{1,0:T(8,128)(2,1)} %own.5), custom_call_target="tpu_custom_call" | custom-call | tf_op jit(solution)/shard_map/pallas_call | solution.py:184
  7.8 1.9 %collective-permute-start.2 = (bf16[1,128,512]{2,1,0:T(8,128)(2,1)S(1)}, bf16[1,128,512]{2,1,0:T(8,128)(2,1)}, u32[]{:S(2)}, u32[]{:S(2)}) collective-permute-start(bf16[1,128,512]{2,1,0:T(8,128)(2,1)S(1)} %fusion), channel_id=1, source_target_pairs={{0,1},{1,0},{2,3},{3,2},{4,5},{5,4},{6,7},{7,6},{8,9},{9,8},{10,11... | collective-permute-start | bytes 393224 | tf_op jit(solution)/shard_map/ppermute | solution.py:44
  9.7 8.2 %collective-permute-done.3 = bf16[2,64,384]{2,1,0:T(8,128)(2,1)S(1)} collective-permute-done((bf16[2,64,384]{2,1,0:T(8,128)(2,1)S(1)}, bf16[2,64,384]{2,1,0:T(8,128)(2,1)S(1)}, u32[]{:S(2)}, u32[]{:S(2)}) %collective-permute-start.3) | collective-permute-done | bytes 98336 | tf_op jit(solution)/shard_map/ppermute | solution.py:166
  18.1 1.8 %collective-permute-start.18 = (bf16[2048,512]{1,0:T(8,128)(2,1)}, bf16[2048,512]{1,0:T(8,128)(2,1)}, u32[]{:S(2)}, u32[]{:S(2)}) collective-permute-start(bf16[2048,512]{1,0:T(8,128)(2,1)} %own.5), channel_id=1, source_target_pairs={{0,16},{8,24},{16,0},{24,8},{1,17},{9,25},{17,1},{25,9},{2,18},{10... | collective-permute-start | bytes 6291464 | tf_op jit(solution)/shard_map/ppermute | solution.py:166
  20.3 2.7 %shard_map.83 = f32[256,512]{1,0:T(8,128)S(1)} custom-call(bf16[2048,128]{1,0:T(8,128)(2,1)} %collective-permute-done.1.mine, bf16[2048,128]{1,0:T(8,128)(2,1)} %collective-permute-done.4.other, bf16[2048,512]{1,0:T(8,128)(2,1)} %own.5), custom_call_target="tpu_custom_call" | custom-call | tf_op jit(solution)/shard_map/pallas_call | solution.py:184
  23.0 1.8 %collective-permute-start.5 = (bf16[1,128,512]{2,1,0:T(8,128)(2,1)S(1)}, bf16[1,128,512]{2,1,0:T(8,128)(2,1)S(1)}, u32[]{:S(2)}, u32[]{:S(2)}) collective-permute-start(bf16[1,128,512]{2,1,0:T(8,128)(2,1)S(1)} %fusion.1), channel_id=1, source_target_pairs={{0,1},{1,0},{2,3},{3,2},{4,5},{5,4},{6,7},{7,6},{8,9},{9,8},{10,11... | collective-permute-start | bytes 393224 | tf_op jit(solution)/shard_map/ppermute | solution.py:44
  24.9 2.6 %collective-permute-start.9 = (bf16[2,64,768]{2,1,0:T(8,128)(2,1)S(1)}, bf16[2,64,768]{2,1,0:T(8,128)(2,1)S(1)}, u32[]{:S(2)}, u32[]{:S(2)}) collective-permute-start(bf16[2,64,768]{2,1,0:T(8,128)(2,1)S(1)} %pad_maximum_fusion.7), channel_id=1, source_target_pairs={{0,4},{1,5},{2,6},{3,7},{4,0},{5,1},{6,2},{7,3},{8,12},{9,13},{10,... | collective-permute-start | bytes 589832 | tf_op jit(solution)/shard_map/ppermute | solution.py:174
  27.5 1.1 collective-permute-done.5
  28.6 1.0 fusion.3
  29.7 1.9 %collective-permute-start.6 = (bf16[2,32,512]{2,1,0:T(8,128)(2,1)S(1)}, bf16[2,32,512]{2,1,0:T(8,128)(2,1)S(1)}, u32[]{:S(2)}, u32[]{:S(2)}) collective-permute-start(bf16[2,32,512]{2,1,0:T(8,128)(2,1)S(1)} %get-tuple-element.80), channel_id=1, source_target_pairs={{0,2},{1,3},{2,0},{3,1},{4,6},{5,7},{6,4},{7,5},{8,10},{9,11},{10,... | collective-permute-start | bytes 196616 | tf_op jit(solution)/shard_map/ppermute | solution.py:53
  31.5 2.6 %collective-permute-start.7 = (bf16[2,32,512]{2,1,0:T(8,128)(2,1)S(1)}, bf16[2,32,512]{2,1,0:T(8,128)(2,1)S(1)}, u32[]{:S(2)}, u32[]{:S(2)}) collective-permute-start(bf16[2,32,512]{2,1,0:T(8,128)(2,1)S(1)} %get-tuple-element.82), channel_id=1, source_target_pairs={{0,4},{1,5},{2,6},{3,7},{4,0},{5,1},{6,2},{7,3},{8,12},{9,13},{10,... | collective-permute-start | bytes 196616 | tf_op jit(solution)/shard_map/ppermute | solution.py:53
  34.2 6.5 %collective-permute-done.9 = bf16[2,64,768]{2,1,0:T(8,128)(2,1)S(1)} collective-permute-done((bf16[2,64,768]{2,1,0:T(8,128)(2,1)S(1)}, bf16[2,64,768]{2,1,0:T(8,128)(2,1)S(1)}, u32[]{:S(2)}, u32[]{:S(2)}) %collective-permute-start.9) | collective-permute-done | bytes 196640 | tf_op jit(solution)/shard_map/ppermute | solution.py:174
  41.7 3.0 %collective-permute-start.10 = (bf16[2,32,512]{2,1,0:T(8,128)(2,1)S(1)}, bf16[2,32,512]{2,1,0:T(8,128)(2,1)S(1)}, u32[]{:S(2)}, u32[]{:S(2)}) collective-permute-start(bf16[2,32,512]{2,1,0:T(8,128)(2,1)S(1)} %add_convert_fusion.1), channel_id=1, source_target_pairs={{0,6},{1,7},{2,4},{3,5},{4,2},{5,3},{6,0},{7,1},{8,14},{9,15},{10,... | collective-permute-start | bytes 196616 | tf_op jit(solution)/shard_map/ppermute | solution.py:53
  45.2 1.0 collective-permute-start.12
  46.6 1.4 %collective-permute-done.10 = bf16[2,32,512]{2,1,0:T(8,128)(2,1)S(1)} collective-permute-done((bf16[2,32,512]{2,1,0:T(8,128)(2,1)S(1)}, bf16[2,32,512]{2,1,0:T(8,128)(2,1)S(1)}, u32[]{:S(2)}, u32[]{:S(2)}) %collective-permute-start.10) | collective-permute-done | bytes 65568 | tf_op jit(solution)/shard_map/ppermute | solution.py:53
  48.0 3.1 %collective-permute-done.11 = bf16[2,32,512]{2,1,0:T(8,128)(2,1)S(1)} collective-permute-done((bf16[2,32,512]{2,1,0:T(8,128)(2,1)S(1)}, bf16[2,32,512]{2,1,0:T(8,128)(2,1)S(1)}, u32[]{:S(2)}, u32[]{:S(2)}) %collective-permute-start.11) | collective-permute-done | bytes 65568 | tf_op jit(solution)/shard_map/ppermute | solution.py:53
  51.2 3.0 %collective-permute-done.13 = bf16[3,64,768]{2,1,0:T(8,128)(2,1)S(1)} collective-permute-done((bf16[3,64,768]{2,1,0:T(8,128)(2,1)S(1)}, bf16[3,64,768]{2,1,0:T(8,128)(2,1)S(1)}, u32[]{:S(2)}, u32[]{:S(2)}) %collective-permute-start.13) | collective-permute-done | bytes 294944 | tf_op jit(solution)/shard_map/ppermute | solution.py:174
  54.8 1.5 %collective-permute-start.14 = (bf16[3,128,768]{2,1,0:T(8,128)(2,1)S(1)}, bf16[3,128,768]{2,1,0:T(8,128)(2,1)S(1)}, u32[]{:S(2)}, u32[]{:S(2)}) collective-permute-start(bf16[3,128,768]{2,1,0:T(8,128)(2,1)S(1)} %pad_maximum_fusion.one), channel_id=1, source_target_pairs={{0,2},{1,3},{2,0},{3,1},{4,6},{5,7},{6,4},{7,5},{8,10},{9,11},{10,... | collective-permute-start | bytes 1769480 | tf_op jit(solution)/shard_map/ppermute | solution.py:221
  56.5 4.3 %collective-permute-done.16 = bf16[2,128,512]{2,1,0:T(8,128)(2,1)S(1)} collective-permute-done((bf16[2,128,512]{2,1,0:T(8,128)(2,1)S(1)}, bf16[2,128,512]{2,1,0:T(8,128)(2,1)S(1)}, u32[]{:S(2)}, u32[]{:S(2)}) %collective-permute-start.16) | collective-permute-done | bytes 262176 | tf_op jit(solution)/shard_map/ppermute | solution.py:53
  60.8 1.6 %collective-permute-start.17 = (bf16[2,128,512]{2,1,0:T(8,128)(2,1)S(1)}, bf16[2,128,512]{2,1,0:T(8,128)(2,1)S(1)}, u32[]{:S(2)}, u32[]{:S(2)}) collective-permute-start(bf16[2,128,512]{2,1,0:T(8,128)(2,1)S(1)} %pad_maximum_fusion.3), channel_id=1, source_target_pairs={{0,16},{8,24},{16,0},{24,8},{1,17},{9,25},{17,1},{25,9},{2,18},{10... | collective-permute-start | bytes 786440 | tf_op jit(solution)/shard_map/ppermute | solution.py:166
  62.4 5.9 %collective-permute-done.14.two = bf16[3,128,768]{2,1,0:T(8,128)(2,1)S(1)} collective-permute-done((bf16[3,128,768]{2,1,0:T(8,128)(2,1)S(1)}, bf16[3,128,768]{2,1,0:T(8,128)(2,1)S(1)}, u32[]{:S(2)}, u32[]{:S(2)}) %collective-permute-start.14) | collective-permute-done | bytes 589856 | tf_op jit(solution)/shard_map/ppermute | solution.py:221
  68.4 1.7 %shard_map.84 = (bf16[512,768]{1,0:T(8,128)(2,1)S(1)}, bf16[256,768]{1,0:T(8,128)(2,1)S(1)}, f32[4,768]{1,0:T(4,128)S(1)}) custom-call(bf16[2048,128]{1,0:T(8,128)(2,1)S(1)} %copy-done.2, bf16[2048,128]{1,0:T(8,128)(2,1)S(1)} %copy-done.4, s32[2]{0:T(128)S(1)} %pad_add_fusion.places, bf16[3,128,768]{2,1,0:T(8,128)(2,1)S(1)} %pad_maximum_fusion.one, ...), custom_call_target="tpu_custom_call" | custom-call | flops 3000000000 | bytes 9000000 | tf_op jit(solution)/shard_map/pallas_call | solution.py:223
  70.0 1.6 %collective-permute-start.15 = (f32[4,768]{1,0:T(4,128)S(1)}, f32[4,768]{1,0:T(4,128)S(1)}, u32[]{:S(2)}, u32[]{:S(2)}) collective-permute-start(f32[4,768]{1,0:T(4,128)S(1)} %get-tuple-element.40), channel_id=1, source_target_pairs={{0,16},{8,24},{16,0},{24,8},{1,17},{9,25},{17,1},{25,9},{2,18},{10... | collective-permute-start | bytes 36872 | tf_op jit(solution)/shard_map/ppermute | solution.py:166
  71.6 2.2 %shard_map.85.factors = bf16[2,2048,512]{2,1,0:T(8,128)(2,1)S(1)} custom-call(bf16[2048,512]{1,0:T(8,128)(2,1)} %own.5, bf16[2048,512]{1,0:T(8,128)(2,1)} %collective-permute-done.18.far), custom_call_target="tpu_custom_call" | custom-call | tf_op jit(solution)/shard_map/pallas_call | solution.py:236
  73.9 2.1 %shard_map.86 = (f32[2048,128]{1,0:T(8,128)S(1)}, bf16[2048,128]{1,0:T(8,128)(2,1)S(1)}) custom-call(s32[1]{0:T(128)} %bitcast.side, f32[4,768]{1,0:T(4,128)S(1)} %maximum_add_fusion.2.middle, bf16[512,768]{1,0:T(8,128)(2,1)S(1)} %get-tuple-element.41.left, bf16[256,768]{1,0:T(8,128)(2,1)S(1)} %get-tuple-element.42.right, ...), custom_call_target="tpu_custom_call" | custom-call | tf_op jit(solution)/shard_map/pallas_call | solution.py:258
  76.8 1.2 %collective-permute-done.19.got = bf16[2048,128]{1,0:T(8,128)(2,1)S(1)} collective-permute-done((bf16[2048,128]{1,0:T(8,128)(2,1)S(1)}, bf16[2048,128]{1,0:T(8,128)(2,1)S(1)}, u32[]{:S(2)}, u32[]{:S(2)}) %collective-permute-start.19) | collective-permute-done | bytes 524320 | tf_op jit(solution)/shard_map/ppermute | solution.py:166
  78.1 1.0 shard_map.87.mine
  79.3 1.8 %collective-permute-done.20.other = bf16[128,2048]{1,0:T(8,128)(2,1)S(1)} collective-permute-done((bf16[128,2048]{1,0:T(8,128)(2,1)S(1)}, bf16[128,2048]{1,0:T(8,128)(2,1)S(1)}, u32[]{:S(2)}, u32[]{:S(2)}) %collective-permute-start.20) | collective-permute-done | bytes 524320 | tf_op jit(solution)/shard_map/ppermute | solution.py:166
  81.8 1.6 %collective-permute-start.21 = (bf16[1,128,512]{2,1,0:T(8,128)(2,1)S(1)}, bf16[1,128,512]{2,1,0:T(8,128)(2,1)S(1)}, u32[]{:S(2)}, u32[]{:S(2)}) collective-permute-start(bf16[1,128,512]{2,1,0:T(8,128)(2,1)S(1)} %dynamic-slice_convert_fusion.1), channel_id=1, source_target_pairs={{0,1},{1,0},{2,3},{3,2},{4,5},{5,4},{6,7},{7,6},{8,9},{9,8},{10,11... | collective-permute-start | bytes 393224 | tf_op jit(solution)/shard_map/ppermute | solution.py:44
  83.4 1.6 %shard_map.88 = (f32[1,256,512]{2,1,0:T(8,128)S(1)}, f32[4,768]{1,0:T(4,128)S(1)}) custom-call(bf16[128,2048]{1,0:T(8,128)(2,1)S(1)} %shard_map.87.mine, bf16[128,2048]{1,0:T(8,128)(2,1)S(1)} %collective-permute-done.20.other, bf16[512,768]{1,0:T(8,128)(2,1)S(1)} %get-tuple-element.41.left, bf16[256,768]{1,0:T(8,128)(2,1)S(1)} %get-tuple-element.42.right, ...), custom_call_target="tpu_custom_call" | custom-call | tf_op jit(solution)/shard_map/pallas_call | solution.py:284
  85.7 1.4 %collective-permute-start.23 = (f32[4,768]{1,0:T(4,128)S(1)}, f32[4,768]{1,0:T(4,128)S(1)}, u32[]{:S(2)}, u32[]{:S(2)}) collective-permute-start(f32[4,768]{1,0:T(4,128)S(1)} %get-tuple-element.51), channel_id=1, source_target_pairs={{0,16},{8,24},{16,0},{24,8},{1,17},{9,25},{17,1},{25,9},{2,18},{10... | collective-permute-start | bytes 36872 | tf_op jit(solution)/shard_map/ppermute | solution.py:166
  87.4 3.0 %collective-permute-done.22 = bf16[1,128,512]{2,1,0:T(8,128)(2,1)S(1)} collective-permute-done((bf16[1,128,512]{2,1,0:T(8,128)(2,1)S(1)}, bf16[1,128,512]{2,1,0:T(8,128)(2,1)S(1)}, u32[]{:S(2)}, u32[]{:S(2)}) %collective-permute-start.22) | collective-permute-done | bytes 131104 | tf_op jit(solution)/shard_map/ppermute | solution.py:44
  90.6 1.8 %collective-permute-start.24 = (bf16[2,32,512]{2,1,0:T(8,128)(2,1)S(1)}, bf16[2,32,512]{2,1,0:T(8,128)(2,1)S(1)}, u32[]{:S(2)}, u32[]{:S(2)}) collective-permute-start(bf16[2,32,512]{2,1,0:T(8,128)(2,1)S(1)} %get-tuple-element.69), channel_id=1, source_target_pairs={{0,2},{1,3},{2,0},{3,1},{4,6},{5,7},{6,4},{7,5},{8,10},{9,11},{10,... | collective-permute-start | bytes 196616 | tf_op jit(solution)/shard_map/ppermute | solution.py:53
  92.4 1.5 %collective-permute-start.25 = (bf16[2,32,512]{2,1,0:T(8,128)(2,1)S(1)}, bf16[2,32,512]{2,1,0:T(8,128)(2,1)S(1)}, u32[]{:S(2)}, u32[]{:S(2)}) collective-permute-start(bf16[2,32,512]{2,1,0:T(8,128)(2,1)S(1)} %get-tuple-element.71), channel_id=1, source_target_pairs={{0,4},{1,5},{2,6},{3,7},{4,0},{5,1},{6,2},{7,3},{8,12},{9,13},{10,... | collective-permute-start | bytes 196616 | tf_op jit(solution)/shard_map/ppermute | solution.py:53
  93.8 1.2 collective-permute-start.26
  95.3 3.5 %collective-permute-done.25 = bf16[2,32,512]{2,1,0:T(8,128)(2,1)S(1)} collective-permute-done((bf16[2,32,512]{2,1,0:T(8,128)(2,1)S(1)}, bf16[2,32,512]{2,1,0:T(8,128)(2,1)S(1)}, u32[]{:S(2)}, u32[]{:S(2)}) %collective-permute-start.25) | collective-permute-done | bytes 65568 | tf_op jit(solution)/shard_map/ppermute | solution.py:53
  98.8 1.2 collective-permute-done.26
  100.1 1.8 %collective-permute-start.27 = (bf16[2,32,512]{2,1,0:T(8,128)(2,1)S(1)}, bf16[2,32,512]{2,1,0:T(8,128)(2,1)S(1)}, u32[]{:S(2)}, u32[]{:S(2)}) collective-permute-start(bf16[2,32,512]{2,1,0:T(8,128)(2,1)S(1)} %add_convert_fusion), channel_id=1, source_target_pairs={{0,6},{1,7},{2,4},{3,5},{4,2},{5,3},{6,0},{7,1},{8,14},{9,15},{10,... | collective-permute-start | bytes 196616 | tf_op jit(solution)/shard_map/ppermute | solution.py:53
  102.4 2.2 %collective-permute-start.29 = (bf16[2,32,512]{2,1,0:T(8,128)(2,1)S(1)}, bf16[2,32,512]{2,1,0:T(8,128)(2,1)S(1)}, u32[]{:S(2)}, u32[]{:S(2)}) collective-permute-start(bf16[2,32,512]{2,1,0:T(8,128)(2,1)S(1)} %add_convert_fusion), channel_id=1, source_target_pairs={{0,2},{1,3},{2,0},{3,1},{4,6},{5,7},{6,4},{7,5},{8,10},{9,11},{10,... | collective-permute-start | bytes 196616 | tf_op jit(solution)/shard_map/ppermute | solution.py:53
  104.5 1.7 %collective-permute-done.27 = bf16[2,32,512]{2,1,0:T(8,128)(2,1)S(1)} collective-permute-done((bf16[2,32,512]{2,1,0:T(8,128)(2,1)S(1)}, bf16[2,32,512]{2,1,0:T(8,128)(2,1)S(1)}, u32[]{:S(2)}, u32[]{:S(2)}) %collective-permute-start.27) | collective-permute-done | bytes 65568 | tf_op jit(solution)/shard_map/ppermute | solution.py:53
  106.2 1.4 %collective-permute-done.28 = bf16[2,32,512]{2,1,0:T(8,128)(2,1)S(1)} collective-permute-done((bf16[2,32,512]{2,1,0:T(8,128)(2,1)S(1)}, bf16[2,32,512]{2,1,0:T(8,128)(2,1)S(1)}, u32[]{:S(2)}, u32[]{:S(2)}) %collective-permute-start.28) | collective-permute-done | bytes 65568 | tf_op jit(solution)/shard_map/ppermute | solution.py:53
  107.7 1.7 %collective-permute-start.30 = (bf16[2,128,512]{2,1,0:T(8,128)(2,1)S(1)}, bf16[2,128,512]{2,1,0:T(8,128)(2,1)S(1)}, u32[]{:S(2)}, u32[]{:S(2)}) collective-permute-start(bf16[2,128,512]{2,1,0:T(8,128)(2,1)S(1)} %pad_maximum_fusion.6.one), channel_id=1, source_target_pairs={{0,1},{1,0},{2,3},{3,2},{4,5},{5,4},{6,7},{7,6},{8,9},{9,8},{10,11... | collective-permute-start | bytes 786440 | tf_op jit(solution)/shard_map/ppermute | solution.py:53
  109.3 4.8 %collective-permute-done.30.two = bf16[2,128,512]{2,1,0:T(8,128)(2,1)S(1)} collective-permute-done((bf16[2,128,512]{2,1,0:T(8,128)(2,1)S(1)}, bf16[2,128,512]{2,1,0:T(8,128)(2,1)S(1)}, u32[]{:S(2)}, u32[]{:S(2)}) %collective-permute-start.30) | collective-permute-done | bytes 262176 | tf_op jit(solution)/shard_map/ppermute | solution.py:53
  114.1 2.1 %shard_map.90 = (f32[2048,128]{1,0:T(8,128)S(1)}, bf16[2048,128]{1,0:T(8,128)(2,1)S(1)}) custom-call(s32[1]{0:T(128)} %bitcast.side, f32[4,768]{1,0:T(4,128)S(1)} %maximum_add_fusion.3.middle, bf16[512,768]{1,0:T(8,128)(2,1)S(1)} %get-tuple-element.41.left, bf16[256,768]{1,0:T(8,128)(2,1)S(1)} %get-tuple-element.42.right, ...), custom_call_target="tpu_custom_call" | custom-call | tf_op jit(solution)/shard_map/pallas_call | solution.py:258
  116.3 1.9 %collective-permute-done.31.got = bf16[2048,128]{1,0:T(8,128)(2,1)S(1)} collective-permute-done((bf16[2048,128]{1,0:T(8,128)(2,1)S(1)}, bf16[2048,128]{1,0:T(8,128)(2,1)S(1)}, u32[]{:S(2)}, u32[]{:S(2)}) %collective-permute-start.31) | collective-permute-done | bytes 524320 | tf_op jit(solution)/shard_map/ppermute | solution.py:166
  118.2 1.7 %shard_map.91 = bf16[2048,128]{1,0:T(8,128)(2,1)} custom-call(f32[4]{0:T(128)S(1)} %copy-done.6, f32[1]{0:T(128)S(6)} %copy.9.pivot, f32[2048,128]{1,0:T(8,128)S(1)} %get-tuple-element.55.mine, bf16[2048,128]{1,0:T(8,128)(2,1)S(1)} %collective-permute-done.31.got, bf16[2048,128]{1,0:T(8,128)(2,1)S(1)} %constant_dynamic-slice_fusion.5.coulomb, ...), custom_call_target="tpu_custom_call" | custom-call | tf_op jit(solution)/shard_map/pallas_call | solution.py:270
  (81 shorter events, 8.2 us)
Async XLA Ops:
  0.0 20.0 %copy-start = (bf16[2048,512]{1,0:T(8,128)(2,1)S(1)}, bf16[2048,512]{1,0:T(8,128)(2,1)}, u32[]{:S(2)}) copy-start(bf16[2048,512]{1,0:T(8,128)(2,1)} %param.9) | copy-start | bytes 6291460
  0.0 18.0 %copy-start.8 = (bf16[64,384]{1,0:T(8,128)(2,1)S(1)}, bf16[64,384]{1,0:T(8,128)(2,1)}, u32[]{:S(2)}) copy-start(bf16[64,384]{1,0:T(8,128)(2,1)} %param.11) | copy-start | bytes 147460
  0.0 18.0 %copy-start.7 = (bf16[64,384]{1,0:T(8,128)(2,1)S(1)}, bf16[64,384]{1,0:T(8,128)(2,1)}, u32[]{:S(2)}) copy-start(bf16[64,384]{1,0:T(8,128)(2,1)} %param.12) | copy-start | bytes 147460
  0.0 4.2 %collective-permute-start = (bf16[2048,128]{1,0:T(8,128)(2,1)}, bf16[2048,128]{1,0:T(8,128)(2,1)S(1)}, u32[]{:S(2)}, u32[]{:S(2)}) collective-permute-start(bf16[2048,128]{1,0:T(8,128)(2,1)} %mine.3), channel_id=1, source_target_pairs={{0,8},{8,0},{16,24},{24,16},{1,9},{9,1},{17,25},{25,17},{2,10},{10... | collective-permute-start | bytes 1572872 | tf_op jit(solution)/shard_map/ppermute | solution.py:166
  0.5 17.5 %collective-permute-start.1 = (bf16[2048,128]{1,0:T(8,128)(2,1)}, bf16[2048,128]{1,0:T(8,128)(2,1)}, u32[]{:S(2)}, u32[]{:S(2)}) collective-permute-start(bf16[2048,128]{1,0:T(8,128)(2,1)} %mine.3), channel_id=1, source_target_pairs={{0,16},{8,24},{16,0},{24,8},{1,17},{9,25},{17,1},{25,9},{2,18},{10... | collective-permute-start | bytes 1572872 | tf_op jit(solution)/shard_map/ppermute | solution.py:166
  4.0 14.0 %collective-permute-start.3 = (bf16[2,64,384]{2,1,0:T(8,128)(2,1)S(1)}, bf16[2,64,384]{2,1,0:T(8,128)(2,1)S(1)}, u32[]{:S(2)}, u32[]{:S(2)}) collective-permute-start(bf16[2,64,384]{2,1,0:T(8,128)(2,1)S(1)} %pad_maximum_fusion.8), channel_id=1, source_target_pairs={{0,16},{8,24},{16,0},{24,8},{1,17},{9,25},{17,1},{25,9},{2,18},{10... | collective-permute-start | bytes 294920 | tf_op jit(solution)/shard_map/ppermute | solution.py:166
  4.2 1.0 copy-start.1
  5.2 12.8 %copy-start.3 = (bf16[2048,128]{1,0:T(8,128)(2,1)}, bf16[2048,128]{1,0:T(8,128)(2,1)S(1)}, u32[]{:S(2)}) copy-start(bf16[2048,128]{1,0:T(8,128)(2,1)S(1)} %collective-permute-done.other) | copy-start | bytes 1572868
  5.2 14.7 %copy-start.5 = (f32[512]{0:T(512)S(1)}, f32[512]{0:T(512)}, u32[]{:S(2)}) copy-start(f32[512]{0:T(512)} %param.14) | copy-start | bytes 6148
  7.8 10.2 %collective-permute-start.2 = (bf16[1,128,512]{2,1,0:T(8,128)(2,1)S(1)}, bf16[1,128,512]{2,1,0:T(8,128)(2,1)}, u32[]{:S(2)}, u32[]{:S(2)}) collective-permute-start(bf16[1,128,512]{2,1,0:T(8,128)(2,1)S(1)} %fusion), channel_id=1, source_target_pairs={{0,1},{1,0},{2,3},{3,2},{4,5},{5,4},{6,7},{7,6},{8,9},{9,8},{10,11... | collective-permute-start | bytes 393224 | tf_op jit(solution)/shard_map/ppermute | solution.py:44
  18.0 2.3 %collective-permute-start.4 = (bf16[2048,128]{1,0:T(8,128)(2,1)}, bf16[2048,128]{1,0:T(8,128)(2,1)}, u32[]{:S(2)}, u32[]{:S(2)}) collective-permute-start(bf16[2048,128]{1,0:T(8,128)(2,1)} %collective-permute-done.1.mine), channel_id=1, source_target_pairs={{0,8},{8,0},{16,24},{24,16},{1,9},{9,1},{17,25},{25,17},{2,10},{10... | collective-permute-start | bytes 1572872 | tf_op jit(solution)/shard_map/ppermute | solution.py:166
  18.1 53.5 %collective-permute-start.18 = (bf16[2048,512]{1,0:T(8,128)(2,1)}, bf16[2048,512]{1,0:T(8,128)(2,1)}, u32[]{:S(2)}, u32[]{:S(2)}) collective-permute-start(bf16[2048,512]{1,0:T(8,128)(2,1)} %own.5), channel_id=1, source_target_pairs={{0,16},{8,24},{16,0},{24,8},{1,17},{9,25},{17,1},{25,9},{2,18},{10... | collective-permute-start | bytes 6291464 | tf_op jit(solution)/shard_map/ppermute | solution.py:166
  23.0 5.6 %collective-permute-start.5 = (bf16[1,128,512]{2,1,0:T(8,128)(2,1)S(1)}, bf16[1,128,512]{2,1,0:T(8,128)(2,1)S(1)}, u32[]{:S(2)}, u32[]{:S(2)}) collective-permute-start(bf16[1,128,512]{2,1,0:T(8,128)(2,1)S(1)} %fusion.1), channel_id=1, source_target_pairs={{0,1},{1,0},{2,3},{3,2},{4,5},{5,4},{6,7},{7,6},{8,9},{9,8},{10,11... | collective-permute-start | bytes 393224 | tf_op jit(solution)/shard_map/ppermute | solution.py:44
  24.9 15.8 %collective-permute-start.9 = (bf16[2,64,768]{2,1,0:T(8,128)(2,1)S(1)}, bf16[2,64,768]{2,1,0:T(8,128)(2,1)S(1)}, u32[]{:S(2)}, u32[]{:S(2)}) collective-permute-start(bf16[2,64,768]{2,1,0:T(8,128)(2,1)S(1)} %pad_maximum_fusion.7), channel_id=1, source_target_pairs={{0,4},{1,5},{2,6},{3,7},{4,0},{5,1},{6,2},{7,3},{8,12},{9,13},{10,... | collective-permute-start | bytes 589832 | tf_op jit(solution)/shard_map/ppermute | solution.py:174
  29.7 11.1 %collective-permute-start.6 = (bf16[2,32,512]{2,1,0:T(8,128)(2,1)S(1)}, bf16[2,32,512]{2,1,0:T(8,128)(2,1)S(1)}, u32[]{:S(2)}, u32[]{:S(2)}) collective-permute-start(bf16[2,32,512]{2,1,0:T(8,128)(2,1)S(1)} %get-tuple-element.80), channel_id=1, source_target_pairs={{0,2},{1,3},{2,0},{3,1},{4,6},{5,7},{6,4},{7,5},{8,10},{9,11},{10,... | collective-permute-start | bytes 196616 | tf_op jit(solution)/shard_map/ppermute | solution.py:53
  31.5 10.1 %collective-permute-start.7 = (bf16[2,32,512]{2,1,0:T(8,128)(2,1)S(1)}, bf16[2,32,512]{2,1,0:T(8,128)(2,1)S(1)}, u32[]{:S(2)}, u32[]{:S(2)}) collective-permute-start(bf16[2,32,512]{2,1,0:T(8,128)(2,1)S(1)} %get-tuple-element.82), channel_id=1, source_target_pairs={{0,4},{1,5},{2,6},{3,7},{4,0},{5,1},{6,2},{7,3},{8,12},{9,13},{10,... | collective-permute-start | bytes 196616 | tf_op jit(solution)/shard_map/ppermute | solution.py:53
  34.1 7.5 %collective-permute-start.8 = (bf16[2,32,512]{2,1,0:T(8,128)(2,1)S(1)}, bf16[2,32,512]{2,1,0:T(8,128)(2,1)S(1)}, u32[]{:S(2)}, u32[]{:S(2)}) collective-permute-start(bf16[2,32,512]{2,1,0:T(8,128)(2,1)S(1)} %get-tuple-element.81), channel_id=1, source_target_pairs={{0,6},{1,7},{2,4},{3,5},{4,2},{5,3},{6,0},{7,1},{8,14},{9,15},{10,... | collective-permute-start | bytes 196616 | tf_op jit(solution)/shard_map/ppermute | solution.py:53
  41.7 6.3 %collective-permute-start.10 = (bf16[2,32,512]{2,1,0:T(8,128)(2,1)S(1)}, bf16[2,32,512]{2,1,0:T(8,128)(2,1)S(1)}, u32[]{:S(2)}, u32[]{:S(2)}) collective-permute-start(bf16[2,32,512]{2,1,0:T(8,128)(2,1)S(1)} %add_convert_fusion.1), channel_id=1, source_target_pairs={{0,6},{1,7},{2,4},{3,5},{4,2},{5,3},{6,0},{7,1},{8,14},{9,15},{10,... | collective-permute-start | bytes 196616 | tf_op jit(solution)/shard_map/ppermute | solution.py:53
  44.7 6.4 %collective-permute-start.11 = (bf16[2,32,512]{2,1,0:T(8,128)(2,1)S(1)}, bf16[2,32,512]{2,1,0:T(8,128)(2,1)S(1)}, u32[]{:S(2)}, u32[]{:S(2)}) collective-permute-start(bf16[2,32,512]{2,1,0:T(8,128)(2,1)S(1)} %add_convert_fusion.1), channel_id=1, source_target_pairs={{0,4},{1,5},{2,6},{3,7},{4,0},{5,1},{6,2},{7,3},{8,12},{9,13},{10,... | collective-permute-start | bytes 196616 | tf_op jit(solution)/shard_map/ppermute | solution.py:53
  45.2 5.9 %collective-permute-start.12 = (bf16[2,32,512]{2,1,0:T(8,128)(2,1)S(1)}, bf16[2,32,512]{2,1,0:T(8,128)(2,1)S(1)}, u32[]{:S(2)}, u32[]{:S(2)}) collective-permute-start(bf16[2,32,512]{2,1,0:T(8,128)(2,1)S(1)} %add_convert_fusion.1), channel_id=1, source_target_pairs={{0,2},{1,3},{2,0},{3,1},{4,6},{5,7},{6,4},{7,5},{8,10},{9,11},{10,... | collective-permute-start | bytes 196616 | tf_op jit(solution)/shard_map/ppermute | solution.py:53
  46.1 8.0 %collective-permute-start.13 = (bf16[3,64,768]{2,1,0:T(8,128)(2,1)S(1)}, bf16[3,64,768]{2,1,0:T(8,128)(2,1)S(1)}, u32[]{:S(2)}, u32[]{:S(2)}) collective-permute-start(bf16[3,64,768]{2,1,0:T(8,128)(2,1)S(1)} %pad_maximum_fusion.1), channel_id=1, source_target_pairs={{0,1},{1,0},{2,3},{3,2},{4,5},{5,4},{6,7},{7,6},{8,9},{9,8},{10,11... | collective-permute-start | bytes 884744 | tf_op jit(solution)/shard_map/ppermute | solution.py:174
  51.1 17.2 %copy-start.2 = (bf16[2048,128]{1,0:T(8,128)(2,1)S(1)}, bf16[2048,128]{1,0:T(8,128)(2,1)}, u32[]{:S(2)}) copy-start(bf16[2048,128]{1,0:T(8,128)(2,1)} %mine.3) | copy-start | bytes 1572868
  51.2 17.2 %copy-start.4 = (bf16[2048,128]{1,0:T(8,128)(2,1)S(1)}, bf16[2048,128]{1,0:T(8,128)(2,1)}, u32[]{:S(2)}) copy-start(bf16[2048,128]{1,0:T(8,128)(2,1)} %copy-done.3) | copy-start | bytes 1572868
  54.2 6.5 %collective-permute-start.16 = (bf16[2,128,512]{2,1,0:T(8,128)(2,1)S(1)}, bf16[2,128,512]{2,1,0:T(8,128)(2,1)S(1)}, u32[]{:S(2)}, u32[]{:S(2)}) collective-permute-start(bf16[2,128,512]{2,1,0:T(8,128)(2,1)S(1)} %pad_maximum_fusion.2), channel_id=1, source_target_pairs={{0,1},{1,0},{2,3},{3,2},{4,5},{5,4},{6,7},{7,6},{8,9},{9,8},{10,11... | collective-permute-start | bytes 786440 | tf_op jit(solution)/shard_map/ppermute | solution.py:53
  54.8 13.5 %collective-permute-start.14 = (bf16[3,128,768]{2,1,0:T(8,128)(2,1)S(1)}, bf16[3,128,768]{2,1,0:T(8,128)(2,1)S(1)}, u32[]{:S(2)}, u32[]{:S(2)}) collective-permute-start(bf16[3,128,768]{2,1,0:T(8,128)(2,1)S(1)} %pad_maximum_fusion.one), channel_id=1, source_target_pairs={{0,2},{1,3},{2,0},{3,1},{4,6},{5,7},{6,4},{7,5},{8,10},{9,11},{10,... | collective-permute-start | bytes 1769480 | tf_op jit(solution)/shard_map/ppermute | solution.py:221
  60.8 13.1 %collective-permute-start.17 = (bf16[2,128,512]{2,1,0:T(8,128)(2,1)S(1)}, bf16[2,128,512]{2,1,0:T(8,128)(2,1)S(1)}, u32[]{:S(2)}, u32[]{:S(2)}) collective-permute-start(bf16[2,128,512]{2,1,0:T(8,128)(2,1)S(1)} %pad_maximum_fusion.3), channel_id=1, source_target_pairs={{0,16},{8,24},{16,0},{24,8},{1,17},{9,25},{17,1},{25,9},{2,18},{10... | collective-permute-start | bytes 786440 | tf_op jit(solution)/shard_map/ppermute | solution.py:166
  70.0 3.9 %collective-permute-start.15 = (f32[4,768]{1,0:T(4,128)S(1)}, f32[4,768]{1,0:T(4,128)S(1)}, u32[]{:S(2)}, u32[]{:S(2)}) collective-permute-start(f32[4,768]{1,0:T(4,128)S(1)} %get-tuple-element.40), channel_id=1, source_target_pairs={{0,16},{8,24},{16,0},{24,8},{1,17},{9,25},{17,1},{25,9},{2,18},{10... | collective-permute-start | bytes 36872 | tf_op jit(solution)/shard_map/ppermute | solution.py:166
  73.9 4.1 %copy-start.6 = (f32[4]{0:T(128)S(1)}, f32[4]{0:T(128)}, u32[]{:S(2)}) copy-start(f32[4]{0:T(128)} %occ.3) | copy-start | bytes 52
  76.1 2.0 %collective-permute-start.19 = (bf16[2048,128]{1,0:T(8,128)(2,1)S(1)}, bf16[2048,128]{1,0:T(8,128)(2,1)S(1)}, u32[]{:S(2)}, u32[]{:S(2)}) collective-permute-start(bf16[2048,128]{1,0:T(8,128)(2,1)S(1)} %get-tuple-element.47), channel_id=1, source_target_pairs={{0,8},{8,0},{16,24},{24,16},{1,9},{9,1},{17,25},{25,17},{2,10},{10... | collective-permute-start | bytes 1572872 | tf_op jit(solution)/shard_map/ppermute | solution.py:166
  79.1 2.0 %collective-permute-start.20 = (bf16[128,2048]{1,0:T(8,128)(2,1)S(1)}, bf16[128,2048]{1,0:T(8,128)(2,1)S(1)}, u32[]{:S(2)}, u32[]{:S(2)}) collective-permute-start(bf16[128,2048]{1,0:T(8,128)(2,1)S(1)} %shard_map.87.mine), channel_id=1, source_target_pairs={{0,8},{8,0},{16,24},{24,16},{1,9},{9,1},{17,25},{25,17},{2,10},{10... | collective-permute-start | bytes 1572872 | tf_op jit(solution)/shard_map/ppermute | solution.py:166
  81.8 5.6 %collective-permute-start.21 = (bf16[1,128,512]{2,1,0:T(8,128)(2,1)S(1)}, bf16[1,128,512]{2,1,0:T(8,128)(2,1)S(1)}, u32[]{:S(2)}, u32[]{:S(2)}) collective-permute-start(bf16[1,128,512]{2,1,0:T(8,128)(2,1)S(1)} %dynamic-slice_convert_fusion.1), channel_id=1, source_target_pairs={{0,1},{1,0},{2,3},{3,2},{4,5},{5,4},{6,7},{7,6},{8,9},{9,8},{10,11... | collective-permute-start | bytes 393224 | tf_op jit(solution)/shard_map/ppermute | solution.py:44
  85.1 5.3 %collective-permute-start.22 = (bf16[1,128,512]{2,1,0:T(8,128)(2,1)S(1)}, bf16[1,128,512]{2,1,0:T(8,128)(2,1)S(1)}, u32[]{:S(2)}, u32[]{:S(2)}) collective-permute-start(bf16[1,128,512]{2,1,0:T(8,128)(2,1)S(1)} %dynamic-slice_convert_fusion), channel_id=1, source_target_pairs={{0,1},{1,0},{2,3},{3,2},{4,5},{5,4},{6,7},{7,6},{8,9},{9,8},{10,11... | collective-permute-start | bytes 393224 | tf_op jit(solution)/shard_map/ppermute | solution.py:44
  85.7 4.8 %collective-permute-start.23 = (f32[4,768]{1,0:T(4,128)S(1)}, f32[4,768]{1,0:T(4,128)S(1)}, u32[]{:S(2)}, u32[]{:S(2)}) collective-permute-start(f32[4,768]{1,0:T(4,128)S(1)} %get-tuple-element.51), channel_id=1, source_target_pairs={{0,16},{8,24},{16,0},{24,8},{1,17},{9,25},{17,1},{25,9},{2,18},{10... | collective-permute-start | bytes 36872 | tf_op jit(solution)/shard_map/ppermute | solution.py:166
  90.6 4.7 %collective-permute-start.24 = (bf16[2,32,512]{2,1,0:T(8,128)(2,1)S(1)}, bf16[2,32,512]{2,1,0:T(8,128)(2,1)S(1)}, u32[]{:S(2)}, u32[]{:S(2)}) collective-permute-start(bf16[2,32,512]{2,1,0:T(8,128)(2,1)S(1)} %get-tuple-element.69), channel_id=1, source_target_pairs={{0,2},{1,3},{2,0},{3,1},{4,6},{5,7},{6,4},{7,5},{8,10},{9,11},{10,... | collective-permute-start | bytes 196616 | tf_op jit(solution)/shard_map/ppermute | solution.py:53
  92.4 6.4 %collective-permute-start.25 = (bf16[2,32,512]{2,1,0:T(8,128)(2,1)S(1)}, bf16[2,32,512]{2,1,0:T(8,128)(2,1)S(1)}, u32[]{:S(2)}, u32[]{:S(2)}) collective-permute-start(bf16[2,32,512]{2,1,0:T(8,128)(2,1)S(1)} %get-tuple-element.71), channel_id=1, source_target_pairs={{0,4},{1,5},{2,6},{3,7},{4,0},{5,1},{6,2},{7,3},{8,12},{9,13},{10,... | collective-permute-start | bytes 196616 | tf_op jit(solution)/shard_map/ppermute | solution.py:53
  93.8 6.2 %collective-permute-start.26 = (bf16[2,32,512]{2,1,0:T(8,128)(2,1)S(1)}, bf16[2,32,512]{2,1,0:T(8,128)(2,1)S(1)}, u32[]{:S(2)}, u32[]{:S(2)}) collective-permute-start(bf16[2,32,512]{2,1,0:T(8,128)(2,1)S(1)} %get-tuple-element.70), channel_id=1, source_target_pairs={{0,6},{1,7},{2,4},{3,5},{4,2},{5,3},{6,0},{7,1},{8,14},{9,15},{10,... | collective-permute-start | bytes 196616 | tf_op jit(solution)/shard_map/ppermute | solution.py:53
  100.1 6.1 %collective-permute-start.27 = (bf16[2,32,512]{2,1,0:T(8,128)(2,1)S(1)}, bf16[2,32,512]{2,1,0:T(8,128)(2,1)S(1)}, u32[]{:S(2)}, u32[]{:S(2)}) collective-permute-start(bf16[2,32,512]{2,1,0:T(8,128)(2,1)S(1)} %add_convert_fusion), channel_id=1, source_target_pairs={{0,6},{1,7},{2,4},{3,5},{4,2},{5,3},{6,0},{7,1},{8,14},{9,15},{10,... | collective-permute-start | bytes 196616 | tf_op jit(solution)/shard_map/ppermute | solution.py:53
  101.9 5.7 %collective-permute-start.28 = (bf16[2,32,512]{2,1,0:T(8,128)(2,1)S(1)}, bf16[2,32,512]{2,1,0:T(8,128)(2,1)S(1)}, u32[]{:S(2)}, u32[]{:S(2)}) collective-permute-start(bf16[2,32,512]{2,1,0:T(8,128)(2,1)S(1)} %add_convert_fusion), channel_id=1, source_target_pairs={{0,4},{1,5},{2,6},{3,7},{4,0},{5,1},{6,2},{7,3},{8,12},{9,13},{10,... | collective-permute-start | bytes 196616 | tf_op jit(solution)/shard_map/ppermute | solution.py:53
  102.4 5.2 %collective-permute-start.29 = (bf16[2,32,512]{2,1,0:T(8,128)(2,1)S(1)}, bf16[2,32,512]{2,1,0:T(8,128)(2,1)S(1)}, u32[]{:S(2)}, u32[]{:S(2)}) collective-permute-start(bf16[2,32,512]{2,1,0:T(8,128)(2,1)S(1)} %add_convert_fusion), channel_id=1, source_target_pairs={{0,2},{1,3},{2,0},{3,1},{4,6},{5,7},{6,4},{7,5},{8,10},{9,11},{10,... | collective-permute-start | bytes 196616 | tf_op jit(solution)/shard_map/ppermute | solution.py:53
  107.7 6.4 %collective-permute-start.30 = (bf16[2,128,512]{2,1,0:T(8,128)(2,1)S(1)}, bf16[2,128,512]{2,1,0:T(8,128)(2,1)S(1)}, u32[]{:S(2)}, u32[]{:S(2)}) collective-permute-start(bf16[2,128,512]{2,1,0:T(8,128)(2,1)S(1)} %pad_maximum_fusion.6.one), channel_id=1, source_target_pairs={{0,1},{1,0},{2,3},{3,2},{4,5},{5,4},{6,7},{7,6},{8,9},{9,8},{10,11... | collective-permute-start | bytes 786440 | tf_op jit(solution)/shard_map/ppermute | solution.py:53
  116.2 2.0 %collective-permute-start.31 = (bf16[2048,128]{1,0:T(8,128)(2,1)S(1)}, bf16[2048,128]{1,0:T(8,128)(2,1)S(1)}, u32[]{:S(2)}, u32[]{:S(2)}) collective-permute-start(bf16[2048,128]{1,0:T(8,128)(2,1)S(1)} %get-tuple-element.56), channel_id=1, source_target_pairs={{0,8},{8,0},{16,24},{24,16},{1,9},{9,1},{17,25},{25,17},{2,10},{10... | collective-permute-start | bytes 1572872 | tf_op jit(solution)/shard_map/ppermute | solution.py:166
